TPU v7x, 32 devices: a whole 2x2x4 slice. The times are simulated.
32 devices in a mesh: dp: 2 (over y), sp: 4 (over z), cp: 4 (over x, core).
Axes of the slice: x: 2, y: 2, z: 4, core: 2. Of those that a mesh axis runs over, the one named last changes fastest.
Arguments:
- tokens: bfloat16 [2, 4096, 1408], P('dp', ('sp', 'cp')), may hold values from -6 to 6
- skip_in: bfloat16 [2, 4096, 1408], P('dp', ('sp', 'cp')), may hold values from -6 to 6
- timestep: bfloat16 [2, 16, 1408], P('dp'), may hold values from -6 to 6
- captions: bfloat16 [2, 16, 333, 1024], P('dp', 'cp'), may hold values from -6 to 6
- null_mask: int32 [2, 16], P('dp'), may hold values 0 or 1
- lengths: int32 [2, 16], replicated, may hold values from 0 to 1024, as said below
- cotangent: bfloat16 [2, 4096, 1408], P('dp', ('sp', 'cp')), may hold values from -6 to 6
- skip_weight: bfloat16 [2816, 1408], P(('dp', 'sp', 'cp')), may hold values from -0.109375 to 0.109375
- shift_weight: bfloat16 [1408, 1408], P(('dp', 'sp', 'cp')), may hold values from -0.15625 to 0.15625
- self_input: bfloat16 [1408, 4224], P(('dp', 'sp', 'cp')), may hold values from -0.15625 to 0.15625
- self_output: bfloat16 [1408, 1408], P(('dp', 'sp', 'cp')), may hold values from -2.5 to 2.5
- cross_query: bfloat16 [1408, 1408], P(('dp', 'sp', 'cp')), may hold values from -0.15625 to 0.15625
- cross_pairs: bfloat16 [1024, 2816], P(('dp', 'sp', 'cp')), may hold values from -0.1875 to 0.1875
- cross_output: bfloat16 [1408, 1408], P(('dp', 'sp', 'cp')), may hold values from -2.5 to 2.5
- expand_weight: bfloat16 [1408, 6144], P(('dp', 'sp', 'cp')), may hold values from -0.15625 to 0.15625
- reduce_weight: bfloat16 [6144, 1408], P(None, ('dp', 'sp', 'cp')), may hold values from -0.078125 to 0.078125
- null_caption: bfloat16 [333, 1024], P(None, ('dp', 'sp', 'cp')), may hold values from -6 to 6
- norm_gains: bfloat16 [4, 1408], P(None, ('dp', 'sp', 'cp')), may hold values from 0.5 to 1.5
Outputs:
- block_out: bfloat16 [2, 4096, 1408], P('dp', ('sp', 'cp'))
- token_grad: bfloat16 [2, 4096, 1408], P('dp', ('sp', 'cp'))
- skip_grad: bfloat16 [2, 4096, 1408], P('dp', ('sp', 'cp'))
- skip_weight_grad: float32 [2816, 1408], P(('dp', 'sp', 'cp'))
- shift_weight_grad: float32 [1408, 1408], P(('dp', 'sp', 'cp'))
- self_input_grad: float32 [1408, 4224], P(('dp', 'sp', 'cp'))
- self_output_grad: float32 [1408, 1408], P(('dp', 'sp', 'cp'))
- cross_query_grad: float32 [1408, 1408], P(('dp', 'sp', 'cp'))
- cross_pairs_grad: float32 [1024, 2816], P(('dp', 'sp', 'cp'))
- cross_output_grad: float32 [1408, 1408], P(('dp', 'sp', 'cp'))
- expand_weight_grad: float32 [1408, 6144], P(('dp', 'sp', 'cp'))
- reduce_weight_grad: float32 [6144, 1408], P(None, ('dp', 'sp', 'cp'))
- null_caption_grad: float32 [333, 1024], P(None, ('dp', 'sp', 'cp'))
- norm_gains_grad: float32 [4, 1408], P(None, ('dp', 'sp', 'cp'))
Inputs may be any that keep to these rules, and one draw needn't show every extreme that they name: `lengths`: row k lists the patch counts of the images of pack k in order, each 256 or 1024, followed by zeros; every pack has at least one image of 1024 patches and at least one zero; the tokens after the last image of a pack, if any, are padding.
All inputs are finite; a program needn't handle non-finite values. No bound on the sum of `null_mask` on one device may be relied on, other than what follows from the above.
Results may differ from a plain program's by a relative error of at most 0.022.
Values may be sent and summed in bfloat16 or wider, within the bound.
No kernel may reach another device: no remote copies, remote signals or barrier semaphores. Data moves between devices by JAX's collectives and lax.ppermute only.
A program may use at most 384 MiB of HBM per device.

v0:
```python
import math

import jax
import jax.numpy as jnp
from jax import lax
from jax.sharding import PartitionSpec as P

D = 1408
HEADS = 16
HEAD = 88
DT = 1024
TEXT = 333
BIG_SIDE = 32
SMALL_SIDE = 16
PACK = 4096
IMGS = 16


epsilon = 1e-06
highest = lax.Precision.HIGHEST


def layer_norm(vector):
    centred = vector - jnp.mean(vector, axis=-1, keepdims=True)
    return centred * lax.rsqrt(jnp.mean(centred * centred, axis=-1, keepdims=True) + epsilon)


def norm_gain(vector, gain):
    return layer_norm(vector) * gain


def segment_info(lengths, positions):
    seg_ends = jnp.cumsum(lengths)
    starts = seg_ends - lengths
    present = lengths > 0
    slot_ids = jnp.arange(lengths.shape[0], dtype=jnp.int32)
    segment = jnp.sum(
        ((seg_ends[None, :] <= positions[:, None]) & present[None, :]).astype(jnp.int32), axis=1
    )
    onehot = segment[:, None] == slot_ids[None, :]
    seg_start = jnp.sum(jnp.where(onehot, starts[None, :], 0), axis=1)
    seg_size = jnp.sum(jnp.where(onehot, lengths[None, :], 0), axis=1)
    side_len = jnp.where(seg_size == BIG_SIDE * BIG_SIDE, BIG_SIDE, SMALL_SIDE).astype(jnp.int32)
    offset = positions - seg_start
    images = jnp.sum(present.astype(jnp.int32))
    return (segment, offset // side_len, offset % side_len, (segment < images).astype(jnp.float32))


def rope_tables(grid_row, grid_col):
    quarter = HEAD // 4
    frequency = jnp.exp(jnp.arange(quarter, dtype=jnp.float32) * (-math.log(10000.0) / quarter))
    angles = jnp.stack(
        [
            grid_row.astype(jnp.float32)[:, None] * frequency,
            grid_col.astype(jnp.float32)[:, None] * frequency,
        ],
        axis=1,
    )
    return (jnp.cos(angles), jnp.sin(angles))


def rotate(vector, cosine, sines):
    quarter = HEAD // 4
    split = vector.reshape(vector.shape[:-1] + (2, 2, quarter))
    former = split[..., 0, :]
    latter = split[..., 1, :]
    cosine = jnp.expand_dims(cosine, -3)
    sines = jnp.expand_dims(sines, -3)
    turned = jnp.stack(
        [former * cosine - latter * sines, former * sines + latter * cosine], axis=-2
    )
    return turned.reshape(vector.shape)


def matmul(left, right):
    return jnp.dot(left, right, preferred_element_type=jnp.float32)


def matmul_back(left, right):
    return lax.dot_general(
        left, right, (((left.ndim - 1,), (1,)), ((), ())), preferred_element_type=jnp.float32
    )


def outer_sum(left, right):
    flat_left = left.reshape(-1, left.shape[-1])
    flat_right = right.reshape(-1, right.shape[-1])
    return lax.dot_general(
        flat_left, flat_right, (((0,), (0,)), ((), ())), preferred_element_type=jnp.float32
    )


def self_forward(query_mat, key_mat, value_mat, query_seg, key_seg):
    scaling = 1.0 / math.sqrt(HEAD)

    def piece_step(piece_id, carried):
        key_here = key_mat[piece_id]
        value_here = value_mat[piece_id]
        seg_here = key_seg[piece_id]

        def compute(current):
            summed, totals = current
            scores = (
                jnp.einsum("qhe,khe->hqk", query_mat, key_here, preferred_element_type=jnp.float32)
                * scaling
            )
            weights = jnp.where(
                query_seg[None, :, None] == seg_here[None, None, :], jnp.exp(scores), 0.0
            )
            summed = summed + jnp.einsum(
                "hqk,khe->qhe",
                weights.astype(jnp.bfloat16),
                value_here,
                preferred_element_type=jnp.float32,
            )
            return (summed, totals + jnp.sum(weights, axis=-1))

        return compute(carried)

    initial = (
        jnp.zeros(query_mat.shape, jnp.float32),
        jnp.zeros((query_mat.shape[1], query_mat.shape[0]), jnp.float32),
    )
    return lax.fori_loop(0, key_mat.shape[0], piece_step, initial)


def self_backward(query_mat, key_mat, value_mat, query_seg, key_seg, grad_out, out_full, totals):
    scaling = 1.0 / math.sqrt(HEAD)
    grad_float = grad_out.astype(jnp.float32)
    scaled_grad = (grad_float / jnp.transpose(totals)[:, :, None]).astype(jnp.bfloat16)
    total_grad = jnp.transpose(-jnp.sum(grad_float * out_full, axis=-1) / jnp.transpose(totals))

    def piece_step(piece_id, carried):
        key_here = key_mat[piece_id]
        value_here = value_mat[piece_id]
        seg_here = key_seg[piece_id]

        def compute(current):
            query_grad, key_grads, value_grads = current
            scores = (
                jnp.einsum("qhe,khe->hqk", query_mat, key_here, preferred_element_type=jnp.float32)
                * scaling
            )
            weights = jnp.where(
                query_seg[None, :, None] == seg_here[None, None, :], jnp.exp(scores), 0.0
            )
            weight_grad = jnp.einsum(
                "qhe,khe->hqk", scaled_grad, value_here, preferred_element_type=jnp.float32
            )
            score_grad = (weights * (weight_grad + total_grad[:, :, None])).astype(jnp.bfloat16)
            query_grad = (
                query_grad
                + jnp.einsum(
                    "hqk,khe->qhe", score_grad, key_here, preferred_element_type=jnp.float32
                )
                * scaling
            )
            key_piece = (
                jnp.einsum(
                    "hqk,qhe->khe", score_grad, query_mat, preferred_element_type=jnp.float32
                )
                * scaling
            )
            value_piece = jnp.einsum(
                "hqk,qhe->khe",
                weights.astype(jnp.bfloat16),
                scaled_grad,
                preferred_element_type=jnp.float32,
            )
            return (
                query_grad,
                key_grads.at[piece_id].set(key_piece),
                value_grads.at[piece_id].set(value_piece),
            )

        return compute(carried)

    initial = (
        jnp.zeros(query_mat.shape, jnp.float32),
        jnp.zeros(key_mat.shape, jnp.float32),
        jnp.zeros(value_mat.shape, jnp.float32),
    )
    return lax.fori_loop(0, key_mat.shape[0], piece_step, initial)


def cross_forward(query_blocks, key_blocks, value_blocks):
    scaling = 1.0 / math.sqrt(HEAD)
    scores = (
        jnp.einsum(
            "pbqhe,pbthe->pbhqt", query_blocks, key_blocks, preferred_element_type=jnp.float32
        )
        * scaling
    )
    weights = jnp.exp(scores)
    totals = jnp.sum(weights, axis=-1)
    summed = jnp.einsum(
        "pbhqt,pbthe->pbqhe",
        weights.astype(jnp.bfloat16),
        value_blocks,
        preferred_element_type=jnp.float32,
    )
    return (summed / jnp.swapaxes(totals, 2, 3)[..., None], totals)


def cross_backward(query_blocks, key_blocks, value_blocks, grad_out, out_full, totals):
    scaling = 1.0 / math.sqrt(HEAD)
    grad_float = grad_out.astype(jnp.float32)
    scaled_grad = (grad_float / jnp.swapaxes(totals, 2, 3)[..., None]).astype(jnp.bfloat16)
    total_grad = jnp.swapaxes(
        -jnp.sum(grad_float * out_full, axis=-1) / jnp.swapaxes(totals, 2, 3), 2, 3
    )
    scores = (
        jnp.einsum(
            "pbqhe,pbthe->pbhqt", query_blocks, key_blocks, preferred_element_type=jnp.float32
        )
        * scaling
    )
    weights = jnp.exp(scores)
    weight_grad = jnp.einsum(
        "pbqhe,pbthe->pbhqt", scaled_grad, value_blocks, preferred_element_type=jnp.float32
    )
    score_grad = (weights * (weight_grad + total_grad[..., None])).astype(jnp.bfloat16)
    query_grad = (
        jnp.einsum("pbhqt,pbthe->pbqhe", score_grad, key_blocks, preferred_element_type=jnp.float32)
        * scaling
    )
    key_grad = (
        jnp.einsum(
            "pbhqt,pbqhe->pbthe", score_grad, query_blocks, preferred_element_type=jnp.float32
        )
        * scaling
    )
    value_grad = jnp.einsum(
        "pbhqt,pbqhe->pbthe",
        weights.astype(jnp.bfloat16),
        scaled_grad,
        preferred_element_type=jnp.float32,
    )
    return (query_grad, key_grad, value_grad)


def shards(
    tokens,
    skip_in,
    timestep,
    captions,
    null_mask,
    lengths,
    cotangent,
    skip_weight,
    shift_weight,
    self_input,
    self_output,
    cross_query,
    cross_pairs,
    cross_output,
    expand_weight,
    reduce_weight,
    null_caption,
    norm_gains,
):
    gathered = (
        lax.all_gather(skip_weight, ("dp", "sp", "cp"), axis=0, tiled=True),
        lax.all_gather(shift_weight, ("dp", "sp", "cp"), axis=0, tiled=True),
        lax.all_gather(self_input, ("dp", "sp", "cp"), axis=0, tiled=True),
        lax.all_gather(self_output, ("dp", "sp", "cp"), axis=0, tiled=True),
        lax.all_gather(cross_query, ("dp", "sp", "cp"), axis=0, tiled=True),
        lax.all_gather(cross_pairs, ("dp", "sp", "cp"), axis=0, tiled=True),
        lax.all_gather(cross_output, ("dp", "sp", "cp"), axis=0, tiled=True),
        lax.all_gather(expand_weight, ("dp", "sp", "cp"), axis=0, tiled=True),
        lax.all_gather(reduce_weight, ("dp", "sp", "cp"), axis=1, tiled=True),
        lax.all_gather(null_caption, ("dp", "sp", "cp"), axis=1, tiled=True),
        lax.all_gather(norm_gains, ("dp", "sp", "cp"), axis=1, tiled=True),
    )
    (
        skip_full,
        shift_full,
        input_full,
        output_full,
        query_full,
        pairs_full,
        cross_full,
        expand_full,
        reduce_full,
        caption_full,
        gain_full,
    ) = gathered
    gain_rows = gain_full.astype(jnp.float32)
    sp_count = lax.axis_size("sp")
    cp_count = lax.axis_size("cp")
    sp_index = lax.axis_index("sp")
    cp_index = lax.axis_index("cp")
    dp_index = lax.axis_index("dp")
    pack_count = tokens.shape[0]
    seg_rows = tokens.shape[1]
    heads_dev = HEADS // sp_count
    width_dev = heads_dev * HEAD
    head_rows = sp_count * seg_rows
    own_lengths = lax.dynamic_slice_in_dim(lengths, dp_index * pack_count, pack_count, 0)
    within = jnp.arange(seg_rows, dtype=jnp.int32)
    block_ids = jnp.arange(sp_count, dtype=jnp.int32)
    piece_ids = jnp.arange(cp_count, dtype=jnp.int32)
    token_pos = (sp_index * cp_count + cp_index) * seg_rows + within
    head_pos = ((block_ids[:, None] * cp_count + cp_index) * seg_rows + within[None, :]).reshape(-1)
    key_pos = (
        (block_ids[None, :, None] * cp_count + piece_ids[:, None, None]) * seg_rows
        + within[None, None, :]
    ).reshape(-1)
    describe = jax.vmap(segment_info, in_axes=(0, None))
    token_seg, token_row, token_col, token_valid = describe(own_lengths, token_pos)
    head_seg = describe(own_lengths, head_pos)[0]
    key_seg = describe(own_lengths, key_pos)[0].reshape(pack_count, cp_count, head_rows)
    slot_ids = jnp.arange(IMGS, dtype=jnp.int32)
    block_pick = (token_seg[:, 0][:, None] == slot_ids[None, :]).astype(jnp.float32)
    time_rows = jnp.einsum(
        "pi,pid->pd", block_pick, timestep.astype(jnp.float32), precision=highest
    )
    silu_rows = jax.nn.silu(time_rows).astype(jnp.bfloat16)
    shifts = matmul(silu_rows, shift_full)
    joined = jnp.concatenate([tokens, skip_in], axis=2)
    mixed = matmul(joined, skip_full)
    base_stream = norm_gain(mixed, gain_rows[0])
    normed_self = (norm_gain(base_stream, gain_rows[1]) + shifts[:, None, :]).astype(jnp.bfloat16)
    projected = matmul(normed_self, input_full)
    cosine, sines = rope_tables(token_row.reshape(-1), token_col.reshape(-1))
    cosine = cosine.reshape(pack_count, seg_rows, 2, HEAD // 4)
    sines = sines.reshape(pack_count, seg_rows, 2, HEAD // 4)

    def turn_norm(raw_part):
        shaped = raw_part.reshape(pack_count, seg_rows, HEADS, HEAD)
        return rotate(layer_norm(shaped), cosine, sines).reshape(pack_count, seg_rows, D)

    query_raw = projected[..., :D]
    key_raw = projected[..., D : 2 * D]
    queries = turn_norm(query_raw).astype(jnp.bfloat16)
    key_rows = turn_norm(key_raw).astype(jnp.bfloat16)
    value_rows = projected[..., 2 * D :].astype(jnp.bfloat16)
    query_heads, key_heads, value_heads = (
        lax.all_to_all(queries, "sp", split_axis=2, concat_axis=1, tiled=True),
        lax.all_to_all(key_rows, "sp", split_axis=2, concat_axis=1, tiled=True),
        lax.all_to_all(value_rows, "sp", split_axis=2, concat_axis=1, tiled=True),
    )
    image_dev = captions.shape[1]
    own_null = lax.dynamic_slice_in_dim(null_mask, cp_index * image_dev, image_dev, 1)
    chosen = jnp.where(own_null[:, :, None, None] > 0, caption_full[None, None], captions)
    pair_cols = jnp.concatenate(
        [
            lax.dynamic_slice_in_dim(pairs_full, sp_index * width_dev, width_dev, 1),
            lax.dynamic_slice_in_dim(pairs_full, D + sp_index * width_dev, width_dev, 1),
        ],
        axis=1,
    )
    paired = matmul(chosen, pair_cols)
    text_raw = paired[..., :width_dev].reshape(pack_count, image_dev, TEXT, heads_dev, HEAD)
    text_keys = (
        layer_norm(text_raw).astype(jnp.bfloat16).reshape(pack_count, image_dev, TEXT, width_dev)
    )
    text_values = paired[..., width_dev:].astype(jnp.bfloat16)
    key_all, value_all, text_key_all, text_value_all = (
        lax.all_gather(key_heads, "cp", axis=1, tiled=True),
        lax.all_gather(value_heads, "cp", axis=1, tiled=True),
        lax.all_gather(text_keys, "cp", axis=1, tiled=True),
        lax.all_gather(text_values, "cp", axis=1, tiled=True),
    )
    query_mats = query_heads.reshape(pack_count, head_rows, heads_dev, HEAD)
    key_mats = key_all.reshape(pack_count, cp_count, head_rows, heads_dev, HEAD)
    value_mats = value_all.reshape(pack_count, cp_count, head_rows, heads_dev, HEAD)

    def attend_pack(member):
        return self_forward(member[0], member[1], member[2], member[3], member[4])

    summed_self, totals_self = lax.map(
        attend_pack, (query_mats, key_mats, value_mats, head_seg, key_seg)
    )
    out_self = summed_self / jnp.swapaxes(totals_self, 1, 2)[..., None]
    attended = lax.all_to_all(
        out_self.astype(jnp.bfloat16).reshape(pack_count, head_rows, width_dev),
        "sp",
        split_axis=1,
        concat_axis=2,
        tiled=True,
    )
    mid_stream = base_stream + matmul(attended, output_full)
    normed_cross = norm_gain(mid_stream, gain_rows[2]).astype(jnp.bfloat16)
    cross_raw = matmul(normed_cross, query_full).reshape(pack_count, seg_rows, HEADS, HEAD)
    cross_queries = layer_norm(cross_raw).astype(jnp.bfloat16).reshape(pack_count, seg_rows, D)
    cross_heads = lax.all_to_all(cross_queries, "sp", split_axis=2, concat_axis=1, tiled=True)
    block_image = head_seg.reshape(pack_count, sp_count, seg_rows)[:, :, 0]
    pick_rows = jax.vmap(lambda lookup, chosen_ids: jnp.take(lookup, chosen_ids, axis=0))
    key_blocks = pick_rows(text_key_all, block_image).reshape(
        pack_count, sp_count, TEXT, heads_dev, HEAD
    )
    value_blocks = pick_rows(text_value_all, block_image).reshape(
        pack_count, sp_count, TEXT, heads_dev, HEAD
    )
    cross_blocks = cross_heads.reshape(pack_count, sp_count, seg_rows, heads_dev, HEAD)
    out_cross, totals_cross = cross_forward(cross_blocks, key_blocks, value_blocks)
    crossed = lax.all_to_all(
        out_cross.astype(jnp.bfloat16).reshape(pack_count, head_rows, width_dev),
        "sp",
        split_axis=1,
        concat_axis=2,
        tiled=True,
    )
    late_stream = mid_stream + matmul(crossed, cross_full)
    normed_ffn = norm_gain(late_stream, gain_rows[3]).astype(jnp.bfloat16)
    expanded = matmul(normed_ffn, expand_full)
    hidden = jax.nn.gelu(expanded, approximate=True).astype(jnp.bfloat16)
    block_out = (late_stream + matmul(hidden, reduce_full)).astype(jnp.bfloat16)
    out_grad = cotangent.astype(jnp.float32) * token_valid[:, :, None]
    reduce_in = out_grad.astype(jnp.bfloat16)
    reduce_grad = outer_sum(hidden, reduce_in)
    gelu_back = jax.vjp(lambda preact: jax.nn.gelu(preact, approximate=True), expanded)[1]
    expand_in = gelu_back(matmul_back(reduce_in, reduce_full))[0].astype(jnp.bfloat16)
    expand_grad = outer_sum(normed_ffn, expand_in)
    ffn_back = jax.vjp(norm_gain, late_stream, gain_rows[3])[1]
    late_part, gain_ffn = ffn_back(matmul_back(expand_in, expand_full))
    late_grad = out_grad + late_part
    cout_in = late_grad.astype(jnp.bfloat16)
    cross_out_grad = outer_sum(crossed, cout_in)
    crossed_grad = matmul_back(cout_in, cross_full).astype(jnp.bfloat16)
    crossed_heads = lax.all_to_all(
        crossed_grad, "sp", split_axis=2, concat_axis=1, tiled=True
    ).reshape(pack_count, sp_count, seg_rows, heads_dev, HEAD)
    cq_grad, ck_block_grad, cv_block_grad = cross_backward(
        cross_blocks, key_blocks, value_blocks, crossed_heads, out_cross, totals_cross
    )
    cq_tokens = lax.all_to_all(
        cq_grad.astype(jnp.bfloat16).reshape(pack_count, head_rows, width_dev),
        "sp",
        split_axis=1,
        concat_axis=2,
        tiled=True,
    )
    cq_norm_back = jax.vjp(layer_norm, cross_raw)[1]
    cross_raw_grad = cq_norm_back(
        cq_tokens.astype(jnp.float32).reshape(pack_count, seg_rows, HEADS, HEAD)
    )[0]
    cross_raw_grad = cross_raw_grad.reshape(pack_count, seg_rows, D).astype(jnp.bfloat16)
    cross_query_grad = outer_sum(normed_cross, cross_raw_grad)
    cross_norm_back = jax.vjp(norm_gain, mid_stream, gain_rows[2])[1]
    mid_part, gain_cross = cross_norm_back(matmul_back(cross_raw_grad, query_full))
    mid_grad = late_grad + mid_part
    self_in = mid_grad.astype(jnp.bfloat16)
    self_out_grad = outer_sum(attended, self_in)
    attended_grad = matmul_back(self_in, output_full).astype(jnp.bfloat16)
    attended_heads = lax.all_to_all(
        attended_grad, "sp", split_axis=2, concat_axis=1, tiled=True
    ).reshape(pack_count, head_rows, heads_dev, HEAD)

    def back_pack(member):
        return self_backward(
            member[0], member[1], member[2], member[3], member[4], member[5], member[6], member[7]
        )

    query_grads, key_grads, value_grads = lax.map(
        back_pack,
        (
            query_mats,
            key_mats,
            value_mats,
            head_seg,
            key_seg,
            attended_heads,
            out_self,
            totals_self,
        ),
    )
    image_pick = (block_image[:, :, None] == slot_ids[None, None, :]).astype(jnp.float32)
    text_key_grads = jnp.einsum(
        "pbi,pbthe->pithe", image_pick, ck_block_grad, precision=highest
    ).reshape(pack_count, IMGS, TEXT, width_dev)
    text_value_grads = jnp.einsum(
        "pbi,pbthe->pithe", image_pick, cv_block_grad, precision=highest
    ).reshape(pack_count, IMGS, TEXT, width_dev)
    key_sums, value_sums, text_key_sums, text_value_sums = (
        lax.psum_scatter(
            key_grads.reshape(pack_count, cp_count * head_rows, width_dev).astype(jnp.bfloat16),
            "cp",
            scatter_dimension=1,
            tiled=True,
        ).astype(jnp.float32),
        lax.psum_scatter(
            value_grads.reshape(pack_count, cp_count * head_rows, width_dev).astype(jnp.bfloat16),
            "cp",
            scatter_dimension=1,
            tiled=True,
        ).astype(jnp.float32),
        lax.psum_scatter(
            text_key_grads.astype(jnp.bfloat16), "cp", scatter_dimension=1, tiled=True
        ).astype(jnp.float32),
        lax.psum_scatter(
            text_value_grads.astype(jnp.bfloat16), "cp", scatter_dimension=1, tiled=True
        ).astype(jnp.float32),
    )
    query_back, key_back, value_back = (
        lax.all_to_all(
            query_grads.astype(jnp.bfloat16).reshape(pack_count, head_rows, width_dev),
            "sp",
            split_axis=1,
            concat_axis=2,
            tiled=True,
        ),
        lax.all_to_all(
            key_sums.astype(jnp.bfloat16), "sp", split_axis=1, concat_axis=2, tiled=True
        ),
        lax.all_to_all(
            value_sums.astype(jnp.bfloat16), "sp", split_axis=1, concat_axis=2, tiled=True
        ),
    )
    query_turn_back = jax.vjp(turn_norm, query_raw)[1]
    key_turn_back = jax.vjp(turn_norm, key_raw)[1]
    query_raw_grad = query_turn_back(query_back.astype(jnp.float32))[0].astype(jnp.bfloat16)
    key_raw_grad = key_turn_back(key_back.astype(jnp.float32))[0].astype(jnp.bfloat16)
    projected_grad = jnp.concatenate([query_raw_grad, key_raw_grad, value_back], axis=2)
    self_input_grad = outer_sum(normed_self, projected_grad)
    normed_self_grad = matmul_back(projected_grad, input_full)
    self_norm_back = jax.vjp(norm_gain, base_stream, gain_rows[1])[1]
    base_part, gain_self = self_norm_back(normed_self_grad)
    shift_grads = jnp.sum(normed_self_grad, axis=1)
    shift_weight_grad = jnp.dot(
        jnp.transpose(silu_rows.astype(jnp.float32)), shift_grads, precision=highest
    )
    base_grad = mid_grad + base_part
    skip_norm_back = jax.vjp(norm_gain, mixed, gain_rows[0])[1]
    mixed_grad, gain_skip = skip_norm_back(base_grad)
    mixed_in = mixed_grad.astype(jnp.bfloat16)
    skip_weight_grad = outer_sum(joined, mixed_in)
    joined_grad = matmul_back(mixed_in, skip_full)
    text_norm_back = jax.vjp(layer_norm, text_raw)[1]
    text_key_in = (
        text_key_sums.astype(jnp.bfloat16)
        .astype(jnp.float32)
        .reshape(pack_count, image_dev, TEXT, heads_dev, HEAD)
    )
    text_raw_grad = (
        text_norm_back(text_key_in)[0]
        .reshape(pack_count, image_dev, TEXT, width_dev)
        .astype(jnp.bfloat16)
    )
    paired_grad = jnp.concatenate([text_raw_grad, text_value_sums.astype(jnp.bfloat16)], axis=3)
    pair_grad_cols = outer_sum(chosen, paired_grad)
    pairs_grad = jnp.zeros((DT, 2 * D), jnp.float32)
    pairs_grad = lax.dynamic_update_slice_in_dim(
        pairs_grad, pair_grad_cols[:, :width_dev], sp_index * width_dev, 1
    )
    pairs_grad = lax.dynamic_update_slice_in_dim(
        pairs_grad, pair_grad_cols[:, width_dev:], D + sp_index * width_dev, 1
    )
    null_sum = jnp.einsum(
        "pi,pitc->tc",
        own_null.astype(jnp.float32),
        paired_grad.astype(jnp.float32),
        precision=highest,
    )
    caption_grad = jnp.dot(
        null_sum, jnp.transpose(pair_cols.astype(jnp.float32)), precision=highest
    )
    gains_grad = jnp.stack([gain_skip, gain_self, gain_cross, gain_ffn])
    reduced = (
        lax.psum_scatter(skip_weight_grad, ("dp", "sp", "cp"), scatter_dimension=0, tiled=True),
        lax.psum_scatter(shift_weight_grad, ("dp", "sp", "cp"), scatter_dimension=0, tiled=True),
        lax.psum_scatter(self_input_grad, ("dp", "sp", "cp"), scatter_dimension=0, tiled=True),
        lax.psum_scatter(self_out_grad, ("dp", "sp", "cp"), scatter_dimension=0, tiled=True),
        lax.psum_scatter(cross_query_grad, ("dp", "sp", "cp"), scatter_dimension=0, tiled=True),
        lax.psum_scatter(pairs_grad, ("dp", "sp", "cp"), scatter_dimension=0, tiled=True),
        lax.psum_scatter(cross_out_grad, ("dp", "sp", "cp"), scatter_dimension=0, tiled=True),
        lax.psum_scatter(expand_grad, ("dp", "sp", "cp"), scatter_dimension=0, tiled=True),
        lax.psum_scatter(reduce_grad, ("dp", "sp", "cp"), scatter_dimension=1, tiled=True),
        lax.psum_scatter(caption_grad, ("dp", "sp", "cp"), scatter_dimension=1, tiled=True),
        lax.psum_scatter(gains_grad, ("dp", "sp", "cp"), scatter_dimension=1, tiled=True),
    )
    factor = lengths.shape[0] * PACK / jnp.sum(lengths).astype(jnp.float32)
    token_grad = (joined_grad[..., :D] * factor).astype(jnp.bfloat16)
    skip_grad = (joined_grad[..., D:] * factor).astype(jnp.bfloat16)
    return (
        block_out,
        token_grad,
        skip_grad,
        reduced[0] * factor,
        reduced[1] * factor,
        reduced[2] * factor,
        reduced[3] * factor,
        reduced[4] * factor,
        reduced[5] * factor,
        reduced[6] * factor,
        reduced[7] * factor,
        reduced[8] * factor,
        reduced[9] * factor,
        reduced[10] * factor,
    )


def solution(mesh):
    placed = (
        P("dp", ("sp", "cp"), None),
        P("dp", ("sp", "cp"), None),
        P("dp", None, None),
        P("dp", "cp", None, None),
        P("dp", None),
        P(),
        P("dp", ("sp", "cp"), None),
        P(("dp", "sp", "cp"), None),
        P(("dp", "sp", "cp"), None),
        P(("dp", "sp", "cp"), None),
        P(("dp", "sp", "cp"), None),
        P(("dp", "sp", "cp"), None),
        P(("dp", "sp", "cp"), None),
        P(("dp", "sp", "cp"), None),
        P(("dp", "sp", "cp"), None),
        P(None, ("dp", "sp", "cp")),
        P(None, ("dp", "sp", "cp")),
        P(None, ("dp", "sp", "cp")),
    )
    return jax.shard_map(
        shards,
        mesh=mesh,
        in_specs=placed,
        out_specs=(
            P("dp", ("sp", "cp"), None),
            P("dp", ("sp", "cp"), None),
            P("dp", ("sp", "cp"), None),
            P(("dp", "sp", "cp"), None),
            P(("dp", "sp", "cp"), None),
            P(("dp", "sp", "cp"), None),
            P(("dp", "sp", "cp"), None),
            P(("dp", "sp", "cp"), None),
            P(("dp", "sp", "cp"), None),
            P(("dp", "sp", "cp"), None),
            P(("dp", "sp", "cp"), None),
            P(None, ("dp", "sp", "cp")),
            P(None, ("dp", "sp", "cp")),
            P(None, ("dp", "sp", "cp")),
        ),
        check_vma=False,
    )
```

profile of v0, /device:TPU:0, one launch (start us, length us, event | category | flops | bytes accessed | tf_op | source)
XLA Modules:
  0.0 3663.8 jit_solution(7538446920761488472)
XLA Ops:
  13.6 43.5 %all-gather = bf16[32,44,4]{1,2,0:T(4,128)(2,1)S(1)} all-gather(bf16[1,44,4]{1,2,0:T(4,128)(2,1)} %bitcast.622), channel_id=1, replica_groups=mesh['dp'=2,'sp'=4,'cp'=4] {'dp','sp','cp'}, dimensions={0}, use_global_device_ids=true | all-gather | bytes 11616 | tf_op jit(solution)/shard_map/all_gather | solution.py:273
  57.9 18.4 all-gather.34.cloned.1.call-done
  85.1 67.9 %all-gather.22.cloned.1.call-done = bf16[2816,1408]{1,0:T(8,128)(2,1)} async-done(((bf16[88,1408]{1,0:T(8,128)(2,1)}), bf16[2816,1408]{1,0:T(8,128)(2,1)}) %all-gather.22.cloned.1.call-update) | async-done | bytes 7929872 | tf_op jit(solution)/shard_map/all_gather | solution.py:263
  160.7 91.8 %all-gather.36.cloned.1.call-done = bf16[32,44,4224]{2,1,0:T(8,128)(2,1)} async-done(((bf16[1,44,4224]{2,1,0:T(8,128)(2,1)}), bf16[32,44,4224]{2,1,0:T(8,128)(2,1)}) %all-gather.36.cloned.1.call-update) | async-done | bytes 11894800 | tf_op jit(solution)/shard_map/all_gather | solution.py:265
  252.5 15.7 reshape.2444
  297.9 34.4 all-to-all-done
  379.3 22.1 all_to_all.159
  406.5 40.1 %all_gather.52 = bf16[333,1024]{0,1:T(8,128)(2,1)S(1)} all-gather(bf16[333,32]{0,1:T(8,128)(2,1)S(1)} %copy-done.133), channel_id=1, replica_groups=mesh['dp'=2,'sp'=4,'cp'=4] {'dp','sp','cp'}, dimensions={1}, use_global_device_ids=true | all-gather | bytes 703296 | tf_op jit(solution)/shard_map/all_gather | solution.py:272
  502.1 21.8 all-to-all-done.2
  550.5 84.4 %while.56 = (s32[]{:T(128)}, f32[1024,4,88]{0,2,1:T(8,128)}, f32[4,1024]{1,0:T(4,128)S(1)}, bf16[4,1024,4,88]{1,3,2,0:T(8,128)(2,1)}, s32[1024]{0:T(1024)S(1)}, ...) while((s32[]{:T(128)}, f32[1024,4,88]{0,2,1:T(8,128)}, ...), condition=%wide.region_16.17_spmd.clone, body=%wide.region_14.16_spmd.clone.sunk | while | flops 1503334400 | bytes 41828480 | solution.py:124
  560.5 10.6 select_add_fusion.4
  571.9 9.6 fusion.250
  581.5 11.0 select_add_fusion.4
  602.5 11.0 select_add_fusion.4
  623.5 11.0 select_add_fusion.4
  705.4 9.4 reduce.103
  736.7 15.3 all-to-all-done.4
  792.6 26.8 all-to-all-done.5
  834.6 21.9 all-gather.44.cloned.1.call-done
  856.5 19.3 reshape.2452
  875.8 10.9 fusion.171
  886.7 98.0 %all-gather.46.cloned.1.call-done = bf16[32,44,6144]{2,1,0:T(8,128)(2,1)} async-done(((bf16[1,44,6144]{2,1,0:T(8,128)(2,1)}), bf16[32,44,6144]{2,1,0:T(8,128)(2,1)}) %all-gather.46.cloned.1.call-update) | async-done | bytes 17301520 | tf_op jit(solution)/shard_map/all_gather | solution.py:271
  984.7 19.1 reshape.2454
  1003.8 14.0 fusion.57
  1017.8 19.9 multiply_reduce_fusion.2
  1061.8 23.8 all_to_all.160
  1135.9 23.3 all_to_all.161
  1235.6 153.9 %while.57 = (s32[]{:T(128)}, f32[1024,4,88]{0,2,1:T(8,128)}, bf16[4,1024,4,88]{1,3,2,0:T(8,128)(2,1)}, bf16[4,1024,4,88]{1,3,2,0:T(8,128)(2,1)}, bf16[4,1024,4,8...) while((s32[]{:T(128)}, f32[1024,4,88]{0,2,1:T(8,128)}, ...), condition=%wide.region_37.39_spmd.clone, body=%wide.region_35.38_spmd.clone.sunk | while | flops 3727753216 | bytes 197234480 | solution.py:183
  1242.1 9.9 fusion.262
  1280.4 9.8 fusion.262
  1318.8 9.8 fusion.262
  1357.3 9.8 fusion.262
  1624.9 18.8 fusion.170
  1648.2 704.2 %fusion.175 = (f32[48,1408]{1,0:T(8,128)S(1)}, f32[48,6144]{1,0:T(8,128)}) fusion(f32[1408,1408]{1,0:T(8,128)} %fusion.186, f32[1408,6144]{1,0:T(8,128)} %fusion.170), kind=kCustom, calls=%all-reduce-scatter.8 | all-reduce-scatter fusion | flops 11599873 | bytes 43982848
  2353.0 20.2 collective-permute-start.13
  2384.3 19.1 fusion.124
  2403.4 411.1 %fusion.6 = f32[6144,48]{0,1:T(8,128)} fusion(f32[6144,1408]{0,1:T(8,128)} %fusion.124), kind=kCustom, calls=%all-reduce-scatter.6 | all-reduce-scatter fusion | flops 9437185 | bytes 35782656
  2816.6 34.6 collective-permute-start.15
  2860.2 18.2 fusion.63
  2881.6 19.9 concatenate.49
  2901.6 19.9 concatenate.50
  2939.7 10.3 fusion.108
  2950.0 521.6 %fusion.174 = (f32[48,1408]{1,0:T(8,128)S(1)}, f32[48,4224]{1,0:T(8,128)S(1)}, f32[48,1408]{1,0:T(8,128)S(1)}, f32[48,1408]{1,0:T(8,128)S(1)}) fusion(f32[1408,1408]{1,0:T(8,128)} %broadcast_multiply_fusion, f32[1408,4224]{1,0:T(8,128)} %fusion.108, f32[1408,1408]{1,0:T(8,128)} %fusion.118, f32[1408,1408]{1,0:T(8,128)} %fusion.168), kind=kCustom, calls=%all-reduce-scatter.7 | all-reduce-scatter fusion | flops 12976129 | bytes 49201152
  3471.6 40.0 %collective-permute-start.1 = (f32[48,1408]{1,0:T(8,128)S(1)}, f32[48,1408]{1,0:T(8,128)}, u32[]{:S(2)}, u32[]{:S(2)}) collective-permute-start(f32[48,1408]{1,0:T(8,128)S(1)} %get-tuple-element.707), channel_id=1, source_target_pairs={{0,2},{1,3},{2,4},{3,5},{4,6},{5,7},{6,8},{7,9},{8,10},{9,11},{10,... | collective-permute-start | bytes 811016
  3542.5 38.1 %all-reduce.12 = f32[4,1408]{1,0:T(4,128)S(1)} all-reduce(f32[4,1408]{1,0:T(4,128)S(1)} %pad_maximum_fusion.6), channel_id=16, replica_groups=mesh['dp'=2,'sp'=4,'cp'=4] {'dp','sp','cp'}, use_global_device_ids=true, to_apply=%region_68.70.clone | all-reduce | flops 5632 | bytes 45056
  3603.8 9.8 collective-permute-done.11
  3613.6 15.8 collective-permute-start.5
  3636.5 14.2 concatenate.45
  (815 shorter events, 979.0 us)
Async XLA Ops:
  7.2 69.0 %all-gather.34.cloned.1.call-start = ((), (), s32[]{:S(2)}) async-start(), calls=%async_computation.31 | async-start | bytes 4460544 | tf_op jit(solution)/shard_map/all_gather | solution.py:264
  7.9 145.1 %all-gather.22.cloned.1.call-start = ((), (), s32[]{:S(2)}) async-start(), calls=%async_computation.19 | async-start | bytes 8177664 | tf_op jit(solution)/shard_map/all_gather | solution.py:263
  8.7 243.8 %all-gather.36.cloned.1.call-start = ((), (), s32[]{:S(2)}) async-start(), calls=%async_computation.32 | async-start | bytes 13381632 | tf_op jit(solution)/shard_map/all_gather | solution.py:265
  9.4 442.4 %all-gather.28.cloned.1.call-start = ((), (), s32[]{:S(2)}) async-start(), calls=%async_computation.22 | async-start | bytes 5947392 | tf_op jit(solution)/shard_map/all_gather | solution.py:268
  293.1 39.2 %all-to-all-start = ((bf16[4,2,45056]{2,1,0:T(2,128)(2,1)}), bf16[4,2,45056]{2,1,0:T(2,128)(2,1)}, u32[]{:S(2)}, u32[]{:S(2)}) async-start(bf16[4,2,45056]{2,1,0:T(2,128)(2,1)} %reshape.2492), calls=%async_computation | async-start | bytes 1441792 | tf_op jit(solution)/shard_map/all_to_all | solution.py:341
  297.3 230.2 %all-gather.24.cloned.1.call-start = ((), (), s32[]{:S(2)}) async-start(), calls=%async_computation.20 | async-start | bytes 3604480 | tf_op jit(solution)/shard_map/all_gather | solution.py:361
  335.9 203.3 %all-gather.26.cloned.1.call-start = ((), (), s32[]{:S(2)}) async-start(), calls=%async_computation.21 | async-start | bytes 3604480 | tf_op jit(solution)/shard_map/all_gather | solution.py:360
  404.9 247.8 %all-gather.38.cloned.1.call-start = ((), (), s32[]{:S(2)}) async-start(), calls=%async_computation.33 | async-start | bytes 4460544 | tf_op jit(solution)/shard_map/all_gather | solution.py:266
  405.7 253.1 %all-gather.40.cloned.1.call-start = ((), (), s32[]{:S(2)}) async-start(), calls=%async_computation.34 | async-start | bytes 4460544 | tf_op jit(solution)/shard_map/all_gather | solution.py:267
  406.4 314.7 %all-gather.32.cloned.1.call-start = ((), (), s32[]{:S(2)}) async-start(), calls=%async_computation.24 | async-start | bytes 5160960 | tf_op jit(solution)/shard_map/all_gather | solution.py:362
  481.8 243.3 %all-gather.30.cloned.1.call-start = ((), (), s32[]{:S(2)}) async-start(), calls=%async_computation.23 | async-start | bytes 5160960 | tf_op jit(solution)/shard_map/all_gather | solution.py:363
  485.0 301.3 %all-gather.42.cloned.1.call-start = ((), (), s32[]{:S(2)}) async-start(), calls=%async_computation.35 | async-start | bytes 4460544 | tf_op jit(solution)/shard_map/all_gather | solution.py:269
  485.7 370.8 %all-gather.44.cloned.1.call-start = ((), (), s32[]{:S(2)}) async-start(), calls=%async_computation.36 | async-start | bytes 19464192 | tf_op jit(solution)/shard_map/all_gather | solution.py:270
  486.3 498.3 %all-gather.46.cloned.1.call-start = ((), (), s32[]{:S(2)}) async-start(), calls=%async_computation.37 | async-start | bytes 19464192 | tf_op jit(solution)/shard_map/all_gather | solution.py:271
  497.3 26.6 all-to-all-start.2
  648.4 24.9 all-to-all-start.3
  716.7 35.4 all-to-all-start.4
  781.4 38.0 %all-to-all-start.5 = ((bf16[4,2,45056]{2,1,0:T(2,128)(2,1)}), bf16[4,2,45056]{2,1,0:T(2,128)(2,1)}, u32[]{:S(2)}, u32[]{:S(2)}) async-start(bf16[4,2,45056]{2,1,0:T(2,128)(2,1)} %reshape.2502), calls=%async_computation.5 | async-start | bytes 1441792 | tf_op jit(solution)/shard_map/all_to_all | solution.py:398
  785.6 623.9 %reduce-scatter.30.cloned.1.call-start = ((), (), s32[]{:S(2)}) async-start(), calls=%async_computation.27 | async-start | bytes 5160960 | tf_op jit(solution)/shard_map/reduce_scatter | solution.py:489
  1203.8 21.5 all-to-all-start.8
  1207.3 220.7 %reduce-scatter.32.cloned.1.call-start = ((), (), s32[]{:S(2)}) async-start(), calls=%async_computation.28 | async-start | bytes 5160960 | tf_op jit(solution)/shard_map/reduce_scatter | solution.py:492
  1222.5 263.6 %reduce-scatter.28.cloned.1.call-start = ((), (), s32[]{:S(2)}) async-start(), calls=%async_computation.26 | async-start | bytes 3604480 | tf_op jit(solution)/shard_map/reduce_scatter | solution.py:483
  1396.9 112.2 %reduce-scatter.26.cloned.1.call-start = ((), (), s32[]{:S(2)}) async-start(), calls=%async_computation.25 | async-start | bytes 3604480 | tf_op jit(solution)/shard_map/reduce_scatter | solution.py:477
  1409.5 2223.9 %reduce-scatter.36.cloned.1.call-start = ((), (), s32[]{:S(2)}) async-start(), calls=%async_computation.30 | async-start | bytes 1622016 | tf_op jit(solution)/shard_map/reduce_scatter | solution.py:570
  1438.0 2214.9 %reduce-scatter.34.cloned.1.call-start = ((), (), s32[]{:S(2)}) async-start(), calls=%async_computation.29 | async-start | bytes 11894784 | tf_op jit(solution)/shard_map/reduce_scatter | solution.py:566
  1481.5 22.9 all-to-all-start.9
  1504.4 24.4 all-to-all-start.11
  1528.8 25.3 all-to-all-start.10
  1533.0 2121.6 %reduce-scatter.38.cloned.1.call-start = ((), (), s32[]{:S(2)}) async-start(), calls=%async_computation.38 | async-start | bytes 16355328
  2353.0 498.2 %collective-permute-start.13 = (f32[48,1408]{1,0:T(8,128)S(1)}, f32[48,1408]{1,0:T(8,128)S(1)}, u32[]{:S(2)}, u32[]{:S(2)}) collective-permute-start(f32[48,1408]{1,0:T(8,128)S(1)} %get-tuple-element.713), channel_id=1, source_target_pairs={{0,2},{1,3},{2,4},{3,5},{4,6},{5,7},{6,8},{7,9},{8,10},{9,11},{10,... | collective-permute-start | bytes 811016
  2373.2 482.3 %collective-permute-start.12 = (f32[48,1408]{1,0:T(8,128)S(1)}, f32[48,1408]{1,0:T(8,128)}, u32[]{:S(2)}, u32[]{:S(2)}) collective-permute-start(f32[48,1408]{1,0:T(8,128)S(1)} %get-tuple-element.713), channel_id=1, source_target_pairs={{0,1},{1,2},{2,3},{3,4},{4,5},{5,6},{6,7},{7,8},{8,9},{9,10},{10,1... | collective-permute-start | bytes 811016
  2377.4 504.3 %collective-permute-start.16 = (f32[48,6144]{1,0:T(8,128)}, f32[48,6144]{1,0:T(8,128)}, u32[]{:S(2)}, u32[]{:S(2)}) collective-permute-start(f32[48,6144]{1,0:T(8,128)} %get-tuple-element.714), channel_id=1, source_target_pairs={{0,2},{1,3},{2,4},{3,5},{4,6},{5,7},{6,8},{7,9},{8,10},{9,11},{10,... | collective-permute-start | bytes 3538952
  2380.1 436.5 %collective-permute-start.14 = (f32[28,1408]{1,0:T(8,128)}, f32[28,1408]{1,0:T(8,128)}, u32[]{:S(2)}, u32[]{:S(2)}) collective-permute-start(f32[28,1408]{1,0:T(8,128)} %slice.204), channel_id=1, source_target_pairs={{0,3},{1,4},{2,5},{3,6},{4,7},{5,8},{6,9},{7,10},{8,11},{9,12},{10... | collective-permute-start | bytes 473096
  2382.1 475.9 %collective-permute-start.17 = (f32[28,6144]{1,0:T(8,128)}, f32[28,6144]{1,0:T(8,128)}, u32[]{:S(2)}, u32[]{:S(2)}) collective-permute-start(f32[28,6144]{1,0:T(8,128)} %slice.205), channel_id=1, source_target_pairs={{0,3},{1,4},{2,5},{3,6},{4,7},{5,8},{6,9},{7,10},{8,11},{9,12},{10... | collective-permute-start | bytes 2064392
  2816.6 65.0 %collective-permute-start.15 = (f32[48,6144]{1,0:T(8,128)}, f32[48,6144]{1,0:T(8,128)}, u32[]{:S(2)}, u32[]{:S(2)}) collective-permute-start(f32[48,6144]{1,0:T(8,128)} %get-tuple-element.714), channel_id=1, source_target_pairs={{0,1},{1,2},{2,3},{3,4},{4,5},{5,6},{6,7},{7,8},{8,9},{9,10},{10,1... | collective-permute-start | bytes 3538952
  2851.2 50.3 %collective-permute-start.19 = (f32[6144,48]{0,1:T(8,128)}, f32[6144,48]{0,1:T(8,128)}, u32[]{:S(2)}, u32[]{:S(2)}) collective-permute-start(f32[6144,48]{0,1:T(8,128)} %fusion.6), channel_id=1, source_target_pairs={{0,2},{1,3},{2,4},{3,5},{4,6},{5,7},{6,8},{7,9},{8,10},{9,11},{10,... | collective-permute-start | bytes 3538952
  2855.6 46.0 %collective-permute-start.18 = (f32[6144,48]{0,1:T(8,128)}, f32[6144,48]{0,1:T(8,128)}, u32[]{:S(2)}, u32[]{:S(2)}) collective-permute-start(f32[6144,48]{0,1:T(8,128)} %fusion.6), channel_id=1, source_target_pairs={{0,1},{1,2},{2,3},{3,4},{4,5},{5,6},{6,7},{7,8},{8,9},{9,10},{10,1... | collective-permute-start | bytes 3538952
  2858.0 43.5 %collective-permute-start.20 = (f32[6144,28]{0,1:T(8,128)}, f32[6144,28]{0,1:T(8,128)}, u32[]{:S(2)}, u32[]{:S(2)}) collective-permute-start(f32[6144,28]{0,1:T(8,128)} %slice.206), channel_id=1, source_target_pairs={{0,3},{1,4},{2,5},{3,6},{4,7},{5,8},{6,9},{7,10},{8,11},{9,12},{10... | collective-permute-start | bytes 2064392
  3471.6 109.7 %collective-permute-start.1 = (f32[48,1408]{1,0:T(8,128)S(1)}, f32[48,1408]{1,0:T(8,128)}, u32[]{:S(2)}, u32[]{:S(2)}) collective-permute-start(f32[48,1408]{1,0:T(8,128)S(1)} %get-tuple-element.707), channel_id=1, source_target_pairs={{0,2},{1,3},{2,4},{3,5},{4,6},{5,7},{6,8},{7,9},{8,10},{9,11},{10,... | collective-permute-start | bytes 811016
  3511.6 74.8 %collective-permute-start = (f32[48,1408]{1,0:T(8,128)S(1)}, f32[48,1408]{1,0:T(8,128)}, u32[]{:S(2)}, u32[]{:S(2)}) collective-permute-start(f32[48,1408]{1,0:T(8,128)S(1)} %get-tuple-element.707), channel_id=1, source_target_pairs={{0,1},{1,2},{2,3},{3,4},{4,5},{5,6},{6,7},{7,8},{8,9},{9,10},{10,1... | collective-permute-start | bytes 811016
  3513.6 80.3 %collective-permute-start.7 = (f32[48,1408]{1,0:T(8,128)S(1)}, f32[48,1408]{1,0:T(8,128)S(1)}, u32[]{:S(2)}, u32[]{:S(2)}) collective-permute-start(f32[48,1408]{1,0:T(8,128)S(1)} %get-tuple-element.709), channel_id=1, source_target_pairs={{0,2},{1,3},{2,4},{3,5},{4,6},{5,7},{6,8},{7,9},{8,10},{9,11},{10,... | collective-permute-start | bytes 811016
  3522.7 76.0 %collective-permute-start.6 = (f32[48,1408]{1,0:T(8,128)S(1)}, f32[48,1408]{1,0:T(8,128)}, u32[]{:S(2)}, u32[]{:S(2)}) collective-permute-start(f32[48,1408]{1,0:T(8,128)S(1)} %get-tuple-element.709), channel_id=1, source_target_pairs={{0,1},{1,2},{2,3},{3,4},{4,5},{5,6},{6,7},{7,8},{8,9},{9,10},{10,1... | collective-permute-start | bytes 811016
  3536.1 55.7 %collective-permute-start.8 = (f32[28,1408]{1,0:T(8,128)S(1)}, f32[28,1408]{1,0:T(8,128)}, u32[]{:S(2)}, u32[]{:S(2)}) collective-permute-start(f32[28,1408]{1,0:T(8,128)S(1)} %slice.202), channel_id=1, source_target_pairs={{0,3},{1,4},{2,5},{3,6},{4,7},{5,8},{6,9},{7,10},{8,11},{9,12},{10... | collective-permute-start | bytes 473096
  3581.3 55.2 %collective-permute-start.4 = (f32[48,4224]{1,0:T(8,128)S(1)}, f32[48,4224]{1,0:T(8,128)}, u32[]{:S(2)}, u32[]{:S(2)}) collective-permute-start(f32[48,4224]{1,0:T(8,128)S(1)} %get-tuple-element.708), channel_id=1, source_target_pairs={{0,2},{1,3},{2,4},{3,5},{4,6},{5,7},{6,8},{7,9},{8,10},{9,11},{10,... | collective-permute-start | bytes 2433032
  3586.4 50.2 %collective-permute-start.3 = (f32[48,4224]{1,0:T(8,128)S(1)}, f32[48,4224]{1,0:T(8,128)}, u32[]{:S(2)}, u32[]{:S(2)}) collective-permute-start(f32[48,4224]{1,0:T(8,128)S(1)} %get-tuple-element.708), channel_id=1, source_target_pairs={{0,1},{1,2},{2,3},{3,4},{4,5},{5,6},{6,7},{7,8},{8,9},{9,10},{10,1... | collective-permute-start | bytes 2433032
  3591.9 38.3 %collective-permute-start.10 = (f32[48,1408]{1,0:T(8,128)S(1)}, f32[48,1408]{1,0:T(8,128)S(1)}, u32[]{:S(2)}, u32[]{:S(2)}) collective-permute-start(f32[48,1408]{1,0:T(8,128)S(1)} %get-tuple-element.710), channel_id=1, source_target_pairs={{0,2},{1,3},{2,4},{3,5},{4,6},{5,7},{6,8},{7,9},{8,10},{9,11},{10,... | collective-permute-start | bytes 811016
  3593.9 36.2 collective-permute-start.9
  3613.6 22.9 collective-permute-start.5
  (168 other events, 7073.4 us)
Sparse Core Ops, SparseCore 0:
  10.9 65.2 all-gather.33
  79.2 73.8 all-gather.21
  155.9 96.5 all-gather.35
  255.3 78.8 all-gather.27
  336.2 25.0 all-gather.23
  405.0 28.9 all-gather.25
  437.0 62.9 all-gather.37
  502.9 65.0 all-gather.39
  570.1 32.3 all-gather.31
  604.5 34.1 all-gather.29
  641.5 69.8 all-gather.41
  714.1 142.3 all-gather.43
  859.4 125.2 all-gather.45
  1113.0 42.2 reduce-scatter.29
  1222.6 44.4 reduce-scatter.31
  1397.0 34.5 reduce-scatter.27
  1434.1 36.3 reduce-scatter.25
  1475.5 98.5 reduce-scatter.35
  1576.4 221.5 reduce-scatter.33
  1800.2 355.4 reduce-scatter.37
where the time goes:
time: 3690 us; the launch traced here: 3660 us
  blocking collectives  1830 us (50%)
  local copies, waits for them, and re-layouts  508 us (14%)
  matrix products  447 us (12%)
  waiting for transfers between devices  439 us (12%)
  other arithmetic  216 us (6%)
  starting transfers between devices  207 us (6%)
    unnamed x4, blocking collectives  1680 us
    unnamed x359, local copies, waits for them, and re-layouts  251 us
    unnamed x22, starting transfers between devices  167 us
    all_gather x1, waiting for transfers between devices, shards(): lax.all_gather(reduce_weight, ('dp', 'sp', 'cp'), axis=1, tiled=True)  98 us
    all_gather x1, waiting for transfers between devices, shards(): lax.all_gather(self_input, ('dp', 'sp', 'cp'), axis=0, tiled=True)  91.8 us
    unnamed x17, other arithmetic  89.9 us
    dot_general x8, matrix products, outer_sum(): lax.dot_general(flat_left, flat_right, (((0,), (0,)), ((), ())), preferre...  74.7 us
  transfers between devices with their start and end apart: 50, of which 15 were waited for; matrix products, arithmetic and copies ran while one was open for 73% of the time, Pallas kernels for 0%

commit v1 on v0

v1 whole, which is shorter than its diff:
```python
import functools
import math

import jax
import jax.numpy as jnp
from jax import lax
from jax.experimental import pallas as pl
from jax.experimental.pallas import tpu as pltpu
from jax.sharding import PartitionSpec as P

D = 1408
HEADS = 16
HEAD = 88
DT = 1024
TEXT = 333
TEXT_PAD = 384
BIG_SIDE = 32
SMALL_SIDE = 16
PACK = 4096
IMGS = 16
CELL = 256
CELLS = PACK // CELL
SCALING = 1.0 / math.sqrt(HEAD)

epsilon = 1e-06
highest = lax.Precision.HIGHEST
bf16 = jnp.bfloat16
f32 = jnp.float32
GROUP = ("dp", "sp")
EVERY = ("dp", "sp", "cp")
HEAD_ORDER = ("cp", "sp")


def layer_norm(vector, axis=-1):
    centred = vector - jnp.mean(vector, axis=axis, keepdims=True)
    return centred * lax.rsqrt(jnp.mean(centred * centred, axis=axis, keepdims=True) + epsilon)


def head_norm(vector):
    return layer_norm(vector, -2)


def norm_gain(vector, gain):
    return layer_norm(vector) * gain


def dot(left, right, left_dim, right_dim):
    return lax.dot_general(
        left, right, (((left_dim,), (right_dim,)), ((), ())), preferred_element_type=f32
    )


def segment_info(lengths, positions):
    seg_ends = jnp.cumsum(lengths)
    starts = seg_ends - lengths
    present = lengths > 0
    slot_ids = jnp.arange(lengths.shape[0], dtype=jnp.int32)
    segment = jnp.sum(
        ((seg_ends[None, :] <= positions[:, None]) & present[None, :]).astype(jnp.int32), axis=1
    )
    onehot = segment[:, None] == slot_ids[None, :]
    seg_start = jnp.sum(jnp.where(onehot, starts[None, :], 0), axis=1)
    seg_size = jnp.sum(jnp.where(onehot, lengths[None, :], 0), axis=1)
    side_len = jnp.where(seg_size == BIG_SIDE * BIG_SIDE, BIG_SIDE, SMALL_SIDE).astype(jnp.int32)
    offset = positions - seg_start
    images = jnp.sum(present.astype(jnp.int32))
    return (segment, offset // side_len, offset % side_len, (segment < images).astype(f32))


def cell_ranges(lengths):
    positions = jnp.arange(CELLS, dtype=jnp.int32) * CELL
    seg_ends = jnp.cumsum(lengths)
    present = lengths > 0
    segment = jnp.sum(
        ((seg_ends[None, :] <= positions[:, None]) & present[None, :]).astype(jnp.int32), axis=1
    )
    same = segment[:, None] == segment[None, :]
    cells = jnp.arange(CELLS, dtype=jnp.int32)
    first = jnp.min(jnp.where(same, cells[None, :], CELLS), axis=1)
    last = jnp.max(jnp.where(same, cells[None, :] + 1, 0), axis=1)
    return (first, last, jnp.sum(lengths) // CELL)


def rope_tables(grid_row, grid_col):
    quarter = HEAD // 4
    frequency = jnp.exp(jnp.arange(quarter, dtype=f32) * (-math.log(10000.0) / quarter))
    angles = jnp.concatenate(
        [
            frequency[:, None] * grid_row.astype(f32)[None, :],
            frequency[:, None] * grid_col.astype(f32)[None, :],
        ],
        axis=0,
    )
    return (jnp.cos(angles), jnp.sin(angles))


def rotate(vector, cosine, sines):
    quarter = HEAD // 4
    one, two, three, four = (
        vector[..., k * quarter : (k + 1) * quarter, :] for k in range(4)
    )
    cos_row, cos_col = cosine[..., :quarter, :], cosine[..., quarter:, :]
    sin_row, sin_col = sines[..., :quarter, :], sines[..., quarter:, :]
    return jnp.concatenate(
        [
            one * cos_row - two * sin_row,
            one * sin_row + two * cos_row,
            three * cos_col - four * sin_col,
            three * sin_col + four * cos_col,
        ],
        axis=-2,
    )


def turn_norm(vector, cosine, sines):
    return rotate(head_norm(vector), cosine, sines)


def swap_core(value):
    return lax.ppermute(value, "cp", [(0, 1), (1, 0), (2, 3), (3, 2)])


def swap_chip(value):
    return lax.ppermute(value, "cp", [(0, 2), (2, 0), (1, 3), (3, 1)])


def gather_cp(value):
    count = lax.axis_size("cp")
    if count != 4:
        return lax.all_gather(value, "cp", axis=0, tiled=False)
    index = lax.axis_index("cp")
    chip, core = index // 2, index % 2
    other = swap_chip(value)
    pair = jnp.where(chip == 0, jnp.stack([value, other]), jnp.stack([other, value]))
    second = swap_core(pair)
    return jnp.where(
        core == 0, jnp.stack([pair, second], axis=1), jnp.stack([second, pair], axis=1)
    ).reshape((4,) + value.shape)


def scatter_cp(partial):
    count = lax.axis_size("cp")
    partial = partial.astype(bf16)
    if count != 4:
        return lax.psum_scatter(partial, "cp", scatter_dimension=0, tiled=False).astype(f32)
    index = lax.axis_index("cp")
    chip, core = index // 2, index % 2
    parts = partial.reshape((2, 2) + partial.shape[1:])
    keep = lax.dynamic_index_in_dim(parts, core, 1, keepdims=False)
    send = lax.dynamic_index_in_dim(parts, 1 - core, 1, keepdims=False)
    both = (keep.astype(f32) + swap_core(send).astype(f32)).astype(bf16)
    keep = lax.dynamic_index_in_dim(both, chip, 0, keepdims=False)
    send = lax.dynamic_index_in_dim(both, 1 - chip, 0, keepdims=False)
    return keep.astype(f32) + swap_chip(send).astype(f32)


def trade_cp(blocks):
    return lax.all_to_all(blocks, "cp", split_axis=0, concat_axis=0, tiled=True)


def flip(block):
    return jnp.transpose(block.astype(f32)).astype(bf16)


def kernel_dot(left, right, left_dim=1, right_dim=0):
    return lax.dot_general(
        left, right, (((left_dim,), (right_dim,)), ((), ())), preferred_element_type=f32
    )


def over_cells(first, last, step, carry):
    count = last - first
    fours = count // 4

    def four(turn, current):
        for k in range(4):
            current = step(first + turn * 4 + k, current)
        return current

    carry = lax.fori_loop(0, fours, four, carry)
    return lax.fori_loop(first + fours * 4, last, step, carry)


def self_forward_kernel(first_ref, last_ref, qkv_ref, out_ref, total_ref, keys):
    pair = pl.program_id(0)
    per = qkv_ref.shape[-1] // CELL

    def where(cell):
        return cell // per, pl.ds(pl.multiple_of((cell % per) * CELL, CELL), CELL)

    def turn_keys(cell, carry):
        chunk, lanes = where(cell)
        keys[cell] = flip(qkv_ref[chunk, 0, 1, :, lanes])
        return carry

    lax.fori_loop(0, CELLS, turn_keys, 0)

    def one_cell(cell, carry):
        chunk, lanes = where(cell)
        query = qkv_ref[chunk, 0, 0, :, lanes]

        def step(other, current):
            summed, totals = current
            key_chunk, key_lanes = where(other)
            weights = jnp.exp(kernel_dot(keys[other], query) * SCALING)
            totals = totals + jnp.sum(weights, axis=0, keepdims=True)
            summed = summed + kernel_dot(
                qkv_ref[key_chunk, 0, 2, :, key_lanes], weights.astype(bf16)
            )
            return (summed, totals)

        summed, totals = over_cells(
            first_ref[pair, cell],
            last_ref[pair, cell],
            step,
            (jnp.zeros((HEAD, CELL), f32), jnp.zeros((1, CELL), f32)),
        )
        out_ref[chunk, 0, :, lanes] = summed / totals
        total_ref[chunk, 0, :, lanes] = totals
        return carry

    lax.fori_loop(0, CELLS, one_cell, 0)


def self_backward_kernel(
    first_ref,
    last_ref,
    valid_ref,
    qkv_ref,
    grad_ref,
    out_ref,
    total_ref,
    result_ref,
    keys,
    values,
    key_sums,
    value_sums,
):
    pair = pl.program_id(0)
    per = qkv_ref.shape[-1] // CELL

    def where(cell):
        return cell // per, pl.ds(pl.multiple_of((cell % per) * CELL, CELL), CELL)

    def prepare(cell, carry):
        chunk, lanes = where(cell)
        keys[cell] = flip(qkv_ref[chunk, 0, 1, :, lanes])
        values[cell] = flip(qkv_ref[chunk, 0, 2, :, lanes])
        key_sums[cell] = jnp.zeros((HEAD, CELL), f32)
        value_sums[cell] = jnp.zeros((HEAD, CELL), f32)
        result_ref[chunk, 0, 0, :, lanes] = jnp.zeros((HEAD, CELL), bf16)
        return carry

    lax.fori_loop(0, CELLS, prepare, 0)

    def one_cell(cell, carry):
        chunk, lanes = where(cell)
        query = qkv_ref[chunk, 0, 0, :, lanes]
        grad = grad_ref[chunk, 0, :, lanes].astype(f32)
        inverse = 1.0 / total_ref[chunk, 0, :, lanes]
        scaled = (grad * inverse).astype(bf16)
        total_grad = (
            -jnp.sum(grad * out_ref[chunk, 0, :, lanes], axis=0, keepdims=True) * inverse
        )

        def step(other, query_sum):
            key_chunk, key_lanes = where(other)
            weights = jnp.exp(kernel_dot(keys[other], query) * SCALING)
            weight_grad = kernel_dot(values[other], scaled)
            score_grad = (weights * (weight_grad + total_grad)).astype(bf16)
            value_sums[other] += kernel_dot(scaled, weights.astype(bf16), 1, 1)
            key_sums[other] += kernel_dot(query, score_grad, 1, 1)
            return query_sum + kernel_dot(qkv_ref[key_chunk, 0, 1, :, key_lanes], score_grad)

        query_sum = over_cells(
            first_ref[pair, cell], last_ref[pair, cell], step, jnp.zeros((HEAD, CELL), f32)
        )
        result_ref[chunk, 0, 0, :, lanes] = (query_sum * SCALING).astype(bf16)
        return carry

    lax.fori_loop(0, valid_ref[pair], one_cell, 0)

    def finish(cell, carry):
        chunk, lanes = where(cell)
        result_ref[chunk, 0, 1, :, lanes] = (key_sums[cell] * SCALING).astype(bf16)
        result_ref[chunk, 0, 2, :, lanes] = value_sums[cell].astype(bf16)
        return carry

    lax.fori_loop(0, CELLS, finish, 0)


def pair_spec(shape):
    block = (shape[0], 1) + shape[2:]
    rest = (0,) * (len(shape) - 2)
    return pl.BlockSpec(block, lambda pair, *_: (0, pair) + rest)


VMEM_LIMIT = 40 * 1024 * 1024


def self_forward(qkv, first, last):
    chunks, pairs, _, _, columns = qkv.shape
    out_shape = (chunks, pairs, HEAD, columns)
    total_shape = (chunks, pairs, 1, columns)
    return pl.pallas_call(
        self_forward_kernel,
        out_shape=(
            jax.ShapeDtypeStruct(out_shape, f32),
            jax.ShapeDtypeStruct(total_shape, f32),
        ),
        grid_spec=pltpu.PrefetchScalarGridSpec(
            num_scalar_prefetch=2,
            grid=(pairs,),
            in_specs=[pair_spec(qkv.shape)],
            out_specs=[pair_spec(out_shape), pair_spec(total_shape)],
            scratch_shapes=[pltpu.VMEM((CELLS, CELL, HEAD), bf16)],
        ),
        compiler_params=pltpu.CompilerParams(vmem_limit_bytes=VMEM_LIMIT),
        name="self_forward",
    )(first, last, qkv)


def self_backward(qkv, grad, out, totals, first, last, valid):
    pairs = qkv.shape[1]
    return pl.pallas_call(
        self_backward_kernel,
        out_shape=jax.ShapeDtypeStruct(qkv.shape, bf16),
        grid_spec=pltpu.PrefetchScalarGridSpec(
            num_scalar_prefetch=3,
            grid=(pairs,),
            in_specs=[
                pair_spec(qkv.shape),
                pair_spec(grad.shape),
                pair_spec(out.shape),
                pair_spec(totals.shape),
            ],
            out_specs=pair_spec(qkv.shape),
            scratch_shapes=[
                pltpu.VMEM((CELLS, CELL, HEAD), bf16),
                pltpu.VMEM((CELLS, CELL, HEAD), bf16),
                pltpu.VMEM((CELLS, HEAD, CELL), f32),
                pltpu.VMEM((CELLS, HEAD, CELL), f32),
            ],
        ),
        compiler_params=pltpu.CompilerParams(vmem_limit_bytes=VMEM_LIMIT),
        name="self_backward",
    )(first, last, valid, qkv, grad, out, totals)


def text_weights(key_block, query):
    scores = kernel_dot(flip(key_block), query) * SCALING
    present = lax.broadcasted_iota(jnp.int32, scores.shape, 0) < TEXT
    return jnp.where(present, jnp.exp(scores), 0.0)


def cross_forward_kernel(query_ref, key_ref, value_ref, out_ref, total_ref):
    for head in range(query_ref.shape[0]):
        weights = text_weights(key_ref[head], query_ref[head])
        totals = jnp.sum(weights, axis=0, keepdims=True)
        out_ref[head] = kernel_dot(value_ref[head], weights.astype(bf16)) / totals
        total_ref[head] = totals


def cross_backward_kernel(
    query_ref,
    key_ref,
    value_ref,
    grad_ref,
    out_ref,
    total_ref,
    query_grad_ref,
    key_grad_ref,
    value_grad_ref,
):
    for head in range(query_ref.shape[0]):
        query, keys = query_ref[head], key_ref[head]
        grad = grad_ref[head].astype(f32)
        inverse = 1.0 / total_ref[head]
        scaled = (grad * inverse).astype(bf16)
        total_grad = -jnp.sum(grad * out_ref[head], axis=0, keepdims=True) * inverse
        weights = text_weights(keys, query)
        weight_grad = kernel_dot(flip(value_ref[head]), scaled)
        score_grad = (weights * (weight_grad + total_grad)).astype(bf16)
        query_grad_ref[head] = kernel_dot(keys, score_grad) * SCALING
        key_grad_ref[head] = kernel_dot(query, score_grad, 1, 1) * SCALING
        value_grad_ref[head] = kernel_dot(scaled, weights.astype(bf16), 1, 1)


HEADS_STEP = 4


def head_spec(shape):
    return pl.BlockSpec((HEADS_STEP,) + shape[1:], lambda step: (step, 0, 0))


def cross_forward(queries, keys, values):
    count, _, rows = queries.shape
    out_shape = (count, HEAD, rows)
    total_shape = (count, 1, rows)
    return pl.pallas_call(
        cross_forward_kernel,
        out_shape=(
            jax.ShapeDtypeStruct(out_shape, f32),
            jax.ShapeDtypeStruct(total_shape, f32),
        ),
        grid=(count // HEADS_STEP,),
        in_specs=[head_spec(queries.shape), head_spec(keys.shape), head_spec(values.shape)],
        out_specs=[head_spec(out_shape), head_spec(total_shape)],
        compiler_params=pltpu.CompilerParams(vmem_limit_bytes=VMEM_LIMIT),
        name="cross_forward",
    )(queries, keys, values)


def cross_backward(queries, keys, values, grad, out, totals):
    inputs = (queries, keys, values, grad, out, totals)
    return pl.pallas_call(
        cross_backward_kernel,
        out_shape=(
            jax.ShapeDtypeStruct(queries.shape, f32),
            jax.ShapeDtypeStruct(keys.shape, f32),
            jax.ShapeDtypeStruct(values.shape, f32),
        ),
        grid=(queries.shape[0] // HEADS_STEP,),
        in_specs=[head_spec(member.shape) for member in inputs],
        out_specs=[head_spec(queries.shape), head_spec(keys.shape), head_spec(values.shape)],
        compiler_params=pltpu.CompilerParams(vmem_limit_bytes=VMEM_LIMIT),
        name="cross_backward",
    )(*inputs)


def shards(
    tokens,
    skip_in,
    timestep,
    captions,
    null_mask,
    lengths,
    cotangent,
    skip_weight,
    shift_weight,
    self_input,
    self_output,
    cross_query,
    cross_pairs,
    cross_output,
    expand_weight,
    reduce_weight,
    null_caption,
    norm_gains,
):
    sp_count, cp_count = lax.axis_size("sp"), lax.axis_size("cp")
    dp_count = lax.axis_size("dp")
    dp_index, sp_index, cp_index = (lax.axis_index(name) for name in EVERY)
    place = (dp_index * sp_count + sp_index) * cp_count + cp_index
    packs, rows = tokens.shape[0], tokens.shape[1]
    held = packs * rows
    chunk = cp_count * rows
    group_heads = HEADS // cp_count
    pairs_dev = packs * group_heads // sp_count
    all_packs = lengths.shape[0]

    def split_columns(weight):
        columns = weight.shape[1] // cp_count
        blocks = jnp.swapaxes(weight.reshape(weight.shape[0], cp_count, columns), 0, 1)
        return trade_cp(blocks).reshape(cp_count * weight.shape[0], columns)

    def join_columns(part):
        count = part.shape[0] // cp_count
        blocks = trade_cp(part.reshape(cp_count, count, part.shape[1]))
        return jnp.swapaxes(blocks, 0, 1).reshape(count, cp_count * part.shape[1])

    def gather_part(weight):
        return lax.all_gather(split_columns(weight), GROUP, axis=0, tiled=True)

    def gather_whole(weight):
        return lax.all_gather(weight, EVERY, axis=0, tiled=True)

    def order_heads(weight):
        split = weight.reshape(weight.shape[0], 3, cp_count, -1)
        return jnp.swapaxes(split, 1, 2).reshape(weight.shape)

    def restore_heads(weight):
        split = weight.reshape(weight.shape[0], cp_count, 3, -1)
        return jnp.swapaxes(split, 1, 2).reshape(weight.shape)

    skip_full = gather_whole(skip_weight)
    input_part = gather_part(order_heads(self_input))
    output_full = gather_whole(self_output)
    query_full = gather_whole(cross_query)
    pairs_full = gather_whole(cross_pairs)
    cross_full = gather_whole(cross_output)
    expand_part = gather_part(expand_weight)
    reduce_part = gather_part(jnp.transpose(reduce_weight))
    gain_rows = lax.all_gather(norm_gains, EVERY, axis=1, tiled=True).astype(f32)
    caption_shard = jnp.pad(jnp.transpose(null_caption), ((0, 0), (0, TEXT_PAD - TEXT)))
    caption_full = jnp.transpose(gather_whole(caption_shard))

    own_lengths = lax.dynamic_slice_in_dim(lengths, dp_index * packs, packs, 0)
    describe = jax.vmap(segment_info, in_axes=(0, None))
    chunk_pos = sp_index * chunk + jnp.arange(chunk, dtype=jnp.int32)
    _, chunk_row, chunk_col, _ = describe(own_lengths, chunk_pos)
    block_pos = jnp.arange(sp_count * cp_count, dtype=jnp.int32) * rows
    all_segments, _, _, all_valid = describe(lengths, block_pos)
    own_segments = lax.dynamic_slice_in_dim(all_segments, dp_index * packs, packs, 0)
    own_valid = lax.dynamic_slice_in_dim(all_valid, dp_index * packs, packs, 0)
    block = sp_index * cp_count + cp_index
    block_image = lax.dynamic_index_in_dim(own_segments, block, 1, keepdims=False)
    block_valid = lax.dynamic_index_in_dim(own_valid, block, 1, keepdims=False)
    token_valid = jnp.broadcast_to(block_valid[:, None], (packs, rows)).reshape(held, 1)
    pair_pack = (sp_index * pairs_dev + jnp.arange(pairs_dev, dtype=jnp.int32)) // group_heads
    first_cells, last_cells, valid_cells = jax.vmap(cell_ranges)(own_lengths)
    first_cells = jnp.take(first_cells, pair_pack, axis=0)
    last_cells = jnp.take(last_cells, pair_pack, axis=0)
    valid_cells = jnp.take(valid_cells, pair_pack, axis=0)

    times = lax.all_gather(timestep, "dp", axis=0, tiled=True)
    silu_all = jax.nn.silu(times.astype(f32)).astype(bf16)
    shard_rows = shift_weight.shape[0]
    silu_own = lax.dynamic_slice_in_dim(silu_all, place * shard_rows, shard_rows, 2)
    shift_table = lax.psum(
        dot(silu_own.reshape(all_packs * IMGS, shard_rows), shift_weight, 1, 0), EVERY
    ).reshape(all_packs, IMGS, D)
    own_table = lax.dynamic_slice_in_dim(shift_table, dp_index * packs, packs, 0)
    slot_ids = jnp.arange(IMGS, dtype=jnp.int32)
    block_pick = (block_image[:, None] == slot_ids[None, :]).astype(f32)
    shifts = jnp.einsum("pi,pid->pd", block_pick, own_table, precision=highest)
    shift_rows = jnp.broadcast_to(shifts[:, None, :], (packs, rows, D)).reshape(held, D)

    image_dev = captions.shape[1]
    near = lax.dynamic_slice_in_dim(own_segments, sp_index * cp_count, cp_count, 1)
    local = jnp.clip(near - cp_index * image_dev, 0, image_dev - 1)
    offered = jnp.stack(
        [
            jnp.stack(
                [
                    lax.dynamic_index_in_dim(captions[p], local[p, k], 0, keepdims=False)
                    for p in range(packs)
                ]
            )
            for k in range(cp_count)
        ]
    )
    offered = jnp.pad(offered, ((0, 0), (0, 0), (0, TEXT_PAD - TEXT), (0, 0)))
    arrived = trade_cp(offered)
    own_null = jnp.take_along_axis(
        null_mask, block_image[:, None], axis=1
    )[:, 0]
    chosen = jnp.stack(
        [
            jnp.where(
                own_null[p] > 0,
                caption_full,
                lax.dynamic_index_in_dim(
                    arrived[:, p], block_image[p] // image_dev, 0, keepdims=False
                ),
            )
            for p in range(packs)
        ]
    )

    joined = jnp.concatenate([tokens.reshape(held, D), skip_in.reshape(held, D)], axis=1)
    mixed = dot(joined, skip_full, 1, 0)
    base_stream = norm_gain(mixed, gain_rows[0])
    normed_self = (norm_gain(base_stream, gain_rows[1]) + shift_rows).astype(bf16)
    normed_all = gather_cp(normed_self)
    projected = dot(input_part, normed_all.reshape(cp_count * held, D), 0, 1)
    projected = jnp.transpose(
        projected.reshape(3, group_heads, HEAD, cp_count, packs, rows), (4, 1, 0, 2, 3, 5)
    ).reshape(packs, group_heads, 3, HEAD, chunk)
    cosine, sines = jax.vmap(rope_tables)(chunk_row, chunk_col)
    cosine, sines = cosine[:, None], sines[:, None]
    query_raw, key_raw = projected[:, :, 0], projected[:, :, 1]
    queries = turn_norm(query_raw, cosine, sines).astype(bf16)
    key_rows = turn_norm(key_raw, cosine, sines).astype(bf16)
    value_rows = projected[:, :, 2].astype(bf16)
    qkv = jnp.stack([queries, key_rows, value_rows], axis=2)

    def to_heads(value):
        value = value.reshape((sp_count, pairs_dev) + value.shape[2:])
        return lax.all_to_all(value, "sp", split_axis=0, concat_axis=0, tiled=True)

    def from_heads(value):
        value = lax.all_to_all(value, "sp", split_axis=0, concat_axis=0, tiled=True)
        return value.reshape((packs, group_heads) + value.shape[2:])

    qkv = to_heads(qkv)
    out_self, totals_self = self_forward(qkv, first_cells, last_cells)

    def to_tokens(value):
        value = value.reshape(sp_count, pairs_dev, HEAD, cp_count, rows)
        value = jnp.transpose(value, (3, 0, 1, 2, 4))
        value = value.reshape(cp_count * sp_count, pairs_dev, HEAD, rows)
        value = lax.all_to_all(value, HEAD_ORDER, split_axis=0, concat_axis=0, tiled=True)
        value = value.reshape(cp_count, packs, group_heads, HEAD, rows)
        return jnp.transpose(value, (0, 2, 3, 1, 4)).reshape(D, held)

    def by_heads(value):
        value = value.reshape(cp_count, group_heads, HEAD, packs, rows)
        value = jnp.transpose(value, (0, 3, 1, 2, 4))
        value = value.reshape(cp_count * sp_count, pairs_dev, HEAD, rows)
        value = lax.all_to_all(value, HEAD_ORDER, split_axis=0, concat_axis=0, tiled=True)
        value = value.reshape(cp_count, sp_count, pairs_dev, HEAD, rows)
        return jnp.transpose(value, (1, 2, 3, 0, 4)).reshape(sp_count, pairs_dev, HEAD, chunk)

    def heads_of(value):
        value = value.reshape(HEADS, HEAD, packs, rows)
        return jnp.transpose(value, (2, 0, 1, 3)).reshape(packs * HEADS, HEAD, rows)

    def rows_of(value):
        value = value.reshape(packs, HEADS, HEAD, rows)
        return jnp.transpose(value, (1, 2, 0, 3)).reshape(D, held)

    attended = to_tokens(out_self.astype(bf16))
    mid_stream = base_stream + dot(attended, output_full, 0, 0)
    normed_cross = norm_gain(mid_stream, gain_rows[2]).astype(bf16)
    cross_raw = heads_of(dot(query_full, normed_cross, 0, 1))
    cross_queries = head_norm(cross_raw).astype(bf16)
    paired = jnp.einsum("cn,ptc->pnt", pairs_full, chosen, preferred_element_type=f32)
    paired = paired.reshape(packs, 2, HEADS, HEAD, TEXT_PAD)
    text_raw = paired[:, 0].reshape(packs * HEADS, HEAD, TEXT_PAD)
    text_keys = head_norm(text_raw).astype(bf16)
    text_values = paired[:, 1].reshape(packs * HEADS, HEAD, TEXT_PAD).astype(bf16)
    out_cross, totals_cross = cross_forward(cross_queries, text_keys, text_values)
    crossed = rows_of(out_cross.astype(bf16))
    late_stream = mid_stream + dot(crossed, cross_full, 0, 0)
    normed_ffn = norm_gain(late_stream, gain_rows[3]).astype(bf16)
    ffn_all = gather_cp(normed_ffn).reshape(cp_count * held, D)
    expanded = dot(ffn_all, expand_part, 1, 0)
    hidden = jax.nn.gelu(expanded, approximate=True).astype(bf16)
    reduced_part = dot(hidden, reduce_part, 1, 1)
    block_out = (
        late_stream + scatter_cp(reduced_part.reshape(cp_count, held, D))
    ).astype(bf16)

    out_grad = cotangent.reshape(held, D).astype(f32) * token_valid
    reduce_in = gather_cp(out_grad.astype(bf16)).reshape(cp_count * held, D)

    def add_group(partial):
        return lax.psum_scatter(partial.astype(bf16), GROUP, scatter_dimension=0, tiled=True)

    reduce_grad = add_group(dot(reduce_in, hidden, 0, 0))
    gelu_back = jax.vjp(lambda preact: jax.nn.gelu(preact, approximate=True), expanded)[1]
    expand_in = gelu_back(dot(reduce_in, reduce_part, 1, 0))[0].astype(bf16)
    expand_grad = add_group(dot(ffn_all, expand_in, 0, 0))
    ffn_back = jax.vjp(norm_gain, late_stream, gain_rows[3])[1]
    ffn_grad = scatter_cp(dot(expand_in, expand_part, 1, 1).reshape(cp_count, held, D))
    late_part, gain_ffn = ffn_back(ffn_grad)
    late_grad = out_grad + late_part

    def column_blocks(value):
        return jnp.swapaxes(value.reshape(value.shape[0], cp_count, -1), 0, 1)

    def row_blocks(value):
        return value.reshape((cp_count, value.shape[0] // cp_count) + value.shape[1:])

    cout_in = late_grad.astype(bf16)
    cross_out_grad = add_group(
        jnp.einsum(
            "skt,stn->kn",
            gather_cp(crossed),
            trade_cp(column_blocks(cout_in)),
            preferred_element_type=f32,
        )
    )
    crossed_grad = heads_of(dot(cross_full, cout_in, 1, 1).astype(bf16))
    cq_grad, ck_grad, cv_grad = cross_backward(
        cross_queries, text_keys, text_values, crossed_grad, out_cross, totals_cross
    )
    cq_grad = cq_grad.astype(bf16).astype(f32)
    cross_raw_grad = rows_of(jax.vjp(head_norm, cross_raw)[1](cq_grad)[0].astype(bf16))
    cross_query_grad = add_group(
        jnp.einsum(
            "stk,snt->kn",
            gather_cp(normed_cross),
            trade_cp(row_blocks(cross_raw_grad)),
            preferred_element_type=f32,
        )
    )
    cross_norm_back = jax.vjp(norm_gain, mid_stream, gain_rows[2])[1]
    mid_part, gain_cross = cross_norm_back(dot(cross_raw_grad, query_full, 0, 1))
    mid_grad = late_grad + mid_part
    self_in = mid_grad.astype(bf16)
    attended_grad = by_heads(dot(output_full, self_in, 1, 1).astype(bf16))
    self_out_grad = add_group(
        jnp.einsum(
            "skt,stn->kn",
            gather_cp(attended),
            trade_cp(column_blocks(self_in)),
            preferred_element_type=f32,
        )
    )
    qkv_grad = from_heads(
        self_backward(
            qkv, attended_grad, out_self, totals_self, first_cells, last_cells, valid_cells
        )
    )
    turn = functools.partial(turn_norm, cosine=cosine, sines=sines)
    query_raw_grad = jax.vjp(turn, query_raw)[1](qkv_grad[:, :, 0].astype(f32))[0].astype(bf16)
    key_raw_grad = jax.vjp(turn, key_raw)[1](qkv_grad[:, :, 1].astype(f32))[0].astype(bf16)
    projected_grad = jnp.stack([query_raw_grad, key_raw_grad, qkv_grad[:, :, 2]], axis=0)
    projected_grad = jnp.transpose(
        projected_grad.reshape(3, packs, group_heads, HEAD, cp_count, rows), (0, 2, 3, 4, 1, 5)
    ).reshape(3 * group_heads * HEAD, cp_count * held)
    self_input_grad = add_group(
        dot(normed_all.reshape(cp_count * held, D), projected_grad, 0, 1)
    )
    normed_self_grad = scatter_cp(
        dot(projected_grad, input_part, 0, 1).reshape(cp_count, held, D)
    )
    self_norm_back = jax.vjp(norm_gain, base_stream, gain_rows[1])[1]
    base_part, gain_self = self_norm_back(normed_self_grad)
    shift_grads = jnp.sum(normed_self_grad.reshape(packs, rows, D), axis=1)
    base_grad = mid_grad + base_part
    skip_norm_back = jax.vjp(norm_gain, mixed, gain_rows[0])[1]
    mixed_grad, gain_skip = skip_norm_back(base_grad)
    mixed_in = mixed_grad.astype(bf16)
    joined_grad = dot(mixed_in, skip_full, 1, 1)
    skip_weight_grad = add_group(
        jnp.einsum(
            "stk,stn->kn",
            gather_cp(joined),
            trade_cp(column_blocks(mixed_in)),
            preferred_element_type=f32,
        )
    )

    ck_grad = ck_grad.astype(bf16).astype(f32)
    text_raw_grad = jax.vjp(head_norm, text_raw)[1](ck_grad)[0].astype(bf16)
    paired_grad = jnp.stack(
        [
            text_raw_grad.reshape(packs, D, TEXT_PAD),
            cv_grad.reshape(packs, D, TEXT_PAD).astype(bf16),
        ],
        axis=1,
    ).reshape(packs, 2 * D, TEXT_PAD)
    pairs_grad = add_group(
        jnp.einsum(
            "sptc,snpt->cn",
            gather_cp(chosen),
            trade_cp(row_blocks(jnp.swapaxes(paired_grad, 0, 1))),
            preferred_element_type=f32,
        )
    )
    null_sum = jnp.einsum(
        "p,pnt->nt", own_null.astype(f32), paired_grad.astype(f32), precision=highest
    )
    caption_grad = dot(pairs_full, null_sum.astype(bf16), 1, 0)
    caption_grad = lax.psum_scatter(
        caption_grad.astype(bf16), EVERY, scatter_dimension=0, tiled=True
    )

    small = jnp.concatenate(
        [jnp.stack([gain_skip, gain_self, gain_cross, gain_ffn]), shift_grads], axis=0
    )
    small = lax.all_gather(small, EVERY, axis=0, tiled=False)
    gain_columns = norm_gains.shape[1]
    gains_grad = jnp.sum(
        lax.dynamic_slice_in_dim(small[:, :4], place * gain_columns, gain_columns, 2), axis=0
    )
    shift_all = small[:, 4:].reshape(dp_count, sp_count * cp_count, packs, D)
    shift_all = jnp.swapaxes(shift_all, 1, 2).reshape(all_packs * sp_count * cp_count, D)
    all_pick = (all_segments[:, :, None] == slot_ids).astype(f32)
    silu_blocks = jnp.einsum("pbi,pik->pbk", all_pick, silu_own.astype(f32), precision=highest)
    shift_weight_grad = lax.dot_general(
        silu_blocks.reshape(all_packs * sp_count * cp_count, shard_rows),
        shift_all,
        (((0,), (0,)), ((), ())),
        precision=highest,
        preferred_element_type=f32,
    )

    factor = all_packs * PACK / jnp.sum(lengths).astype(f32)

    def finish(part):
        return join_columns(part).astype(f32) * factor

    token_shape = (packs, rows, D)
    return (
        block_out.reshape(token_shape),
        (joined_grad[:, :D] * factor).astype(bf16).reshape(token_shape),
        (joined_grad[:, D:] * factor).astype(bf16).reshape(token_shape),
        finish(skip_weight_grad),
        shift_weight_grad * factor,
        restore_heads(join_columns(self_input_grad)).astype(f32) * factor,
        finish(self_out_grad),
        finish(cross_query_grad),
        finish(pairs_grad),
        finish(cross_out_grad),
        finish(expand_grad),
        jnp.transpose(join_columns(reduce_grad)).astype(f32) * factor,
        jnp.transpose(caption_grad)[:TEXT].astype(f32) * factor,
        gains_grad * factor,
    )


def solution(mesh):
    token_spec = P("dp", ("sp", "cp"), None)
    by_rows = P(EVERY, None)
    by_columns = P(None, EVERY)
    return jax.shard_map(
        shards,
        mesh=mesh,
        in_specs=(
            token_spec,
            token_spec,
            P("dp", None, None),
            P("dp", "cp", None, None),
            P("dp", None),
            P(),
            token_spec,
            by_rows,
            by_rows,
            by_rows,
            by_rows,
            by_rows,
            by_rows,
            by_rows,
            by_rows,
            by_columns,
            by_columns,
            by_columns,
        ),
        out_specs=(
            token_spec,
            token_spec,
            token_spec,
            by_rows,
            by_rows,
            by_rows,
            by_rows,
            by_rows,
            by_rows,
            by_rows,
            by_rows,
            by_columns,
            by_columns,
            by_columns,
        ),
        check_vma=False,
    )
```

time: 3690 us -> 1600 us (0.43)
  blocking collectives: 1830 us -> 192 us
  waiting for transfers between devices: 439 us -> 780 us
  local copies, waits for them, and re-layouts: 508 us -> 168 us
  matrix products: 447 us -> 149 us
  starting transfers between devices: 207 us -> 92 us
  other arithmetic: 216 us -> 129 us
  Pallas kernels: 0 us -> 46.4 us
    unnamed x4 -> x0, blocking collectives: 1680 us -> none
    dot_general x63 -> x28, matrix products: 447 us -> 149 us  [the longest x19 111 us: dot(): lax.dot_general(left, right, (((left_dim,), (right_dim,)), ((), ())), pre...]
    reduce_scatter x6 -> x8, waiting for transfers between devices: 0.06 us -> 267 us  [add_group(): lax.psum_scatter(partial.astype(bf16), GROUP, scatter_dimension=0, tiled=...]
    unnamed x359 -> x243, local copies, waits for them, and re-layouts: 251 us -> 64.1 us
    unnamed x22 -> x1, starting transfers between devices: 167 us -> 0.04 us
    ppermute x0 -> x22, waiting for transfers between devices: none -> 104 us  [the longest x11 104 us: swap_chip(): return lax.ppermute(value, 'cp', [(0, 2), (2, 0), (1, 3), (3, 1)])]
    all_gather x13 -> x8, waiting for transfers between devices: 298 us -> 195 us  [the longest x5 166 us: gather_whole(): return lax.all_gather(weight, EVERY, axis=0, tiled=True)]
    all_gather x2 -> x4, blocking collectives: 83.6 us -> 180 us  [the longest x1 78.7 us: gather_whole(): return lax.all_gather(weight, EVERY, axis=0, tiled=True)]
  transfers between devices with their start and end apart: 50 -> 60, of which waited for: 15 -> 32; matrix products, arithmetic and copies ran while one was open for 73% -> 26% of each run, Pallas kernels for 0% -> 3%
where the time goes in v1:
time: 1600 us; the launch traced here: 1590 us
  waiting for transfers between devices  780 us (49%)
  blocking collectives  192 us (12%)
  local copies, waits for them, and re-layouts  168 us (10%)
  matrix products  149 us (9%)
  other arithmetic  129 us (8%)
  starting transfers between devices  92 us (6%)
  Pallas kernels  46.4 us (3%)
  between operations  33.9 us (2%)
    reduce_scatter x8, waiting for transfers between devices, add_group(): lax.psum_scatter(partial.astype(bf16), GROUP, scatter_dimension=0, tiled=...  267 us
    all_gather x5, waiting for transfers between devices, gather_whole(): return lax.all_gather(weight, EVERY, axis=0, tiled=True)  166 us
    dot_general x19, matrix products, dot(): lax.dot_general(left, right, (((left_dim,), (right_dim,)), ((), ())), pre...  111 us
    ppermute x11, waiting for transfers between devices, swap_chip(): return lax.ppermute(value, 'cp', [(0, 2), (2, 0), (1, 3), (3, 1)])  104 us
    all_to_all x16, waiting for transfers between devices, trade_cp(): return lax.all_to_all(blocks, 'cp', split_axis=0, concat_axis=0, tiled=True)  85.7 us
    all_gather x1, blocking collectives, gather_whole(): return lax.all_gather(weight, EVERY, axis=0, tiled=True)  78.7 us
    unnamed x243, local copies, waits for them, and re-layouts  64.1 us
    all_to_all x16, starting transfers between devices, trade_cp(): return lax.all_to_all(blocks, 'cp', split_axis=0, concat_axis=0, tiled=True)  61.4 us
  transfers between devices with their start and end apart: 60, of which 32 were waited for; matrix products, arithmetic and copies ran while one was open for 26% of the time, Pallas kernels for 3%

profile of v1, /device:TPU:0, one launch (start us, length us, event | category | flops | bytes accessed | tf_op | source)
XLA Modules:
  0.0 1590.3 jit_solution(6255524692983363209)
XLA Ops:
  7.3 6.1 all_gather.41
  16.7 11.3 all_to_all.105
  48.2 46.4 %all-gather.1 = bf16[32,44,4]{1,2,0:T(4,128)(2,1)S(1)} all-gather(bf16[1,44,4]{1,2,0:T(4,128)(2,1)S(1)} %bitcast.570), channel_id=1, replica_groups=mesh['dp'=2,'sp'=4,'cp'=4] {'dp','sp','cp'}, dimensions={0}, use_global_device_ids=true | all-gather | bytes 11616 | tf_op jit(solution)/shard_map/all_gather | solution.py:494
  98.7 10.8 constant_dynamic-slice_fusion.4
  109.5 30.0 %all-reduce.12.cloned.1.call-done = f32[2,16,1408]{2,1,0:T(8,128)} async-done(((f32[2,16,1408]{2,1,0:T(8,128)}), f32[2,16,1408]{2,1,0:T(8,128)}) %all-reduce.12.cloned.1.call-update) | async-done | bytes 180240 | tf_op jit(solution)/shard_map/psum | solution.py:520
  141.2 78.2 %all-gather.15.cloned.1.call-done = bf16[2816,1408]{1,0:T(8,128)(2,1)} async-done(((bf16[88,1408]{1,0:T(8,128)(2,1)}), bf16[2816,1408]{1,0:T(8,128)(2,1)}) %all-gather.15.cloned.1.call-update) | async-done | bytes 7929872 | tf_op jit(solution)/shard_map/all_gather | solution.py:476
  219.5 6.2 fusion.109
  242.2 6.5 collective-permute-done
  267.9 14.5 all-gather.17.cloned.1.call-done
  282.3 8.4 convolution_bitcast_fusion.2
  301.7 6.0 reshape.2260
  321.4 35.8 %all-to-all-done.3 = bf16[4,1,384,1024]{3,2,1,0:T(8,128)(2,1)} async-done(((bf16[4,1,384,1024]{3,2,1,0:T(8,128)(2,1)}), bf16[4,1,384,1024]{3,2,1,0:T(8,128)(2,1)}, u32[]{:S(2)}, u32[]{:S(2)}) %all-to-all-start.3) | async-done | bytes 3145760 | tf_op jit(solution)/shard_map/all_to_all | solution.py:158
  370.4 78.7 %all_gather.45 = bf16[1024,384]{1,0:T(8,128)(2,1)S(1)} all-gather(bf16[32,384]{1,0:T(8,128)(2,1)S(1)} %pad.32), channel_id=1, replica_groups=mesh['dp'=2,'sp'=4,'cp'=4] {'dp','sp','cp'}, dimensions={0}, use_global_device_ids=true | all-gather | bytes 811008 | tf_op jit(solution)/shard_map/all_gather | solution.py:476
  461.2 11.8 collective-permute-done.18
  475.9 6.0 reshape.2348
  481.9 6.0 reshape.2350
  487.9 24.9 %all-gather.29.cloned.1.call-done = bf16[32,44,1408]{2,1,0:T(8,128)(2,1)} async-done(((bf16[1,44,1408]{2,1,0:T(8,128)(2,1)}), bf16[32,44,1408]{2,1,0:T(8,128)(2,1)}) %all-gather.29.cloned.1.call-update) | async-done | bytes 3964944 | tf_op jit(solution)/shard_map/all_gather | solution.py:476
  512.8 6.0 reshape.2352
  518.8 62.5 %all-gather.19.cloned.1.call-done = bf16[1024,2816]{1,0:T(8,128)(2,1)} async-done(((bf16[32,2816]{1,0:T(8,128)(2,1)}), bf16[1024,2816]{1,0:T(8,128)(2,1)}) %all-gather.19.cloned.1.call-update) | async-done | bytes 5767184 | tf_op jit(solution)/shard_map/all_gather | solution.py:476
  581.3 7.2 convolution_bitcast_fusion.1
  594.4 12.9 self_forward.1
  622.0 34.1 %all-to-all-done.2 = bf16[16,1,88,256]{3,2,1,0:T(8,128)(2,1)} async-done(((bf16[16,1,88,256]{3,2,1,0:T(8,128)(2,1)}), bf16[16,1,88,256]{3,2,1,0:T(8,128)(2,1)}, u32[]{:S(2)}, u32[]{:S(2)}) %all-to-all-start.2) | async-done | bytes 720928 | tf_op jit(solution)/shard_map/all_to_all | solution.py:593
  684.7 16.4 %collective-permute-done.2 = bf16[256,1408]{1,0:T(8,128)(2,1)S(1)} collective-permute-done((bf16[256,1408]{1,0:T(8,128)(2,1)S(1)}, bf16[256,1408]{1,0:T(8,128)(2,1)S(1)}, u32[]{:S(2)}, u32[]{:S(2)}) %collective-permute-start.2) | collective-permute-done | bytes 720928 | tf_op jit(solution)/shard_map/ppermute | solution.py:124
  705.8 10.8 collective-permute-done.20
  722.0 9.5 fusion.114
  731.4 15.3 all-gather.23.cloned.1.call-done
  746.7 11.5 fusion.6
  786.3 13.2 collective-permute-done.9
  800.1 14.0 collective-permute-done.5
  827.9 6.7 cross_backward.1
  938.7 14.8 all-to-all-done.15
  953.5 6.0 bitcast_convert_fusion
  962.4 9.6 convolution_convert_fusion.1
  985.7 21.6 %all-to-all-done.6 = bf16[16,1,88,256]{3,2,1,0:T(8,128)(2,1)S(1)} async-done(((bf16[16,1,88,256]{3,2,1,0:T(8,128)(2,1)}), bf16[16,1,88,256]{3,2,1,0:T(8,128)(2,1)S(1)}, u32[]{:S(2)}, u32[]{:S(2)}) %all-to-all-start.6) | async-done | bytes 720928 | tf_op jit(solution)/shard_map/all_to_all | solution.py:601
  1011.8 21.9 %self_backward.1 = bf16[4,1,3,88,1024]{4,3,2,1,0:T(8,128)(2,1)S(1)} custom-call(s32[1,16]{1,0:T(1,128)S(1)} %get-tuple-element.220.first_ref, s32[1,16]{1,0:T(1,128)S(1)} %get-tuple-element.221.last_ref, s32[1]{0:T(128)S(6)} %select_n.534.valid_ref, bf16[4,1,3,88,1024]{4,3,2,1,0:T(8,128)(2,1)S(1)} %all-to-all-done.1.qkv_ref, ...), custom_call_target="tpu_custom_call" | custom-call | tf_op jit(solution)/shard_map/self_backward/pallas_call | solution.py:325
  1039.1 10.6 convolution_convert_fusion
  1049.8 39.1 %all-to-all-done.7 = bf16[4,1,3,88,1024]{4,3,2,1,0:T(8,128)(2,1)S(1)} async-done(((bf16[4,1,3,88,1024]{4,3,2,1,0:T(8,128)(2,1)}), bf16[4,1,3,88,1024]{4,3,2,1,0:T(8,128)(2,1)S(1)}, u32[]{:S(2)}, u32[]{:S(2)}) %all-to-all-start.7) | async-done | bytes 2162720 | tf_op jit(solution)/shard_map/all_to_all | solution.py:583
  1109.4 8.2 convolution_convert_fusion.2
  1120.8 21.1 %collective-permute-done.12 = bf16[256,2816]{1,0:T(8,128)(2,1)S(1)} collective-permute-done((bf16[256,2816]{1,0:T(8,128)(2,1)}, bf16[256,2816]{1,0:T(8,128)(2,1)S(1)}, u32[]{:S(2)}, u32[]{:S(2)}) %collective-permute-start.12) | collective-permute-done | bytes 1441824 | tf_op jit(solution)/shard_map/ppermute | solution.py:124
  1146.6 10.0 collective-permute-done.11
  1169.6 6.4 maximum_select_fusion
  1185.9 7.5 fusion.11
  1209.7 21.8 %reduce-scatter.28.cloned.1.call-done = bf16[128,704]{1,0:T(8,128)(2,1)} async-done(((bf16[1024,704]{1,0:T(8,128)(2,1)}), bf16[128,704]{1,0:T(8,128)(2,1)}) %reduce-scatter.28.cloned.1.call-update) | async-done | bytes 180240 | tf_op jit(solution)/shard_map/reduce_scatter | solution.py:639
  1241.4 82.7 %reduce-scatter.24.cloned.1.call-done = bf16[176,1536]{1,0:T(8,128)(2,1)} async-done(((bf16[1408,1536]{1,0:T(8,128)(2,1)}), bf16[176,1536]{1,0:T(8,128)(2,1)}) %reduce-scatter.24.cloned.1.call-update) | async-done | bytes 540688 | tf_op jit(solution)/shard_map/reduce_scatter | solution.py:639
  1329.6 87.8 %reduce-scatter.26.cloned.1.call-done = bf16[176,1536]{1,0:T(8,128)(2,1)} async-done(((bf16[1408,1536]{1,0:T(8,128)(2,1)}), bf16[176,1536]{1,0:T(8,128)(2,1)}) %reduce-scatter.26.cloned.1.call-update) | async-done | bytes 540688 | tf_op jit(solution)/shard_map/reduce_scatter | solution.py:639
  1419.4 49.2 %all-gather.5 = f32[32,5,1408]{2,1,0:T(8,128)S(1)} all-gather(f32[1,5,1408]{2,1,0:T(8,128)S(1)} %bitcast.559), channel_id=2, replica_groups=mesh['dp'=2,'sp'=4,'cp'=4] {'dp','sp','cp'}, dimensions={0}, use_global_device_ids=true | all-gather | bytes 929280 | tf_op jit(solution)/shard_map/all_gather | solution.py:755
  1483.8 17.2 %reduce-scatter.16.cloned.1.call-done = bf16[176,1056]{1,0:T(8,128)(2,1)} async-done(((bf16[1408,1056]{1,0:T(8,128)(2,1)}), bf16[176,1056]{1,0:T(8,128)(2,1)}) %reduce-scatter.16.cloned.1.call-update) | async-done | bytes 371728 | tf_op jit(solution)/shard_map/reduce_scatter | solution.py:639
  1514.4 57.8 %reduce-scatter.14.cloned.1.call-done = bf16[352,352]{1,0:T(8,128)(2,1)} async-done(((bf16[2816,352]{1,0:T(8,128)(2,1)}), bf16[352,352]{1,0:T(8,128)(2,1)}) %reduce-scatter.14.cloned.1.call-update) | async-done | bytes 247824 | tf_op jit(solution)/shard_map/reduce_scatter | solution.py:639
  (611 shorter events, 455.6 us)
Async XLA Ops:
  7.2 132.3 %all-reduce.12.cloned.1.call-start = ((), (), s32[]{:S(2)}) async-start(), calls=%async_computation.31 | async-start | bytes 360448 | tf_op jit(solution)/shard_map/psum | solution.py:520
  14.9 204.6 %all-gather.15.cloned.1.call-start = ((), (), s32[]{:S(2)}) async-start(), calls=%async_computation.30 | async-start | bytes 8177664 | tf_op jit(solution)/shard_map/all_gather | solution.py:476
  15.6 266.7 %all-gather.17.cloned.1.call-start = ((), (), s32[]{:S(2)}) async-start(), calls=%async_computation.32 | async-start | bytes 3649536 | tf_op jit(solution)/shard_map/all_gather | solution.py:473
  29.0 446.9 %all-gather.25.cloned.1.call-start = ((), (), s32[]{:S(2)}) async-start(), calls=%async_computation.43 | async-start | bytes 4460544 | tf_op jit(solution)/shard_map/all_gather | solution.py:476
  29.6 452.4 %all-gather.27.cloned.1.call-start = ((), (), s32[]{:S(2)}) async-start(), calls=%async_computation.44 | async-start | bytes 4460544 | tf_op jit(solution)/shard_map/all_gather | solution.py:476
  30.2 482.6 %all-gather.29.cloned.1.call-start = ((), (), s32[]{:S(2)}) async-start(), calls=%async_computation.45 | async-start | bytes 4460544 | tf_op jit(solution)/shard_map/all_gather | solution.py:476
  30.7 550.6 %all-gather.19.cloned.1.call-start = ((), (), s32[]{:S(2)}) async-start(), calls=%async_computation.33 | async-start | bytes 5947392 | tf_op jit(solution)/shard_map/all_gather | solution.py:476
  32.7 203.6 %all-to-all-start.4 = ((bf16[4,44,1536]{2,1,0:T(8,128)(2,1)}), bf16[4,44,1536]{2,1,0:T(8,128)(2,1)S(1)}, u32[]{:S(2)}, u32[]{:S(2)}) async-start(bf16[4,44,1536]{2,1,0:T(8,128)(2,1)} %bitcast.473), calls=%async_computation.4 | async-start | bytes 1179648 | tf_op jit(solution)/shard_map/all_to_all | solution.py:158
  39.7 327.9 %collective-permute-start.6 = (bf16[256,1408]{1,0:T(8,128)(2,1)}, bf16[256,1408]{1,0:T(8,128)(2,1)}, u32[]{:S(2)}, u32[]{:S(2)}) collective-permute-start(bf16[256,1408]{1,0:T(8,128)(2,1)} %get-tuple-element.199), channel_id=1, source_target_pairs={{0,2},{2,0},{1,3},{3,1},{4,6},{6,4},{5,7},{7,5},{8,10},{10,8},{9,1... | collective-permute-start | bytes 2162696 | tf_op jit(solution)/shard_map/ppermute | solution.py:124
  229.4 19.3 %collective-permute-start = (bf16[256,1408]{1,0:T(8,128)(2,1)}, bf16[256,1408]{1,0:T(8,128)(2,1)}, u32[]{:S(2)}, u32[]{:S(2)}) collective-permute-start(bf16[256,1408]{1,0:T(8,128)(2,1)} %add_convert_fusion.5), channel_id=1, source_target_pairs={{0,2},{2,0},{1,3},{3,1},{4,6},{6,4},{5,7},{7,5},{8,10},{10,8},{9,1... | collective-permute-start | bytes 2162696 | tf_op jit(solution)/shard_map/ppermute | solution.py:124
  236.3 71.4 %all-to-all-start.5 = ((bf16[4,44,1536]{2,1,0:T(8,128)(2,1)}), bf16[4,44,1536]{2,1,0:T(8,128)(2,1)}, u32[]{:S(2)}, u32[]{:S(2)}) async-start(bf16[4,44,1536]{2,1,0:T(8,128)(2,1)} %bitcast.541), calls=%async_computation.5 | async-start | bytes 1179648 | tf_op jit(solution)/shard_map/all_to_all | solution.py:158
  240.5 481.5 %all-gather.21.cloned.1.call-start = ((), (), s32[]{:S(2)}) async-start(), calls=%async_computation.34 | async-start | bytes 4866048 | tf_op jit(solution)/shard_map/all_gather | solution.py:473
  307.7 49.4 %all-to-all-start.3 = ((bf16[4,1,384,1024]{3,2,1,0:T(8,128)(2,1)}), bf16[4,1,384,1024]{3,2,1,0:T(8,128)(2,1)}, u32[]{:S(2)}, u32[]{:S(2)}) async-start(bf16[4,1,384,1024]{3,2,1,0:T(8,128)(2,1)} %fusion.15), calls=%async_computation.3 | async-start | bytes 6291456 | tf_op jit(solution)/shard_map/all_to_all | solution.py:158
  357.1 237.3 %all-to-all-start.1 = ((bf16[4,1,3,88,1024]{4,3,2,1,0:T(8,128)(2,1)}), bf16[4,1,3,88,1024]{4,3,2,1,0:T(8,128)(2,1)S(1)}, u32[]{:S(2)}, u32[]{:S(2)}) async-start(bf16[4,1,3,88,1024]{4,3,2,1,0:T(8,128)(2,1)} %maximum_bitcast_fusion), calls=%async_computation.1 | async-start | bytes 4325376 | tf_op jit(solution)/shard_map/all_to_all | solution.py:580
  361.2 385.6 %all-gather.23.cloned.1.call-start = ((), (), s32[]{:S(2)}) async-start(), calls=%async_computation.35 | async-start | bytes 4866048 | tf_op jit(solution)/shard_map/all_gather | solution.py:473
  370.4 86.7 %collective-permute-start.7 = (bf16[2,256,1408]{2,1,0:T(8,128)(2,1)}, bf16[2,256,1408]{2,1,0:T(8,128)(2,1)}, u32[]{:S(2)}, u32[]{:S(2)}) collective-permute-start(bf16[2,256,1408]{2,1,0:T(8,128)(2,1)} %maximum_select_fusion.14), channel_id=1, source_target_pairs={{0,1},{1,0},{2,3},{3,2},{4,5},{5,4},{6,7},{7,6},{8,9},{9,8},{10,11... | collective-permute-start | bytes 4325384 | tf_op jit(solution)/shard_map/ppermute | solution.py:120
  452.1 20.9 %collective-permute-start.18 = (bf16[1,384,1024]{2,1,0:T(8,128)(2,1)S(1)}, bf16[1,384,1024]{2,1,0:T(8,128)(2,1)}, u32[]{:S(2)}, u32[]{:S(2)}) collective-permute-start(bf16[1,384,1024]{2,1,0:T(8,128)(2,1)S(1)} %bitcast.504), channel_id=1, source_target_pairs={{0,2},{2,0},{1,3},{3,1},{4,6},{6,4},{5,7},{7,5},{8,10},{10,8},{9,1... | collective-permute-start | bytes 2359304 | tf_op jit(solution)/shard_map/ppermute | solution.py:124
  475.9 458.5 %collective-permute-start.19 = (bf16[2,1,384,1024]{3,2,1,0:T(8,128)(2,1)}, bf16[2,1,384,1024]{3,2,1,0:T(8,128)(2,1)}, u32[]{:S(2)}, u32[]{:S(2)}) collective-permute-start(bf16[2,1,384,1024]{3,2,1,0:T(8,128)(2,1)} %maximum_select_fusion.10), channel_id=1, source_target_pairs={{0,1},{1,0},{2,3},{3,2},{4,5},{5,4},{6,7},{7,6},{8,9},{9,8},{10,11... | collective-permute-start | bytes 4718600 | tf_op jit(solution)/shard_map/ppermute | solution.py:120
  612.2 43.8 %all-to-all-start.2 = ((bf16[16,1,88,256]{3,2,1,0:T(8,128)(2,1)}), bf16[16,1,88,256]{3,2,1,0:T(8,128)(2,1)}, u32[]{:S(2)}, u32[]{:S(2)}) async-start(bf16[16,1,88,256]{3,2,1,0:T(8,128)(2,1)} %bitcast.52), calls=%async_computation.2 | async-start | bytes 1441792 | tf_op jit(solution)/shard_map/all_to_all | solution.py:593
  616.6 559.5 %reduce-scatter.30.cloned.1.call-start = ((), (), s32[]{:S(2)}) async-start(), calls=%async_computation.47 | async-start | bytes 811008
  682.0 19.1 %collective-permute-start.2 = (bf16[256,1408]{1,0:T(8,128)(2,1)S(1)}, bf16[256,1408]{1,0:T(8,128)(2,1)S(1)}, u32[]{:S(2)}, u32[]{:S(2)}) collective-permute-start(bf16[256,1408]{1,0:T(8,128)(2,1)S(1)} %multiply_convert_fusion.3), channel_id=1, source_target_pairs={{0,2},{2,0},{1,3},{3,1},{4,6},{6,4},{5,7},{7,5},{8,10},{10,8},{9,1... | collective-permute-start | bytes 2162696 | tf_op jit(solution)/shard_map/ppermute | solution.py:124
  682.8 33.8 %collective-permute-start.20 = (bf16[1408,256]{1,0:T(8,128)(2,1)S(1)}, bf16[1408,256]{1,0:T(8,128)(2,1)S(1)}, u32[]{:S(2)}, u32[]{:S(2)}) collective-permute-start(bf16[1408,256]{1,0:T(8,128)(2,1)S(1)} %bitcast.495), channel_id=1, source_target_pairs={{0,2},{2,0},{1,3},{3,1},{4,6},{6,4},{5,7},{7,5},{8,10},{10,8},{9,1... | collective-permute-start | bytes 2162696 | tf_op jit(solution)/shard_map/ppermute | solution.py:124
  701.4 18.2 %collective-permute-start.3 = (bf16[2,256,1408]{2,1,0:T(8,128)(2,1)S(1)}, bf16[2,256,1408]{2,1,0:T(8,128)(2,1)S(1)}, u32[]{:S(2)}, u32[]{:S(2)}) collective-permute-start(bf16[2,256,1408]{2,1,0:T(8,128)(2,1)S(1)} %maximum_select_fusion.13), channel_id=1, source_target_pairs={{0,1},{1,0},{2,3},{3,2},{4,5},{5,4},{6,7},{7,6},{8,9},{9,8},{10,11... | collective-permute-start | bytes 4325384 | tf_op jit(solution)/shard_map/ppermute | solution.py:120
  702.6 67.2 %collective-permute-start.16 = (bf16[256,1408]{1,0:T(8,128)(2,1)}, bf16[256,1408]{1,0:T(8,128)(2,1)}, u32[]{:S(2)}, u32[]{:S(2)}) collective-permute-start(bf16[256,1408]{1,0:T(8,128)(2,1)} %multiply_convert_fusion.5), channel_id=1, source_target_pairs={{0,2},{2,0},{1,3},{3,1},{4,6},{6,4},{5,7},{7,5},{8,10},{10,8},{9,1... | collective-permute-start | bytes 2162696 | tf_op jit(solution)/shard_map/ppermute | solution.py:124
  703.0 73.3 %collective-permute-start.14 = (bf16[1408,256]{1,0:T(8,128)(2,1)}, bf16[1408,256]{1,0:T(8,128)(2,1)}, u32[]{:S(2)}, u32[]{:S(2)}) collective-permute-start(bf16[1408,256]{1,0:T(8,128)(2,1)} %bitcast.53), channel_id=1, source_target_pairs={{0,2},{2,0},{1,3},{3,1},{4,6},{6,4},{5,7},{7,5},{8,10},{10,8},{9,1... | collective-permute-start | bytes 2162696 | tf_op jit(solution)/shard_map/ppermute | solution.py:124
  717.9 130.3 %collective-permute-start.21 = (bf16[2,1408,256]{2,1,0:T(8,128)(2,1)}, bf16[2,1408,256]{2,1,0:T(8,128)(2,1)}, u32[]{:S(2)}, u32[]{:S(2)}) collective-permute-start(bf16[2,1408,256]{2,1,0:T(8,128)(2,1)} %maximum_select_fusion.19), channel_id=1, source_target_pairs={{0,1},{1,0},{2,3},{3,2},{4,5},{5,4},{6,7},{7,6},{8,9},{9,8},{10,11... | collective-permute-start | bytes 4325384 | tf_op jit(solution)/shard_map/ppermute | solution.py:120
  764.0 16.1 %collective-permute-start.8 = (bf16[2,256,1408]{2,1,0:T(8,128)(2,1)S(1)}, bf16[2,256,1408]{2,1,0:T(8,128)(2,1)S(1)}, u32[]{:S(2)}, u32[]{:S(2)}) collective-permute-start(bf16[2,256,1408]{2,1,0:T(8,128)(2,1)S(1)} %dynamic-slice_bitcast_fusion.1), channel_id=1, source_target_pairs={{0,1},{1,0},{2,3},{3,2},{4,5},{5,4},{6,7},{7,6},{8,9},{9,8},{10,11... | collective-permute-start | bytes 4325384 | tf_op jit(solution)/shard_map/ppermute | solution.py:120
  776.3 83.6 %collective-permute-start.17 = (bf16[2,256,1408]{2,1,0:T(8,128)(2,1)}, bf16[2,256,1408]{2,1,0:T(8,128)(2,1)}, u32[]{:S(2)}, u32[]{:S(2)}) collective-permute-start(bf16[2,256,1408]{2,1,0:T(8,128)(2,1)} %maximum_select_fusion.17), channel_id=1, source_target_pairs={{0,1},{1,0},{2,3},{3,2},{4,5},{5,4},{6,7},{7,6},{8,9},{9,8},{10,11... | collective-permute-start | bytes 4325384 | tf_op jit(solution)/shard_map/ppermute | solution.py:120
  780.4 19.1 %collective-permute-start.9 = (bf16[256,1408]{1,0:T(8,128)(2,1)S(1)}, bf16[256,1408]{1,0:T(8,128)(2,1)S(1)}, u32[]{:S(2)}, u32[]{:S(2)}) collective-permute-start(bf16[256,1408]{1,0:T(8,128)(2,1)S(1)} %dynamic-slice_bitcast_fusion.4), channel_id=1, source_target_pairs={{0,2},{2,0},{1,3},{3,1},{4,6},{6,4},{5,7},{7,5},{8,10},{10,8},{9,1... | collective-permute-start | bytes 2162696 | tf_op jit(solution)/shard_map/ppermute | solution.py:124
  782.4 31.6 %collective-permute-start.5 = (bf16[256,1408]{1,0:T(8,128)(2,1)S(1)}, bf16[256,1408]{1,0:T(8,128)(2,1)S(1)}, u32[]{:S(2)}, u32[]{:S(2)}) collective-permute-start(bf16[256,1408]{1,0:T(8,128)(2,1)S(1)} %dynamic-slice_bitcast_fusion.5), channel_id=1, source_target_pairs={{0,2},{2,0},{1,3},{3,1},{4,6},{6,4},{5,7},{7,5},{8,10},{10,8},{9,1... | collective-permute-start | bytes 2162696 | tf_op jit(solution)/shard_map/ppermute | solution.py:124
  799.5 111.8 %collective-permute-start.15 = (bf16[2,1408,256]{2,1,0:T(8,128)(2,1)}, bf16[2,1408,256]{2,1,0:T(8,128)(2,1)}, u32[]{:S(2)}, u32[]{:S(2)}) collective-permute-start(bf16[2,1408,256]{2,1,0:T(8,128)(2,1)} %maximum_select_fusion.15), channel_id=1, source_target_pairs={{0,1},{1,0},{2,3},{3,2},{4,5},{5,4},{6,7},{7,6},{8,9},{9,8},{10,11... | collective-permute-start | bytes 4325384 | tf_op jit(solution)/shard_map/ppermute | solution.py:120
  859.8 317.9 %reduce-scatter.22.cloned.1.call-start = ((), (), s32[]{:S(2)}) async-start(), calls=%async_computation.40 | async-start | bytes 1216512 | tf_op jit(solution)/shard_map/reduce_scatter | solution.py:639
  883.8 295.5 %reduce-scatter.20.cloned.1.call-start = ((), (), s32[]{:S(2)}) async-start(), calls=%async_computation.39 | async-start | bytes 1216512 | tf_op jit(solution)/shard_map/reduce_scatter | solution.py:639
  922.4 31.1 %all-to-all-start.15 = ((bf16[4,704,1,384]{3,1,2,0:T(8,128)(2,1)}), bf16[4,704,1,384]{3,1,2,0:T(8,128)(2,1)}, u32[]{:S(2)}, u32[]{:S(2)}) async-start(bf16[4,704,1,384]{3,1,2,0:T(8,128)(2,1)} %bitcast.502), calls=%async_computation.19 | async-start | bytes 4325376 | tf_op jit(solution)/shard_map/all_to_all | solution.py:158
  926.9 254.0 %reduce-scatter.18.cloned.1.call-start = ((), (), s32[]{:S(2)}) async-start(), calls=%async_computation.38 | async-start | bytes 1216512 | tf_op jit(solution)/shard_map/reduce_scatter | solution.py:639
  931.6 299.9 %reduce-scatter.28.cloned.1.call-start = ((), (), s32[]{:S(2)}) async-start(), calls=%async_computation.46 | async-start | bytes 1769472 | tf_op jit(solution)/shard_map/reduce_scatter | solution.py:639
  962.2 362.0 %reduce-scatter.24.cloned.1.call-start = ((), (), s32[]{:S(2)}) async-start(), calls=%async_computation.41 | async-start | bytes 4866048 | tf_op jit(solution)/shard_map/reduce_scatter | solution.py:639
  979.8 27.5 %all-to-all-start.6 = ((bf16[16,1,88,256]{3,2,1,0:T(8,128)(2,1)}), bf16[16,1,88,256]{3,2,1,0:T(8,128)(2,1)S(1)}, u32[]{:S(2)}, u32[]{:S(2)}) async-start(bf16[16,1,88,256]{3,2,1,0:T(8,128)(2,1)} %bitcast.534), calls=%async_computation.6 | async-start | bytes 1441792 | tf_op jit(solution)/shard_map/all_to_all | solution.py:601
  1035.0 53.9 %all-to-all-start.7 = ((bf16[4,1,3,88,1024]{4,3,2,1,0:T(8,128)(2,1)}), bf16[4,1,3,88,1024]{4,3,2,1,0:T(8,128)(2,1)S(1)}, u32[]{:S(2)}, u32[]{:S(2)}) async-start(bf16[4,1,3,88,1024]{4,3,2,1,0:T(8,128)(2,1)} %copy-done.7), calls=%async_computation.7 | async-start | bytes 4325376 | tf_op jit(solution)/shard_map/all_to_all | solution.py:583
  1038.6 378.7 %reduce-scatter.26.cloned.1.call-start = ((), (), s32[]{:S(2)}) async-start(), calls=%async_computation.42 | async-start | bytes 4866048 | tf_op jit(solution)/shard_map/reduce_scatter | solution.py:639
  1049.7 451.2 %reduce-scatter.16.cloned.1.call-start = ((), (), s32[]{:S(2)}) async-start(), calls=%async_computation.37 | async-start | bytes 3649536 | tf_op jit(solution)/shard_map/reduce_scatter | solution.py:639
  1107.2 34.6 %collective-permute-start.12 = (bf16[256,2816]{1,0:T(8,128)(2,1)}, bf16[256,2816]{1,0:T(8,128)(2,1)S(1)}, u32[]{:S(2)}, u32[]{:S(2)}) collective-permute-start(bf16[256,2816]{1,0:T(8,128)(2,1)} %get-tuple-element.188), channel_id=1, source_target_pairs={{0,2},{2,0},{1,3},{3,1},{4,6},{6,4},{5,7},{7,5},{8,10},{10,8},{9,1... | collective-permute-start | bytes 4325384 | tf_op jit(solution)/shard_map/ppermute | solution.py:124
  1119.9 36.7 %collective-permute-start.11 = (bf16[256,1408]{1,0:T(8,128)(2,1)S(1)}, bf16[256,1408]{1,0:T(8,128)(2,1)S(1)}, u32[]{:S(2)}, u32[]{:S(2)}) collective-permute-start(bf16[256,1408]{1,0:T(8,128)(2,1)S(1)} %dynamic-slice_bitcast_fusion.3), channel_id=1, source_target_pairs={{0,2},{2,0},{1,3},{3,1},{4,6},{6,4},{5,7},{7,5},{8,10},{10,8},{9,1... | collective-permute-start | bytes 2162696 | tf_op jit(solution)/shard_map/ppermute | solution.py:124
  1144.0 25.6 %collective-permute-start.13 = (bf16[2,256,2816]{2,1,0:T(8,128)(2,1)}, bf16[2,256,2816]{2,1,0:T(8,128)(2,1)}, u32[]{:S(2)}, u32[]{:S(2)}) collective-permute-start(bf16[2,256,2816]{2,1,0:T(8,128)(2,1)} %maximum_select_fusion.6), channel_id=1, source_target_pairs={{0,1},{1,0},{2,3},{3,2},{4,5},{5,4},{6,7},{7,6},{8,9},{9,8},{10,11... | collective-permute-start | bytes 8650760 | tf_op jit(solution)/shard_map/ppermute | solution.py:120
  1165.2 17.3 %all-to-all-start.8 = ((bf16[4,256,352]{1,2,0:T(8,128)(2,1)}), bf16[4,256,352]{1,2,0:T(8,128)(2,1)}, u32[]{:S(2)}, u32[]{:S(2)}) async-start(bf16[4,256,352]{1,2,0:T(8,128)(2,1)} %bitcast.533), calls=%async_computation.8 | async-start | bytes 1441792 | tf_op jit(solution)/shard_map/all_to_all | solution.py:158
  1185.8 386.4 %reduce-scatter.14.cloned.1.call-start = ((), (), s32[]{:S(2)}) async-start(), calls=%async_computation.36 | async-start | bytes 2433024 | tf_op jit(solution)/shard_map/reduce_scatter | solution.py:639
  1326.1 151.8 %all-to-all-start.19 = ((bf16[4,44,1536]{2,1,0:T(8,128)(2,1)}), bf16[4,44,1536]{2,1,0:T(8,128)(2,1)S(1)}, u32[]{:S(2)}, u32[]{:S(2)}) async-start(bf16[4,44,1536]{2,1,0:T(8,128)(2,1)} %reshape.2291), calls=%async_computation.25 | async-start | bytes 1179648 | tf_op jit(solution)/shard_map/all_to_all | solution.py:158
  1477.9 24.9 %all-to-all-start.20 = ((bf16[4,44,1536]{2,1,0:T(8,128)(2,1)}), bf16[4,44,1536]{2,1,0:T(8,128)(2,1)S(1)}, u32[]{:S(2)}, u32[]{:S(2)}) async-start(bf16[4,44,1536]{2,1,0:T(8,128)(2,1)} %reshape.2292), calls=%async_computation.27 | async-start | bytes 1179648 | tf_op jit(solution)/shard_map/all_to_all | solution.py:158
  (126 other events, 3089.2 us)
Sparse Core Ops, SparseCore 0:
  15.0 124.4 all-reduce.11
  142.4 76.9 all-gather.14
  222.1 60.1 all-gather.16
  285.1 69.8 all-gather.24
  357.7 91.2 all-gather.26
  451.7 61.0 all-gather.28
  515.7 65.5 all-gather.18
  583.4 86.9 all-gather.20
  672.5 74.1 all-gather.22
  848.4 93.7 reduce-scatter.29
  945.6 62.4 reduce-scatter.21
  1012.0 87.7 reduce-scatter.19
  1103.8 60.6 reduce-scatter.17
  1167.7 63.6 reduce-scatter.27
  1235.3 88.7 reduce-scatter.23
  1327.6 89.7 reduce-scatter.25
  1421.3 79.6 reduce-scatter.15
  1504.7 67.5 reduce-scatter.13

commit v2 on v1

--- a/solution.py
+++ b/solution.py
@@ -116,49 +116,125 @@
     return rotate(head_norm(vector), cosine, sines)
 
 
-def swap_core(value):
-    return lax.ppermute(value, "cp", [(0, 1), (1, 0), (2, 3), (3, 2)])
-
-
-def swap_chip(value):
-    return lax.ppermute(value, "cp", [(0, 2), (2, 0), (1, 3), (3, 1)])
+def trade_bit(value, axis, bit):
+    count = lax.axis_size(axis)
+    return lax.ppermute(value, axis, [(k, k ^ bit) for k in range(count)])
+
+
+def bits_of(axis):
+    count = lax.axis_size(axis)
+    return [1 << k for k in range(count.bit_length() - 1)]
+
+
+def has_bit(axis, bit):
+    return (lax.axis_index(axis) // bit) % 2 == 1
+
+
+def pieces_cp(value):
+    pieces = [value]
+    found = {0: value}
+    for bit in reversed(bits_of("cp")):
+        for key in list(found):
+            found[key | bit] = trade_bit(found[key], "cp", bit)
+    pieces = [found[key] for key in range(lax.axis_size("cp"))]
+    return pieces
+
+
+def reorder_cp(pieces):
+    for bit in bits_of("cp"):
+        high = has_bit("cp", bit)
+        pieces = [
+            jnp.where(high, pieces[key ^ bit], pieces[key]) for key in range(len(pieces))
+        ]
+    return pieces
 
 
 def gather_cp(value):
+    return jnp.stack(reorder_cp(pieces_cp(value)))
+
+
+def scatter_cp(pieces):
+    pieces = [piece.astype(bf16) for piece in pieces]
+    for bit in bits_of("cp"):
+        pieces = [
+            (
+                pieces[key].astype(f32) + trade_bit(pieces[key + 1], "cp", bit).astype(f32)
+            ).astype(f32 if len(pieces) == 2 else bf16)
+            for key in range(0, len(pieces), 2)
+        ]
+    return pieces[0]
+
+
+def after(value, *others):
+    for other in others:
+        value = value + (other[(0,) * other.ndim].astype(f32) * 0.0).astype(value.dtype)
+    return value
+
+
+def exchange_cp(pieces):
     count = lax.axis_size("cp")
-    if count != 4:
-        return lax.all_gather(value, "cp", axis=0, tiled=False)
-    index = lax.axis_index("cp")
-    chip, core = index // 2, index % 2
-    other = swap_chip(value)
-    pair = jnp.where(chip == 0, jnp.stack([value, other]), jnp.stack([other, value]))
-    second = swap_core(pair)
-    return jnp.where(
-        core == 0, jnp.stack([pair, second], axis=1), jnp.stack([second, pair], axis=1)
-    ).reshape((4,) + value.shape)
-
-
-def scatter_cp(partial):
-    count = lax.axis_size("cp")
-    partial = partial.astype(bf16)
-    if count != 4:
-        return lax.psum_scatter(partial, "cp", scatter_dimension=0, tiled=False).astype(f32)
-    index = lax.axis_index("cp")
-    chip, core = index // 2, index % 2
-    parts = partial.reshape((2, 2) + partial.shape[1:])
-    keep = lax.dynamic_index_in_dim(parts, core, 1, keepdims=False)
-    send = lax.dynamic_index_in_dim(parts, 1 - core, 1, keepdims=False)
-    both = (keep.astype(f32) + swap_core(send).astype(f32)).astype(bf16)
-    keep = lax.dynamic_index_in_dim(both, chip, 0, keepdims=False)
-    send = lax.dynamic_index_in_dim(both, 1 - chip, 0, keepdims=False)
-    return keep.astype(f32) + swap_chip(send).astype(f32)
+    return [pieces[0]] + [
+        lax.ppermute(pieces[key], "cp", [(k, k ^ key) for k in range(count)])
+        for key in range(1, count)
+    ]
 
 
 def trade_cp(blocks):
     return lax.all_to_all(blocks, "cp", split_axis=0, concat_axis=0, tiled=True)
 
 
+def send_cp(blocks):
+    return reorder_cp(exchange_cp(reorder_cp(blocks)))
+
+
+def group_steps():
+    steps = [("dp", bit, bit * lax.axis_size("sp")) for bit in bits_of("dp")]
+    return steps + [("sp", bit, bit) for bit in bits_of("sp")]
+
+
+def group_differences():
+    differences = [0]
+    for _, _, weight in reversed(group_steps()):
+        differences = differences + [key ^ weight for key in differences]
+    return differences
+
+
+def scatter_group_halves(keep, send, waits):
+    for step, (axis, bit, _) in enumerate(group_steps()):
+        came = trade_bit(send, axis, bit).astype(f32)
+        total = after(keep.astype(f32) + came, waits[step]).astype(bf16)
+        half = total.shape[0] // 2
+        keep, send = total[:half], total[half:]
+        if step == len(group_steps()) - 1:
+            return total
+    return None
+
+
+def gather_every(value):
+    for axis in reversed(EVERY):
+        for bit in bits_of(axis):
+            other = trade_bit(value, axis, bit)
+            value = jnp.where(
+                has_bit(axis, bit), jnp.stack([other, value]), jnp.stack([value, other])
+            )
+    depth = sum(len(bits_of(axis)) for axis in EVERY)
+    return value.reshape((-1,) + value.shape[depth:])
+
+
+def scatter_every(value):
+    for axis in EVERY:
+        for bit in reversed(bits_of(axis)):
+            halves = value.reshape((2, -1) + value.shape[1:])
+            high = has_bit(axis, bit)
+            keep = jnp.where(high, halves[1], halves[0])
+            send = jnp.where(high, halves[0], halves[1])
+            value = keep + trade_bit(send, axis, bit)
+    return value[0]
+
+
 def flip(block):
+    if block.shape[0] % 128 == 0 and block.shape[1] % 128 == 0:
+        return jnp.transpose(block)
     return jnp.transpose(block.astype(f32)).astype(bf16)
 
 
@@ -181,12 +257,14 @@
     return lax.fori_loop(first + fours * 4, last, step, carry)
 
 
-def self_forward_kernel(first_ref, last_ref, qkv_ref, out_ref, total_ref, keys):
+def self_forward_kernel(first_ref, last_ref, turned_ref, qkv_ref, *refs):
+    out_ref, total_ref, keys = refs[-3:]
     pair = pl.program_id(0)
     per = qkv_ref.shape[-1] // CELL
 
     def where(cell):
-        return cell // per, pl.ds(pl.multiple_of((cell % per) * CELL, CELL), CELL)
+        lanes = ((cell % per) ^ turned_ref[0]) * CELL
+        return cell // per, pl.ds(pl.multiple_of(lanes, CELL), CELL)
 
     def turn_keys(cell, carry):
         chunk, lanes = where(cell)
@@ -226,21 +304,20 @@
     first_ref,
     last_ref,
     valid_ref,
+    turned_ref,
     qkv_ref,
     grad_ref,
     out_ref,
     total_ref,
-    result_ref,
-    keys,
-    values,
-    key_sums,
-    value_sums,
+    *refs,
 ):
+    result_ref, keys, values, key_sums, value_sums = refs[-5:]
     pair = pl.program_id(0)
     per = qkv_ref.shape[-1] // CELL
 
     def where(cell):
-        return cell // per, pl.ds(pl.multiple_of((cell % per) * CELL, CELL), CELL)
+        lanes = ((cell % per) ^ turned_ref[0]) * CELL
+        return cell // per, pl.ds(pl.multiple_of(lanes, CELL), CELL)
 
     def prepare(cell, carry):
         chunk, lanes = where(cell)
@@ -295,10 +372,13 @@
     return pl.BlockSpec(block, lambda pair, *_: (0, pair) + rest)
 
 
-VMEM_LIMIT = 40 * 1024 * 1024
-
-
-def self_forward(qkv, first, last):
+VMEM_WHOLE = pl.BlockSpec(memory_space=pltpu.VMEM)
+SMEM_WHOLE = pl.BlockSpec(memory_space=pltpu.SMEM)
+ANY_WHOLE = pl.BlockSpec(memory_space=pl.ANY)
+VMEM_LIMIT = 48 * 1024 * 1024
+
+
+def self_forward(qkv, first, last, turned, stamps):
     chunks, pairs, _, _, columns = qkv.shape
     out_shape = (chunks, pairs, HEAD, columns)
     total_shape = (chunks, pairs, 1, columns)
@@ -309,31 +389,33 @@
             jax.ShapeDtypeStruct(total_shape, f32),
         ),
         grid_spec=pltpu.PrefetchScalarGridSpec(
-            num_scalar_prefetch=2,
+            num_scalar_prefetch=3,
             grid=(pairs,),
-            in_specs=[pair_spec(qkv.shape)],
+            in_specs=[pair_spec(qkv.shape)] + [pl.BlockSpec(memory_space=pl.ANY)] * len(stamps),
             out_specs=[pair_spec(out_shape), pair_spec(total_shape)],
             scratch_shapes=[pltpu.VMEM((CELLS, CELL, HEAD), bf16)],
         ),
         compiler_params=pltpu.CompilerParams(vmem_limit_bytes=VMEM_LIMIT),
+        cost_estimate=pl.CostEstimate(flops=10**10, bytes_accessed=8 << 20, transcendentals=0),
         name="self_forward",
-    )(first, last, qkv)
-
-
-def self_backward(qkv, grad, out, totals, first, last, valid):
+    )(first, last, turned, qkv, *stamps)
+
+
+def self_backward(qkv, grad, out, totals, first, last, valid, turned, stamps):
     pairs = qkv.shape[1]
     return pl.pallas_call(
         self_backward_kernel,
         out_shape=jax.ShapeDtypeStruct(qkv.shape, bf16),
         grid_spec=pltpu.PrefetchScalarGridSpec(
-            num_scalar_prefetch=3,
+            num_scalar_prefetch=4,
             grid=(pairs,),
             in_specs=[
                 pair_spec(qkv.shape),
                 pair_spec(grad.shape),
                 pair_spec(out.shape),
                 pair_spec(totals.shape),
-            ],
+            ]
+            + [pl.BlockSpec(memory_space=pl.ANY)] * len(stamps),
             out_specs=pair_spec(qkv.shape),
             scratch_shapes=[
                 pltpu.VMEM((CELLS, CELL, HEAD), bf16),
@@ -343,8 +425,9 @@
             ],
         ),
         compiler_params=pltpu.CompilerParams(vmem_limit_bytes=VMEM_LIMIT),
+        cost_estimate=pl.CostEstimate(flops=18 * 10**9, bytes_accessed=16 << 20, transcendentals=0),
         name="self_backward",
-    )(first, last, valid, qkv, grad, out, totals)
+    )(first, last, valid, turned, qkv, grad, out, totals, *stamps)
 
 
 def text_weights(key_block, query):
@@ -426,6 +509,699 @@
         compiler_params=pltpu.CompilerParams(vmem_limit_bytes=VMEM_LIMIT),
         name="cross_backward",
     )(*inputs)
+
+
+def unpack_kernel(width, text, bucket_ref, stamp_ref, *outs):
+    padded = width + -width % 128
+    for part in range(3):
+        block = bucket_ref[:, part * padded : (part + 1) * padded]
+        outs[part][...] = flip(block)[:width]
+    rows = D * text // DT
+    for group in range(DT // text):
+        outs[3][group * text : (group + 1) * text, :] = bucket_ref[
+            group * rows : group * rows + text, 3 * padded : 3 * padded + 2 * width
+        ]
+
+
+def unpack_mid(bucket, width, text, stamp):
+    part = jax.ShapeDtypeStruct((width, D), bf16)
+    return pl.pallas_call(
+        functools.partial(unpack_kernel, width, text),
+        out_shape=(part, part, part, jax.ShapeDtypeStruct((DT, 2 * width), bf16)),
+        in_specs=[VMEM_WHOLE, ANY_WHOLE],
+        out_specs=[VMEM_WHOLE] * 4,
+        compiler_params=pltpu.CompilerParams(vmem_limit_bytes=VMEM_LIMIT),
+        cost_estimate=pl.CostEstimate(flops=1, bytes_accessed=12 << 20, transcendentals=0),
+        name="unpack_mid",
+    )(bucket, stamp)
+
+
+def turn_over_kernel(value_ref, out_ref):
+    out_ref[...] = flip(value_ref[...])
+
+
+def turn_over(value):
+    return pl.pallas_call(
+        turn_over_kernel,
+        out_shape=jax.ShapeDtypeStruct(value.shape[::-1], value.dtype),
+        in_specs=[pl.BlockSpec(memory_space=pltpu.VMEM)],
+        out_specs=pl.BlockSpec(memory_space=pltpu.VMEM),
+        compiler_params=pltpu.CompilerParams(vmem_limit_bytes=VMEM_LIMIT),
+        cost_estimate=pl.CostEstimate(flops=1, bytes_accessed=2 << 20, transcendentals=0),
+        name="turn_over",
+    )(value)
+
+
+def expand_grads_kernel(*refs):
+    left = jnp.concatenate([ref[...] for ref in refs[:-2]], axis=1)
+    refs[-1][...] = kernel_dot(left, refs[-2][...]).astype(bf16)
+
+
+def expand_grads(pieces, right):
+    steps = 4
+    rows, width = D // steps, right.shape[1]
+    return pl.pallas_call(
+        expand_grads_kernel,
+        out_shape=jax.ShapeDtypeStruct((D, width), bf16),
+        grid=(steps,),
+        in_specs=[pl.BlockSpec((rows, pieces[0].shape[1]), lambda g: (g, 0))] * len(pieces)
+        + [pl.BlockSpec(right.shape, lambda g: (0, 0))],
+        out_specs=pl.BlockSpec((rows, width), lambda g: (g, 0)),
+        compiler_params=pltpu.CompilerParams(vmem_limit_bytes=VMEM_LIMIT),
+        cost_estimate=pl.CostEstimate(
+            flops=2 * D * right.shape[0] * width, bytes_accessed=12 << 20, transcendentals=0
+        ),
+        name="expand_grads",
+    )(*pieces, right)
+
+
+def reduce_grads_kernel(group_ref, *refs):
+    pieces, (right_ref, keep_ref, send_ref) = refs[:-3], refs[-3:]
+    step, steps = pl.program_id(0), pl.num_programs(0)
+    left = jnp.concatenate([ref[...] for ref in pieces], axis=1)
+    product = kernel_dot(left, right_ref[...]).astype(bf16)
+
+    @pl.when(step < steps // 2)
+    def _():
+        keep_ref[...] = product
+
+    @pl.when(step >= steps // 2)
+    def _():
+        send_ref[...] = product
+
+
+def reduce_grads(pieces, right, groups):
+    steps, width = groups.shape[0], right.shape[1]
+    rows, half = D // steps, steps // 2
+    shape = jax.ShapeDtypeStruct((D // 2, width), bf16)
+    return pl.pallas_call(
+        reduce_grads_kernel,
+        out_shape=(shape, shape),
+        grid_spec=pltpu.PrefetchScalarGridSpec(
+            num_scalar_prefetch=1,
+            grid=(steps,),
+            in_specs=[
+                pl.BlockSpec((rows, pieces[0].shape[1]), lambda g, group: (group[g], 0))
+            ]
+            * len(pieces)
+            + [pl.BlockSpec(right.shape, lambda g, group: (0, 0))],
+            out_specs=[
+                pl.BlockSpec((rows, width), lambda g, group: (jnp.minimum(g, half - 1), 0)),
+                pl.BlockSpec((rows, width), lambda g, group: (jnp.maximum(g - half, 0), 0)),
+            ],
+        ),
+        compiler_params=pltpu.CompilerParams(vmem_limit_bytes=VMEM_LIMIT),
+        cost_estimate=pl.CostEstimate(
+            flops=2 * D * right.shape[0] * width, bytes_accessed=12 << 20, transcendentals=0
+        ),
+        name="reduce_grads",
+    )(groups, *pieces, right)
+
+
+def mid_grads_kernel(count, width, *refs):
+    lefts, rights, texts, pairs = (refs[k * count : (k + 1) * count] for k in range(4))
+    out_ref = refs[4 * count + 1]
+    rows = out_ref.shape[0]
+    padded = width + -width % 128
+    for part in range(3):
+        product = sum(
+            kernel_dot(left[part], right[part], 1, 1) for left, right in zip(lefts, rights)
+        )
+        product = jnp.concatenate([product, jnp.zeros((rows, padded - width), f32)], axis=1)
+        out_ref[:, part * padded : (part + 1) * padded] = product.astype(bf16)
+    text = texts[0].shape[0]
+    product = sum(kernel_dot(left[...], right[...], 1, 1) for left, right in zip(texts, pairs))
+    rest = out_ref.shape[1] - 3 * padded
+    product = jnp.concatenate([product, jnp.zeros((text, rest - 2 * width), f32)], axis=1)
+    out_ref[:text, 3 * padded :] = product.astype(bf16)
+    out_ref[text:, 3 * padded :] = jnp.zeros((rows - text, rest), bf16)
+
+
+def mid_grads_bucket(lefts, rights, texts, pairs, stamp, groups):
+    count, width = len(lefts), rights[0].shape[1]
+    rows, text = D // groups, DT // groups
+    columns = 3 * (width + -width % 128) + 2 * width + -2 * width % 128
+    return pl.pallas_call(
+        functools.partial(mid_grads_kernel, count, width),
+        out_shape=jax.ShapeDtypeStruct((D, columns), bf16),
+        grid=(groups,),
+        in_specs=[pl.BlockSpec((3, rows, lefts[0].shape[2]), lambda g: (0, g, 0))] * count
+        + [pl.BlockSpec(rights[0].shape, lambda g: (0, 0, 0))] * count
+        + [pl.BlockSpec((text, texts[0].shape[1]), lambda g: (g, 0))] * count
+        + [pl.BlockSpec(pairs[0].shape, lambda g: (0, 0))] * count
+        + [ANY_WHOLE],
+        out_specs=pl.BlockSpec((rows, columns), lambda g: (g, 0)),
+        compiler_params=pltpu.CompilerParams(vmem_limit_bytes=VMEM_LIMIT),
+        cost_estimate=pl.CostEstimate(
+            flops=10 * D * D * width, bytes_accessed=24 << 20, transcendentals=0
+        ),
+        name="mid_grads",
+    )(*lefts, *rights, *texts, *pairs, stamp)
+
+
+def skip_grads_kernel(count, width, *refs):
+    rights, lefts = refs[:count], refs[count : 2 * count]
+    input_ref, out_ref = refs[2 * count :]
+    product = sum(kernel_dot(left[...], right[...]) for left, right in zip(lefts, rights))
+    padded = width + -width % 128
+    quarter = width // (2 * count)
+    product = jnp.transpose(product)
+    group_rows = count * quarter
+    fill = jnp.zeros((group_rows, padded - width), f32)
+    for group in range(product.shape[0] // width):
+        for part in range(2):
+            starts = [
+                group * width + (2 * k + part) * quarter for k in range(count)
+            ]
+            block = jnp.concatenate(
+                [product[start : start + quarter] for start in starts], axis=0
+            )
+            out_ref[
+                group * group_rows : (group + 1) * group_rows,
+                part * padded : (part + 1) * padded,
+            ] = jnp.concatenate([block, fill], axis=1).astype(bf16)
+    out_ref[:, 2 * padded : 2 * padded + input_ref.shape[1]] = input_ref[...]
+    rest = out_ref.shape[1] - 2 * padded - input_ref.shape[1]
+    out_ref[:, 2 * padded + input_ref.shape[1] :] = jnp.zeros((out_ref.shape[0], rest), bf16)
+
+
+def skip_grads_bucket(lefts, rights, inputs):
+    count, width = len(lefts), lefts[0].shape[0]
+    columns = 2 * (width + -width % 128) + inputs.shape[1] + -inputs.shape[1] % 128
+    return pl.pallas_call(
+        functools.partial(skip_grads_kernel, count, width),
+        out_shape=jax.ShapeDtypeStruct((D, columns), bf16),
+        grid=(2,),
+        in_specs=[pl.BlockSpec((rights[0].shape[0], D), lambda g: (0, g))] * count
+        + [pl.BlockSpec(lefts[0].shape, lambda g: (0, 0))] * count
+        + [pl.BlockSpec((D // 2, inputs.shape[1]), lambda g: (g, 0))],
+        out_specs=pl.BlockSpec((D // 2, columns), lambda g: (g, 0)),
+        compiler_params=pltpu.CompilerParams(vmem_limit_bytes=VMEM_LIMIT),
+        cost_estimate=pl.CostEstimate(
+            flops=4 * D * width * count * 256, bytes_accessed=16 << 20, transcendentals=0
+        ),
+        name="skip_grads",
+    )(*rights, *lefts, inputs)
+
+
+def finish_kernel(factor_ref, blocks_ref, skip_ref, input_ref):
+    factor = factor_ref[0, 0]
+    count, shard, _ = blocks_ref.shape
+    width = skip_ref.shape[1] // count
+    padded = width + -width % 128
+    blocks = [blocks_ref[k].astype(f32) * factor for k in range(count)]
+    for part in range(2):
+        skip_ref[part * shard : (part + 1) * shard, :] = jnp.concatenate(
+            [block[:, part * padded : part * padded + width] for block in blocks], axis=1
+        )
+    input_ref[...] = jnp.concatenate(
+        [
+            block[:, 2 * padded + part * width : 2 * padded + (part + 1) * width]
+            for part in range(3)
+            for block in blocks
+        ],
+        axis=1,
+    )
+
+
+def finish_head(blocks, factor):
+    count, shard, _ = blocks.shape
+    return pl.pallas_call(
+        finish_kernel,
+        out_shape=(
+            jax.ShapeDtypeStruct((2 * shard, D), f32),
+            jax.ShapeDtypeStruct((shard, 3 * D), f32),
+        ),
+        in_specs=[pl.BlockSpec(memory_space=pltpu.SMEM), pl.BlockSpec(memory_space=pltpu.VMEM)],
+        out_specs=[pl.BlockSpec(memory_space=pltpu.VMEM)] * 2,
+        compiler_params=pltpu.CompilerParams(vmem_limit_bytes=VMEM_LIMIT),
+        cost_estimate=pl.CostEstimate(flops=1, bytes_accessed=2 << 20, transcendentals=0),
+        name="finish_head",
+    )(factor.reshape(1, 1), blocks)
+
+
+def norm_rows(value):
+    centred = value - jnp.mean(value, axis=0, keepdims=True)
+    scale = lax.rsqrt(jnp.mean(centred * centred, axis=0, keepdims=True) + epsilon)
+    return centred * scale, scale
+
+
+def norm_rows_back(normed, scale, grad):
+    return scale * (
+        grad
+        - jnp.mean(grad, axis=0, keepdims=True)
+        - normed * jnp.mean(grad * normed, axis=0, keepdims=True)
+    )
+
+
+def fetch(sources, targets, sems, base):
+    copies = [
+        pltpu.make_async_copy(source, target, sems.at[base + k])
+        for k, (source, target) in enumerate(zip(sources, targets))
+    ]
+    for copy in copies:
+        copy.start()
+    return copies
+
+
+def mix_kernel(count, padded, *refs):
+    index_ref, bucket_ref = refs[:2]
+    pieces = refs[2 : 2 + count]
+    out_ref, weight = refs[2 + count :]
+    width = weight.shape[1]
+    half = width // 2
+    for group in range(weight.shape[0] // width):
+        for part in range(2):
+            start = group * width + part * half
+            weight[start : start + half, :] = bucket_ref[
+                group * half : (group + 1) * half, part * padded : part * padded + width
+            ]
+    for piece in range(count):
+        out_ref[piece ^ index_ref[0]] = kernel_dot(pieces[piece][...], weight[...]).astype(bf16)
+
+
+def mix(index, bucket, pieces, width):
+    count, padded = len(pieces), width + -width % 128
+    rows = pieces[0].shape[0]
+    return pl.pallas_call(
+        functools.partial(mix_kernel, count, padded),
+        out_shape=jax.ShapeDtypeStruct((count, rows, width), bf16),
+        grid=(1,),
+        in_specs=[SMEM_WHOLE, pl.BlockSpec((D, 2 * padded), lambda g: (0, 0))]
+        + [pl.BlockSpec(pieces[0].shape, lambda g: (0, 0))] * count,
+        out_specs=pl.BlockSpec((count, rows, width), lambda g: (0, 0, 0)),
+        scratch_shapes=[pltpu.VMEM((2 * D, width), bf16)],
+        compiler_params=pltpu.CompilerParams(vmem_limit_bytes=VMEM_LIMIT),
+        cost_estimate=pl.CostEstimate(
+            flops=4 * D * width * count * rows, bytes_accessed=8 << 20, transcendentals=0
+        ),
+        name="mix",
+    )(index, bucket, *pieces)
+
+
+def mixed_rows(blocks_ref, stage):
+    width = blocks_ref.shape[2]
+    for block in range(blocks_ref.shape[0]):
+        turned = jnp.transpose(blocks_ref[block].astype(f32))
+        stage[block * width : (block + 1) * width, :] = turned
+    return stage[...]
+
+
+def start_kernel(blocks_ref, gain_ref, shift_ref, base_ref, normed_ref, stage):
+    base = norm_rows(mixed_rows(blocks_ref, stage))[0] * gain_ref[:, 0:1]
+    base_ref[...] = base
+    normed = norm_rows(base)[0] * gain_ref[:, 1:2] + shift_ref[...]
+    normed_ref[...] = normed.astype(bf16)
+
+
+def start_forward(blocks, gains, shift):
+    tokens = blocks.shape[1]
+    return pl.pallas_call(
+        start_kernel,
+        out_shape=(
+            jax.ShapeDtypeStruct((D, tokens), f32),
+            jax.ShapeDtypeStruct((D, tokens), bf16),
+        ),
+        in_specs=[VMEM_WHOLE] * 3,
+        out_specs=[VMEM_WHOLE] * 2,
+        scratch_shapes=[pltpu.VMEM((D, tokens), f32)],
+        compiler_params=pltpu.CompilerParams(vmem_limit_bytes=VMEM_LIMIT),
+        cost_estimate=pl.CostEstimate(flops=1, bytes_accessed=8 << 20, transcendentals=0),
+        name="start_forward",
+    )(blocks, gains, shift)
+
+
+def start_back_kernel(
+    blocks_ref, gain_ref, base_ref, mid_grad_ref, grad_ref, out_ref, sums_ref, stage
+):
+    normed, scale = norm_rows(base_ref[...])
+    grad = grad_ref[...]
+    sums_ref[:, 1:2] = jnp.sum(grad * normed, axis=1, keepdims=True)
+    sums_ref[:, 2:3] = jnp.sum(grad, axis=1, keepdims=True)
+    base_grad = mid_grad_ref[...] + norm_rows_back(normed, scale, grad * gain_ref[:, 1:2])
+    normed, scale = norm_rows(mixed_rows(blocks_ref, stage))
+    sums_ref[:, 0:1] = jnp.sum(base_grad * normed, axis=1, keepdims=True)
+    mixed_grad = norm_rows_back(normed, scale, base_grad * gain_ref[:, 0:1]).astype(bf16)
+    width = out_ref.shape[1]
+    for block in range(out_ref.shape[0]):
+        out_ref[block] = mixed_grad[block * width : (block + 1) * width]
+
+
+def start_backward(blocks, gains, base, mid_grad, grad):
+    count, tokens, width = blocks.shape
+    return pl.pallas_call(
+        start_back_kernel,
+        out_shape=(
+            jax.ShapeDtypeStruct((count, width, tokens), bf16),
+            jax.ShapeDtypeStruct((D, 3), f32),
+        ),
+        in_specs=[VMEM_WHOLE] * 5,
+        out_specs=[VMEM_WHOLE] * 2,
+        scratch_shapes=[pltpu.VMEM((D, tokens), f32)],
+        compiler_params=pltpu.CompilerParams(vmem_limit_bytes=VMEM_LIMIT),
+        cost_estimate=pl.CostEstimate(flops=1, bytes_accessed=10 << 20, transcendentals=0),
+        name="start_backward",
+    )(blocks, gains, base, mid_grad, grad)
+
+
+def middle_forward_kernel(count, *refs):
+    index_ref, attended_ref, base_ref, gain_ref, key_ref, value_ref = refs[:6]
+    sources = refs[6 : 6 + 3 * count]
+    (
+        mid_ref,
+        late_ref,
+        lefts_ref,
+        raw_ref,
+        query_ref,
+        out_ref,
+        total_ref,
+        ffn_ref,
+    ) = refs[6 + 3 * count : 14 + 3 * count]
+    weights, sems = refs[14 + 3 * count :]
+    copies = fetch(sources, [weights.at[k] for k in range(3 * count)], sems, 0)
+    index = index_ref[0]
+    width = D // count
+    heads = HEADS // count
+
+    def rows_of_piece(piece):
+        return pl.ds(pl.multiple_of((piece ^ index) * width, 32), width)
+
+    attended = attended_ref[...]
+    for piece in range(count):
+        copies[piece].wait()
+        rows = rows_of_piece(piece)
+        mid_ref[rows, :] = base_ref[rows, :] + kernel_dot(weights[piece], attended)
+    normed = (norm_rows(mid_ref[...])[0] * gain_ref[:, 2:3]).astype(bf16)
+    lefts_ref[0] = normed
+    lefts_ref[2] = attended
+    for piece in range(count):
+        copies[count + piece].wait()
+        product = kernel_dot(weights[count + piece], normed)
+        for head in range(heads):
+            raw_ref[(piece ^ index) * heads + head] = product[head * HEAD : (head + 1) * HEAD]
+    for head in range(HEADS):
+        query = norm_rows(raw_ref[head])[0].astype(bf16)
+        query_ref[head] = query
+        attention = text_weights(key_ref[head], query)
+        totals = jnp.sum(attention, axis=0, keepdims=True)
+        out = kernel_dot(value_ref[head], attention.astype(bf16)) / totals
+        out_ref[head * HEAD : (head + 1) * HEAD, :] = out
+        total_ref[head] = totals
+    crossed = out_ref[...].astype(bf16)
+    lefts_ref[1] = crossed
+    for piece in range(count):
+        copies[2 * count + piece].wait()
+        rows = rows_of_piece(piece)
+        late_ref[rows, :] = mid_ref[rows, :] + kernel_dot(weights[2 * count + piece], crossed)
+    ffn_ref[...] = (norm_rows(late_ref[...])[0] * gain_ref[:, 3:4]).astype(bf16)
+
+
+def middle_forward(index, attended, base, gains, keys, values, weights):
+    count = len(weights) // 3
+    tokens = attended.shape[1]
+    stream = jax.ShapeDtypeStruct((D, tokens), f32)
+    by_head = (HEADS, HEAD, tokens)
+    return pl.pallas_call(
+        functools.partial(middle_forward_kernel, count),
+        out_shape=(
+            stream,
+            stream,
+            jax.ShapeDtypeStruct((3, D, tokens), bf16),
+            jax.ShapeDtypeStruct(by_head, f32),
+            jax.ShapeDtypeStruct(by_head, bf16),
+            stream,
+            jax.ShapeDtypeStruct((HEADS, 1, tokens), f32),
+            jax.ShapeDtypeStruct((D, tokens), bf16),
+        ),
+        in_specs=[SMEM_WHOLE] + [VMEM_WHOLE] * 5 + [ANY_WHOLE] * (3 * count),
+        out_specs=[VMEM_WHOLE] * 8,
+        scratch_shapes=[
+            pltpu.VMEM((3 * count, D // count, D), bf16),
+            pltpu.SemaphoreType.DMA((3 * count,)),
+        ],
+        compiler_params=pltpu.CompilerParams(vmem_limit_bytes=VMEM_LIMIT),
+        cost_estimate=pl.CostEstimate(
+            flops=10 * D * D * tokens, bytes_accessed=24 << 20, transcendentals=0
+        ),
+        name="middle_forward",
+    )(index, attended, base, gains, keys, values, *weights)
+
+
+def middle_backward_kernel(count, stamps, *refs):
+    (
+        index_ref,
+        ffn_grad_ref,
+        out_grad_ref,
+        late_ref,
+        mid_ref,
+        gain_ref,
+        query_ref,
+        key_ref,
+        value_ref,
+        out_ref,
+        total_ref,
+        raw_ref,
+    ) = refs[:12]
+    sources = refs[12 : 12 + 3 * count]
+    (
+        late_grad_ref,
+        raw_grad_ref,
+        mid_grad_ref,
+        mid_round_ref,
+        attended_grad_ref,
+        key_grad_ref,
+        value_grad_ref,
+        gain_grad_ref,
+    ) = refs[12 + stamps + 3 * count : 20 + stamps + 3 * count]
+    weights, stage, sems = refs[20 + stamps + 3 * count :]
+    order = [2, 1, 0]
+    copies = []
+    for place in order:
+        copies += fetch(
+            sources[place * count : (place + 1) * count],
+            [weights.at[place * count + k] for k in range(count)],
+            sems,
+            place * count,
+        )
+    index = index_ref[0]
+    width = D // count
+
+    def through(place, turn, source_ref):
+        total = 0.0
+        for piece in range(count):
+            copies[turn * count + piece].wait()
+            rows = pl.ds(pl.multiple_of((piece ^ index) * width, 32), width)
+            total = total + kernel_dot(flip(source_ref[rows, :]), weights[place * count + piece])
+        return jnp.transpose(total)
+
+    normed, scale = norm_rows(late_ref[...])
+    grad = ffn_grad_ref[...]
+    gain_grad_ref[:, 1:2] = jnp.sum(grad * normed, axis=1, keepdims=True)
+    late_grad = out_grad_ref[...].astype(f32) + norm_rows_back(
+        normed, scale, grad * gain_ref[:, 3:4]
+    )
+    mid_grad_ref[...] = late_grad
+    late_grad_ref[...] = late_grad.astype(bf16)
+    stage[...] = through(2, 0, late_grad_ref).astype(bf16).astype(f32)
+    for head in range(HEADS):
+        rows = slice(head * HEAD, (head + 1) * HEAD)
+        query, keys = query_ref[head], key_ref[head]
+        grad = stage[rows, :]
+        inverse = 1.0 / total_ref[head]
+        scaled = (grad * inverse).astype(bf16)
+        total_grad = -jnp.sum(grad * out_ref[rows, :], axis=0, keepdims=True) * inverse
+        attention = text_weights(keys, query)
+        weight_grad = kernel_dot(flip(value_ref[head]), scaled)
+        score_grad = (attention * (weight_grad + total_grad)).astype(bf16)
+        query_grad = (kernel_dot(keys, score_grad) * SCALING).astype(bf16).astype(f32)
+        key_grad_ref[head] = kernel_dot(query, score_grad, 1, 1) * SCALING
+        value_grad_ref[head] = kernel_dot(scaled, attention.astype(bf16), 1, 1)
+        normed, scale = norm_rows(raw_ref[head])
+        stage[rows, :] = norm_rows_back(normed, scale, query_grad)
+    raw_grad_ref[...] = stage[...].astype(bf16)
+    grad = through(1, 1, raw_grad_ref)
+    normed, scale = norm_rows(mid_ref[...])
+    gain_grad_ref[:, 0:1] = jnp.sum(grad * normed, axis=1, keepdims=True)
+    mid_grad = mid_grad_ref[...] + norm_rows_back(normed, scale, grad * gain_ref[:, 2:3])
+    mid_grad_ref[...] = mid_grad
+    mid_round_ref[...] = mid_grad.astype(bf16)
+    attended_grad_ref[...] = through(0, 2, mid_round_ref).astype(bf16)
+
+
+def middle_backward(index, arrays, weights, stamps):
+    count = len(weights) // 3
+    tokens = arrays[0].shape[1]
+    rounded = jax.ShapeDtypeStruct((D, tokens), bf16)
+    texts = jax.ShapeDtypeStruct((HEADS, HEAD, TEXT_PAD), f32)
+    return pl.pallas_call(
+        functools.partial(middle_backward_kernel, count, len(stamps)),
+        out_shape=(
+            rounded,
+            rounded,
+            jax.ShapeDtypeStruct((D, tokens), f32),
+            rounded,
+            rounded,
+            texts,
+            texts,
+            jax.ShapeDtypeStruct((D, 2), f32),
+        ),
+        in_specs=[SMEM_WHOLE]
+        + [VMEM_WHOLE] * 11
+        + [ANY_WHOLE] * (3 * count + len(stamps)),
+        out_specs=[VMEM_WHOLE] * 8,
+        scratch_shapes=[
+            pltpu.VMEM((3 * count, D // count, D), bf16),
+            pltpu.VMEM((D, tokens), f32),
+            pltpu.SemaphoreType.DMA((3 * count,)),
+        ],
+        compiler_params=pltpu.CompilerParams(vmem_limit_bytes=VMEM_LIMIT),
+        cost_estimate=pl.CostEstimate(
+            flops=14 * D * D * tokens, bytes_accessed=30 << 20, transcendentals=0
+        ),
+        name="middle_backward",
+    )(index, *arrays, *weights, *stamps)
+
+
+GELU_SCALE = math.sqrt(2.0 / math.pi)
+
+
+def ffn_kernel(count, *refs):
+    inputs, grads = refs[:count], refs[count : 2 * count]
+    expand_ref, reduce_ref, hidden_ref, expand_in_ref = refs[2 * count : 2 * count + 4]
+    outputs = refs[2 * count + 4 :]
+    back_refs, out_refs = outputs[:count], outputs[count : 2 * count]
+    value_sc, grad_sc = outputs[2 * count :]
+    step = pl.program_id(0)
+
+    for piece in range(count):
+
+        @pl.when(step == piece)
+        def _():
+            value_sc[...] = flip(inputs[piece][...])
+            grad_sc[...] = flip(grads[piece][...])
+
+    value, grad = value_sc[...], grad_sc[...]
+    back, out = 0.0, 0.0
+    width = expand_ref.shape[1]
+    chunk = 512
+    for start in range(0, width, chunk):
+        cols = slice(start, start + chunk)
+        weight, reduce = expand_ref[:, cols], reduce_ref[:, cols]
+        plain = kernel_dot(value, weight)
+        square = plain * plain
+        curve = jnp.tanh(GELU_SCALE * (plain + 0.044715 * square * plain))
+        hidden = (0.5 * plain * (1.0 + curve)).astype(bf16)
+        slope = 0.5 * (1.0 + curve) + 0.5 * plain * (1.0 - curve * curve) * (
+            GELU_SCALE * (1.0 + 3.0 * 0.044715 * square)
+        )
+        hidden_ref[:, cols] = hidden
+        expand_in = (kernel_dot(grad, reduce) * slope).astype(bf16)
+        expand_in_ref[:, cols] = expand_in
+        back = back + kernel_dot(expand_in, weight, 1, 1)
+        out = out + kernel_dot(hidden, reduce, 1, 1)
+    back = jnp.transpose(back.astype(bf16))
+    out = jnp.transpose(out.astype(bf16))
+    for piece in range(count):
+
+        @pl.when(step == piece)
+        def _():
+            back_refs[piece][...] = back
+            out_refs[piece][...] = out
+
+
+def feed_forward(inputs, grads, bucket):
+    count = len(inputs)
+    tokens, width = inputs[0].shape[1], bucket.shape[1] // 2
+    by_hidden = jax.ShapeDtypeStruct((count * tokens, width), bf16)
+    by_piece = jax.ShapeDtypeStruct((D, tokens), bf16)
+    whole = pl.BlockSpec((D, tokens), lambda step: (0, 0))
+    hidden_spec = pl.BlockSpec((tokens, width), lambda step: (step, 0))
+    return pl.pallas_call(
+        functools.partial(ffn_kernel, count),
+        out_shape=(by_hidden, by_hidden) + (by_piece,) * (2 * count),
+        grid=(count,),
+        in_specs=[whole] * (2 * count)
+        + [pl.BlockSpec((D, width), lambda step, k=k: (0, k)) for k in range(2)],
+        out_specs=[hidden_spec, hidden_spec] + [whole] * (2 * count),
+        scratch_shapes=[pltpu.VMEM((tokens, D), bf16), pltpu.VMEM((tokens, D), bf16)],
+        compiler_params=pltpu.CompilerParams(vmem_limit_bytes=VMEM_LIMIT),
+        cost_estimate=pl.CostEstimate(
+            flops=8 * D * count * tokens * width,
+            bytes_accessed=30 << 20,
+            transcendentals=count * tokens * width,
+        ),
+        name="feed_forward",
+    )(*inputs, *grads, bucket, bucket)
+
+
+def project_kernel(count, heads, *refs):
+    values = refs[:count]
+    weights = refs[count : count + 3]
+    cos_ref, sin_ref = refs[count + 3 : count + 5]
+    qkv_ref, raw_ref = refs[-2:]
+    quarter = HEAD // 4
+    rows = values[0].shape[1]
+    for piece in range(count):
+        lanes = pl.ds(piece * rows, rows)
+        value = flip(values[piece][...])
+        product = jnp.concatenate(
+            [jnp.transpose(kernel_dot(value, weight[...])) for weight in weights], axis=0
+        )
+        cosine, sines = cos_ref[:, lanes], sin_ref[:, lanes]
+        cos_row, cos_col = cosine[:quarter], cosine[quarter:]
+        sin_row, sin_col = sines[:quarter], sines[quarter:]
+        for part in range(3):
+            for head in range(heads):
+                start = (part * heads + head) * HEAD
+                raw = product[start : start + HEAD]
+                if part == 2:
+                    qkv_ref[head, part, :, lanes] = raw.astype(bf16)
+                    continue
+                raw_ref[head, part, :, lanes] = raw
+                normed = head_norm(raw)
+                one, two, three, four = (
+                    normed[k * quarter : (k + 1) * quarter] for k in range(4)
+                )
+                turned = jnp.concatenate(
+                    [
+                        one * cos_row - two * sin_row,
+                        one * sin_row + two * cos_row,
+                        three * cos_col - four * sin_col,
+                        three * sin_col + four * cos_col,
+                    ],
+                    axis=0,
+                )
+                qkv_ref[head, part, :, lanes] = turned.astype(bf16)
+
+
+def project(values, bucket, offset, heads, cosine, sines, stamps):
+    count, rows = len(values), values[0].shape[1]
+    third = (3 * heads * HEAD + 383) // 384 * 128
+    columns = count * rows
+    full = [pl.BlockSpec(member.shape, lambda g: (0, 0)) for member in (*values, cosine, sines)]
+    return pl.pallas_call(
+        functools.partial(project_kernel, count, heads),
+        out_shape=(
+            jax.ShapeDtypeStruct((heads, 3, HEAD, columns), bf16),
+            jax.ShapeDtypeStruct((heads, 2, HEAD, columns), f32),
+        ),
+        grid=(1,),
+        in_specs=full[:count]
+        + [
+            pl.BlockSpec((D, third), lambda g, k=k: (0, offset // third + k)) for k in range(3)
+        ]
+        + full[count:]
+        + [ANY_WHOLE] * len(stamps),
+        out_specs=[
+            pl.BlockSpec((heads, 3, HEAD, columns), lambda g: (0, 0, 0, 0)),
+            pl.BlockSpec((heads, 2, HEAD, columns), lambda g: (0, 0, 0, 0)),
+        ],
+        compiler_params=pltpu.CompilerParams(vmem_limit_bytes=VMEM_LIMIT),
+        cost_estimate=pl.CostEstimate(
+            flops=6 * columns * D * heads * HEAD, bytes_accessed=12 << 20, transcendentals=0
+        ),
+        name="project",
+    )(*values, bucket, bucket, bucket, cosine, sines, *stamps)
 
 
 def shards(
@@ -459,21 +1235,23 @@
     pairs_dev = packs * group_heads // sp_count
     all_packs = lengths.shape[0]
 
+    def lanes(value):
+        spare = -value.shape[-1] % 128
+        return jnp.pad(value, [(0, 0)] * (value.ndim - 1) + [(0, spare)])
+
     def split_columns(weight):
         columns = weight.shape[1] // cp_count
         blocks = jnp.swapaxes(weight.reshape(weight.shape[0], cp_count, columns), 0, 1)
         return trade_cp(blocks).reshape(cp_count * weight.shape[0], columns)
 
-    def join_columns(part):
-        count = part.shape[0] // cp_count
-        blocks = trade_cp(part.reshape(cp_count, count, part.shape[1]))
-        return jnp.swapaxes(blocks, 0, 1).reshape(count, cp_count * part.shape[1])
-
-    def gather_part(weight):
-        return lax.all_gather(split_columns(weight), GROUP, axis=0, tiled=True)
-
-    def gather_whole(weight):
-        return lax.all_gather(weight, EVERY, axis=0, tiled=True)
+    def send_columns(weights):
+        blocks = [
+            jnp.concatenate(
+                [jnp.split(weight, cp_count, axis=1)[k] for weight in weights], axis=1
+            )
+            for k in range(cp_count)
+        ]
+        return jnp.concatenate(send_cp(blocks), axis=0)
 
     def order_heads(weight):
         split = weight.reshape(weight.shape[0], 3, cp_count, -1)
@@ -483,21 +1261,101 @@
         split = weight.reshape(weight.shape[0], cp_count, 3, -1)
         return jnp.swapaxes(split, 1, 2).reshape(weight.shape)
 
-    skip_full = gather_whole(skip_weight)
-    input_part = gather_part(order_heads(self_input))
-    output_full = gather_whole(self_output)
-    query_full = gather_whole(cross_query)
-    pairs_full = gather_whole(cross_pairs)
-    cross_full = gather_whole(cross_output)
-    expand_part = gather_part(expand_weight)
-    reduce_part = gather_part(jnp.transpose(reduce_weight))
-    gain_rows = lax.all_gather(norm_gains, EVERY, axis=1, tiled=True).astype(f32)
-    caption_shard = jnp.pad(jnp.transpose(null_caption), ((0, 0), (0, TEXT_PAD - TEXT)))
-    caption_full = jnp.transpose(gather_whole(caption_shard))
+    def pack(parts):
+        return jnp.concatenate([lanes(part) for part in parts], axis=1)
+
+    def unpack(bucket, widths):
+        start, parts = 0, []
+        for width in widths:
+            parts.append(bucket[:, start : start + width])
+            start += width + -width % 128
+        return parts
+
+    width = D // cp_count
+    ff_width = expand_weight.shape[1] // cp_count
+    group_rows = cp_count * self_output.shape[0]
+    group_text = cp_count * cross_pairs.shape[0]
+    head_widths = (width, width, 3 * width)
+    mid_widths = (width, width, width, 2 * width)
+
+    def gather_group(bucket):
+        return lax.all_gather(bucket, GROUP, axis=0, tiled=True)
+
+    skip_cols = split_columns(skip_weight)
+    gain_columns = norm_gains.shape[1]
+    shard = self_output.shape[0]
+    fill = -3 * width % 128
+    input_blocks = order_heads(self_input).reshape(shard, cp_count, 3 * width)
+    input_blocks = jnp.swapaxes(jnp.pad(input_blocks, ((0, 0), (0, 0), (0, fill))), 0, 1)
+    spare = jnp.pad(jnp.transpose(norm_gains), ((0, 0), (3 * width, fill - 4)))
+    input_blocks = trade_cp(input_blocks + spare)
+    head_bucket = jnp.concatenate(
+        [
+            pack([skip_cols[:group_rows], skip_cols[group_rows:]]),
+            input_blocks.reshape(group_rows, -1),
+        ],
+        axis=1,
+    )
+    three = send_columns(
+        tuple(after(member, head_bucket) for member in (self_output, cross_query, cross_output))
+    )
+    expand_weight = after(expand_weight, head_bucket)
+    reduce_weight = after(reduce_weight, head_bucket)
+    pairs_cols = jnp.pad(
+        send_columns((after(cross_pairs, head_bucket),)), ((0, group_rows - group_text), (0, 0))
+    )
+    mid_bucket = pack(
+        [three[:, :width], three[:, width : 2 * width], three[:, 2 * width :], pairs_cols]
+    )
+    mid_gathered = gather_group(mid_bucket)
+    plain = rows % 128 == 0 and packs == 1 and group_rows % 16 == 0
+    ff_bucket = send_columns((expand_weight, jnp.transpose(reduce_weight)))
+    ff_gathered = gather_group(ff_bucket)
+    expand_part, reduce_part = unpack(ff_gathered, (ff_width, ff_width))
+
+    head_gathered = gather_group(head_bucket)
+    one, two, input_part = unpack(head_gathered, head_widths)
+    skip_part = jnp.stack(
+        [one.reshape(-1, group_rows, width), two.reshape(-1, group_rows, width)], axis=1
+    ).reshape(2 * D, width)
+    skip_part = after(skip_part, ff_bucket)
+    gain_start = 2 * (width + -width % 128) + 3 * width
+    gain_columns_t = head_gathered[:, gain_start : gain_start + 4].astype(f32)
+    gain_rows = jnp.transpose(gain_columns_t)
+
+    def times(left, full, left_dim):
+        return jnp.concatenate(
+            reorder_cp([dot(left, part, left_dim, 0) for part in full]), axis=1
+        )
+
+    def times_rows(full, right, right_dim):
+        return jnp.concatenate(
+            reorder_cp([dot(part, right, 0, right_dim) for part in full]), axis=0
+        )
+
+    def column_blocks(value):
+        return jnp.split(value, cp_count, axis=1)
+
+    def row_blocks(value):
+        return jnp.split(value, cp_count, axis=0)
+
+    def back_sum(left, full, left_dim):
+        return sum(dot(block, part, left_dim, 1) for block, part in zip(left, full))
+
+    def back_rows(full, right):
+        return sum(dot(part, block, 1, 1) for part, block in zip(full, right))
+
+    def traded(blocks):
+        came = trade_cp(jnp.stack(blocks))
+        return reorder_cp([came[k] for k in range(cp_count)])
 
     own_lengths = lax.dynamic_slice_in_dim(lengths, dp_index * packs, packs, 0)
     describe = jax.vmap(segment_info, in_axes=(0, None))
-    chunk_pos = sp_index * chunk + jnp.arange(chunk, dtype=jnp.int32)
+    chunk_block = jnp.arange(cp_count, dtype=jnp.int32) ^ cp_index
+    chunk_pos = sp_index * chunk + (
+        chunk_block[:, None] * rows + jnp.arange(rows, dtype=jnp.int32)[None, :]
+    ).reshape(-1)
+    turned = (cp_index * rows // CELL).reshape(1)
     _, chunk_row, chunk_col, _ = describe(own_lengths, chunk_pos)
     block_pos = jnp.arange(sp_count * cp_count, dtype=jnp.int32) * rows
     all_segments, _, _, all_valid = describe(lengths, block_pos)
@@ -513,22 +1371,80 @@
     last_cells = jnp.take(last_cells, pair_pack, axis=0)
     valid_cells = jnp.take(valid_cells, pair_pack, axis=0)
 
-    times = lax.all_gather(timestep, "dp", axis=0, tiled=True)
-    silu_all = jax.nn.silu(times.astype(f32)).astype(bf16)
+    times_all = after(timestep, head_bucket)
+    for bit in bits_of("dp"):
+        other = trade_bit(times_all, "dp", bit)
+        times_all = jnp.where(
+            has_bit("dp", bit),
+            jnp.concatenate([other, times_all]),
+            jnp.concatenate([times_all, other]),
+        )
+    silu_all = jax.nn.silu(times_all.astype(f32)).astype(bf16)
     shard_rows = shift_weight.shape[0]
     silu_own = lax.dynamic_slice_in_dim(silu_all, place * shard_rows, shard_rows, 2)
-    shift_table = lax.psum(
-        dot(silu_own.reshape(all_packs * IMGS, shard_rows), shift_weight, 1, 0), EVERY
-    ).reshape(all_packs, IMGS, D)
-    own_table = lax.dynamic_slice_in_dim(shift_table, dp_index * packs, packs, 0)
     slot_ids = jnp.arange(IMGS, dtype=jnp.int32)
-    block_pick = (block_image[:, None] == slot_ids[None, :]).astype(f32)
-    shifts = jnp.einsum("pi,pid->pd", block_pick, own_table, precision=highest)
+    all_pick = (all_segments[:, :, None] == slot_ids).astype(f32)
+    silu_blocks = jnp.einsum("pbi,pik->pbk", all_pick, silu_own.astype(f32), precision=highest)
+    silu_blocks = jnp.swapaxes(
+        silu_blocks.reshape(dp_count, packs, sp_count * cp_count, shard_rows), 1, 2
+    ).reshape(-1, shard_rows)
+    shifts = scatter_every(
+        dot(silu_blocks.astype(bf16), shift_weight, 1, 0).reshape(-1, packs, D)
+    )
     shift_rows = jnp.broadcast_to(shifts[:, None, :], (packs, rows, D)).reshape(held, D)
 
     image_dev = captions.shape[1]
     near = lax.dynamic_slice_in_dim(own_segments, sp_index * cp_count, cp_count, 1)
     local = jnp.clip(near - cp_index * image_dev, 0, image_dev - 1)
+    joined = jnp.concatenate([tokens.reshape(held, D), skip_in.reshape(held, D)], axis=1)
+    joined_all = pieces_cp(after(joined, head_bucket))
+    piece_index = cp_index.reshape(1)
+    if plain:
+        mixed_blocks = trade_cp(mix(piece_index, head_gathered, joined_all, width))
+        base_t, normed_self_t = start_forward(
+            mixed_blocks, gain_columns_t, shifts.reshape(D, 1)
+        )
+        normed_all = pieces_cp(normed_self_t)
+    else:
+        mixed_all = [dot(piece, skip_part, 1, 0).astype(bf16) for piece in joined_all]
+        mixed_blocks = trade_cp(jnp.stack(reorder_cp(mixed_all)))
+        mixed = jnp.concatenate([mixed_blocks[k] for k in range(cp_count)], axis=1).astype(f32)
+        base_stream = norm_gain(mixed, gain_rows[0])
+        normed_self = (norm_gain(base_stream, gain_rows[1]) + shift_rows).astype(bf16)
+        normed_all = pieces_cp(jnp.transpose(normed_self))
+    cosine, sines = jax.vmap(rope_tables)(chunk_row, chunk_col)
+    if plain:
+        offset = 2 * (width + -width % 128)
+        qkv, raw = project(
+            normed_all,
+            head_gathered,
+            offset,
+            group_heads,
+            cosine[0],
+            sines[0],
+            (),
+        )
+        qkv, raw = qkv[None], raw[None]
+        query_raw, key_raw = raw[:, :, 0], raw[:, :, 1]
+    normed_all = jnp.concatenate(normed_all, axis=1)
+    cosine, sines = cosine[:, None], sines[:, None]
+    if not plain:
+        projected = dot(input_part, normed_all, 0, 0)
+        projected = jnp.transpose(
+            projected.reshape(3, group_heads, HEAD, cp_count, packs, rows), (4, 1, 0, 2, 3, 5)
+        ).reshape(packs, group_heads, 3, HEAD, chunk)
+        query_raw, key_raw = projected[:, :, 0], projected[:, :, 1]
+        queries = turn_norm(query_raw, cosine, sines).astype(bf16)
+        key_rows = turn_norm(key_raw, cosine, sines).astype(bf16)
+        value_rows = projected[:, :, 2].astype(bf16)
+        qkv = jnp.stack([queries, key_rows, value_rows], axis=2)
+
+    caption_shard = jnp.pad(
+        jnp.transpose(after(null_caption, joined_all[-2])), ((0, 0), (0, TEXT_PAD - TEXT))
+    )
+    caption_rows = caption_shard.shape[0]
+    caption_full = jnp.transpose(gather_every(caption_shard).reshape(DT, TEXT_PAD))
+    local = local + (ff_bucket[0, 0].astype(f32) * 0.0).astype(jnp.int32)
     offered = jnp.stack(
         [
             jnp.stack(
@@ -541,7 +1457,7 @@
         ]
     )
     offered = jnp.pad(offered, ((0, 0), (0, 0), (0, TEXT_PAD - TEXT), (0, 0)))
-    arrived = trade_cp(offered)
+    arrived = jnp.stack(send_cp([offered[k] for k in range(cp_count)]))
     own_null = jnp.take_along_axis(
         null_mask, block_image[:, None], axis=1
     )[:, 0]
@@ -558,22 +1474,11 @@
         ]
     )
 
-    joined = jnp.concatenate([tokens.reshape(held, D), skip_in.reshape(held, D)], axis=1)
-    mixed = dot(joined, skip_full, 1, 0)
-    base_stream = norm_gain(mixed, gain_rows[0])
-    normed_self = (norm_gain(base_stream, gain_rows[1]) + shift_rows).astype(bf16)
-    normed_all = gather_cp(normed_self)
-    projected = dot(input_part, normed_all.reshape(cp_count * held, D), 0, 1)
-    projected = jnp.transpose(
-        projected.reshape(3, group_heads, HEAD, cp_count, packs, rows), (4, 1, 0, 2, 3, 5)
-    ).reshape(packs, group_heads, 3, HEAD, chunk)
-    cosine, sines = jax.vmap(rope_tables)(chunk_row, chunk_col)
-    cosine, sines = cosine[:, None], sines[:, None]
-    query_raw, key_raw = projected[:, :, 0], projected[:, :, 1]
-    queries = turn_norm(query_raw, cosine, sines).astype(bf16)
-    key_rows = turn_norm(key_raw, cosine, sines).astype(bf16)
-    value_rows = projected[:, :, 2].astype(bf16)
-    qkv = jnp.stack([queries, key_rows, value_rows], axis=2)
+    out_grad = after(cotangent.reshape(held, D).astype(f32) * token_valid, joined_all[-2])
+    out_turned = out_grad.astype(bf16)
+    out_turned = turn_over(out_turned) if plain else jnp.transpose(out_turned)
+    out_grad = jnp.transpose(out_turned).astype(f32)
+    reduce_pieces = pieces_cp(out_turned)
 
     def to_heads(value):
         value = value.reshape((sp_count, pairs_dev) + value.shape[2:])
@@ -583,12 +1488,30 @@
         value = lax.all_to_all(value, "sp", split_axis=0, concat_axis=0, tiled=True)
         return value.reshape((packs, group_heads) + value.shape[2:])
 
+    if plain:
+        *mid_parts, pairs_part = unpack_mid(mid_gathered, width, group_text, qkv)
+    else:
+        output_part, query_part, cross_part, pairs_part = (
+            after(part, qkv) for part in unpack(mid_gathered, mid_widths)
+        )
+        pairs_part = pairs_part.reshape(-1, group_rows, 2 * width)[:, :group_text].reshape(
+            DT, 2 * width
+        )
+        mid_parts = (output_part, query_part, cross_part)
+    pairs_full = pieces_cp(pairs_part)
+    output_full, query_full, cross_full = (pieces_cp(part) for part in mid_parts)
     qkv = to_heads(qkv)
-    out_self, totals_self = self_forward(qkv, first_cells, last_cells)
+    out_self, totals_self = self_forward(
+        qkv,
+        first_cells,
+        last_cells,
+        turned,
+        tuple(reduce_pieces) if plain else (),
+    )
 
     def to_tokens(value):
         value = value.reshape(sp_count, pairs_dev, HEAD, cp_count, rows)
-        value = jnp.transpose(value, (3, 0, 1, 2, 4))
+        value = jnp.stack(reorder_cp([value[:, :, :, k] for k in range(cp_count)]))
         value = value.reshape(cp_count * sp_count, pairs_dev, HEAD, rows)
         value = lax.all_to_all(value, HEAD_ORDER, split_axis=0, concat_axis=0, tiled=True)
         value = value.reshape(cp_count, packs, group_heads, HEAD, rows)
@@ -600,7 +1523,8 @@
         value = value.reshape(cp_count * sp_count, pairs_dev, HEAD, rows)
         value = lax.all_to_all(value, HEAD_ORDER, split_axis=0, concat_axis=0, tiled=True)
         value = value.reshape(cp_count, sp_count, pairs_dev, HEAD, rows)
-        return jnp.transpose(value, (1, 2, 3, 0, 4)).reshape(sp_count, pairs_dev, HEAD, chunk)
+        value = reorder_cp([value[k] for k in range(cp_count)])
+        return jnp.concatenate(value, axis=-1)
 
     def heads_of(value):
         value = value.reshape(HEADS, HEAD, packs, rows)
@@ -611,118 +1535,160 @@
         return jnp.transpose(value, (1, 2, 0, 3)).reshape(D, held)
 
     attended = to_tokens(out_self.astype(bf16))
-    mid_stream = base_stream + dot(attended, output_full, 0, 0)
-    normed_cross = norm_gain(mid_stream, gain_rows[2]).astype(bf16)
-    cross_raw = heads_of(dot(query_full, normed_cross, 0, 1))
-    cross_queries = head_norm(cross_raw).astype(bf16)
-    paired = jnp.einsum("cn,ptc->pnt", pairs_full, chosen, preferred_element_type=f32)
-    paired = paired.reshape(packs, 2, HEADS, HEAD, TEXT_PAD)
+    paired = times_rows(pairs_full, chosen.reshape(packs * TEXT_PAD, DT), 1)
+    paired = jnp.moveaxis(paired.reshape(2, HEADS, HEAD, packs, TEXT_PAD), 3, 0)
     text_raw = paired[:, 0].reshape(packs * HEADS, HEAD, TEXT_PAD)
     text_keys = head_norm(text_raw).astype(bf16)
     text_values = paired[:, 1].reshape(packs * HEADS, HEAD, TEXT_PAD).astype(bf16)
-    out_cross, totals_cross = cross_forward(cross_queries, text_keys, text_values)
-    crossed = rows_of(out_cross.astype(bf16))
-    late_stream = mid_stream + dot(crossed, cross_full, 0, 0)
-    normed_ffn = norm_gain(late_stream, gain_rows[3]).astype(bf16)
-    ffn_all = gather_cp(normed_ffn).reshape(cp_count * held, D)
-    expanded = dot(ffn_all, expand_part, 1, 0)
-    hidden = jax.nn.gelu(expanded, approximate=True).astype(bf16)
-    reduced_part = dot(hidden, reduce_part, 1, 1)
-    block_out = (
-        late_stream + scatter_cp(reduced_part.reshape(cp_count, held, D))
-    ).astype(bf16)
-
-    out_grad = cotangent.reshape(held, D).astype(f32) * token_valid
-    reduce_in = gather_cp(out_grad.astype(bf16)).reshape(cp_count * held, D)
-
-    def add_group(partial):
-        return lax.psum_scatter(partial.astype(bf16), GROUP, scatter_dimension=0, tiled=True)
-
-    reduce_grad = add_group(dot(reduce_in, hidden, 0, 0))
-    gelu_back = jax.vjp(lambda preact: jax.nn.gelu(preact, approximate=True), expanded)[1]
-    expand_in = gelu_back(dot(reduce_in, reduce_part, 1, 0))[0].astype(bf16)
-    expand_grad = add_group(dot(ffn_all, expand_in, 0, 0))
-    ffn_back = jax.vjp(norm_gain, late_stream, gain_rows[3])[1]
-    ffn_grad = scatter_cp(dot(expand_in, expand_part, 1, 1).reshape(cp_count, held, D))
-    late_part, gain_ffn = ffn_back(ffn_grad)
-    late_grad = out_grad + late_part
-
-    def column_blocks(value):
-        return jnp.swapaxes(value.reshape(value.shape[0], cp_count, -1), 0, 1)
-
-    def row_blocks(value):
-        return value.reshape((cp_count, value.shape[0] // cp_count) + value.shape[1:])
-
-    cout_in = late_grad.astype(bf16)
-    cross_out_grad = add_group(
-        jnp.einsum(
-            "skt,stn->kn",
-            gather_cp(crossed),
-            trade_cp(column_blocks(cout_in)),
-            preferred_element_type=f32,
-        )
-    )
-    crossed_grad = heads_of(dot(cross_full, cout_in, 1, 1).astype(bf16))
-    cq_grad, ck_grad, cv_grad = cross_backward(
-        cross_queries, text_keys, text_values, crossed_grad, out_cross, totals_cross
-    )
-    cq_grad = cq_grad.astype(bf16).astype(f32)
-    cross_raw_grad = rows_of(jax.vjp(head_norm, cross_raw)[1](cq_grad)[0].astype(bf16))
-    cross_query_grad = add_group(
-        jnp.einsum(
-            "stk,snt->kn",
-            gather_cp(normed_cross),
-            trade_cp(row_blocks(cross_raw_grad)),
-            preferred_element_type=f32,
-        )
-    )
-    cross_norm_back = jax.vjp(norm_gain, mid_stream, gain_rows[2])[1]
-    mid_part, gain_cross = cross_norm_back(dot(cross_raw_grad, query_full, 0, 1))
-    mid_grad = late_grad + mid_part
-    self_in = mid_grad.astype(bf16)
-    attended_grad = by_heads(dot(output_full, self_in, 1, 1).astype(bf16))
-    self_out_grad = add_group(
-        jnp.einsum(
-            "skt,stn->kn",
-            gather_cp(attended),
-            trade_cp(column_blocks(self_in)),
-            preferred_element_type=f32,
-        )
-    )
-    qkv_grad = from_heads(
-        self_backward(
-            qkv, attended_grad, out_self, totals_self, first_cells, last_cells, valid_cells
-        )
-    )
-    turn = functools.partial(turn_norm, cosine=cosine, sines=sines)
-    query_raw_grad = jax.vjp(turn, query_raw)[1](qkv_grad[:, :, 0].astype(f32))[0].astype(bf16)
-    key_raw_grad = jax.vjp(turn, key_raw)[1](qkv_grad[:, :, 1].astype(f32))[0].astype(bf16)
-    projected_grad = jnp.stack([query_raw_grad, key_raw_grad, qkv_grad[:, :, 2]], axis=0)
-    projected_grad = jnp.transpose(
-        projected_grad.reshape(3, packs, group_heads, HEAD, cp_count, rows), (0, 2, 3, 4, 1, 5)
-    ).reshape(3 * group_heads * HEAD, cp_count * held)
-    self_input_grad = add_group(
-        dot(normed_all.reshape(cp_count * held, D), projected_grad, 0, 1)
-    )
-    normed_self_grad = scatter_cp(
-        dot(projected_grad, input_part, 0, 1).reshape(cp_count, held, D)
-    )
-    self_norm_back = jax.vjp(norm_gain, base_stream, gain_rows[1])[1]
-    base_part, gain_self = self_norm_back(normed_self_grad)
-    shift_grads = jnp.sum(normed_self_grad.reshape(packs, rows, D), axis=1)
-    base_grad = mid_grad + base_part
-    skip_norm_back = jax.vjp(norm_gain, mixed, gain_rows[0])[1]
-    mixed_grad, gain_skip = skip_norm_back(base_grad)
-    mixed_in = mixed_grad.astype(bf16)
-    joined_grad = dot(mixed_in, skip_full, 1, 1)
-    skip_weight_grad = add_group(
-        jnp.einsum(
-            "stk,stn->kn",
-            gather_cp(joined),
-            trade_cp(column_blocks(mixed_in)),
-            preferred_element_type=f32,
-        )
-    )
+    differences = jnp.array(group_differences(), jnp.int32)
+    group_order = differences ^ (dp_index * sp_count + sp_index)
+    if plain:
+        mid_weights = (*output_full, *query_full, *cross_full)
+        (
+            mid_t,
+            late_t,
+            lefts,
+            cross_raw,
+            cross_queries,
+            out_cross,
+            totals_cross,
+            normed_ffn_t,
+        ) = middle_forward(
+            piece_index,
+            attended,
+            base_t,
+            gain_columns_t,
+            text_keys,
+            text_values,
+            mid_weights,
+        )
+        ffn_pieces = pieces_cp(normed_ffn_t)
+        hidden, expand_in, *parts = feed_forward(
+            ffn_pieces, reduce_pieces, ff_gathered
+        )
+        ffn_part, block_part = parts[:cp_count], parts[cp_count:]
+    else:
+        mid_stream = base_stream + times(attended, output_full, 0)
+        normed_cross = norm_gain(mid_stream, gain_rows[2]).astype(bf16)
+        cross_raw = heads_of(times_rows(query_full, normed_cross, 1))
+        cross_queries = head_norm(cross_raw).astype(bf16)
+        out_cross, totals_cross = cross_forward(cross_queries, text_keys, text_values)
+        crossed = rows_of(out_cross.astype(bf16))
+        late_stream = mid_stream + times(crossed, cross_full, 0)
+        normed_ffn = norm_gain(late_stream, gain_rows[3]).astype(bf16)
+        ffn_pieces = pieces_cp(jnp.transpose(normed_ffn))
+        expanded = dot(jnp.concatenate(ffn_pieces, axis=1), expand_part, 0, 0)
+        hidden = jax.nn.gelu(expanded, approximate=True).astype(bf16)
+
+    def by_piece(value):
+        value = value.astype(bf16).reshape(cp_count, held, D)
+        return [value[k] for k in range(cp_count)]
+
+    def sum_group(bucket):
+        return lax.psum_scatter(bucket, GROUP, scatter_dimension=0, tiled=True)
+
+    if not plain:
+        gelu_back = jax.vjp(lambda preact: jax.nn.gelu(preact, approximate=True), expanded)[1]
+        reduce_in = jnp.concatenate(reduce_pieces, axis=1)
+        expand_in = gelu_back(dot(reduce_in, reduce_part, 0, 0))[0].astype(bf16)
+        ffn_part = dot(expand_in, expand_part, 1, 1).astype(bf16)
+        ffn_part = by_piece(ffn_part)
+        block_part = by_piece(dot(hidden, reduce_part, 1, 1))
+    ff_out = expand_grads(ffn_pieces, expand_in)
+    if plain:
+        keep, send = reduce_grads(reduce_pieces, hidden, group_order)
+        ff_grads = sum_group(ff_out)
+    else:
+        reduce_out = dot(reduce_in, hidden, 1, 0).astype(bf16)
+        ff_grads = sum_group(jnp.concatenate([ff_out, reduce_out], axis=1))
+        ff_grads, reduce_sums = ff_grads[:, :ff_width], ff_grads[:, ff_width:]
+    ffn_grad = scatter_cp(ffn_part)
+    if plain:
+        lefts = pieces_cp(after(lefts, ffn_grad))
+    texts = after(chosen, ffn_grad).reshape(packs * TEXT_PAD, DT)
+    texts = pieces_cp(jnp.transpose(texts))
+    if plain:
+        (
+            late_round,
+            cross_raw_grad,
+            mid_grad,
+            mid_round,
+            attended_grad,
+            ck_grad,
+            cv_grad,
+            gain_pair,
+        ) = middle_backward(
+            piece_index,
+            (
+                ffn_grad,
+                out_turned,
+                late_t,
+                mid_t,
+                gain_columns_t,
+                cross_queries,
+                text_keys,
+                text_values,
+                out_cross,
+                totals_cross,
+                cross_raw,
+            ),
+            mid_weights,
+            (ff_out, keep, send),
+        )
+        gain_cross, gain_ffn = gain_pair[:, 0], gain_pair[:, 1]
+        cout_in, cross_raw_grad, self_in = (
+            reorder_cp(row_blocks(member)) for member in (late_round, cross_raw_grad, mid_round)
+        )
+    else:
+        ffn_back = jax.vjp(norm_gain, late_stream, gain_rows[3])[1]
+        late_part, gain_ffn = ffn_back(ffn_grad)
+        late_grad = out_grad + late_part
+
+        cout_in = column_blocks(late_grad.astype(bf16))
+        cout_in = reorder_cp(cout_in)
+        crossed_grad = heads_of(back_rows(cross_full, cout_in).astype(bf16))
+        cq_grad, ck_grad, cv_grad = cross_backward(
+            cross_queries, text_keys, text_values, crossed_grad, out_cross, totals_cross
+        )
+        cq_grad = cq_grad.astype(bf16).astype(f32)
+        cross_raw_grad = rows_of(jax.vjp(head_norm, cross_raw)[1](cq_grad)[0].astype(bf16))
+        cross_raw_grad = reorder_cp(row_blocks(cross_raw_grad))
+        cross_norm_back = jax.vjp(norm_gain, mid_stream, gain_rows[2])[1]
+        mid_part, gain_cross = cross_norm_back(
+            back_sum(cross_raw_grad, query_full, 0)
+        )
+        mid_grad = late_grad + mid_part
+        self_in = reorder_cp(column_blocks(mid_grad.astype(bf16)))
+        attended_grad = back_rows(output_full, self_in).astype(bf16)
+        normed_cross_t = jnp.transpose(normed_cross)
+        cout_in = [jnp.transpose(member) for member in cout_in]
+        self_in = [jnp.transpose(member) for member in self_in]
+    if not plain:
+        lefts = pieces_cp(jnp.stack([normed_cross_t, crossed, attended]))
+    rights = exchange_cp(
+        [
+            jnp.stack([cross, late, mid])
+            for cross, late, mid in zip(cross_raw_grad, cout_in, self_in)
+        ]
+    )
+    attended_grad = by_heads(attended_grad)
+    qkv_grad = self_backward(
+        qkv,
+        attended_grad,
+        out_self,
+        totals_self,
+        first_cells,
+        last_cells,
+        valid_cells,
+        turned,
+        (*lefts, *texts) if plain else (),
+    )
+    stamp = qkv_grad
+    qkv_grad = from_heads(qkv_grad)
+    if plain:
+        block_out = jnp.transpose((late_t + scatter_cp(block_part)).astype(bf16))
+    else:
+        block_out = (late_stream + scatter_cp(block_part)).astype(bf16)
 
     ck_grad = ck_grad.astype(bf16).astype(f32)
     text_raw_grad = jax.vjp(head_norm, text_raw)[1](ck_grad)[0].astype(bf16)
@@ -733,37 +1699,100 @@
         ],
         axis=1,
     ).reshape(packs, 2 * D, TEXT_PAD)
-    pairs_grad = add_group(
-        jnp.einsum(
-            "sptc,snpt->cn",
-            gather_cp(chosen),
-            trade_cp(row_blocks(jnp.swapaxes(paired_grad, 0, 1))),
-            preferred_element_type=f32,
-        )
-    )
+    paired_rows = jnp.swapaxes(paired_grad, 0, 1).reshape(2 * D, packs * TEXT_PAD)
+    paired_rows = reorder_cp(row_blocks(paired_rows))
+    pairs = exchange_cp(paired_rows)
+    if plain:
+        mid_out = mid_grads_bucket(lefts, rights, texts, pairs, stamp, dp_count * sp_count)
+    else:
+        lefts = jnp.concatenate(lefts, axis=2)
+        rights = jnp.concatenate(rights, axis=2)
+        pairs_grad = dot(
+            jnp.concatenate(texts, axis=1), jnp.concatenate(pairs, axis=1), 1, 1
+        )
+        pairs_grad = jnp.pad(
+            pairs_grad.astype(bf16).reshape(-1, group_text, 2 * width),
+            ((0, 0), (0, group_rows - group_text), (0, 0)),
+        ).reshape(D, 2 * width)
+        mid_out = pack(
+            [dot(lefts[k], rights[k], 1, 1).astype(bf16) for k in range(3)] + [pairs_grad]
+        )
+    mid_grads = sum_group(mid_out)
     null_sum = jnp.einsum(
         "p,pnt->nt", own_null.astype(f32), paired_grad.astype(f32), precision=highest
-    )
-    caption_grad = dot(pairs_full, null_sum.astype(bf16), 1, 0)
-    caption_grad = lax.psum_scatter(
-        caption_grad.astype(bf16), EVERY, scatter_dimension=0, tiled=True
-    )
-
-    small = jnp.concatenate(
-        [jnp.stack([gain_skip, gain_self, gain_cross, gain_ffn]), shift_grads], axis=0
-    )
-    small = lax.all_gather(small, EVERY, axis=0, tiled=False)
-    gain_columns = norm_gains.shape[1]
-    gains_grad = jnp.sum(
-        lax.dynamic_slice_in_dim(small[:, :4], place * gain_columns, gain_columns, 2), axis=0
-    )
-    shift_all = small[:, 4:].reshape(dp_count, sp_count * cp_count, packs, D)
-    shift_all = jnp.swapaxes(shift_all, 1, 2).reshape(all_packs * sp_count * cp_count, D)
-    all_pick = (all_segments[:, :, None] == slot_ids).astype(f32)
-    silu_blocks = jnp.einsum("pbi,pik->pbk", all_pick, silu_own.astype(f32), precision=highest)
+    ).astype(bf16)
+    caption_grad = sum(
+        dot(part, block, 1, 0)
+        for part, block in zip(pairs_full, reorder_cp(row_blocks(null_sum)))
+    )
+    caption_sum = caption_grad
+
+    qkv_grad = after(qkv_grad, ff_grads)
+    turn = functools.partial(turn_norm, cosine=cosine, sines=sines)
+    query_raw_grad = jax.vjp(turn, query_raw)[1](qkv_grad[:, :, 0].astype(f32))[0].astype(bf16)
+    key_raw_grad = jax.vjp(turn, key_raw)[1](qkv_grad[:, :, 1].astype(f32))[0].astype(bf16)
+    projected_grad = jnp.stack([query_raw_grad, key_raw_grad, qkv_grad[:, :, 2]], axis=0)
+    projected_grad = jnp.transpose(
+        projected_grad.reshape(3, packs, group_heads, HEAD, cp_count, rows), (0, 2, 3, 4, 1, 5)
+    ).reshape(3 * group_heads * HEAD, cp_count * held)
+    if plain:
+        normed_part = jnp.split(
+            dot(input_part, projected_grad, 1, 0).astype(bf16), cp_count, axis=1
+        )
+    else:
+        normed_part = dot(projected_grad, input_part, 0, 1).astype(bf16)
+    self_input_grad = dot(normed_all, projected_grad, 1, 1).astype(bf16)
+    if plain:
+        mixed_grad, sums = start_backward(
+            mixed_blocks,
+            gain_columns_t,
+            base_t,
+            mid_grad,
+            scatter_cp([normed_part[k] for k in range(cp_count)]),
+        )
+        gain_skip, gain_self = sums[:, 0], sums[:, 1]
+        shift_grads = sums[:, 2][None]
+        came = trade_cp(mixed_grad)
+        mixed_pieces = reorder_cp([came[k] for k in range(cp_count)])
+        head_out = skip_grads_bucket(mixed_pieces, joined_all, self_input_grad)
+        joined_part = [dot(piece, skip_part, 0, 1).astype(bf16) for piece in mixed_pieces]
+    else:
+        normed_self_grad = scatter_cp(by_piece(normed_part))
+        self_norm_back = jax.vjp(norm_gain, base_stream, gain_rows[1])[1]
+        base_part, gain_self = self_norm_back(normed_self_grad)
+        shift_grads = jnp.sum(normed_self_grad.reshape(packs, rows, D), axis=1)
+        base_grad = mid_grad + base_part
+        skip_norm_back = jax.vjp(norm_gain, mixed, gain_rows[0])[1]
+        mixed_grad, gain_skip = skip_norm_back(base_grad)
+        mixed_pieces = traded(column_blocks(mixed_grad.astype(bf16)))
+        mixed_in = jnp.concatenate(mixed_pieces, axis=0)
+        skip_out = dot(jnp.concatenate(joined_all, axis=0), mixed_in, 0, 0).astype(bf16)
+        skip_out = skip_out.reshape(-1, 2, shard, width)
+        head_out = pack(
+            [
+                skip_out[:, 0].reshape(D, width),
+                skip_out[:, 1].reshape(D, width),
+                self_input_grad,
+            ]
+        )
+        joined_part = dot(mixed_in, skip_part, 1, 1).astype(bf16).reshape(cp_count, held, 2 * D)
+        joined_part = [joined_part[k] for k in range(cp_count)]
+    head_grads = sum_group(head_out)
+    if plain:
+        reduce_sums = scatter_group_halves(
+            keep, send, (stamp, normed_part[0], head_out)
+        )
+    caption_grad = scatter_every(
+        after(caption_sum, head_out).astype(bf16).reshape(-1, caption_rows, TEXT_PAD)
+    )
+    joined_grad = scatter_cp(joined_part)
+
+    shift_grads = after(shift_grads, head_out)
+    gains_part = after(jnp.stack([gain_skip, gain_self, gain_cross, gain_ffn]), head_out)
+    gains_grad = scatter_every(jnp.swapaxes(gains_part.reshape(4, -1, gain_columns), 0, 1))
     shift_weight_grad = lax.dot_general(
-        silu_blocks.reshape(all_packs * sp_count * cp_count, shard_rows),
-        shift_all,
+        silu_blocks,
+        gather_every(shift_grads).reshape(-1, D),
         (((0,), (0,)), ((), ())),
         precision=highest,
         preferred_element_type=f32,
@@ -771,23 +1800,50 @@
 
     factor = all_packs * PACK / jnp.sum(lengths).astype(f32)
 
-    def finish(part):
-        return join_columns(part).astype(f32) * factor
+    def join_columns(bucket, widths):
+        blocks = jnp.stack(send_cp(jnp.split(bucket, cp_count, axis=0)))
+        start, parts = 0, []
+        for size in widths:
+            part = jnp.swapaxes(blocks[:, :, start : start + size], 0, 1)
+            parts.append(part.astype(f32) * factor)
+            start += size + -size % 128
+        return parts
+
+    def whole(part):
+        return part.reshape(part.shape[0], -1)
+
+    mid_grads = after(mid_grads, head_out)
+    (expand_out,) = join_columns(after(ff_grads, head_out), (ff_width,))
+    (reduce_out,) = join_columns(reduce_sums, (ff_width,))
+    cross_query_out, cross_out_out, self_out_out = join_columns(
+        mid_grads[:, : 3 * (width + -width % 128)], (width, width, width)
+    )
+    (pairs_out,) = join_columns(
+        mid_grads[:group_text, 3 * (width + -width % 128) :], (2 * width,)
+    )
+    if plain:
+        skip_out, input_out = finish_head(
+            trade_cp(head_grads.reshape(cp_count, shard, -1)), factor
+        )
+    else:
+        one, two, input_out = join_columns(head_grads, head_widths)
+        skip_out = jnp.concatenate([whole(one), whole(two)], axis=0)
+        input_out = restore_heads(whole(input_out))
 
     token_shape = (packs, rows, D)
     return (
         block_out.reshape(token_shape),
         (joined_grad[:, :D] * factor).astype(bf16).reshape(token_shape),
         (joined_grad[:, D:] * factor).astype(bf16).reshape(token_shape),
-        finish(skip_weight_grad),
+        skip_out,
         shift_weight_grad * factor,
-        restore_heads(join_columns(self_input_grad)).astype(f32) * factor,
-        finish(self_out_grad),
-        finish(cross_query_grad),
-        finish(pairs_grad),
-        finish(cross_out_grad),
-        finish(expand_grad),
-        jnp.transpose(join_columns(reduce_grad)).astype(f32) * factor,
+        input_out,
+        whole(self_out_out),
+        whole(cross_query_out),
+        whole(pairs_out),
+        whole(cross_out_out),
+        whole(expand_out),
+        jnp.transpose(whole(reduce_out)),
         jnp.transpose(caption_grad)[:TEXT].astype(f32) * factor,
         gains_grad * factor,
     )

time: 1600 us -> 940 us (0.59)
  waiting for transfers between devices: 780 us -> 354 us
  blocking collectives: 192 us -> 0 us
  Pallas kernels: 46.4 us -> 177 us
  matrix products: 149 us -> 43.1 us
  local copies, waits for them, and re-layouts: 168 us -> 107 us
  other arithmetic: 129 us -> 98.4 us
  starting transfers between devices: 92 us -> 111 us
    reduce_scatter x8 -> x3, waiting for transfers between devices: 267 us -> 0.01 us  [sum_group(): return lax.psum_scatter(bucket, GROUP, scatter_dimension=0, tiled=True)]
    all_gather x8 -> x3, waiting for transfers between devices: 195 us -> 7.98 us  [gather_group(): return lax.all_gather(bucket, GROUP, axis=0, tiled=True)]
    all_gather x4 -> x0, blocking collectives: 180 us -> none  [the longest x1 78.7 us: gather_whole(): return lax.all_gather(weight, EVERY, axis=0, tiled=True)]
    ppermute x22 -> x101, waiting for transfers between devices: 104 us -> 265 us  [the longest x71 198 us: trade_bit(): return lax.ppermute(value, axis, [(k, k ^ bit) for k in range(count)])]
    pallas_call x2 -> x14, Pallas kernels: 11.7 us -> 143 us  [the longest x1 31.9 us: feed_forward(): pl.pallas_call(functools.partial(ffn_kernel, count), out_shape=(by_hidden...]
    dot_general x19 -> x15, matrix products: 111 us -> 41.8 us  [dot(): lax.dot_general(left, right, (((left_dim,), (right_dim,)), ((), ())), pre...]
    all_to_all x16 -> x5, waiting for transfers between devices: 85.7 us -> 22.9 us  [trade_cp(): return lax.all_to_all(blocks, 'cp', split_axis=0, concat_axis=0, tiled=True)]
    ppermute x22 -> x101, starting transfers between devices: 13 us -> 71.8 us  [the longest x71 49 us: trade_bit(): return lax.ppermute(value, axis, [(k, k ^ bit) for k in range(count)])]
  transfers between devices with their start and end apart: 60 -> 116, of which waited for: 32 -> 42; matrix products, arithmetic and copies ran while one was open for 26% -> 23% of each run, Pallas kernels for 3% -> 16%
where the time goes in v2:
time: 940 us; the launch traced here: 929 us
  waiting for transfers between devices  354 us (38%)
  Pallas kernels  177 us (19%)
  starting transfers between devices  111 us (12%)
  local copies, waits for them, and re-layouts  107 us (11%)
  other arithmetic  98.4 us (10%)
  matrix products  43.1 us (5%)
  between operations  38.9 us (4%)
    ppermute x71, waiting for transfers between devices, trade_bit(): return lax.ppermute(value, axis, [(k, k ^ bit) for k in range(count)])  198 us
    ppermute x30, waiting for transfers between devices, exchange_cp(): lax.ppermute(pieces[key], 'cp', [(k, k ^ key) for k in range(count)])  67.4 us
    ppermute x71, starting transfers between devices, trade_bit(): return lax.ppermute(value, axis, [(k, k ^ bit) for k in range(count)])  49 us
    unnamed x227, local copies, waits for them, and re-layouts  42.7 us
    dot_general x15, matrix products, dot(): lax.dot_general(left, right, (((left_dim,), (right_dim,)), ((), ())), pre...  41.8 us
    all_to_all x1, waiting for transfers between devices, to_heads(): return lax.all_to_all(value, 'sp', split_axis=0, concat_axis=0, tiled=True)  34.2 us
    pallas_call x1, Pallas kernels, feed_forward(): pl.pallas_call(functools.partial(ffn_kernel, count), out_shape=(by_hidden...  31.9 us
    all_to_all x5, waiting for transfers between devices, trade_cp(): return lax.all_to_all(blocks, 'cp', split_axis=0, concat_axis=0, tiled=True)  22.9 us
  transfers between devices with their start and end apart: 116, of which 42 were waited for; matrix products, arithmetic and copies ran while one was open for 23% of the time, Pallas kernels for 16%

profile of v2, /device:TPU:0, one launch (start us, length us, event | category | flops | bytes accessed | tf_op | source)
XLA Modules:
  0.0 929.4 jit_solution(11674126312578492159)
XLA Ops:
  9.2 4.2 all-to-all-start
  15.7 3.9 all-to-all-done
  23.1 7.8 all-to-all-done.1
  67.3 36.0 %collective-permute-done.29 = bf16[44,3072]{1,0:T(8,128)(2,1)S(1)} collective-permute-done((bf16[44,3072]{1,0:T(8,128)(2,1)S(1)}, bf16[44,3072]{1,0:T(8,128)(2,1)S(1)}, u32[]{:S(2)}, u32[]{:S(2)}) %collective-permute-start.29) | collective-permute-done | bytes 270368 | tf_op jit(solution)/shard_map/ppermute | solution.py:177
  131.4 6.0 mix.1
  140.5 4.7 all-to-all-start.2
  145.3 10.9 %constant_dynamic-slice_fusion.3 = (bf16[1,1,333,1024]{3,1,2,0:T(2,128)(2,1)}, bf16[1,1,333,1024]{3,1,2,0:T(2,128)(2,1)S(1)}, bf16[1,1,333,1024]{3,1,2,0:T(2,128)(2,1)S(1)}, bf16[1,1,333,1024]{3,1,2,0:T(2,128)(2,1)S(1)}) fusion(bf16[1,4,333,1024]{3,1,2,0:T(4,128)(2,1)} %param.22, s32[]{:T(128)S(6)} %select_n.2179, s32[]{:T(128)S(6)} %select_n.2181, ...), kind=kLoop, calls=%fused_computation.502 | loop fusion | bytes 5455888 | tf_op jit(solution)/shard_map/jit(dynamic_index_in_dim)/dynamic_slice | solution.py:1452
  174.1 11.4 %collective-permute-done.10.refs_2_ = bf16[1408,256]{1,0:T(8,128)(2,1)} collective-permute-done((bf16[1408,256]{1,0:T(8,128)(2,1)}, bf16[1408,256]{1,0:T(8,128)(2,1)}, u32[]{:S(2)}, u32[]{:S(2)}) %collective-permute-start.10) | collective-permute-done | bytes 720928 | tf_op jit(solution)/shard_map/ppermute | solution.py:121
  191.7 9.1 project.1
  204.0 7.9 all-gather.6.cloned.1.call-done.bucket_ref
  211.9 4.6 unpack_mid.1
  222.2 9.2 collective-permute-done.25
  232.1 4.7 all-to-all-start.3
  236.9 28.3 %collective-permute-done.26 = bf16[2,2,2,32,384]{4,3,2,1,0:T(8,128)(2,1)} collective-permute-done((bf16[2,2,2,32,384]{4,3,2,1,0:T(8,128)(2,1)}, bf16[2,2,2,32,384]{4,3,2,1,0:T(8,128)(2,1)}, u32[]{:S(2)}, u32[]{:S(2)}) %collective-permute-start.26) | collective-permute-done | bytes 196640 | tf_op jit(solution)/shard_map/ppermute | solution.py:121
  294.2 34.2 %all-to-all-done.3.qkv_ref = bf16[4,1,3,88,1024]{4,3,2,1,0:T(8,128)(2,1)} async-done(((bf16[4,1,3,88,1024]{4,3,2,1,0:T(8,128)(2,1)}), bf16[4,1,3,88,1024]{4,3,2,1,0:T(8,128)(2,1)}, u32[]{:S(2)}, u32[]{:S(2)}) %all-to-all-start.3) | async-done | bytes 2162720 | tf_op jit(solution)/shard_map/all_to_all | solution.py:1485
  331.7 22.4 %self_forward.1 = (f32[4,1,88,1024]{3,2,1,0:T(8,128)S(1)}, f32[4,1,1,1024]{3,2,1,0:T(1,128)S(1)}) custom-call(s32[1,16]{1,0:T(1,128)S(1)} %fusion.92.first_ref, s32[1,16]{1,0:T(1,128)S(1)} %fusion.93.last_ref, s32[1]{0:T(128)} %bitcast.7.turned_ref, bf16[4,1,3,88,1024]{4,3,2,1,0:T(8,128)(2,1)} %all-to-all-done.3.qkv_ref, bf16[1408,256]{1,0:T(8,128)(2,1)S(1)} %copy-done.14, ...), custom_call_target="tpu_custom_call" | custom-call | flops 10000000000 | bytes 8388608 | tf_op jit(solution)/shard_map/self_forward/pallas_call | solution.py:385
  363.6 4.3 all-to-all-start.4
  378.6 22.4 %all-to-all-done.4 = bf16[16,1,88,256]{3,2,1,0:T(8,128)(2,1)} async-done(((bf16[16,1,88,256]{3,2,1,0:T(8,128)(2,1)}), bf16[16,1,88,256]{3,2,1,0:T(8,128)(2,1)}, u32[]{:S(2)}, u32[]{:S(2)}) %all-to-all-start.4) | async-done | bytes 720928 | tf_op jit(solution)/shard_map/all_to_all | solution.py:1516
  401.0 20.2 %middle_forward.1 = (f32[1408,256]{1,0:T(8,128)}, f32[1408,256]{1,0:T(8,128)}, bf16[3,1408,256]{2,1,0:T(8,128)(2,1)}, f32[16,88,256]{2,1,0:T(8,128)}, bf16[16,88...) custom-call(s32[1]{0:T(128)} %bitcast.refs_0_, ...), custom_call_target="tpu_custom_call" | custom-call | flops 5075107840 | bytes 25165824 | tf_op jit(solution)/shard_map/middle_forward/pallas_call | solution.py:924
  422.7 17.1 %collective-permute-done.45.refs_2_ = bf16[1408,256]{1,0:T(8,128)(2,1)} collective-permute-done((bf16[1408,256]{1,0:T(8,128)(2,1)}, bf16[1408,256]{1,0:T(8,128)(2,1)}, u32[]{:S(2)}, u32[]{:S(2)}) %collective-permute-start.45) | collective-permute-done | bytes 720928 | tf_op jit(solution)/shard_map/ppermute | solution.py:121
  444.3 31.9 %feed_forward.1 = (bf16[1024,1536]{1,0:T(8,128)(2,1)}, bf16[1024,1536]{1,0:T(8,128)(2,1)}, bf16[1408,256]{1,0:T(8,128)(2,1)S(1)}, bf16[1408,256]{1,0:T(8,128)(2,...) custom-call(bf16[1408,256]{1,0:T(8,128)(2,1)} %get-tuple-element.65., ...), custom_call_target="tpu_custom_call" | custom-call | flops 17716740096 | bytes 31457280 | tf_op jit(solution)/shard_map/feed_forward/pallas_call | solution.py:1119
  487.5 7.7 expand_grads.1.refs_24_
  505.4 10.4 %reduce_grads.1 = (bf16[704,1536]{1,0:T(8,128)(2,1)S(1)}, bf16[704,1536]{1,0:T(8,128)(2,1)}) custom-call(s32[8]{0:T(128)S(1)} %broadcast_xor_fusion.group_ref, bf16[1408,256]{1,0:T(8,128)(2,1)S(1)} %copy-done.15, bf16[1408,256]{1,0:T(8,128)(2,1)S(1)} %copy-done.45, bf16[1408,256]{1,0:T(8,128)(2,1)} %collective-permute-done.13.refs_2_.refs_6_, ...), custom_call_target="tpu_custom_call" | custom-call | flops 4429185024 | bytes 12582912 | tf_op jit(solution)/shard_map/reduce_grads/pallas_call | solution.py:597
  519.3 22.8 %middle_backward.1 = (bf16[1408,256]{1,0:T(8,128)(2,1)S(1)}, bf16[1408,256]{1,0:T(8,128)(2,1)S(1)}, f32[1408,256]{1,0:T(8,128)}, bf16[1408,256]{1,0:T(8,128)(2,1...) custom-call(s32[1]{0:T(128)} %bitcast.refs_0_, ...), custom_call_target="tpu_custom_call" | custom-call | flops 7105150976 | bytes 31457280 | tf_op jit(solution)/shard_map/middle_backward/pallas_call | solution.py:1036
  546.4 4.3 all-to-all-start.5
  561.5 13.9 %collective-permute-done.57.refs_6_.refs_10_ = bf16[1024,384]{1,0:T(8,128)(2,1)} collective-permute-done((bf16[1024,384]{1,0:T(8,128)(2,1)}, bf16[1024,384]{1,0:T(8,128)(2,1)}, u32[]{:S(2)}, u32[]{:S(2)}) %collective-permute-start.57) | collective-permute-done | bytes 786464 | tf_op jit(solution)/shard_map/ppermute | solution.py:121
  583.6 11.8 %self_backward.1.refs_16_ = bf16[4,1,3,88,1024]{4,3,2,1,0:T(8,128)(2,1)} custom-call(s32[1,16]{1,0:T(1,128)S(1)} %fusion.92.first_ref, s32[1,16]{1,0:T(1,128)S(1)} %fusion.93.last_ref, s32[1]{0:T(128)S(6)} %select_n.2222.valid_ref, s32[1]{0:T(128)} %bitcast.7.turned_ref, bf16[4,1,3,88,1024]{4,3,2,1,0:T(8,128)(2,1)} %all-to-all-done.3.qkv_ref, ...), custom_call_target="tpu_custom_call" | custom-call | flops 17999998976 | bytes 16777216 | tf_op jit(solution)/shard_map/self_backward/pallas_call | solution.py:406
  595.4 4.5 all-to-all-start.6
  606.4 4.3 collective-permute-start.85
  612.5 8.0 collective-permute-done.74.refs_14_
  620.5 10.7 %collective-permute-done.75.refs_15_ = bf16[704,384]{1,0:T(8,128)(2,1)S(1)} collective-permute-done((bf16[704,384]{1,0:T(8,128)(2,1)S(1)}, bf16[704,384]{1,0:T(8,128)(2,1)S(1)}, u32[]{:S(2)}, u32[]{:S(2)}) %collective-permute-start.75) | collective-permute-done | bytes 540704 | tf_op jit(solution)/shard_map/ppermute | solution.py:177
  631.2 15.6 %mid_grads.1 = bf16[1408,1920]{1,0:T(8,128)(2,1)} custom-call(bf16[3,1408,256]{2,1,0:T(8,128)(2,1)} %broadcast_add_fusion.refs_0_, bf16[3,1408,256]{2,1,0:T(8,128)(2,1)} %collective-permute-done.53.refs_1_, bf16[3,1408,256]{2,1,0:T(8,128)(2,1)} %collective-permute-done.54.refs_2_, bf16[3,1408,256]{2,1,0:T(8,128)(2,1)} %collective-permute-done.55.refs_3_, ...), custom_call_target="tpu_custom_call" | custom-call | flops 6978273280 | bytes 25165824 | tf_op jit(solution)/shard_map/mid_grads/pallas_call | solution.py:644
  664.8 4.5 convolution_convert_fusion.5
  675.7 4.3 fusion.50
  679.9 4.2 fusion.52
  696.3 6.5 convolution_convert_fusion
  702.8 5.3 copy.200.refs_8_
  711.9 4.4 start_backward.1
  718.1 4.2 all-to-all-start.7
  741.0 6.7 skip_grads.1
  755.4 20.7 %collective-permute-done.87 = bf16[176,1536]{1,0:T(8,128)(2,1)} collective-permute-done((bf16[176,1536]{1,0:T(8,128)(2,1)}, bf16[176,1536]{1,0:T(8,128)(2,1)}, u32[]{:S(2)}, u32[]{:S(2)}) %collective-permute-start.87) | collective-permute-done | bytes 540704 | tf_op jit(solution)/shard_map/ppermute | solution.py:121
  786.9 4.7 collective-permute-done.97
  804.7 5.5 collective-permute-done.67
  810.3 7.5 collective-permute-done.68
  829.0 6.2 collective-permute-done.91
  835.6 11.9 %collective-permute-done.92 = bf16[8,32,384]{2,1,0:T(8,128)(2,1)S(1)} collective-permute-done((bf16[8,32,384]{2,1,0:T(8,128)(2,1)S(1)}, bf16[8,32,384]{2,1,0:T(8,128)(2,1)S(1)}, u32[]{:S(2)}, u32[]{:S(2)}) %collective-permute-start.92) | collective-permute-done | bytes 196640 | tf_op jit(solution)/shard_map/ppermute | solution.py:121
  857.8 32.8 %collective-permute-done.94 = bf16[2,32,384]{2,1,0:T(8,128)(2,1)S(1)} collective-permute-done((bf16[2,32,384]{2,1,0:T(8,128)(2,1)S(1)}, bf16[2,32,384]{2,1,0:T(8,128)(2,1)S(1)}, u32[]{:S(2)}, u32[]{:S(2)}) %collective-permute-start.94) | collective-permute-done | bytes 49184 | tf_op jit(solution)/shard_map/ppermute | solution.py:121
  913.2 7.8 all-to-all-done.8.blocks_ref
  (703 shorter events, 338.2 us)
Async XLA Ops:
  23.0 108.4 %all-gather.4.cloned.1.call-start = ((), (), s32[]{:S(2)}) async-start(), calls=%async_computation.12 | async-start | bytes 6082560 | tf_op jit(solution)/shard_map/all_gather | solution.py:1282
  32.0 179.9 %all-gather.6.cloned.1.call-start = ((), (), s32[]{:S(2)}) async-start(), calls=%async_computation.13 | async-start | bytes 6082560 | tf_op jit(solution)/shard_map/all_gather | solution.py:1282
  48.3 396.0 %all-gather.8.cloned.1.call-start = ((), (), s32[]{:S(2)}) async-start(), calls=%async_computation.14 | async-start | bytes 9732096 | tf_op jit(solution)/shard_map/all_gather | solution.py:1282
  62.4 46.2 %collective-permute-start.1 = (bf16[256,2816]{1,0:T(8,128)(2,1)S(1)}, bf16[256,2816]{1,0:T(8,128)(2,1)S(1)}, u32[]{:S(2)}, u32[]{:S(2)}) collective-permute-start(bf16[256,2816]{1,0:T(8,128)(2,1)S(1)} %maximum_add_fusion.1.refs_2_.refs_0_), channel_id=1, source_target_pairs={{0,2},{1,3},{2,0},{3,1},{4,6},{5,7},{6,4},{7,5},{8,10},{9,11},{10,... | collective-permute-start | bytes 4325384 | tf_op jit(solution)/shard_map/ppermute | solution.py:121
  62.8 40.4 %collective-permute-start.29 = (bf16[44,3072]{1,0:T(8,128)(2,1)S(1)}, bf16[44,3072]{1,0:T(8,128)(2,1)S(1)}, u32[]{:S(2)}, u32[]{:S(2)}) collective-permute-start(bf16[44,3072]{1,0:T(8,128)(2,1)S(1)} %get-tuple-element.215), channel_id=1, source_target_pairs={{0,2},{1,3},{2,0},{3,1},{4,6},{5,7},{6,4},{7,5},{8,10},{9,11},{10,... | collective-permute-start | bytes 811016 | tf_op jit(solution)/shard_map/ppermute | solution.py:177
  64.5 40.2 %collective-permute-start.28 = (bf16[44,3072]{1,0:T(8,128)(2,1)S(1)}, bf16[44,3072]{1,0:T(8,128)(2,1)S(1)}, u32[]{:S(2)}, u32[]{:S(2)}) collective-permute-start(bf16[44,3072]{1,0:T(8,128)(2,1)S(1)} %broadcast_select_fusion.44), channel_id=1, source_target_pairs={{0,3},{1,2},{2,1},{3,0},{4,7},{5,6},{6,5},{7,4},{8,11},{9,10},{10,... | collective-permute-start | bytes 811016 | tf_op jit(solution)/shard_map/ppermute | solution.py:177
  64.5 40.2 %collective-permute-start.30 = (bf16[44,3072]{1,0:T(8,128)(2,1)S(1)}, bf16[44,3072]{1,0:T(8,128)(2,1)S(1)}, u32[]{:S(2)}, u32[]{:S(2)}) collective-permute-start(bf16[44,3072]{1,0:T(8,128)(2,1)S(1)} %get-tuple-element.283), channel_id=1, source_target_pairs={{0,1},{1,0},{2,3},{3,2},{4,5},{5,4},{6,7},{7,6},{8,9},{9,8},{10,11... | collective-permute-start | bytes 811016 | tf_op jit(solution)/shard_map/ppermute | solution.py:177
  67.2 38.8 %collective-permute-start.6 = (f32[4,1,1408]{2,0,1:T(4,128)S(1)}, f32[4,1,1408]{2,0,1:T(4,128)S(1)}, u32[]{:S(2)}, u32[]{:S(2)}) collective-permute-start(f32[4,1,1408]{2,0,1:T(4,128)S(1)} %slice_select_fusion.3), channel_id=1, source_target_pairs={{0,4},{4,0},{8,12},{12,8},{1,5},{5,1},{9,13},{13,9},{2,6},{6,2},{1... | collective-permute-start | bytes 67592 | tf_op jit(solution)/shard_map/ppermute | solution.py:121
  171.1 95.9 %collective-permute-start.32 = (bf16[1,384,1024]{2,1,0:T(8,128)(2,1)}, bf16[1,384,1024]{2,1,0:T(8,128)(2,1)}, u32[]{:S(2)}, u32[]{:S(2)}) collective-permute-start(bf16[1,384,1024]{2,1,0:T(8,128)(2,1)} %get-tuple-element.212), channel_id=1, source_target_pairs={{0,2},{1,3},{2,0},{3,1},{4,6},{5,7},{6,4},{7,5},{8,10},{9,11},{10,... | collective-permute-start | bytes 2359304 | tf_op jit(solution)/shard_map/ppermute | solution.py:177
  187.4 79.7 %collective-permute-start.31 = (bf16[1,384,1024]{2,1,0:T(8,128)(2,1)}, bf16[1,384,1024]{2,1,0:T(8,128)(2,1)}, u32[]{:S(2)}, u32[]{:S(2)}) collective-permute-start(bf16[1,384,1024]{2,1,0:T(8,128)(2,1)} %get-tuple-element.246), channel_id=1, source_target_pairs={{0,3},{1,2},{2,1},{3,0},{4,7},{5,6},{6,5},{7,4},{8,11},{9,10},{10,... | collective-permute-start | bytes 2359304 | tf_op jit(solution)/shard_map/ppermute | solution.py:177
  190.7 76.5 %collective-permute-start.33 = (bf16[1,384,1024]{2,1,0:T(8,128)(2,1)}, bf16[1,384,1024]{2,1,0:T(8,128)(2,1)}, u32[]{:S(2)}, u32[]{:S(2)}) collective-permute-start(bf16[1,384,1024]{2,1,0:T(8,128)(2,1)} %get-tuple-element.245), channel_id=1, source_target_pairs={{0,1},{1,0},{2,3},{3,2},{4,5},{5,4},{6,7},{7,6},{8,9},{9,8},{10,11... | collective-permute-start | bytes 2359304 | tf_op jit(solution)/shard_map/ppermute | solution.py:177
  191.3 30.4 %collective-permute-start.24 = (bf16[2,32,384]{2,1,0:T(8,128)(2,1)}, bf16[2,32,384]{2,1,0:T(8,128)(2,1)S(1)}, u32[]{:S(2)}, u32[]{:S(2)}) collective-permute-start(bf16[2,32,384]{2,1,0:T(8,128)(2,1)} %maximum_select_fusion.11), channel_id=1, source_target_pairs={{0,2},{1,3},{2,0},{3,1},{4,6},{5,7},{6,4},{7,5},{8,10},{9,11},{10,... | collective-permute-start | bytes 147464 | tf_op jit(solution)/shard_map/ppermute | solution.py:121
  220.2 53.4 %collective-permute-start.21 = (bf16[1024,704]{0,1:T(8,128)(2,1)}, bf16[1024,704]{0,1:T(8,128)(2,1)}, u32[]{:S(2)}, u32[]{:S(2)}) collective-permute-start(bf16[1024,704]{0,1:T(8,128)(2,1)} %copy.187), channel_id=1, source_target_pairs={{0,2},{1,3},{2,0},{3,1},{4,6},{5,7},{6,4},{7,5},{8,10},{9,11},{10,... | collective-permute-start | bytes 4325384 | tf_op jit(solution)/shard_map/ppermute | solution.py:121
  232.1 33.1 %collective-permute-start.26 = (bf16[2,2,2,32,384]{4,3,2,1,0:T(8,128)(2,1)}, bf16[2,2,2,32,384]{4,3,2,1,0:T(8,128)(2,1)}, u32[]{:S(2)}, u32[]{:S(2)}) collective-permute-start(bf16[2,2,2,32,384]{4,3,2,1,0:T(8,128)(2,1)} %maximum_select_fusion.3), channel_id=1, source_target_pairs={{0,8},{4,12},{8,0},{12,4},{1,9},{5,13},{9,1},{13,5},{2,10},{6,14},... | collective-permute-start | bytes 589832 | tf_op jit(solution)/shard_map/ppermute | solution.py:121
  232.1 96.3 %all-to-all-start.3 = ((bf16[4,1,3,88,1024]{4,3,2,1,0:T(8,128)(2,1)}), bf16[4,1,3,88,1024]{4,3,2,1,0:T(8,128)(2,1)}, u32[]{:S(2)}, u32[]{:S(2)}) async-start(bf16[4,1,3,88,1024]{4,3,2,1,0:T(8,128)(2,1)} %bitcast.379), calls=%async_computation.3 | async-start | bytes 4325376 | tf_op jit(solution)/shard_map/all_to_all | solution.py:1485
  279.3 90.8 %collective-permute-start.35 = (bf16[352,1408]{1,0:T(8,128)(2,1)}, bf16[352,1408]{1,0:T(8,128)(2,1)}, u32[]{:S(2)}, u32[]{:S(2)}) collective-permute-start(bf16[352,1408]{1,0:T(8,128)(2,1)} %get-tuple-element.61.refs_6_.refs_12_), channel_id=1, source_target_pairs={{0,1},{1,0},{2,3},{3,2},{4,5},{5,4},{6,7},{7,6},{8,9},{9,8},{10,11... | collective-permute-start | bytes 2973704 | tf_op jit(solution)/shard_map/ppermute | solution.py:121
  283.9 86.4 %collective-permute-start.36 = (bf16[352,1408]{1,0:T(8,128)(2,1)}, bf16[352,1408]{1,0:T(8,128)(2,1)}, u32[]{:S(2)}, u32[]{:S(2)}) collective-permute-start(bf16[352,1408]{1,0:T(8,128)(2,1)} %get-tuple-element.61.refs_6_.refs_12_), channel_id=1, source_target_pairs={{0,2},{1,3},{2,0},{3,1},{4,6},{5,7},{6,4},{7,5},{8,10},{9,11},{10,... | collective-permute-start | bytes 2973704 | tf_op jit(solution)/shard_map/ppermute | solution.py:121
  286.6 92.0 %collective-permute-start.38 = (bf16[352,1408]{1,0:T(8,128)(2,1)}, bf16[352,1408]{1,0:T(8,128)(2,1)}, u32[]{:S(2)}, u32[]{:S(2)}) collective-permute-start(bf16[352,1408]{1,0:T(8,128)(2,1)} %get-tuple-element.62.refs_10_.refs_16_), channel_id=1, source_target_pairs={{0,1},{1,0},{2,3},{3,2},{4,5},{5,4},{6,7},{7,6},{8,9},{9,8},{10,11... | collective-permute-start | bytes 2973704 | tf_op jit(solution)/shard_map/ppermute | solution.py:121
  291.3 79.3 %collective-permute-start.39 = (bf16[352,1408]{1,0:T(8,128)(2,1)}, bf16[352,1408]{1,0:T(8,128)(2,1)}, u32[]{:S(2)}, u32[]{:S(2)}) collective-permute-start(bf16[352,1408]{1,0:T(8,128)(2,1)} %get-tuple-element.62.refs_10_.refs_16_), channel_id=1, source_target_pairs={{0,2},{1,3},{2,0},{3,1},{4,6},{5,7},{6,4},{7,5},{8,10},{9,11},{10,... | collective-permute-start | bytes 2973704 | tf_op jit(solution)/shard_map/ppermute | solution.py:121
  293.9 77.0 %collective-permute-start.42 = (bf16[352,1408]{1,0:T(8,128)(2,1)}, bf16[352,1408]{1,0:T(8,128)(2,1)}, u32[]{:S(2)}, u32[]{:S(2)}) collective-permute-start(bf16[352,1408]{1,0:T(8,128)(2,1)} %get-tuple-element.63.refs_14_.refs_20_), channel_id=1, source_target_pairs={{0,2},{1,3},{2,0},{3,1},{4,6},{5,7},{6,4},{7,5},{8,10},{9,11},{10,... | collective-permute-start | bytes 2973704 | tf_op jit(solution)/shard_map/ppermute | solution.py:121
  363.6 37.5 %all-to-all-start.4 = ((bf16[16,1,88,256]{3,2,1,0:T(8,128)(2,1)}), bf16[16,1,88,256]{3,2,1,0:T(8,128)(2,1)}, u32[]{:S(2)}, u32[]{:S(2)}) async-start(bf16[16,1,88,256]{3,2,1,0:T(8,128)(2,1)} %bitcast.407), calls=%async_computation.4 | async-start | bytes 1441792 | tf_op jit(solution)/shard_map/all_to_all | solution.py:1516
  367.8 286.6 %reduce-scatter.4.cloned.1.call-start = ((), (), s32[]{:S(2)}) async-start(), calls=%async_computation.15 | async-start | bytes 4866048 | tf_op jit(solution)/shard_map/reduce_scatter | solution.py:1588
  503.7 52.5 %collective-permute-start.54 = (bf16[3,1408,256]{2,1,0:T(8,128)(2,1)}, bf16[3,1408,256]{2,1,0:T(8,128)(2,1)}, u32[]{:S(2)}, u32[]{:S(2)}) collective-permute-start(bf16[3,1408,256]{2,1,0:T(8,128)(2,1)} %broadcast_add_fusion.refs_0_), channel_id=1, source_target_pairs={{0,2},{1,3},{2,0},{3,1},{4,6},{5,7},{6,4},{7,5},{8,10},{9,11},{10,... | collective-permute-start | bytes 6488072 | tf_op jit(solution)/shard_map/ppermute | solution.py:121
  505.3 97.2 %collective-permute-start.48 = (bf16[1408,256]{1,0:T(8,128)(2,1)}, bf16[1408,256]{1,0:T(8,128)(2,1)}, u32[]{:S(2)}, u32[]{:S(2)}) collective-permute-start(bf16[1408,256]{1,0:T(8,128)(2,1)} %get-tuple-element.69), channel_id=1, source_target_pairs={{0,1},{1,0},{2,3},{3,2},{4,5},{5,4},{6,7},{7,6},{8,9},{9,8},{10,11... | collective-permute-start | bytes 2162696 | tf_op jit(solution)/shard_map/ppermute | solution.py:121
  517.2 66.4 %collective-permute-start.53 = (bf16[3,1408,256]{2,1,0:T(8,128)(2,1)}, bf16[3,1408,256]{2,1,0:T(8,128)(2,1)}, u32[]{:S(2)}, u32[]{:S(2)}) collective-permute-start(bf16[3,1408,256]{2,1,0:T(8,128)(2,1)} %broadcast_add_fusion.refs_0_), channel_id=1, source_target_pairs={{0,1},{1,0},{2,3},{3,2},{4,5},{5,4},{6,7},{7,6},{8,9},{9,8},{10,11... | collective-permute-start | bytes 6488072 | tf_op jit(solution)/shard_map/ppermute | solution.py:121
  518.6 62.1 %collective-permute-start.56 = (bf16[1024,384]{1,0:T(8,128)(2,1)}, bf16[1024,384]{1,0:T(8,128)(2,1)}, u32[]{:S(2)}, u32[]{:S(2)}) collective-permute-start(bf16[1024,384]{1,0:T(8,128)(2,1)} %add_bitcast_fusion.1.refs_4_.refs_8_), channel_id=1, source_target_pairs={{0,1},{1,0},{2,3},{3,2},{4,5},{5,4},{6,7},{7,6},{8,9},{9,8},{10,11... | collective-permute-start | bytes 2359304 | tf_op jit(solution)/shard_map/ppermute | solution.py:121
  518.6 56.8 %collective-permute-start.57 = (bf16[1024,384]{1,0:T(8,128)(2,1)}, bf16[1024,384]{1,0:T(8,128)(2,1)}, u32[]{:S(2)}, u32[]{:S(2)}) collective-permute-start(bf16[1024,384]{1,0:T(8,128)(2,1)} %add_bitcast_fusion.1.refs_4_.refs_8_), channel_id=1, source_target_pairs={{0,2},{1,3},{2,0},{3,1},{4,6},{5,7},{6,4},{7,5},{8,10},{9,11},{10,... | collective-permute-start | bytes 2359304 | tf_op jit(solution)/shard_map/ppermute | solution.py:121
  546.4 32.8 %all-to-all-start.5 = ((bf16[16,1,88,256]{3,2,1,0:T(8,128)(2,1)}), bf16[16,1,88,256]{3,2,1,0:T(8,128)(2,1)}, u32[]{:S(2)}, u32[]{:S(2)}) async-start(bf16[16,1,88,256]{3,2,1,0:T(8,128)(2,1)} %bitcast.380), calls=%async_computation.5 | async-start | bytes 1441792 | tf_op jit(solution)/shard_map/all_to_all | solution.py:1524
  556.2 27.4 %collective-permute-start.55 = (bf16[3,1408,256]{2,1,0:T(8,128)(2,1)}, bf16[3,1408,256]{2,1,0:T(8,128)(2,1)}, u32[]{:S(2)}, u32[]{:S(2)}) collective-permute-start(bf16[3,1408,256]{2,1,0:T(8,128)(2,1)} %collective-permute-done.54.refs_2_), channel_id=1, source_target_pairs={{0,1},{1,0},{2,3},{3,2},{4,5},{5,4},{6,7},{7,6},{8,9},{9,8},{10,11... | collective-permute-start | bytes 6488072 | tf_op jit(solution)/shard_map/ppermute | solution.py:121
  582.0 24.4 %collective-permute-start.71 = (bf16[3,352,256]{2,1,0:T(8,128)(2,1)}, bf16[3,352,256]{2,1,0:T(8,128)(2,1)}, u32[]{:S(2)}, u32[]{:S(2)}) collective-permute-start(bf16[3,352,256]{2,1,0:T(8,128)(2,1)} %pad_maximum_fusion.8), channel_id=1, source_target_pairs={{0,2},{1,3},{2,0},{3,1},{4,6},{5,7},{6,4},{7,5},{8,10},{9,11},{10,... | collective-permute-start | bytes 1622024 | tf_op jit(solution)/shard_map/ppermute | solution.py:177
  583.5 27.1 %collective-permute-start.72 = (bf16[3,352,256]{2,1,0:T(8,128)(2,1)}, bf16[3,352,256]{2,1,0:T(8,128)(2,1)}, u32[]{:S(2)}, u32[]{:S(2)}) collective-permute-start(bf16[3,352,256]{2,1,0:T(8,128)(2,1)} %pad_maximum_fusion.9), channel_id=1, source_target_pairs={{0,3},{1,2},{2,1},{3,0},{4,7},{5,6},{6,5},{7,4},{8,11},{9,10},{10,... | collective-permute-start | bytes 1622024 | tf_op jit(solution)/shard_map/ppermute | solution.py:177
  595.4 60.9 %all-to-all-start.6 = ((bf16[4,1,3,88,1024]{4,3,2,1,0:T(8,128)(2,1)}), bf16[4,1,3,88,1024]{4,3,2,1,0:T(8,128)(2,1)}, u32[]{:S(2)}, u32[]{:S(2)}) async-start(bf16[4,1,3,88,1024]{4,3,2,1,0:T(8,128)(2,1)} %self_backward.1.refs_16_), calls=%async_computation.6 | async-start | bytes 4325376 | tf_op jit(solution)/shard_map/all_to_all | solution.py:1488
  599.9 296.7 %reduce-scatter.8.cloned.1.call-start = ((), (), s32[]{:S(2)}) async-start(), calls=%async_computation.17 | async-start | bytes 6082560 | tf_op jit(solution)/shard_map/reduce_scatter | solution.py:1588
  604.1 27.1 %collective-permute-start.75 = (bf16[704,384]{1,0:T(8,128)(2,1)S(1)}, bf16[704,384]{1,0:T(8,128)(2,1)S(1)}, u32[]{:S(2)}, u32[]{:S(2)}) collective-permute-start(bf16[704,384]{1,0:T(8,128)(2,1)S(1)} %get-tuple-element.257), channel_id=1, source_target_pairs={{0,3},{1,2},{2,1},{3,0},{4,7},{5,6},{6,5},{7,4},{8,11},{9,10},{10,... | collective-permute-start | bytes 1622024 | tf_op jit(solution)/shard_map/ppermute | solution.py:177
  606.4 83.8 %collective-permute-start.85 = (bf16[704,1536]{1,0:T(8,128)(2,1)}, bf16[704,1536]{1,0:T(8,128)(2,1)}, u32[]{:S(2)}, u32[]{:S(2)}) collective-permute-start(bf16[704,1536]{1,0:T(8,128)(2,1)} %get-tuple-element.82.refs_26_), channel_id=1, source_target_pairs={{0,16},{16,0},{1,17},{17,1},{2,18},{18,2},{3,19},{19,3},{4,20},{20... | collective-permute-start | bytes 6488072 | tf_op jit(solution)/shard_map/ppermute | solution.py:121
  610.7 40.4 %collective-permute-start.47 = (bf16[1408,256]{1,0:T(8,128)(2,1)}, bf16[1408,256]{1,0:T(8,128)(2,1)}, u32[]{:S(2)}, u32[]{:S(2)}) collective-permute-start(bf16[1408,256]{1,0:T(8,128)(2,1)} %get-tuple-element.67), channel_id=1, source_target_pairs={{0,1},{1,0},{2,3},{3,2},{4,5},{5,4},{6,7},{7,6},{8,9},{9,8},{10,11... | collective-permute-start | bytes 2162696 | tf_op jit(solution)/shard_map/ppermute | solution.py:121
  611.0 40.1 %collective-permute-start.49 = (bf16[1408,256]{1,0:T(8,128)(2,1)}, bf16[1408,256]{1,0:T(8,128)(2,1)}, u32[]{:S(2)}, u32[]{:S(2)}) collective-permute-start(bf16[1408,256]{1,0:T(8,128)(2,1)} %add_convert_fusion.13), channel_id=1, source_target_pairs={{0,2},{1,3},{2,0},{3,1},{4,6},{5,7},{6,4},{7,5},{8,10},{9,11},{10,... | collective-permute-start | bytes 2162696 | tf_op jit(solution)/shard_map/ppermute | solution.py:121
  695.1 29.6 %collective-permute-start.86 = (bf16[352,1536]{1,0:T(8,128)(2,1)}, bf16[352,1536]{1,0:T(8,128)(2,1)}, u32[]{:S(2)}, u32[]{:S(2)}) collective-permute-start(bf16[352,1536]{1,0:T(8,128)(2,1)} %slice.547), channel_id=1, source_target_pairs={{0,4},{4,0},{8,12},{12,8},{1,5},{5,1},{9,13},{13,9},{2,6},{6,2},{1... | collective-permute-start | bytes 3244040 | tf_op jit(solution)/shard_map/ppermute | solution.py:121
  722.3 182.1 %reduce-scatter.6.cloned.1.call-start = ((), (), s32[]{:S(2)}) async-start(), calls=%async_computation.16 | async-start | bytes 6082560 | tf_op jit(solution)/shard_map/reduce_scatter | solution.py:1588
  727.4 48.7 %collective-permute-start.87 = (bf16[176,1536]{1,0:T(8,128)(2,1)}, bf16[176,1536]{1,0:T(8,128)(2,1)}, u32[]{:S(2)}, u32[]{:S(2)}) collective-permute-start(bf16[176,1536]{1,0:T(8,128)(2,1)} %slice.550), channel_id=1, source_target_pairs={{0,8},{4,12},{8,0},{12,4},{1,9},{5,13},{9,1},{13,5},{2,10},{6,14},... | collective-permute-start | bytes 1622024 | tf_op jit(solution)/shard_map/ppermute | solution.py:121
  738.4 114.6 %collective-permute-start.63 = (bf16[256,2816]{1,0:T(8,128)(2,1)}, bf16[256,2816]{1,0:T(8,128)(2,1)}, u32[]{:S(2)}, u32[]{:S(2)}) collective-permute-start(bf16[256,2816]{1,0:T(8,128)(2,1)} %convolution_convert_fusion.1), channel_id=1, source_target_pairs={{0,1},{1,0},{2,3},{3,2},{4,5},{5,4},{6,7},{7,6},{8,9},{9,8},{10,11... | collective-permute-start | bytes 4325384 | tf_op jit(solution)/shard_map/ppermute | solution.py:121
  740.5 152.1 %collective-permute-start.62 = (bf16[256,2816]{1,0:T(8,128)(2,1)}, bf16[256,2816]{1,0:T(8,128)(2,1)}, u32[]{:S(2)}, u32[]{:S(2)}) collective-permute-start(bf16[256,2816]{1,0:T(8,128)(2,1)} %convolution_convert_fusion.3), channel_id=1, source_target_pairs={{0,1},{1,0},{2,3},{3,2},{4,5},{5,4},{6,7},{7,6},{8,9},{9,8},{10,11... | collective-permute-start | bytes 4325384 | tf_op jit(solution)/shard_map/ppermute | solution.py:121
  751.1 31.8 %collective-permute-start.65 = (f32[1,1408]{1,0:T(1,128)S(1)}, f32[1,1408]{1,0:T(1,128)S(1)}, u32[]{:S(2)}, u32[]{:S(2)}) collective-permute-start(f32[1,1408]{1,0:T(1,128)S(1)} %add.708), channel_id=1, source_target_pairs={{0,1},{1,0},{2,3},{3,2},{4,5},{5,4},{6,7},{7,6},{8,9},{9,8},{10,11... | collective-permute-start | bytes 16904 | tf_op jit(solution)/shard_map/ppermute | solution.py:121
  752.1 65.8 %collective-permute-start.82 = (bf16[44,1536]{1,0:T(8,128)(2,1)}, bf16[44,1536]{1,0:T(8,128)(2,1)S(1)}, u32[]{:S(2)}, u32[]{:S(2)}) collective-permute-start(bf16[44,1536]{1,0:T(8,128)(2,1)} %get-tuple-element.342), channel_id=1, source_target_pairs={{0,3},{1,2},{2,1},{3,0},{4,7},{5,6},{6,5},{7,4},{8,11},{9,10},{10,... | collective-permute-start | bytes 405512 | tf_op jit(solution)/shard_map/ppermute | solution.py:177
  776.1 42.9 %collective-permute-start.83 = (bf16[44,1536]{1,0:T(8,128)(2,1)}, bf16[44,1536]{1,0:T(8,128)(2,1)}, u32[]{:S(2)}, u32[]{:S(2)}) collective-permute-start(bf16[44,1536]{1,0:T(8,128)(2,1)} %get-tuple-element.201), channel_id=1, source_target_pairs={{0,2},{1,3},{2,0},{3,1},{4,6},{5,7},{6,4},{7,5},{8,10},{9,11},{10,... | collective-permute-start | bytes 405512 | tf_op jit(solution)/shard_map/ppermute | solution.py:177
  827.5 30.1 %collective-permute-start.69 = (f32[2,2,2,2,1,1408]{5,3,2,1,0,4:T(2,128)S(1)}, f32[2,2,2,2,1,1408]{5,3,2,1,0,4:T(2,128)S(1)}, u32[]{:S(2)}, u32[]{:S(2)}) collective-permute-start(f32[2,2,2,2,1,1408]{5,3,2,1,0,4:T(2,128)S(1)} %maximum_select_fusion.9), channel_id=1, source_target_pairs={{0,16},{16,0},{1,17},{17,1},{2,18},{18,2},{3,19},{19,3},{4,20},{20... | collective-permute-start | bytes 270344 | tf_op jit(solution)/shard_map/ppermute | solution.py:121
  855.4 37.2 %collective-permute-start.64 = (bf16[256,2816]{1,0:T(8,128)(2,1)S(1)}, bf16[256,2816]{1,0:T(8,128)(2,1)S(1)}, u32[]{:S(2)}, u32[]{:S(2)}) collective-permute-start(bf16[256,2816]{1,0:T(8,128)(2,1)S(1)} %add_convert_fusion.1), channel_id=1, source_target_pairs={{0,2},{1,3},{2,0},{3,1},{4,6},{5,7},{6,4},{7,5},{8,10},{9,11},{10,... | collective-permute-start | bytes 4325384 | tf_op jit(solution)/shard_map/ppermute | solution.py:121
  856.8 33.9 %collective-permute-start.94 = (bf16[2,32,384]{2,1,0:T(8,128)(2,1)S(1)}, bf16[2,32,384]{2,1,0:T(8,128)(2,1)S(1)}, u32[]{:S(2)}, u32[]{:S(2)}) collective-permute-start(bf16[2,32,384]{2,1,0:T(8,128)(2,1)S(1)} %broadcast_select_fusion.135), channel_id=1, source_target_pairs={{0,2},{1,3},{2,0},{3,1},{4,6},{5,7},{6,4},{7,5},{8,10},{9,11},{10,... | collective-permute-start | bytes 147464 | tf_op jit(solution)/shard_map/ppermute | solution.py:121
  (176 other events, 1385.9 us)
Sparse Core Ops, SparseCore 0:
  32.1 91.2 all-gather.3
  125.5 86.4 all-gather.5
  214.0 186.0 all-gather.7
  495.3 93.1 reduce-scatter.3
  646.9 129.6 reduce-scatter.7
  780.6 111.5 reduce-scatter.5

commit v3 on v2

--- a/solution.py
+++ b/solution.py
@@ -199,9 +199,9 @@
     return differences
 
 
-def scatter_group_halves(keep, send, waits):
+def scatter_group_halves(keep, send, first, waits):
     for step, (axis, bit, _) in enumerate(group_steps()):
-        came = trade_bit(send, axis, bit).astype(f32)
+        came = (trade_bit(send, axis, bit) if step else first).astype(f32)
         total = after(keep.astype(f32) + came, waits[step]).astype(bf16)
         half = total.shape[0] // 2
         keep, send = total[:half], total[half:]
@@ -211,25 +211,50 @@
 
 
 def gather_every(value):
-    for axis in reversed(EVERY):
-        for bit in bits_of(axis):
+    dims = []
+    for axis in ("dp", "sp", "cp"):
+        for bit in reversed(bits_of(axis)):
             other = trade_bit(value, axis, bit)
             value = jnp.where(
                 has_bit(axis, bit), jnp.stack([other, value]), jnp.stack([value, other])
             )
-    depth = sum(len(bits_of(axis)) for axis in EVERY)
+            dims.append((axis, bit))
+    depth = len(dims)
+    value = jnp.transpose(
+        value, tuple(reversed(range(depth))) + tuple(range(depth, value.ndim))
+    )
     return value.reshape((-1,) + value.shape[depth:])
 
 
 def scatter_every(value):
-    for axis in EVERY:
-        for bit in reversed(bits_of(axis)):
-            halves = value.reshape((2, -1) + value.shape[1:])
+    cp_count = lax.axis_size("cp")
+    value = jnp.swapaxes(value.reshape((-1, cp_count) + value.shape[1:]), 0, 1)
+    for axis in ("cp", "dp", "sp"):
+        for bit in reversed(bits_of(axis)) if axis != "cp" else bits_of(axis):
+            if axis == "cp":
+                halves = value.reshape((-1, 2) + value.shape[1:])
+                first, second = halves[:, 0], halves[:, 1]
+            else:
+                halves = value.reshape((2, -1) + value.shape[1:])
+                first, second = halves[0], halves[1]
             high = has_bit(axis, bit)
-            keep = jnp.where(high, halves[1], halves[0])
-            send = jnp.where(high, halves[0], halves[1])
+            keep = jnp.where(high, second, first)
+            send = jnp.where(high, first, second)
             value = keep + trade_bit(send, axis, bit)
+        if axis == "cp":
+            value = value[0]
     return value[0]
+
+
+def send_every(value):
+    count = lax.axis_size("dp") * lax.axis_size("sp") * lax.axis_size("cp")
+    value = jnp.broadcast_to(value[None], (count,) + value.shape)
+    return lax.all_to_all(value, EVERY, split_axis=0, concat_axis=0, tiled=True)
+
+
+def sum_every(value):
+    came = lax.all_to_all(value, EVERY, split_axis=0, concat_axis=0, tiled=True)
+    return jnp.sum(came.astype(f32), axis=0)
 
 
 def flip(block):
@@ -257,8 +282,8 @@
     return lax.fori_loop(first + fours * 4, last, step, carry)
 
 
-def self_forward_kernel(first_ref, last_ref, turned_ref, qkv_ref, *refs):
-    out_ref, total_ref, keys = refs[-3:]
+def self_forward_kernel(per_cell, first_ref, last_ref, turned_ref, qkv_ref, *refs):
+    out_ref, total_ref, *sent_ref, keys = refs[-4:] if per_cell else refs[-3:]
     pair = pl.program_id(0)
     per = qkv_ref.shape[-1] // CELL
 
@@ -293,7 +318,10 @@
             step,
             (jnp.zeros((HEAD, CELL), f32), jnp.zeros((1, CELL), f32)),
         )
-        out_ref[chunk, 0, :, lanes] = summed / totals
+        out = summed / totals
+        out_ref[chunk, 0, :, lanes] = out
+        if per_cell:
+            sent_ref[0][cell % per, chunk, 0] = out.astype(bf16)
         total_ref[chunk, 0, :, lanes] = totals
         return carry
 
@@ -333,7 +361,10 @@
     def one_cell(cell, carry):
         chunk, lanes = where(cell)
         query = qkv_ref[chunk, 0, 0, :, lanes]
-        grad = grad_ref[chunk, 0, :, lanes].astype(f32)
+        if len(grad_ref.shape) == 5:
+            grad = grad_ref[cell % per, chunk, 0].astype(f32)
+        else:
+            grad = grad_ref[chunk, 0, :, lanes].astype(f32)
         inverse = 1.0 / total_ref[chunk, 0, :, lanes]
         scaled = (grad * inverse).astype(bf16)
         total_grad = (
@@ -378,21 +409,26 @@
 VMEM_LIMIT = 48 * 1024 * 1024
 
 
-def self_forward(qkv, first, last, turned, stamps):
+def self_forward(qkv, first, last, turned, stamps, per_cell):
     chunks, pairs, _, _, columns = qkv.shape
     out_shape = (chunks, pairs, HEAD, columns)
     total_shape = (chunks, pairs, 1, columns)
+    sent_shape = (columns // CELL, chunks, pairs, HEAD, CELL)
+    sent_spec = pl.BlockSpec(
+        sent_shape[:2] + (1,) + sent_shape[3:], lambda pair, *_: (0, 0, pair, 0, 0)
+    )
     return pl.pallas_call(
-        self_forward_kernel,
+        functools.partial(self_forward_kernel, per_cell),
         out_shape=(
             jax.ShapeDtypeStruct(out_shape, f32),
             jax.ShapeDtypeStruct(total_shape, f32),
-        ),
+        )
+        + (jax.ShapeDtypeStruct(sent_shape, bf16),) * per_cell,
         grid_spec=pltpu.PrefetchScalarGridSpec(
             num_scalar_prefetch=3,
             grid=(pairs,),
             in_specs=[pair_spec(qkv.shape)] + [pl.BlockSpec(memory_space=pl.ANY)] * len(stamps),
-            out_specs=[pair_spec(out_shape), pair_spec(total_shape)],
+            out_specs=[pair_spec(out_shape), pair_spec(total_shape)] + [sent_spec] * per_cell,
             scratch_shapes=[pltpu.VMEM((CELLS, CELL, HEAD), bf16)],
         ),
         compiler_params=pltpu.CompilerParams(vmem_limit_bytes=VMEM_LIMIT),
@@ -411,7 +447,11 @@
             grid=(pairs,),
             in_specs=[
                 pair_spec(qkv.shape),
-                pair_spec(grad.shape),
+                pair_spec(grad.shape)
+                if grad.ndim == 4
+                else pl.BlockSpec(
+                    grad.shape[:2] + (1,) + grad.shape[3:], lambda pair, *_: (0, 0, pair, 0, 0)
+                ),
                 pair_spec(out.shape),
                 pair_spec(totals.shape),
             ]
@@ -536,43 +576,93 @@
     )(bucket, stamp)
 
 
-def turn_over_kernel(value_ref, out_ref):
+def offer_kernel(count, which_ref, captions_ref, *refs):
+    outputs = refs[-2 - count : -2]
+    stage, sems = refs[-2:]
+    copies = [
+        pltpu.make_async_copy(captions_ref.at[0, which_ref[k]], stage.at[k], sems.at[k])
+        for k in range(count)
+    ]
+    for copy in copies:
+        copy.start()
+    for k in range(count):
+        copies[k].wait()
+        rest = jnp.zeros((TEXT_PAD - TEXT, stage.shape[2]), f32)
+        outputs[k][...] = jnp.concatenate([stage[k].astype(f32), rest], axis=0).astype(bf16)
+
+
+def offer(which, captions, stamps):
+    count = which.shape[0]
+    shape = jax.ShapeDtypeStruct((TEXT_PAD, captions.shape[3]), bf16)
+    return pl.pallas_call(
+        functools.partial(offer_kernel, count),
+        out_shape=(shape,) * count,
+        in_specs=[SMEM_WHOLE] + [ANY_WHOLE] * (1 + len(stamps)),
+        out_specs=[VMEM_WHOLE] * count,
+        scratch_shapes=[
+            pltpu.VMEM((count, TEXT, captions.shape[3]), bf16),
+            pltpu.SemaphoreType.DMA((count,)),
+        ],
+        compiler_params=pltpu.CompilerParams(vmem_limit_bytes=VMEM_LIMIT),
+        cost_estimate=pl.CostEstimate(flops=1, bytes_accessed=8 << 20, transcendentals=0),
+        name="offer",
+    )(which, captions, *stamps)
+
+
+def gate(values, stamps):
+    def kernel(*refs):
+        pass
+
+    return pl.pallas_call(
+        kernel,
+        out_shape=tuple(jax.ShapeDtypeStruct(value.shape, value.dtype) for value in values),
+        in_specs=[ANY_WHOLE] * (len(values) + len(stamps)),
+        out_specs=[ANY_WHOLE] * len(values),
+        input_output_aliases={k: k for k in range(len(values))},
+        cost_estimate=pl.CostEstimate(flops=1, bytes_accessed=1, transcendentals=0),
+        name="gate",
+    )(*values, *stamps)
+
+
+def turn_over_kernel(value_ref, *refs):
+    out_ref = refs[-1]
     out_ref[...] = flip(value_ref[...])
 
 
-def turn_over(value):
+def turn_over(value, stamps):
     return pl.pallas_call(
         turn_over_kernel,
         out_shape=jax.ShapeDtypeStruct(value.shape[::-1], value.dtype),
-        in_specs=[pl.BlockSpec(memory_space=pltpu.VMEM)],
-        out_specs=pl.BlockSpec(memory_space=pltpu.VMEM),
+        in_specs=[VMEM_WHOLE] + [ANY_WHOLE] * len(stamps),
+        out_specs=VMEM_WHOLE,
         compiler_params=pltpu.CompilerParams(vmem_limit_bytes=VMEM_LIMIT),
         cost_estimate=pl.CostEstimate(flops=1, bytes_accessed=2 << 20, transcendentals=0),
         name="turn_over",
-    )(value)
-
-
-def expand_grads_kernel(*refs):
-    left = jnp.concatenate([ref[...] for ref in refs[:-2]], axis=1)
-    refs[-1][...] = kernel_dot(left, refs[-2][...]).astype(bf16)
-
-
-def expand_grads(pieces, right):
-    steps = 4
+    )(value, *stamps)
+
+
+def expand_grads_kernel(count, *refs):
+    left = jnp.concatenate([ref[...] for ref in refs[:count]], axis=1)
+    refs[-1][...] = kernel_dot(left, refs[count][...]).astype(bf16)
+
+
+def expand_grads(pieces, right, stamps):
+    steps = 2
     rows, width = D // steps, right.shape[1]
     return pl.pallas_call(
-        expand_grads_kernel,
+        functools.partial(expand_grads_kernel, len(pieces)),
         out_shape=jax.ShapeDtypeStruct((D, width), bf16),
         grid=(steps,),
         in_specs=[pl.BlockSpec((rows, pieces[0].shape[1]), lambda g: (g, 0))] * len(pieces)
-        + [pl.BlockSpec(right.shape, lambda g: (0, 0))],
+        + [pl.BlockSpec(right.shape, lambda g: (0, 0))]
+        + [ANY_WHOLE] * len(stamps),
         out_specs=pl.BlockSpec((rows, width), lambda g: (g, 0)),
         compiler_params=pltpu.CompilerParams(vmem_limit_bytes=VMEM_LIMIT),
         cost_estimate=pl.CostEstimate(
             flops=2 * D * right.shape[0] * width, bytes_accessed=12 << 20, transcendentals=0
         ),
         name="expand_grads",
-    )(*pieces, right)
+    )(*pieces, right, *stamps)
 
 
 def reduce_grads_kernel(group_ref, *refs):
@@ -618,34 +708,43 @@
     )(groups, *pieces, right)
 
 
-def mid_grads_kernel(count, width, *refs):
-    lefts, rights, texts, pairs = (refs[k * count : (k + 1) * count] for k in range(4))
-    out_ref = refs[4 * count + 1]
-    rows = out_ref.shape[0]
+def mid_grads_kernel(count, width, groups, *refs):
+    lefts, third, rights, texts, pairs = (refs[k * count : (k + 1) * count] for k in range(5))
+    out_ref = refs[5 * count + 1]
+    rows = out_ref.shape[0] // groups
     padded = width + -width % 128
     for part in range(3):
         product = sum(
-            kernel_dot(left[part], right[part], 1, 1) for left, right in zip(lefts, rights)
-        )
-        product = jnp.concatenate([product, jnp.zeros((rows, padded - width), f32)], axis=1)
+            kernel_dot(left[part] if part < 2 else last[...], right[part], 1, 1)
+            for left, last, right in zip(lefts, third, rights)
+        )
+        product = jnp.concatenate(
+            [product, jnp.zeros((product.shape[0], padded - width), f32)], axis=1
+        )
         out_ref[:, part * padded : (part + 1) * padded] = product.astype(bf16)
-    text = texts[0].shape[0]
+    text = texts[0].shape[0] // groups
     product = sum(kernel_dot(left[...], right[...], 1, 1) for left, right in zip(texts, pairs))
     rest = out_ref.shape[1] - 3 * padded
-    product = jnp.concatenate([product, jnp.zeros((text, rest - 2 * width), f32)], axis=1)
-    out_ref[:text, 3 * padded :] = product.astype(bf16)
-    out_ref[text:, 3 * padded :] = jnp.zeros((rows - text, rest), bf16)
-
-
-def mid_grads_bucket(lefts, rights, texts, pairs, stamp, groups):
+    product = jnp.concatenate(
+        [product, jnp.zeros((product.shape[0], rest - 2 * width), f32)], axis=1
+    ).astype(bf16)
+    for group in range(groups):
+        start = group * rows
+        out_ref[start : start + text, 3 * padded :] = product[group * text : (group + 1) * text]
+        out_ref[start + text : start + rows, 3 * padded :] = jnp.zeros((rows - text, rest), bf16)
+
+
+def mid_grads_bucket(lefts, third, rights, texts, pairs, stamp, groups):
     count, width = len(lefts), rights[0].shape[1]
-    rows, text = D // groups, DT // groups
+    steps = 2
+    rows, text = D // steps, DT // steps
     columns = 3 * (width + -width % 128) + 2 * width + -2 * width % 128
     return pl.pallas_call(
-        functools.partial(mid_grads_kernel, count, width),
+        functools.partial(mid_grads_kernel, count, width, groups // steps),
         out_shape=jax.ShapeDtypeStruct((D, columns), bf16),
-        grid=(groups,),
-        in_specs=[pl.BlockSpec((3, rows, lefts[0].shape[2]), lambda g: (0, g, 0))] * count
+        grid=(steps,),
+        in_specs=[pl.BlockSpec((2, rows, lefts[0].shape[2]), lambda g: (0, g, 0))] * count
+        + [pl.BlockSpec((rows, third[0].shape[1]), lambda g: (g, 0))] * count
         + [pl.BlockSpec(rights[0].shape, lambda g: (0, 0, 0))] * count
         + [pl.BlockSpec((text, texts[0].shape[1]), lambda g: (g, 0))] * count
         + [pl.BlockSpec(pairs[0].shape, lambda g: (0, 0))] * count
@@ -656,12 +755,12 @@
             flops=10 * D * D * width, bytes_accessed=24 << 20, transcendentals=0
         ),
         name="mid_grads",
-    )(*lefts, *rights, *texts, *pairs, stamp)
+    )(*lefts, *third, *rights, *texts, *pairs, stamp)
 
 
 def skip_grads_kernel(count, width, *refs):
     rights, lefts = refs[:count], refs[count : 2 * count]
-    input_ref, out_ref = refs[2 * count :]
+    input_ref, gain_ref, out_ref = refs[2 * count :]
     product = sum(kernel_dot(left[...], right[...]) for left, right in zip(lefts, rights))
     padded = width + -width % 128
     quarter = width // (2 * count)
@@ -682,10 +781,13 @@
             ] = jnp.concatenate([block, fill], axis=1).astype(bf16)
     out_ref[:, 2 * padded : 2 * padded + input_ref.shape[1]] = input_ref[...]
     rest = out_ref.shape[1] - 2 * padded - input_ref.shape[1]
-    out_ref[:, 2 * padded + input_ref.shape[1] :] = jnp.zeros((out_ref.shape[0], rest), bf16)
-
-
-def skip_grads_bucket(lefts, rights, inputs):
+    gains = jnp.concatenate(
+        [gain_ref[...], jnp.zeros((out_ref.shape[0], rest - gain_ref.shape[1]), f32)], axis=1
+    )
+    out_ref[:, 2 * padded + input_ref.shape[1] :] = gains.astype(bf16)
+
+
+def skip_grads_bucket(lefts, rights, inputs, gains):
     count, width = len(lefts), lefts[0].shape[0]
     columns = 2 * (width + -width % 128) + inputs.shape[1] + -inputs.shape[1] % 128
     return pl.pallas_call(
@@ -694,17 +796,17 @@
         grid=(2,),
         in_specs=[pl.BlockSpec((rights[0].shape[0], D), lambda g: (0, g))] * count
         + [pl.BlockSpec(lefts[0].shape, lambda g: (0, 0))] * count
-        + [pl.BlockSpec((D // 2, inputs.shape[1]), lambda g: (g, 0))],
+        + [pl.BlockSpec((D // 2, member.shape[1]), lambda g: (g, 0)) for member in (inputs, gains)],
         out_specs=pl.BlockSpec((D // 2, columns), lambda g: (g, 0)),
         compiler_params=pltpu.CompilerParams(vmem_limit_bytes=VMEM_LIMIT),
         cost_estimate=pl.CostEstimate(
             flops=4 * D * width * count * 256, bytes_accessed=16 << 20, transcendentals=0
         ),
         name="skip_grads",
-    )(*rights, *lefts, inputs)
-
-
-def finish_kernel(factor_ref, blocks_ref, skip_ref, input_ref):
+    )(*rights, *lefts, inputs, gains)
+
+
+def finish_kernel(factor_ref, blocks_ref, skip_ref, input_ref, gain_ref):
     factor = factor_ref[0, 0]
     count, shard, _ = blocks_ref.shape
     width = skip_ref.shape[1] // count
@@ -714,6 +816,8 @@
         skip_ref[part * shard : (part + 1) * shard, :] = jnp.concatenate(
             [block[:, part * padded : part * padded + width] for block in blocks], axis=1
         )
+    start = 2 * padded + 3 * width
+    gain_ref[...] = sum(block[:, start : start + 4] for block in blocks)
     input_ref[...] = jnp.concatenate(
         [
             block[:, 2 * padded + part * width : 2 * padded + (part + 1) * width]
@@ -731,9 +835,10 @@
         out_shape=(
             jax.ShapeDtypeStruct((2 * shard, D), f32),
             jax.ShapeDtypeStruct((shard, 3 * D), f32),
-        ),
-        in_specs=[pl.BlockSpec(memory_space=pltpu.SMEM), pl.BlockSpec(memory_space=pltpu.VMEM)],
-        out_specs=[pl.BlockSpec(memory_space=pltpu.VMEM)] * 2,
+            jax.ShapeDtypeStruct((shard, 4), f32),
+        ),
+        in_specs=[SMEM_WHOLE, VMEM_WHOLE],
+        out_specs=[VMEM_WHOLE] * 3,
         compiler_params=pltpu.CompilerParams(vmem_limit_bytes=VMEM_LIMIT),
         cost_estimate=pl.CostEstimate(flops=1, bytes_accessed=2 << 20, transcendentals=0),
         name="finish_head",
@@ -767,7 +872,7 @@
 def mix_kernel(count, padded, *refs):
     index_ref, bucket_ref = refs[:2]
     pieces = refs[2 : 2 + count]
-    out_ref, weight = refs[2 + count :]
+    out_ref, weight = refs[-2:]
     width = weight.shape[1]
     half = width // 2
     for group in range(weight.shape[0] // width):
@@ -780,7 +885,7 @@
         out_ref[piece ^ index_ref[0]] = kernel_dot(pieces[piece][...], weight[...]).astype(bf16)
 
 
-def mix(index, bucket, pieces, width):
+def mix(index, bucket, pieces, width, stamps):
     count, padded = len(pieces), width + -width % 128
     rows = pieces[0].shape[0]
     return pl.pallas_call(
@@ -788,7 +893,8 @@
         out_shape=jax.ShapeDtypeStruct((count, rows, width), bf16),
         grid=(1,),
         in_specs=[SMEM_WHOLE, pl.BlockSpec((D, 2 * padded), lambda g: (0, 0))]
-        + [pl.BlockSpec(pieces[0].shape, lambda g: (0, 0))] * count,
+        + [pl.BlockSpec(pieces[0].shape, lambda g: (0, 0))] * count
+        + [ANY_WHOLE] * len(stamps),
         out_specs=pl.BlockSpec((count, rows, width), lambda g: (0, 0, 0)),
         scratch_shapes=[pltpu.VMEM((2 * D, width), bf16)],
         compiler_params=pltpu.CompilerParams(vmem_limit_bytes=VMEM_LIMIT),
@@ -796,7 +902,7 @@
             flops=4 * D * width * count * rows, bytes_accessed=8 << 20, transcendentals=0
         ),
         name="mix",
-    )(index, bucket, *pieces)
+    )(index, bucket, *pieces, *stamps)
 
 
 def mixed_rows(blocks_ref, stage):
@@ -893,7 +999,6 @@
         mid_ref[rows, :] = base_ref[rows, :] + kernel_dot(weights[piece], attended)
     normed = (norm_rows(mid_ref[...])[0] * gain_ref[:, 2:3]).astype(bf16)
     lefts_ref[0] = normed
-    lefts_ref[2] = attended
     for piece in range(count):
         copies[count + piece].wait()
         product = kernel_dot(weights[count + piece], normed)
@@ -926,7 +1031,7 @@
         out_shape=(
             stream,
             stream,
-            jax.ShapeDtypeStruct((3, D, tokens), bf16),
+            jax.ShapeDtypeStruct((2, D, tokens), bf16),
             jax.ShapeDtypeStruct(by_head, f32),
             jax.ShapeDtypeStruct(by_head, bf16),
             stream,
@@ -1065,73 +1170,112 @@
 GELU_SCALE = math.sqrt(2.0 / math.pi)
 
 
-def ffn_kernel(count, *refs):
+def ffn_kernel(count, stamps, *refs):
     inputs, grads = refs[:count], refs[count : 2 * count]
-    expand_ref, reduce_ref, hidden_ref, expand_in_ref = refs[2 * count : 2 * count + 4]
-    outputs = refs[2 * count + 4 :]
-    back_refs, out_refs = outputs[:count], outputs[count : 2 * count]
-    value_sc, grad_sc = outputs[2 * count :]
-    step = pl.program_id(0)
-
+    expand_ref, reduce_ref = refs[2 * count : 2 * count + 2]
+    hidden_ref, expand_in_ref, *outputs = refs[2 * count + 2 + stamps :]
+    back_refs = outputs[:count]
+    value_sc, grad_sc, back_sc = outputs[count:]
+    step, steps = pl.program_id(0), pl.num_programs(0)
+    tokens = inputs[0].shape[1]
+
+    @pl.when(step == 0)
+    def _():
+        for piece in range(count):
+            rows = slice(piece * tokens, (piece + 1) * tokens)
+            value_sc[rows, :] = flip(inputs[piece][...])
+            grad_sc[rows, :] = flip(grads[piece][...])
+
+    weight = expand_ref[...]
+    for half in range(2):
+        rows = slice(half * count * tokens // 2, (half + 1) * count * tokens // 2)
+        plain = kernel_dot(value_sc[rows, :], weight)
+        square = plain * plain
+        curve = jnp.tanh(plain * (GELU_SCALE + (GELU_SCALE * 0.044715) * square))
+        above, half_plain = 1.0 + curve, 0.5 * plain
+        hidden_ref[rows, :] = (half_plain * above).astype(bf16)
+        steep = GELU_SCALE + (GELU_SCALE * 3.0 * 0.044715) * square
+        slope = above * (0.5 + half_plain * (1.0 - curve) * steep)
+        expand_in_ref[rows, :] = (kernel_dot(grad_sc[rows, :], reduce_ref[...]) * slope).astype(
+            bf16
+        )
     for piece in range(count):
-
-        @pl.when(step == piece)
+        rows = slice(piece * tokens, (piece + 1) * tokens)
+        part = kernel_dot(weight, expand_in_ref[rows, :], 1, 1)
+
+        @pl.when(step == 0)
         def _():
-            value_sc[...] = flip(inputs[piece][...])
-            grad_sc[...] = flip(grads[piece][...])
-
-    value, grad = value_sc[...], grad_sc[...]
-    back, out = 0.0, 0.0
-    width = expand_ref.shape[1]
-    chunk = 512
-    for start in range(0, width, chunk):
-        cols = slice(start, start + chunk)
-        weight, reduce = expand_ref[:, cols], reduce_ref[:, cols]
-        plain = kernel_dot(value, weight)
-        square = plain * plain
-        curve = jnp.tanh(GELU_SCALE * (plain + 0.044715 * square * plain))
-        hidden = (0.5 * plain * (1.0 + curve)).astype(bf16)
-        slope = 0.5 * (1.0 + curve) + 0.5 * plain * (1.0 - curve * curve) * (
-            GELU_SCALE * (1.0 + 3.0 * 0.044715 * square)
-        )
-        hidden_ref[:, cols] = hidden
-        expand_in = (kernel_dot(grad, reduce) * slope).astype(bf16)
-        expand_in_ref[:, cols] = expand_in
-        back = back + kernel_dot(expand_in, weight, 1, 1)
-        out = out + kernel_dot(hidden, reduce, 1, 1)
-    back = jnp.transpose(back.astype(bf16))
-    out = jnp.transpose(out.astype(bf16))
-    for piece in range(count):
-
-        @pl.when(step == piece)
+            back_sc[piece] = part
+
+        @pl.when((step > 0) & (step < steps - 1))
         def _():
-            back_refs[piece][...] = back
-            out_refs[piece][...] = out
-
-
-def feed_forward(inputs, grads, bucket):
+            back_sc[piece] += part
+
+        @pl.when(step == steps - 1)
+        def _():
+            back_refs[piece][...] = (back_sc[piece] + part).astype(bf16)
+
+
+def feed_forward(inputs, grads, bucket, stamps):
     count = len(inputs)
     tokens, width = inputs[0].shape[1], bucket.shape[1] // 2
+    steps = 3
+    chunk = width // steps
     by_hidden = jax.ShapeDtypeStruct((count * tokens, width), bf16)
     by_piece = jax.ShapeDtypeStruct((D, tokens), bf16)
     whole = pl.BlockSpec((D, tokens), lambda step: (0, 0))
-    hidden_spec = pl.BlockSpec((tokens, width), lambda step: (step, 0))
+    hidden_spec = pl.BlockSpec((count * tokens, chunk), lambda step: (0, step))
     return pl.pallas_call(
-        functools.partial(ffn_kernel, count),
-        out_shape=(by_hidden, by_hidden) + (by_piece,) * (2 * count),
-        grid=(count,),
+        functools.partial(ffn_kernel, count, len(stamps)),
+        out_shape=(by_hidden, by_hidden) + (by_piece,) * count,
+        grid=(steps,),
         in_specs=[whole] * (2 * count)
-        + [pl.BlockSpec((D, width), lambda step, k=k: (0, k)) for k in range(2)],
-        out_specs=[hidden_spec, hidden_spec] + [whole] * (2 * count),
-        scratch_shapes=[pltpu.VMEM((tokens, D), bf16), pltpu.VMEM((tokens, D), bf16)],
+        + [pl.BlockSpec((D, chunk), lambda step, k=k: (0, k * steps + step)) for k in range(2)]
+        + [ANY_WHOLE] * len(stamps),
+        out_specs=[hidden_spec, hidden_spec] + [whole] * count,
+        scratch_shapes=[
+            pltpu.VMEM((count * tokens, D), bf16),
+            pltpu.VMEM((count * tokens, D), bf16),
+            pltpu.VMEM((count, D, tokens), f32),
+        ],
         compiler_params=pltpu.CompilerParams(vmem_limit_bytes=VMEM_LIMIT),
         cost_estimate=pl.CostEstimate(
-            flops=8 * D * count * tokens * width,
-            bytes_accessed=30 << 20,
+            flops=6 * D * count * tokens * width,
+            bytes_accessed=24 << 20,
             transcendentals=count * tokens * width,
         ),
         name="feed_forward",
-    )(*inputs, *grads, bucket, bucket)
+    )(*inputs, *grads, bucket, bucket, *stamps)
+
+
+def reduce_kernel(count, hidden_ref, reduce_ref, stamp_ref, *outputs):
+    tokens = hidden_ref.shape[0] // count
+    for piece in range(count):
+        hidden = hidden_ref[piece * tokens : (piece + 1) * tokens, :]
+        outputs[piece][...] = kernel_dot(reduce_ref[...], hidden, 1, 1).astype(bf16)
+
+
+def reduce_parts(hidden, bucket, stamp, count):
+    width = hidden.shape[1]
+    tokens = hidden.shape[0] // count
+    by_piece = jax.ShapeDtypeStruct((D, tokens), bf16)
+    whole = pl.BlockSpec((D, tokens), lambda step: (0, 0))
+    return pl.pallas_call(
+        functools.partial(reduce_kernel, count),
+        out_shape=(by_piece,) * count,
+        grid=(1,),
+        in_specs=[
+            pl.BlockSpec(hidden.shape, lambda step: (0, 0)),
+            pl.BlockSpec((D, width), lambda step: (0, 1)),
+            ANY_WHOLE,
+        ],
+        out_specs=[whole] * count,
+        compiler_params=pltpu.CompilerParams(vmem_limit_bytes=VMEM_LIMIT),
+        cost_estimate=pl.CostEstimate(
+            flops=2 * D * count * tokens * width, bytes_accessed=12 << 20, transcendentals=0
+        ),
+        name="reduce_parts",
+    )(hidden, bucket, stamp)
 
 
 def project_kernel(count, heads, *refs):
@@ -1308,7 +1452,7 @@
         [three[:, :width], three[:, width : 2 * width], three[:, 2 * width :], pairs_cols]
     )
     mid_gathered = gather_group(mid_bucket)
-    plain = rows % 128 == 0 and packs == 1 and group_rows % 16 == 0
+    plain = rows == CELL and packs == 1 and group_rows % 16 == 0
     ff_bucket = send_columns((expand_weight, jnp.transpose(reduce_weight)))
     ff_gathered = gather_group(ff_bucket)
     expand_part, reduce_part = unpack(ff_gathered, (ff_width, ff_width))
@@ -1396,11 +1540,16 @@
     image_dev = captions.shape[1]
     near = lax.dynamic_slice_in_dim(own_segments, sp_index * cp_count, cp_count, 1)
     local = jnp.clip(near - cp_index * image_dev, 0, image_dev - 1)
+    caption_shard = jnp.pad(
+        jnp.transpose(after(null_caption, head_bucket)), ((0, 0), (0, TEXT_PAD - TEXT))
+    )
+    caption_rows = caption_shard.shape[0]
+    caption_full = jnp.transpose(gather_every(caption_shard).reshape(DT, TEXT_PAD))
     joined = jnp.concatenate([tokens.reshape(held, D), skip_in.reshape(held, D)], axis=1)
     joined_all = pieces_cp(after(joined, head_bucket))
     piece_index = cp_index.reshape(1)
     if plain:
-        mixed_blocks = trade_cp(mix(piece_index, head_gathered, joined_all, width))
+        mixed_blocks = trade_cp(mix(piece_index, head_gathered, joined_all, width, (caption_full,)))
         base_t, normed_self_t = start_forward(
             mixed_blocks, gain_columns_t, shifts.reshape(D, 1)
         )
@@ -1439,25 +1588,23 @@
         value_rows = projected[:, :, 2].astype(bf16)
         qkv = jnp.stack([queries, key_rows, value_rows], axis=2)
 
-    caption_shard = jnp.pad(
-        jnp.transpose(after(null_caption, joined_all[-2])), ((0, 0), (0, TEXT_PAD - TEXT))
-    )
-    caption_rows = caption_shard.shape[0]
-    caption_full = jnp.transpose(gather_every(caption_shard).reshape(DT, TEXT_PAD))
-    local = local + (ff_bucket[0, 0].astype(f32) * 0.0).astype(jnp.int32)
-    offered = jnp.stack(
-        [
-            jnp.stack(
-                [
-                    lax.dynamic_index_in_dim(captions[p], local[p, k], 0, keepdims=False)
-                    for p in range(packs)
-                ]
-            )
-            for k in range(cp_count)
-        ]
-    )
-    offered = jnp.pad(offered, ((0, 0), (0, 0), (0, TEXT_PAD - TEXT), (0, 0)))
-    arrived = jnp.stack(send_cp([offered[k] for k in range(cp_count)]))
+    if plain:
+        offered = offer(local[0, jnp.arange(cp_count) ^ cp_index], captions, (qkv,))
+        arrived = jnp.stack(reorder_cp(exchange_cp(list(offered))))[:, None]
+    else:
+        offered = jnp.stack(
+            [
+                jnp.stack(
+                    [
+                        lax.dynamic_index_in_dim(captions[p], local[p, k], 0, keepdims=False)
+                        for p in range(packs)
+                    ]
+                )
+                for k in range(cp_count)
+            ]
+        )
+        offered = jnp.pad(offered, ((0, 0), (0, 0), (0, TEXT_PAD - TEXT), (0, 0)))
+        arrived = jnp.stack(send_cp([offered[k] for k in range(cp_count)]))
     own_null = jnp.take_along_axis(
         null_mask, block_image[:, None], axis=1
     )[:, 0]
@@ -1474,9 +1621,9 @@
         ]
     )
 
-    out_grad = after(cotangent.reshape(held, D).astype(f32) * token_valid, joined_all[-2])
+    out_grad = cotangent.reshape(held, D).astype(f32) * token_valid
     out_turned = out_grad.astype(bf16)
-    out_turned = turn_over(out_turned) if plain else jnp.transpose(out_turned)
+    out_turned = turn_over(out_turned, (qkv,)) if plain else jnp.transpose(out_turned)
     out_grad = jnp.transpose(out_turned).astype(f32)
     reduce_pieces = pieces_cp(out_turned)
 
@@ -1489,7 +1636,9 @@
         return value.reshape((packs, group_heads) + value.shape[2:])
 
     if plain:
-        *mid_parts, pairs_part = unpack_mid(mid_gathered, width, group_text, qkv)
+        *mid_parts, pairs_part = unpack_mid(
+            mid_gathered, width, group_text, reduce_pieces[2]
+        )
     else:
         output_part, query_part, cross_part, pairs_part = (
             after(part, qkv) for part in unpack(mid_gathered, mid_widths)
@@ -1501,12 +1650,13 @@
     pairs_full = pieces_cp(pairs_part)
     output_full, query_full, cross_full = (pieces_cp(part) for part in mid_parts)
     qkv = to_heads(qkv)
-    out_self, totals_self = self_forward(
+    out_self, totals_self, *sent = self_forward(
         qkv,
         first_cells,
         last_cells,
         turned,
         tuple(reduce_pieces) if plain else (),
+        int(plain),
     )
 
     def to_tokens(value):
@@ -1534,7 +1684,16 @@
         value = value.reshape(packs, HEADS, HEAD, rows)
         return jnp.transpose(value, (1, 2, 0, 3)).reshape(D, held)
 
-    attended = to_tokens(out_self.astype(bf16))
+    if plain:
+        attended = lax.all_to_all(
+            sent[0].reshape(cp_count * sp_count, pairs_dev, HEAD, rows),
+            HEAD_ORDER,
+            split_axis=0,
+            concat_axis=0,
+            tiled=True,
+        ).reshape(D, held)
+    else:
+        attended = to_tokens(out_self.astype(bf16))
     paired = times_rows(pairs_full, chosen.reshape(packs * TEXT_PAD, DT), 1)
     paired = jnp.moveaxis(paired.reshape(2, HEADS, HEAD, packs, TEXT_PAD), 3, 0)
     text_raw = paired[:, 0].reshape(packs * HEADS, HEAD, TEXT_PAD)
@@ -1563,10 +1722,11 @@
             mid_weights,
         )
         ffn_pieces = pieces_cp(normed_ffn_t)
-        hidden, expand_in, *parts = feed_forward(
-            ffn_pieces, reduce_pieces, ff_gathered
-        )
-        ffn_part, block_part = parts[:cp_count], parts[cp_count:]
+        (lefts,) = gate((lefts,), (ffn_pieces[2],))
+        lefts_other = trade_bit(lefts, "cp", 2)
+        hidden, expand_in, *ffn_part = feed_forward(
+            ffn_pieces, reduce_pieces, ff_gathered, ()
+        )
     else:
         mid_stream = base_stream + times(attended, output_full, 0)
         normed_cross = norm_gain(mid_stream, gain_rows[2]).astype(bf16)
@@ -1594,19 +1754,22 @@
         ffn_part = dot(expand_in, expand_part, 1, 1).astype(bf16)
         ffn_part = by_piece(ffn_part)
         block_part = by_piece(dot(hidden, reduce_part, 1, 1))
-    ff_out = expand_grads(ffn_pieces, expand_in)
+    ff_out = expand_grads(ffn_pieces, expand_in, (lefts_other,) if plain else ())
     if plain:
         keep, send = reduce_grads(reduce_pieces, hidden, group_order)
+        first_half = trade_bit(send, *group_steps()[0][:2])
         ff_grads = sum_group(ff_out)
     else:
         reduce_out = dot(reduce_in, hidden, 1, 0).astype(bf16)
         ff_grads = sum_group(jnp.concatenate([ff_out, reduce_out], axis=1))
         ff_grads, reduce_sums = ff_grads[:, :ff_width], ff_grads[:, ff_width:]
     ffn_grad = scatter_cp(ffn_part)
+    texts = jnp.transpose(chosen.reshape(packs * TEXT_PAD, DT))
     if plain:
-        lefts = pieces_cp(after(lefts, ffn_grad))
-    texts = after(chosen, ffn_grad).reshape(packs * TEXT_PAD, DT)
-    texts = pieces_cp(jnp.transpose(texts))
+        attended, texts = gate((attended, texts), (ff_out,))
+        attended_all = pieces_cp(attended)
+        lefts = [lefts, trade_bit(lefts, "cp", 1), lefts_other, trade_bit(lefts_other, "cp", 1)]
+    texts = pieces_cp(texts)
     if plain:
         (
             late_round,
@@ -1633,9 +1796,8 @@
                 cross_raw,
             ),
             mid_weights,
-            (ff_out, keep, send),
-        )
-        gain_cross, gain_ffn = gain_pair[:, 0], gain_pair[:, 1]
+            (ff_out,),
+        )
         cout_in, cross_raw_grad, self_in = (
             reorder_cp(row_blocks(member)) for member in (late_round, cross_raw_grad, mid_round)
         )
@@ -1664,14 +1826,24 @@
         cout_in = [jnp.transpose(member) for member in cout_in]
         self_in = [jnp.transpose(member) for member in self_in]
     if not plain:
-        lefts = pieces_cp(jnp.stack([normed_cross_t, crossed, attended]))
+        lefts = pieces_cp(jnp.stack([normed_cross_t, crossed]))
+        attended_all = pieces_cp(attended)
     rights = exchange_cp(
         [
             jnp.stack([cross, late, mid])
             for cross, late, mid in zip(cross_raw_grad, cout_in, self_in)
         ]
     )
-    attended_grad = by_heads(attended_grad)
+    if plain:
+        attended_grad = lax.all_to_all(
+            attended_grad.reshape(cp_count * sp_count, pairs_dev, HEAD, rows),
+            HEAD_ORDER,
+            split_axis=0,
+            concat_axis=0,
+            tiled=True,
+        ).reshape(cp_count, sp_count, pairs_dev, HEAD, rows)
+    else:
+        attended_grad = by_heads(attended_grad)
     qkv_grad = self_backward(
         qkv,
         attended_grad,
@@ -1681,11 +1853,12 @@
         last_cells,
         valid_cells,
         turned,
-        (*lefts, *texts) if plain else (),
+        (first_half, *rights[1:]) if plain else (),
     )
     stamp = qkv_grad
     qkv_grad = from_heads(qkv_grad)
     if plain:
+        block_part = reduce_parts(hidden, ff_gathered, stamp, cp_count)
         block_out = jnp.transpose((late_t + scatter_cp(block_part)).astype(bf16))
     else:
         block_out = (late_stream + scatter_cp(block_part)).astype(bf16)
@@ -1703,9 +1876,12 @@
     paired_rows = reorder_cp(row_blocks(paired_rows))
     pairs = exchange_cp(paired_rows)
     if plain:
-        mid_out = mid_grads_bucket(lefts, rights, texts, pairs, stamp, dp_count * sp_count)
+        mid_out = mid_grads_bucket(
+            lefts, attended_all, rights, texts, pairs, stamp, dp_count * sp_count
+        )
     else:
         lefts = jnp.concatenate(lefts, axis=2)
+        lefts = [lefts[0], lefts[1], jnp.concatenate(attended_all, axis=1)]
         rights = jnp.concatenate(rights, axis=2)
         pairs_grad = dot(
             jnp.concatenate(texts, axis=1), jnp.concatenate(pairs, axis=1), 1, 1
@@ -1718,13 +1894,19 @@
             [dot(lefts[k], rights[k], 1, 1).astype(bf16) for k in range(3)] + [pairs_grad]
         )
     mid_grads = sum_group(mid_out)
-    null_sum = jnp.einsum(
-        "p,pnt->nt", own_null.astype(f32), paired_grad.astype(f32), precision=highest
-    ).astype(bf16)
-    caption_grad = sum(
-        dot(part, block, 1, 0)
-        for part, block in zip(pairs_full, reorder_cp(row_blocks(null_sum)))
-    )
+    if plain:
+        near_null = jnp.take_along_axis(null_mask, near, axis=1)[0]
+        near_null = near_null[jnp.arange(cp_count) ^ cp_index].astype(bf16)
+        null_sum = sum(pairs[k].astype(f32) * near_null[k].astype(f32) for k in range(cp_count))
+        caption_grad = dot(pairs_part, null_sum.astype(bf16), 1, 0)
+    else:
+        null_sum = jnp.einsum(
+            "p,pnt->nt", own_null.astype(f32), paired_grad.astype(f32), precision=highest
+        ).astype(bf16)
+        caption_grad = sum(
+            dot(part, block, 1, 0)
+            for part, block in zip(pairs_full, reorder_cp(row_blocks(null_sum)))
+        )
     caption_sum = caption_grad
 
     qkv_grad = after(qkv_grad, ff_grads)
@@ -1750,11 +1932,15 @@
             mid_grad,
             scatter_cp([normed_part[k] for k in range(cp_count)]),
         )
-        gain_skip, gain_self = sums[:, 0], sums[:, 1]
         shift_grads = sums[:, 2][None]
         came = trade_cp(mixed_grad)
         mixed_pieces = reorder_cp([came[k] for k in range(cp_count)])
-        head_out = skip_grads_bucket(mixed_pieces, joined_all, self_input_grad)
+        head_out = skip_grads_bucket(
+            mixed_pieces,
+            joined_all,
+            self_input_grad,
+            jnp.concatenate([sums[:, :2], gain_pair], axis=1),
+        )
         joined_part = [dot(piece, skip_part, 0, 1).astype(bf16) for piece in mixed_pieces]
     else:
         normed_self_grad = scatter_cp(by_piece(normed_part))
@@ -1780,7 +1966,7 @@
     head_grads = sum_group(head_out)
     if plain:
         reduce_sums = scatter_group_halves(
-            keep, send, (stamp, normed_part[0], head_out)
+            keep, send, first_half, (stamp, normed_part[0], head_out)
         )
     caption_grad = scatter_every(
         after(caption_sum, head_out).astype(bf16).reshape(-1, caption_rows, TEXT_PAD)
@@ -1788,11 +1974,12 @@
     joined_grad = scatter_cp(joined_part)
 
     shift_grads = after(shift_grads, head_out)
-    gains_part = after(jnp.stack([gain_skip, gain_self, gain_cross, gain_ffn]), head_out)
-    gains_grad = scatter_every(jnp.swapaxes(gains_part.reshape(4, -1, gain_columns), 0, 1))
+    if not plain:
+        gains_part = jnp.stack([gain_skip, gain_self, gain_cross, gain_ffn])
+        gains_grad = scatter_every(jnp.swapaxes(gains_part.reshape(4, -1, gain_columns), 0, 1))
     shift_weight_grad = lax.dot_general(
         silu_blocks,
-        gather_every(shift_grads).reshape(-1, D),
+        send_every(shift_grads).reshape(-1, D),
         (((0,), (0,)), ((), ())),
         precision=highest,
         preferred_element_type=f32,
@@ -1822,13 +2009,15 @@
         mid_grads[:group_text, 3 * (width + -width % 128) :], (2 * width,)
     )
     if plain:
-        skip_out, input_out = finish_head(
+        skip_out, input_out, gains_grad = finish_head(
             trade_cp(head_grads.reshape(cp_count, shard, -1)), factor
         )
+        gains_grad = jnp.transpose(gains_grad)
     else:
         one, two, input_out = join_columns(head_grads, head_widths)
         skip_out = jnp.concatenate([whole(one), whole(two)], axis=0)
         input_out = restore_heads(whole(input_out))
+        gains_grad = gains_grad * factor
 
     token_shape = (packs, rows, D)
     return (
@@ -1845,7 +2034,7 @@
         whole(expand_out),
         jnp.transpose(whole(reduce_out)),
         jnp.transpose(caption_grad)[:TEXT].astype(f32) * factor,
-        gains_grad * factor,
+        gains_grad,
     )
 
 

time: 940 us -> 904 us (0.962)
  other arithmetic: 98.4 us -> 79.6 us
  waiting for transfers between devices: 354 us -> 336 us
  starting transfers between devices: 111 us -> 125 us
    all_to_all x1, waiting for transfers between devices: 34.2 us -> 0.01 us  [to_heads(): return lax.all_to_all(value, 'sp', split_axis=0, concat_axis=0, tiled=True)]
    all_to_all x2 -> x3, waiting for transfers between devices: 23.7 us -> 0.01 us  [the longest x1 0.01 us: shards(): lax.all_to_all(sent[0].reshape(cp_count * sp_count, pairs_dev, HEAD, rows...]
    reduce_scatter x3, waiting for transfers between devices: 0.01 us -> 22.7 us  [sum_group(): return lax.psum_scatter(bucket, GROUP, scatter_dimension=0, tiled=True)]
    ppermute x71 -> x64, waiting for transfers between devices: 198 us -> 181 us  [trade_bit(): return lax.ppermute(value, axis, [(k, k ^ bit) for k in range(count)])]
    unnamed x227, local copies, waits for them, and re-layouts: 42.7 us -> 57.6 us
    all_gather x3, waiting for transfers between devices: 7.98 us -> 22.3 us  [gather_group(): return lax.all_gather(bucket, GROUP, axis=0, tiled=True)]
    all_to_all x2 -> x3, starting transfers between devices: 8.55 us -> 22.5 us  [the longest x1 11.8 us: send_every(): return lax.all_to_all(value, EVERY, split_axis=0, concat_axis=0, tiled=True)]
    dynamic_slice x1 -> x0, local copies, waits for them, and re-layouts: 10.9 us -> none  [shards(): lax.dynamic_index_in_dim(captions[p], local[p, k], 0, keepdims=False)]
  transfers between devices with their start and end apart: 116 -> 110, of which waited for: 42 -> 41; matrix products, arithmetic and copies ran while one was open for 23% -> 19% of each run, Pallas kernels for 16% -> 20%
where the time goes in v3:
time: 904 us; the launch traced here: 898 us
  waiting for transfers between devices  336 us (37%)
  Pallas kernels  178 us (20%)
  starting transfers between devices  125 us (14%)
  local copies, waits for them, and re-layouts  106 us (12%)
  other arithmetic  79.6 us (9%)
  matrix products  42.1 us (5%)
  between operations  31.5 us (3%)
    ppermute x64, waiting for transfers between devices, trade_bit(): return lax.ppermute(value, axis, [(k, k ^ bit) for k in range(count)])  181 us
    ppermute x30, waiting for transfers between devices, exchange_cp(): lax.ppermute(pieces[key], 'cp', [(k, k ^ key) for k in range(count)])  77.3 us
    unnamed x227, local copies, waits for them, and re-layouts  57.6 us
    ppermute x64, starting transfers between devices, trade_bit(): return lax.ppermute(value, axis, [(k, k ^ bit) for k in range(count)])  50.6 us
    dot_general x12, matrix products, dot(): lax.dot_general(left, right, (((left_dim,), (right_dim,)), ((), ())), pre...  40.2 us
    all_to_all x5, waiting for transfers between devices, trade_cp(): return lax.all_to_all(blocks, 'cp', split_axis=0, concat_axis=0, tiled=True)  32.5 us
    pallas_call x1, Pallas kernels, feed_forward(): pl.pallas_call(functools.partial(ffn_kernel, count, len(stamps)), out_sha...  29.5 us
    reduce_scatter x3, waiting for transfers between devices, sum_group(): return lax.psum_scatter(bucket, GROUP, scatter_dimension=0, tiled=True)  22.7 us
  transfers between devices with their start and end apart: 110, of which 41 were waited for; matrix products, arithmetic and copies ran while one was open for 19% of the time, Pallas kernels for 20%

profile of v3, /device:TPU:0, one launch (start us, length us, event | category | flops | bytes accessed | tf_op | source)
XLA Modules:
  0.0 897.8 jit_solution(1363478182708923455)
XLA Ops:
  23.1 7.8 all-to-all-done.1
  60.0 5.1 collective-permute-done.4
  66.6 4.8 collective-permute-done.5
  75.5 30.0 %collective-permute-done.10 = f32[1,8,1,1408]{3,2,1,0:T(1,128)} collective-permute-done((f32[1,8,1,1408]{3,2,1,0:T(1,128)S(1)}, f32[1,8,1,1408]{3,2,1,0:T(1,128)}, u32[]{:S(2)}, u32[]{:S(2)}) %collective-permute-start.10) | collective-permute-done | bytes 45088 | tf_op jit(solution)/shard_map/ppermute | solution.py:121
  115.9 4.8 collective-permute-done.6
  127.8 5.7 mix.1
  136.6 4.4 all-to-all-start.2
  143.3 8.7 all-to-all-done.2
  158.8 17.1 %collective-permute-done.15.refs_2_ = bf16[1408,256]{1,0:T(8,128)(2,1)} collective-permute-done((bf16[1408,256]{1,0:T(8,128)(2,1)}, bf16[1408,256]{1,0:T(8,128)(2,1)}, u32[]{:S(2)}, u32[]{:S(2)}) %collective-permute-start.15) | collective-permute-done | bytes 720928 | tf_op jit(solution)/shard_map/ppermute | solution.py:121
  178.5 10.2 %project.1 = (bf16[4,3,88,1024]{3,2,1,0:T(8,128)(2,1)}, f32[4,2,88,1024]{3,2,1,0:T(8,128)}) custom-call(bf16[1408,256]{1,0:T(8,128)(2,1)} %get-tuple-element.64.refs_0_, bf16[1408,256]{1,0:T(8,128)(2,1)} %collective-permute-done.14.refs_1_, bf16[1408,256]{1,0:T(8,128)(2,1)} %collective-permute-done.15.refs_2_, ...), custom_call_target="tpu_custom_call" | custom-call | flops 3045064704 | bytes 12582912 | tf_op jit(solution)/shard_map/project/pallas_call | solution.py:1326
  188.7 4.7 all-to-all-start.3
  197.0 4.2 copy.182.captions_ref
  209.6 22.3 %all-gather.6.cloned.1.call-done.bucket_ref = bf16[1408,1920]{1,0:T(8,128)(2,1)} async-done(((bf16[176,1920]{1,0:T(8,128)(2,1)}), bf16[1408,1920]{1,0:T(8,128)(2,1)}) %all-gather.6.cloned.1.call-update) | async-done | bytes 5406736 | tf_op jit(solution)/shard_map/all_gather | solution.py:1426
  231.8 4.3 unpack_mid.1
  261.1 18.6 %collective-permute-done.26 = bf16[1024,704]{0,1:T(8,128)(2,1)} collective-permute-done((bf16[1024,704]{0,1:T(8,128)(2,1)}, bf16[1024,704]{0,1:T(8,128)(2,1)}, u32[]{:S(2)}, u32[]{:S(2)}) %collective-permute-start.26) | collective-permute-done | bytes 1441824 | tf_op jit(solution)/shard_map/ppermute | solution.py:121
  288.9 11.1 %self_forward.1 = (f32[4,1,88,1024]{3,2,1,0:T(8,128)S(1)}, f32[4,1,1,1024]{3,2,1,0:T(1,128)S(1)}, bf16[4,4,1,88,256]{4,3,2,1,0:T(8,128)(2,1)S(1)}) custom-call(s32[1,16]{1,0:T(1,128)S(1)} %get-tuple-element.396.first_ref, s32[1,16]{1,0:T(1,128)S(1)} %get-tuple-element.397.last_ref, s32[1]{0:T(128)} %bitcast.7.turned_ref, ...), custom_call_target="tpu_custom_call" | custom-call | flops 10000000000 | bytes 8388608 | tf_op jit(solution)/shard_map/self_forward/pallas_call | solution.py:420
  302.0 4.9 all-to-all-start.4
  315.8 18.8 %collective-permute-done.36.refs_12_.refs_18_ = bf16[352,1408]{1,0:T(8,128)(2,1)} collective-permute-done((bf16[352,1408]{1,0:T(8,128)(2,1)}, bf16[352,1408]{1,0:T(8,128)(2,1)}, u32[]{:S(2)}, u32[]{:S(2)}) %collective-permute-start.36) | collective-permute-done | bytes 991264 | tf_op jit(solution)/shard_map/ppermute | solution.py:121
  334.7 23.2 %collective-permute-done.39.refs_16_.refs_22_ = bf16[352,1408]{1,0:T(8,128)(2,1)S(1)} collective-permute-done((bf16[352,1408]{1,0:T(8,128)(2,1)}, bf16[352,1408]{1,0:T(8,128)(2,1)S(1)}, u32[]{:S(2)}, u32[]{:S(2)}) %collective-permute-start.39) | collective-permute-done | bytes 991264 | tf_op jit(solution)/shard_map/ppermute | solution.py:121
  363.4 20.0 %middle_forward.1 = (f32[1408,256]{1,0:T(8,128)}, f32[1408,256]{1,0:T(8,128)}, bf16[2,1408,256]{2,1,0:T(8,128)(2,1)}, f32[16,88,256]{2,1,0:T(8,128)}, bf16[16,88...) custom-call(s32[1]{0:T(128)} %bitcast.refs_0_, ...), custom_call_target="tpu_custom_call" | custom-call | flops 5075107840 | bytes 25165824 | tf_op jit(solution)/shard_map/middle_forward/pallas_call | solution.py:1029
  385.1 18.1 %collective-permute-done.42.refs_2_.refs_1_ = bf16[1408,256]{1,0:T(8,128)(2,1)} collective-permute-done((bf16[1408,256]{1,0:T(8,128)(2,1)}, bf16[1408,256]{1,0:T(8,128)(2,1)}, u32[]{:S(2)}, u32[]{:S(2)}) %collective-permute-start.42) | collective-permute-done | bytes 720928 | tf_op jit(solution)/shard_map/ppermute | solution.py:121
  405.7 29.5 %feed_forward.1 = (bf16[1024,1536]{1,0:T(8,128)(2,1)}, bf16[1024,1536]{1,0:T(8,128)(2,1)}, bf16[1408,256]{1,0:T(8,128)(2,1)S(1)}, bf16[1408,256]{1,0:T(8,128)(2,...) custom-call(bf16[1408,256]{1,0:T(8,128)(2,1)} %get-tuple-element.77.refs_0_, ...), custom_call_target="tpu_custom_call" | custom-call | flops 13287555072 | bytes 25165824 | tf_op jit(solution)/shard_map/feed_forward/pallas_call | solution.py:1228
  441.0 8.7 expand_grads.1.refs_24_.refs_2_
  449.7 11.1 %reduce_grads.1 = (bf16[704,1536]{1,0:T(8,128)(2,1)S(1)}, bf16[704,1536]{1,0:T(8,128)(2,1)}) custom-call(s32[8]{0:T(128)S(1)} %broadcast_xor_fusion.group_ref, bf16[1408,256]{1,0:T(8,128)(2,1)} %turn_over.1.refs_0_.refs_4_.refs_2_, bf16[1408,256]{1,0:T(8,128)(2,1)} %collective-permute-done.17.refs_1_.refs_5_, ...), custom_call_target="tpu_custom_call" | custom-call | flops 4429185024 | bytes 12582912 | tf_op jit(solution)/shard_map/reduce_grads/pallas_call | solution.py:687
  465.8 22.2 %middle_backward.1 = (bf16[1408,256]{1,0:T(8,128)(2,1)S(1)}, bf16[1408,256]{1,0:T(8,128)(2,1)S(1)}, f32[1408,256]{1,0:T(8,128)}, bf16[1408,256]{1,0:T(8,128)(2,1...) custom-call(s32[1]{0:T(128)} %bitcast.refs_0_, ...), custom_call_target="tpu_custom_call" | custom-call | flops 7105150976 | bytes 31457280 | tf_op jit(solution)/shard_map/middle_backward/pallas_call | solution.py:1141
  492.3 5.9 all-to-all-start.5
  510.9 10.0 %collective-permute-done.53.refs_2_.refs_10_ = bf16[3,352,256]{2,1,0:T(8,128)(2,1)S(1)} collective-permute-done((bf16[3,352,256]{2,1,0:T(8,128)(2,1)S(1)}, bf16[3,352,256]{2,1,0:T(8,128)(2,1)S(1)}, u32[]{:S(2)}, u32[]{:S(2)}) %collective-permute-start.53) | collective-permute-done | bytes 540704 | tf_op jit(solution)/shard_map/ppermute | solution.py:177
  522.8 9.0 %collective-permute-done.54.refs_3_.refs_11_ = bf16[3,352,256]{2,1,0:T(8,128)(2,1)S(1)} collective-permute-done((bf16[3,352,256]{2,1,0:T(8,128)(2,1)S(1)}, bf16[3,352,256]{2,1,0:T(8,128)(2,1)S(1)}, u32[]{:S(2)}, u32[]{:S(2)}) %collective-permute-start.54) | collective-permute-done | bytes 540704 | tf_op jit(solution)/shard_map/ppermute | solution.py:177
  538.7 14.6 %self_backward.1.stamp_ref.refs_20_ = bf16[4,1,3,88,1024]{4,3,2,1,0:T(8,128)(2,1)S(1)} custom-call(s32[1,16]{1,0:T(1,128)S(1)} %get-tuple-element.396.first_ref, s32[1,16]{1,0:T(1,128)S(1)} %get-tuple-element.397.last_ref, s32[1]{0:T(128)S(6)} %select_n.1619.valid_ref, s32[1]{0:T(128)} %bitcast.7.turned_ref, ...), custom_call_target="tpu_custom_call" | custom-call | flops 17999998976 | bytes 16777216 | tf_op jit(solution)/shard_map/self_backward/pallas_call | solution.py:442
  554.7 5.0 all-to-all-start.6
  579.8 6.6 collective-permute-done.73.refs_18_
  586.3 9.7 %collective-permute-done.74.refs_19_ = bf16[704,384]{1,0:T(8,128)(2,1)S(1)} collective-permute-done((bf16[704,384]{1,0:T(8,128)(2,1)}, bf16[704,384]{1,0:T(8,128)(2,1)S(1)}, u32[]{:S(2)}, u32[]{:S(2)}) %collective-permute-start.74) | collective-permute-done | bytes 540704 | tf_op jit(solution)/shard_map/ppermute | solution.py:177
  597.8 12.7 %mid_grads.1 = bf16[1408,1920]{1,0:T(8,128)(2,1)} custom-call(bf16[2,1408,256]{2,1,0:T(8,128)(2,1)} %gate.2.refs_0_, bf16[2,1408,256]{2,1,0:T(8,128)(2,1)} %collective-permute-done.64.refs_1_, bf16[2,1408,256]{2,1,0:T(8,128)(2,1)} %collective-permute-done.50.refs_5_.refs_2_, bf16[2,1408,256]{2,1,0:T(8,128)(2,1)} %collective-permute-done.65.refs_3_, ...), custom_call_target="tpu_custom_call" | custom-call | flops 6978273280 | bytes 25165824 | tf_op jit(solution)/shard_map/mid_grads/pallas_call | solution.py:742
  614.9 8.7 reduce_parts.1
  638.2 4.5 convolution_convert_fusion.5
  655.1 10.2 %collective-permute-done.57 = bf16[1408,256]{1,0:T(8,128)(2,1)S(1)} collective-permute-done((bf16[1408,256]{1,0:T(8,128)(2,1)S(1)}, bf16[1408,256]{1,0:T(8,128)(2,1)S(1)}, u32[]{:S(2)}, u32[]{:S(2)}) %collective-permute-start.57) | collective-permute-done | bytes 720928 | tf_op jit(solution)/shard_map/ppermute | solution.py:121
  671.0 7.7 convolution_convert_fusion
  678.7 5.4 copy.192.refs_8_
  687.8 4.3 start_backward.1
  710.5 6.6 skip_grads.1
  728.7 11.8 %all-to-all-start.9 = ((f32[32,1,1408]{2,1,0:T(1,128)}), f32[32,1,1408]{2,1,0:T(1,128)S(1)}, u32[]{:S(2)}, u32[]{:S(2)}) async-start(f32[32,1,1408]{2,1,0:T(1,128)} %broadcast_in_dim.175), calls=%async_computation.11 | async-start | bytes 360448 | tf_op jit(solution)/shard_map/all_to_all | solution.py:252
  763.6 4.2 collective-permute-done.90
  767.9 8.3 collective-permute-start.91
  776.3 5.3 collective-permute-done.91
  804.9 27.9 %collective-permute-done.78 = bf16[32,768]{1,0:T(8,128)(2,1)S(1)} collective-permute-done((bf16[32,768]{1,0:T(8,128)(2,1)S(1)}, bf16[32,768]{1,0:T(8,128)(2,1)S(1)}, u32[]{:S(2)}, u32[]{:S(2)}) %collective-permute-start.78) | collective-permute-done | bytes 49184 | tf_op jit(solution)/shard_map/ppermute | solution.py:177
  844.3 5.1 convert_add_fusion
  849.4 22.7 %reduce-scatter.6.cloned.1.call-done = bf16[176,1920]{1,0:T(8,128)(2,1)} async-done(((bf16[1408,1920]{1,0:T(8,128)(2,1)}), bf16[176,1920]{1,0:T(8,128)(2,1)}) %reduce-scatter.6.cloned.1.call-update) | async-done | bytes 675856 | tf_op jit(solution)/shard_map/reduce_scatter | solution.py:1748
  880.8 8.0 all-to-all-done.8.blocks_ref
  (660 shorter events, 332.0 us)
Async XLA Ops:
  23.0 103.1 %all-gather.4.cloned.1.call-start = ((), (), s32[]{:S(2)}) async-start(), calls=%async_computation.13 | async-start | bytes 6082560 | tf_op jit(solution)/shard_map/all_gather | solution.py:1426
  32.0 199.8 %all-gather.6.cloned.1.call-start = ((), (), s32[]{:S(2)}) async-start(), calls=%async_computation.14 | async-start | bytes 6082560 | tf_op jit(solution)/shard_map/all_gather | solution.py:1426
  47.5 356.2 %all-gather.8.cloned.1.call-start = ((), (), s32[]{:S(2)}) async-start(), calls=%async_computation.15 | async-start | bytes 9732096 | tf_op jit(solution)/shard_map/all_gather | solution.py:1426
  48.2 77.9 %collective-permute-start = (bf16[256,2816]{1,0:T(8,128)(2,1)S(1)}, bf16[256,2816]{1,0:T(8,128)(2,1)S(1)}, u32[]{:S(2)}, u32[]{:S(2)}) collective-permute-start(bf16[256,2816]{1,0:T(8,128)(2,1)S(1)} %maximum_add_fusion.1.refs_2_.refs_0_), channel_id=1, source_target_pairs={{0,1},{1,0},{2,3},{3,2},{4,5},{5,4},{6,7},{7,6},{8,9},{9,8},{10,11... | collective-permute-start | bytes 4325384 | tf_op jit(solution)/shard_map/ppermute | solution.py:121
  71.4 38.9 %collective-permute-start.1 = (bf16[256,2816]{1,0:T(8,128)(2,1)S(1)}, bf16[256,2816]{1,0:T(8,128)(2,1)}, u32[]{:S(2)}, u32[]{:S(2)}) collective-permute-start(bf16[256,2816]{1,0:T(8,128)(2,1)S(1)} %maximum_add_fusion.1.refs_2_.refs_0_), channel_id=1, source_target_pairs={{0,2},{1,3},{2,0},{3,1},{4,6},{5,7},{6,4},{7,5},{8,10},{9,11},{10,... | collective-permute-start | bytes 4325384 | tf_op jit(solution)/shard_map/ppermute | solution.py:121
  73.2 32.3 %collective-permute-start.10 = (f32[1,8,1,1408]{3,2,1,0:T(1,128)S(1)}, f32[1,8,1,1408]{3,2,1,0:T(1,128)}, u32[]{:S(2)}, u32[]{:S(2)}) collective-permute-start(f32[1,8,1,1408]{3,2,1,0:T(1,128)S(1)} %fusion.67), channel_id=1, source_target_pairs={{0,2},{1,3},{2,0},{3,1},{4,6},{5,7},{6,4},{7,5},{8,10},{9,11},{10,... | collective-permute-start | bytes 135176 | tf_op jit(solution)/shard_map/ppermute | solution.py:121
  188.7 100.2 %all-to-all-start.3 = ((bf16[4,1,3,88,1024]{4,3,2,1,0:T(8,128)(2,1)}), bf16[4,1,3,88,1024]{4,3,2,1,0:T(8,128)(2,1)}, u32[]{:S(2)}, u32[]{:S(2)}) async-start(bf16[4,1,3,88,1024]{4,3,2,1,0:T(8,128)(2,1)} %bitcast.52), calls=%async_computation.3 | async-start | bytes 4325376 | tf_op jit(solution)/shard_map/all_to_all | solution.py:1632
  196.4 35.4 %collective-permute-start.18 = (bf16[1408,256]{1,0:T(8,128)(2,1)}, bf16[1408,256]{1,0:T(8,128)(2,1)}, u32[]{:S(2)}, u32[]{:S(2)}) collective-permute-start(bf16[1408,256]{1,0:T(8,128)(2,1)} %turn_over.1.refs_0_.refs_4_.refs_2_), channel_id=1, source_target_pairs={{0,2},{1,3},{2,0},{3,1},{4,6},{5,7},{6,4},{7,5},{8,10},{9,11},{10,... | collective-permute-start | bytes 2162696 | tf_op jit(solution)/shard_map/ppermute | solution.py:121
  207.2 41.3 %collective-permute-start.29 = (bf16[384,1024]{1,0:T(8,128)(2,1)}, bf16[384,1024]{1,0:T(8,128)(2,1)}, u32[]{:S(2)}, u32[]{:S(2)}) collective-permute-start(bf16[384,1024]{1,0:T(8,128)(2,1)} %get-tuple-element.70), channel_id=1, source_target_pairs={{0,2},{1,3},{2,0},{3,1},{4,6},{5,7},{6,4},{7,5},{8,10},{9,11},{10,... | collective-permute-start | bytes 2359304 | tf_op jit(solution)/shard_map/ppermute | solution.py:177
  208.9 40.1 %collective-permute-start.28 = (bf16[384,1024]{1,0:T(8,128)(2,1)}, bf16[384,1024]{1,0:T(8,128)(2,1)}, u32[]{:S(2)}, u32[]{:S(2)}) collective-permute-start(bf16[384,1024]{1,0:T(8,128)(2,1)} %get-tuple-element.69), channel_id=1, source_target_pairs={{0,3},{1,2},{2,1},{3,0},{4,7},{5,6},{6,5},{7,4},{8,11},{9,10},{10,... | collective-permute-start | bytes 2359304 | tf_op jit(solution)/shard_map/ppermute | solution.py:177
  208.9 40.6 %collective-permute-start.30 = (bf16[384,1024]{1,0:T(8,128)(2,1)}, bf16[384,1024]{1,0:T(8,128)(2,1)}, u32[]{:S(2)}, u32[]{:S(2)}) collective-permute-start(bf16[384,1024]{1,0:T(8,128)(2,1)} %get-tuple-element.71), channel_id=1, source_target_pairs={{0,1},{1,0},{2,3},{3,2},{4,5},{5,4},{6,7},{7,6},{8,9},{9,8},{10,11... | collective-permute-start | bytes 2359304 | tf_op jit(solution)/shard_map/ppermute | solution.py:177
  241.0 38.6 %collective-permute-start.26 = (bf16[1024,704]{0,1:T(8,128)(2,1)}, bf16[1024,704]{0,1:T(8,128)(2,1)}, u32[]{:S(2)}, u32[]{:S(2)}) collective-permute-start(bf16[1024,704]{0,1:T(8,128)(2,1)} %copy.181), channel_id=1, source_target_pairs={{0,2},{1,3},{2,0},{3,1},{4,6},{5,7},{6,4},{7,5},{8,10},{9,11},{10,... | collective-permute-start | bytes 4325384 | tf_op jit(solution)/shard_map/ppermute | solution.py:121
  242.0 41.1 %collective-permute-start.31 = (bf16[1024,704]{0,1:T(8,128)(2,1)}, bf16[1024,704]{0,1:T(8,128)(2,1)}, u32[]{:S(2)}, u32[]{:S(2)}) collective-permute-start(bf16[1024,704]{0,1:T(8,128)(2,1)} %copy.181), channel_id=1, source_target_pairs={{0,1},{1,0},{2,3},{3,2},{4,5},{5,4},{6,7},{7,6},{8,9},{9,8},{10,11... | collective-permute-start | bytes 4325384 | tf_op jit(solution)/shard_map/ppermute | solution.py:121
  248.5 38.6 %collective-permute-start.17 = (bf16[1408,256]{1,0:T(8,128)(2,1)}, bf16[1408,256]{1,0:T(8,128)(2,1)}, u32[]{:S(2)}, u32[]{:S(2)}) collective-permute-start(bf16[1408,256]{1,0:T(8,128)(2,1)} %turn_over.1.refs_0_.refs_4_.refs_2_), channel_id=1, source_target_pairs={{0,1},{1,0},{2,3},{3,2},{4,5},{5,4},{6,7},{7,6},{8,9},{9,8},{10,11... | collective-permute-start | bytes 2162696 | tf_op jit(solution)/shard_map/ppermute | solution.py:121
  249.1 64.5 %collective-permute-start.32 = (bf16[352,1408]{1,0:T(8,128)(2,1)}, bf16[352,1408]{1,0:T(8,128)(2,1)}, u32[]{:S(2)}, u32[]{:S(2)}) collective-permute-start(bf16[352,1408]{1,0:T(8,128)(2,1)} %get-tuple-element.73.refs_6_.refs_12_), channel_id=1, source_target_pairs={{0,1},{1,0},{2,3},{3,2},{4,5},{5,4},{6,7},{7,6},{8,9},{9,8},{10,11... | collective-permute-start | bytes 2973704 | tf_op jit(solution)/shard_map/ppermute | solution.py:121
  249.5 37.9 %collective-permute-start.19 = (bf16[1408,256]{1,0:T(8,128)(2,1)}, bf16[1408,256]{1,0:T(8,128)(2,1)}, u32[]{:S(2)}, u32[]{:S(2)}) collective-permute-start(bf16[1408,256]{1,0:T(8,128)(2,1)} %collective-permute-done.18.refs_2_.stamp_ref.refs_6_), channel_id=1, source_target_pairs={{0,1},{1,0},{2,3},{3,2},{4,5},{5,4},{6,7},{7,6},{8,9},{9,8},{10,11... | collective-permute-start | bytes 2162696 | tf_op jit(solution)/shard_map/ppermute | solution.py:121
  283.1 32.2 %collective-permute-start.33 = (bf16[352,1408]{1,0:T(8,128)(2,1)}, bf16[352,1408]{1,0:T(8,128)(2,1)}, u32[]{:S(2)}, u32[]{:S(2)}) collective-permute-start(bf16[352,1408]{1,0:T(8,128)(2,1)} %get-tuple-element.73.refs_6_.refs_12_), channel_id=1, source_target_pairs={{0,2},{1,3},{2,0},{3,1},{4,6},{5,7},{6,4},{7,5},{8,10},{9,11},{10,... | collective-permute-start | bytes 2973704 | tf_op jit(solution)/shard_map/ppermute | solution.py:121
  287.1 73.4 %collective-permute-start.35 = (bf16[352,1408]{1,0:T(8,128)(2,1)}, bf16[352,1408]{1,0:T(8,128)(2,1)}, u32[]{:S(2)}, u32[]{:S(2)}) collective-permute-start(bf16[352,1408]{1,0:T(8,128)(2,1)} %get-tuple-element.74.refs_10_.refs_16_), channel_id=1, source_target_pairs={{0,1},{1,0},{2,3},{3,2},{4,5},{5,4},{6,7},{7,6},{8,9},{9,8},{10,11... | collective-permute-start | bytes 2973704 | tf_op jit(solution)/shard_map/ppermute | solution.py:121
  287.4 47.3 %collective-permute-start.36 = (bf16[352,1408]{1,0:T(8,128)(2,1)}, bf16[352,1408]{1,0:T(8,128)(2,1)}, u32[]{:S(2)}, u32[]{:S(2)}) collective-permute-start(bf16[352,1408]{1,0:T(8,128)(2,1)} %get-tuple-element.74.refs_10_.refs_16_), channel_id=1, source_target_pairs={{0,2},{1,3},{2,0},{3,1},{4,6},{5,7},{6,4},{7,5},{8,10},{9,11},{10,... | collective-permute-start | bytes 2973704 | tf_op jit(solution)/shard_map/ppermute | solution.py:121
  302.0 61.4 %all-to-all-start.4 = ((bf16[16,1,88,256]{3,2,1,0:T(8,128)(2,1)}), bf16[16,1,88,256]{3,2,1,0:T(8,128)(2,1)}, u32[]{:S(2)}, u32[]{:S(2)}) async-start(bf16[16,1,88,256]{3,2,1,0:T(8,128)(2,1)} %bitcast.393), calls=%async_computation.4 | async-start | bytes 1441792 | tf_op jit(solution)/shard_map/all_to_all | solution.py:1688
  306.9 320.3 %reduce-scatter.4.cloned.1.call-start = ((), (), s32[]{:S(2)}) async-start(), calls=%async_computation.16 | async-start | bytes 4866048 | tf_op jit(solution)/shard_map/reduce_scatter | solution.py:1748
  307.5 50.4 %collective-permute-start.39 = (bf16[352,1408]{1,0:T(8,128)(2,1)}, bf16[352,1408]{1,0:T(8,128)(2,1)S(1)}, u32[]{:S(2)}, u32[]{:S(2)}) collective-permute-start(bf16[352,1408]{1,0:T(8,128)(2,1)} %copy-done.24), channel_id=1, source_target_pairs={{0,2},{1,3},{2,0},{3,1},{4,6},{5,7},{6,4},{7,5},{8,10},{9,11},{10,... | collective-permute-start | bytes 2973704 | tf_op jit(solution)/shard_map/ppermute | solution.py:121
  315.3 45.2 %collective-permute-start.38 = (bf16[352,1408]{1,0:T(8,128)(2,1)S(1)}, bf16[352,1408]{1,0:T(8,128)(2,1)S(1)}, u32[]{:S(2)}, u32[]{:S(2)}) collective-permute-start(bf16[352,1408]{1,0:T(8,128)(2,1)S(1)} %copy-done.25), channel_id=1, source_target_pairs={{0,1},{1,0},{2,3},{3,2},{4,5},{5,4},{6,7},{7,6},{8,9},{9,8},{10,11... | collective-permute-start | bytes 2973704 | tf_op jit(solution)/shard_map/ppermute | solution.py:121
  315.3 46.1 %collective-permute-start.34 = (bf16[352,1408]{1,0:T(8,128)(2,1)}, bf16[352,1408]{1,0:T(8,128)(2,1)S(1)}, u32[]{:S(2)}, u32[]{:S(2)}) collective-permute-start(bf16[352,1408]{1,0:T(8,128)(2,1)} %collective-permute-done.33.refs_8_.refs_14_), channel_id=1, source_target_pairs={{0,1},{1,0},{2,3},{3,2},{4,5},{5,4},{6,7},{7,6},{8,9},{9,8},{10,11... | collective-permute-start | bytes 2973704 | tf_op jit(solution)/shard_map/ppermute | solution.py:121
  403.1 37.9 %collective-permute-start.50 = (bf16[2,1408,256]{2,1,0:T(8,128)(2,1)}, bf16[2,1408,256]{2,1,0:T(8,128)(2,1)}, u32[]{:S(2)}, u32[]{:S(2)}) collective-permute-start(bf16[2,1408,256]{2,1,0:T(8,128)(2,1)} %gate.2.refs_0_), channel_id=1, source_target_pairs={{0,2},{1,3},{2,0},{3,1},{4,6},{5,7},{6,4},{7,5},{8,10},{9,11},{10,... | collective-permute-start | bytes 4325384 | tf_op jit(solution)/shard_map/ppermute | solution.py:121
  438.8 124.4 %collective-permute-start.64 = (bf16[2,1408,256]{2,1,0:T(8,128)(2,1)}, bf16[2,1408,256]{2,1,0:T(8,128)(2,1)}, u32[]{:S(2)}, u32[]{:S(2)}) collective-permute-start(bf16[2,1408,256]{2,1,0:T(8,128)(2,1)} %gate.2.refs_0_), channel_id=1, source_target_pairs={{0,1},{1,0},{2,3},{3,2},{4,5},{5,4},{6,7},{7,6},{8,9},{9,8},{10,11... | collective-permute-start | bytes 4325384 | tf_op jit(solution)/shard_map/ppermute | solution.py:121
  462.2 70.9 %collective-permute-start.51 = (bf16[704,1536]{1,0:T(8,128)(2,1)}, bf16[704,1536]{1,0:T(8,128)(2,1)}, u32[]{:S(2)}, u32[]{:S(2)}) collective-permute-start(bf16[704,1536]{1,0:T(8,128)(2,1)} %get-tuple-element.93), channel_id=1, source_target_pairs={{0,16},{16,0},{1,17},{17,1},{2,18},{18,2},{3,19},{19,3},{4,20},{20... | collective-permute-start | bytes 6488072 | tf_op jit(solution)/shard_map/ppermute | solution.py:121
  492.3 41.9 %all-to-all-start.5 = ((bf16[16,1,88,256]{3,2,1,0:T(8,128)(2,1)}), bf16[16,1,88,256]{3,2,1,0:T(8,128)(2,1)}, u32[]{:S(2)}, u32[]{:S(2)}) async-start(bf16[16,1,88,256]{3,2,1,0:T(8,128)(2,1)} %bitcast.392), calls=%async_computation.5 | async-start | bytes 1441792 | tf_op jit(solution)/shard_map/all_to_all | solution.py:1838
  510.5 53.4 %collective-permute-start.66 = (bf16[1408,256]{1,0:T(8,128)(2,1)}, bf16[1408,256]{1,0:T(8,128)(2,1)}, u32[]{:S(2)}, u32[]{:S(2)}) collective-permute-start(bf16[1408,256]{1,0:T(8,128)(2,1)} %get-tuple-element.108.refs_4_), channel_id=1, source_target_pairs={{0,1},{1,0},{2,3},{3,2},{4,5},{5,4},{6,7},{7,6},{8,9},{9,8},{10,11... | collective-permute-start | bytes 2162696 | tf_op jit(solution)/shard_map/ppermute | solution.py:121
  521.7 49.2 %collective-permute-start.67 = (bf16[1408,256]{1,0:T(8,128)(2,1)}, bf16[1408,256]{1,0:T(8,128)(2,1)}, u32[]{:S(2)}, u32[]{:S(2)}) collective-permute-start(bf16[1408,256]{1,0:T(8,128)(2,1)} %get-tuple-element.108.refs_4_), channel_id=1, source_target_pairs={{0,2},{1,3},{2,0},{3,1},{4,6},{5,7},{6,4},{7,5},{8,10},{9,11},{10,... | collective-permute-start | bytes 2162696 | tf_op jit(solution)/shard_map/ppermute | solution.py:121
  532.7 39.3 %collective-permute-start.69 = (bf16[1024,384]{1,0:T(8,128)(2,1)}, bf16[1024,384]{1,0:T(8,128)(2,1)}, u32[]{:S(2)}, u32[]{:S(2)}) collective-permute-start(bf16[1024,384]{1,0:T(8,128)(2,1)} %get-tuple-element.109.refs_12_), channel_id=1, source_target_pairs={{0,1},{1,0},{2,3},{3,2},{4,5},{5,4},{6,7},{7,6},{8,9},{9,8},{10,11... | collective-permute-start | bytes 2359304 | tf_op jit(solution)/shard_map/ppermute | solution.py:121
  533.1 39.2 %collective-permute-start.70 = (bf16[1024,384]{1,0:T(8,128)(2,1)}, bf16[1024,384]{1,0:T(8,128)(2,1)}, u32[]{:S(2)}, u32[]{:S(2)}) collective-permute-start(bf16[1024,384]{1,0:T(8,128)(2,1)} %get-tuple-element.109.refs_12_), channel_id=1, source_target_pairs={{0,2},{1,3},{2,0},{3,1},{4,6},{5,7},{6,4},{7,5},{8,10},{9,11},{10,... | collective-permute-start | bytes 2359304 | tf_op jit(solution)/shard_map/ppermute | solution.py:121
  554.7 74.4 %all-to-all-start.6 = ((bf16[4,1,3,88,1024]{4,3,2,1,0:T(8,128)(2,1)}), bf16[4,1,3,88,1024]{4,3,2,1,0:T(8,128)(2,1)}, u32[]{:S(2)}, u32[]{:S(2)}) async-start(bf16[4,1,3,88,1024]{4,3,2,1,0:T(8,128)(2,1)} %copy-done.13), calls=%async_computation.6 | async-start | bytes 4325376 | tf_op jit(solution)/shard_map/all_to_all | solution.py:1635
  559.8 241.9 %reduce-scatter.8.cloned.1.call-start = ((), (), s32[]{:S(2)}) async-start(), calls=%async_computation.18 | async-start | bytes 6082560 | tf_op jit(solution)/shard_map/reduce_scatter | solution.py:1748
  563.9 32.2 %collective-permute-start.65 = (bf16[2,1408,256]{2,1,0:T(8,128)(2,1)}, bf16[2,1408,256]{2,1,0:T(8,128)(2,1)}, u32[]{:S(2)}, u32[]{:S(2)}) collective-permute-start(bf16[2,1408,256]{2,1,0:T(8,128)(2,1)} %collective-permute-done.50.refs_5_.refs_2_), channel_id=1, source_target_pairs={{0,1},{1,0},{2,3},{3,2},{4,5},{5,4},{6,7},{7,6},{8,9},{9,8},{10,11... | collective-permute-start | bytes 4325384 | tf_op jit(solution)/shard_map/ppermute | solution.py:121
  626.5 28.6 %collective-permute-start.55 = (bf16[1408,256]{1,0:T(8,128)(2,1)}, bf16[1408,256]{1,0:T(8,128)(2,1)}, u32[]{:S(2)}, u32[]{:S(2)}) collective-permute-start(bf16[1408,256]{1,0:T(8,128)(2,1)} %get-tuple-element.98), channel_id=1, source_target_pairs={{0,1},{1,0},{2,3},{3,2},{4,5},{5,4},{6,7},{7,6},{8,9},{9,8},{10,11... | collective-permute-start | bytes 2162696 | tf_op jit(solution)/shard_map/ppermute | solution.py:121
  650.4 47.7 %collective-permute-start.84 = (bf16[352,1536]{1,0:T(8,128)(2,1)}, bf16[352,1536]{1,0:T(8,128)(2,1)}, u32[]{:S(2)}, u32[]{:S(2)}) collective-permute-start(bf16[352,1536]{1,0:T(8,128)(2,1)} %slice.376), channel_id=1, source_target_pairs={{0,4},{4,0},{8,12},{12,8},{1,5},{5,1},{9,13},{13,9},{2,6},{6,2},{1... | collective-permute-start | bytes 3244040 | tf_op jit(solution)/shard_map/ppermute | solution.py:121
  652.8 32.0 %collective-permute-start.58 = (bf16[1408,256]{1,0:T(8,128)(2,1)}, bf16[1408,256]{1,0:T(8,128)(2,1)}, u32[]{:S(2)}, u32[]{:S(2)}) collective-permute-start(bf16[1408,256]{1,0:T(8,128)(2,1)} %get-tuple-element.251), channel_id=1, source_target_pairs={{0,1},{1,0},{2,3},{3,2},{4,5},{5,4},{6,7},{7,6},{8,9},{9,8},{10,11... | collective-permute-start | bytes 2162696 | tf_op jit(solution)/shard_map/ppermute | solution.py:121
  654.0 30.8 %collective-permute-start.60 = (bf16[1408,256]{1,0:T(8,128)(2,1)}, bf16[1408,256]{1,0:T(8,128)(2,1)}, u32[]{:S(2)}, u32[]{:S(2)}) collective-permute-start(bf16[1408,256]{1,0:T(8,128)(2,1)} %add_convert_fusion.6), channel_id=1, source_target_pairs={{0,2},{1,3},{2,0},{3,1},{4,6},{5,7},{6,4},{7,5},{8,10},{9,11},{10,... | collective-permute-start | bytes 2162696 | tf_op jit(solution)/shard_map/ppermute | solution.py:121
  698.0 174.0 %reduce-scatter.6.cloned.1.call-start = ((), (), s32[]{:S(2)}) async-start(), calls=%async_computation.17 | async-start | bytes 6082560 | tf_op jit(solution)/shard_map/reduce_scatter | solution.py:1748
  701.0 50.8 %collective-permute-start.85 = (bf16[176,1536]{1,0:T(8,128)(2,1)}, bf16[176,1536]{1,0:T(8,128)(2,1)}, u32[]{:S(2)}, u32[]{:S(2)}) collective-permute-start(bf16[176,1536]{1,0:T(8,128)(2,1)} %slice.379), channel_id=1, source_target_pairs={{0,8},{4,12},{8,0},{12,4},{1,9},{5,13},{9,1},{13,5},{2,10},{6,14},... | collective-permute-start | bytes 1622024 | tf_op jit(solution)/shard_map/ppermute | solution.py:121
  727.3 68.9 %collective-permute-start.62 = (bf16[256,2816]{1,0:T(8,128)(2,1)}, bf16[256,2816]{1,0:T(8,128)(2,1)}, u32[]{:S(2)}, u32[]{:S(2)}) collective-permute-start(bf16[256,2816]{1,0:T(8,128)(2,1)} %convolution_convert_fusion.1), channel_id=1, source_target_pairs={{0,1},{1,0},{2,3},{3,2},{4,5},{5,4},{6,7},{7,6},{8,9},{9,8},{10,11... | collective-permute-start | bytes 4325384 | tf_op jit(solution)/shard_map/ppermute | solution.py:121
  727.4 116.9 %collective-permute-start.61 = (bf16[256,2816]{1,0:T(8,128)(2,1)}, bf16[256,2816]{1,0:T(8,128)(2,1)}, u32[]{:S(2)}, u32[]{:S(2)}) collective-permute-start(bf16[256,2816]{1,0:T(8,128)(2,1)} %convolution_convert_fusion.3), channel_id=1, source_target_pairs={{0,1},{1,0},{2,3},{3,2},{4,5},{5,4},{6,7},{7,6},{8,9},{9,8},{10,11... | collective-permute-start | bytes 4325384 | tf_op jit(solution)/shard_map/ppermute | solution.py:121
  728.7 61.9 %all-to-all-start.9 = ((f32[32,1,1408]{2,1,0:T(1,128)}), f32[32,1,1408]{2,1,0:T(1,128)S(1)}, u32[]{:S(2)}, u32[]{:S(2)}) async-start(f32[32,1,1408]{2,1,0:T(1,128)} %broadcast_in_dim.175), calls=%async_computation.11 | async-start | bytes 360448 | tf_op jit(solution)/shard_map/all_to_all | solution.py:252
  799.3 45.1 %collective-permute-start.63 = (bf16[256,2816]{1,0:T(8,128)(2,1)S(1)}, bf16[256,2816]{1,0:T(8,128)(2,1)}, u32[]{:S(2)}, u32[]{:S(2)}) collective-permute-start(bf16[256,2816]{1,0:T(8,128)(2,1)S(1)} %add_convert_fusion.1), channel_id=1, source_target_pairs={{0,2},{1,3},{2,0},{3,1},{4,6},{5,7},{6,4},{7,5},{8,10},{9,11},{10,... | collective-permute-start | bytes 4325384 | tf_op jit(solution)/shard_map/ppermute | solution.py:121
  802.8 30.0 %collective-permute-start.78 = (bf16[32,768]{1,0:T(8,128)(2,1)S(1)}, bf16[32,768]{1,0:T(8,128)(2,1)S(1)}, u32[]{:S(2)}, u32[]{:S(2)}) collective-permute-start(bf16[32,768]{1,0:T(8,128)(2,1)S(1)} %get-tuple-element.306), channel_id=1, source_target_pairs={{0,3},{1,2},{2,1},{3,0},{4,7},{5,6},{6,5},{7,4},{8,11},{9,10},{10,... | collective-permute-start | bytes 147464 | tf_op jit(solution)/shard_map/ppermute | solution.py:177
  802.9 32.2 %collective-permute-start.79 = (bf16[32,768]{1,0:T(8,128)(2,1)S(1)}, bf16[32,768]{1,0:T(8,128)(2,1)S(1)}, u32[]{:S(2)}, u32[]{:S(2)}) collective-permute-start(bf16[32,768]{1,0:T(8,128)(2,1)S(1)} %get-tuple-element.217), channel_id=1, source_target_pairs={{0,2},{1,3},{2,0},{3,1},{4,6},{5,7},{6,4},{7,5},{8,10},{9,11},{10,... | collective-permute-start | bytes 147464 | tf_op jit(solution)/shard_map/ppermute | solution.py:177
  803.0 32.8 %collective-permute-start.80 = (bf16[32,768]{1,0:T(8,128)(2,1)S(1)}, bf16[32,768]{1,0:T(8,128)(2,1)S(1)}, u32[]{:S(2)}, u32[]{:S(2)}) collective-permute-start(bf16[32,768]{1,0:T(8,128)(2,1)S(1)} %get-tuple-element.305), channel_id=1, source_target_pairs={{0,1},{1,0},{2,3},{3,2},{4,5},{5,4},{6,7},{7,6},{8,9},{9,8},{10,11... | collective-permute-start | bytes 147464 | tf_op jit(solution)/shard_map/ppermute | solution.py:177
  (171 other events, 1330.3 us)
Sparse Core Ops, SparseCore 0:
  32.1 91.7 all-gather.3
  126.6 105.1 all-gather.5
  233.9 151.3 all-gather.7
  449.8 104.2 reduce-scatter.3
  612.2 142.6 reduce-scatter.7
  759.0 113.0 reduce-scatter.5

commit v4 on v3

--- a/solution.py
+++ b/solution.py
@@ -552,15 +552,14 @@
 
 
 def unpack_kernel(width, text, bucket_ref, stamp_ref, *outs):
-    padded = width + -width % 128
+    whole = flip(bucket_ref[:, : 3 * width + -3 * width % 128])
     for part in range(3):
-        block = bucket_ref[:, part * padded : (part + 1) * padded]
-        outs[part][...] = flip(block)[:width]
+        outs[part][...] = whole[part * width : (part + 1) * width]
     rows = D * text // DT
+    folded = 2 * width * DT // D
     for group in range(DT // text):
-        outs[3][group * text : (group + 1) * text, :] = bucket_ref[
-            group * rows : group * rows + text, 3 * padded : 3 * padded + 2 * width
-        ]
+        block = bucket_ref[group * rows : (group + 1) * rows, 3 * width : 3 * width + folded]
+        outs[3][group * text : (group + 1) * text, :] = unfold_rows(block)
 
 
 def unpack_mid(bucket, width, text, stamp):
@@ -624,6 +623,24 @@
     )(*values, *stamps)
 
 
+def caption_kernel(count, null_ref, *refs):
+    total = sum(refs[k][...].astype(f32) * null_ref[0, k] for k in range(count))
+    refs[-1][...] = kernel_dot(refs[count][...], total.astype(bf16)).astype(bf16)
+
+
+def caption_product(nulls, pairs, weight, stamp):
+    count = len(pairs)
+    return pl.pallas_call(
+        functools.partial(caption_kernel, count),
+        out_shape=jax.ShapeDtypeStruct((weight.shape[0], pairs[0].shape[1]), bf16),
+        in_specs=[SMEM_WHOLE] + [VMEM_WHOLE] * (count + 1) + [ANY_WHOLE],
+        out_specs=VMEM_WHOLE,
+        compiler_params=pltpu.CompilerParams(vmem_limit_bytes=VMEM_LIMIT),
+        cost_estimate=pl.CostEstimate(flops=10**9, bytes_accessed=5 << 20, transcendentals=0),
+        name="caption_product",
+    )(nulls, *pairs, weight, stamp)
+
+
 def turn_over_kernel(value_ref, *refs):
     out_ref = refs[-1]
     out_ref[...] = flip(value_ref[...])
@@ -665,8 +682,9 @@
     )(*pieces, right, *stamps)
 
 
-def reduce_grads_kernel(group_ref, *refs):
-    pieces, (right_ref, keep_ref, send_ref) = refs[:-3], refs[-3:]
+def reduce_grads_kernel(count, group_ref, *refs):
+    pieces, right_ref = refs[:count], refs[count]
+    keep_ref, send_ref = refs[-2:]
     step, steps = pl.program_id(0), pl.num_programs(0)
     left = jnp.concatenate([ref[...] for ref in pieces], axis=1)
     product = kernel_dot(left, right_ref[...]).astype(bf16)
@@ -680,12 +698,12 @@
         send_ref[...] = product
 
 
-def reduce_grads(pieces, right, groups):
+def reduce_grads(pieces, right, groups, stamps):
     steps, width = groups.shape[0], right.shape[1]
     rows, half = D // steps, steps // 2
     shape = jax.ShapeDtypeStruct((D // 2, width), bf16)
     return pl.pallas_call(
-        reduce_grads_kernel,
+        functools.partial(reduce_grads_kernel, len(pieces)),
         out_shape=(shape, shape),
         grid_spec=pltpu.PrefetchScalarGridSpec(
             num_scalar_prefetch=1,
@@ -694,7 +712,8 @@
                 pl.BlockSpec((rows, pieces[0].shape[1]), lambda g, group: (group[g], 0))
             ]
             * len(pieces)
-            + [pl.BlockSpec(right.shape, lambda g, group: (0, 0))],
+            + [pl.BlockSpec(right.shape, lambda g, group: (0, 0))]
+            + [ANY_WHOLE] * len(stamps),
             out_specs=[
                 pl.BlockSpec((rows, width), lambda g, group: (jnp.minimum(g, half - 1), 0)),
                 pl.BlockSpec((rows, width), lambda g, group: (jnp.maximum(g - half, 0), 0)),
@@ -705,40 +724,77 @@
             flops=2 * D * right.shape[0] * width, bytes_accessed=12 << 20, transcendentals=0
         ),
         name="reduce_grads",
-    )(groups, *pieces, right)
+    )(groups, *pieces, right, *stamps)
+
+
+def fold_rows(value):
+    rows, columns = value.shape
+    k, m = rows // 8, columns // 11
+    over = value[:, 8 * m :]
+    below = jnp.concatenate(
+        [
+            over[: 3 * k],
+            over[3 * k : 6 * k],
+            jnp.concatenate(
+                [
+                    over[6 * k :, : 2 * m],
+                    jnp.concatenate([over[6 * k : 7 * k, 2 * m :], over[7 * k :, 2 * m :]], axis=1),
+                ],
+                axis=0,
+            ),
+        ],
+        axis=1,
+    )
+    return jnp.concatenate([value[:, : 8 * m], below], axis=0)
+
+
+def unfold_rows(value):
+    rows, columns = value.shape
+    k, m = rows // 11, columns // 8
+    below = value[8 * k :]
+    last = below[2 * k :, 6 * m :]
+    over = jnp.concatenate(
+        [
+            below[:, : 3 * m],
+            below[:, 3 * m : 6 * m],
+            jnp.concatenate(
+                [below[: 2 * k, 6 * m :], jnp.concatenate([last[:, :m], last[:, m:]], axis=0)],
+                axis=1,
+            ),
+        ],
+        axis=0,
+    )
+    return jnp.concatenate([value[: 8 * k], over], axis=1)
 
 
 def mid_grads_kernel(count, width, groups, *refs):
     lefts, third, rights, texts, pairs = (refs[k * count : (k + 1) * count] for k in range(5))
     out_ref = refs[5 * count + 1]
     rows = out_ref.shape[0] // groups
-    padded = width + -width % 128
-    for part in range(3):
-        product = sum(
+    products = [
+        sum(
             kernel_dot(left[part] if part < 2 else last[...], right[part], 1, 1)
             for left, last, right in zip(lefts, third, rights)
         )
-        product = jnp.concatenate(
-            [product, jnp.zeros((product.shape[0], padded - width), f32)], axis=1
-        )
-        out_ref[:, part * padded : (part + 1) * padded] = product.astype(bf16)
+        for part in range(3)
+    ]
     text = texts[0].shape[0] // groups
     product = sum(kernel_dot(left[...], right[...], 1, 1) for left, right in zip(texts, pairs))
-    rest = out_ref.shape[1] - 3 * padded
-    product = jnp.concatenate(
-        [product, jnp.zeros((product.shape[0], rest - 2 * width), f32)], axis=1
-    ).astype(bf16)
     for group in range(groups):
-        start = group * rows
-        out_ref[start : start + text, 3 * padded :] = product[group * text : (group + 1) * text]
-        out_ref[start + text : start + rows, 3 * padded :] = jnp.zeros((rows - text, rest), bf16)
+        here = slice(group * rows, (group + 1) * rows)
+        block = [member[here] for member in products]
+        block.append(fold_rows(product[group * text : (group + 1) * text]))
+        rest = out_ref.shape[1] - sum(member.shape[1] for member in block)
+        block.append(jnp.zeros((rows, rest), f32))
+        out_ref[here, :] = jnp.concatenate(block, axis=1).astype(bf16)
 
 
 def mid_grads_bucket(lefts, third, rights, texts, pairs, stamp, groups):
     count, width = len(lefts), rights[0].shape[1]
     steps = 2
     rows, text = D // steps, DT // steps
-    columns = 3 * (width + -width % 128) + 2 * width + -2 * width % 128
+    columns = 3 * width + 2 * width * DT // D
+    columns += -columns % 128
     return pl.pallas_call(
         functools.partial(mid_grads_kernel, count, width, groups // steps),
         out_shape=jax.ShapeDtypeStruct((D, columns), bf16),
@@ -762,34 +818,32 @@
     rights, lefts = refs[:count], refs[count : 2 * count]
     input_ref, gain_ref, out_ref = refs[2 * count :]
     product = sum(kernel_dot(left[...], right[...]) for left, right in zip(lefts, rights))
-    padded = width + -width % 128
     quarter = width // (2 * count)
     product = jnp.transpose(product)
     group_rows = count * quarter
-    fill = jnp.zeros((group_rows, padded - width), f32)
+    rest = out_ref.shape[1] - 5 * width - gain_ref.shape[1]
     for group in range(product.shape[0] // width):
-        for part in range(2):
-            starts = [
-                group * width + (2 * k + part) * quarter for k in range(count)
-            ]
-            block = jnp.concatenate(
-                [product[start : start + quarter] for start in starts], axis=0
+        rows = slice(group * group_rows, (group + 1) * group_rows)
+        halves = [
+            jnp.concatenate(
+                [
+                    product[start : start + quarter]
+                    for start in (
+                        group * width + (2 * k + part) * quarter for k in range(count)
+                    )
+                ],
+                axis=0,
             )
-            out_ref[
-                group * group_rows : (group + 1) * group_rows,
-                part * padded : (part + 1) * padded,
-            ] = jnp.concatenate([block, fill], axis=1).astype(bf16)
-    out_ref[:, 2 * padded : 2 * padded + input_ref.shape[1]] = input_ref[...]
-    rest = out_ref.shape[1] - 2 * padded - input_ref.shape[1]
-    gains = jnp.concatenate(
-        [gain_ref[...], jnp.zeros((out_ref.shape[0], rest - gain_ref.shape[1]), f32)], axis=1
-    )
-    out_ref[:, 2 * padded + input_ref.shape[1] :] = gains.astype(bf16)
+            for part in range(2)
+        ]
+        block = [input_ref[rows, :].astype(f32), *halves, gain_ref[rows, :]]
+        block.append(jnp.zeros((group_rows, rest), f32))
+        out_ref[rows, :] = jnp.concatenate(block, axis=1).astype(bf16)
 
 
 def skip_grads_bucket(lefts, rights, inputs, gains):
     count, width = len(lefts), lefts[0].shape[0]
-    columns = 2 * (width + -width % 128) + inputs.shape[1] + -inputs.shape[1] % 128
+    columns = 5 * width + -5 * width % 128
     return pl.pallas_call(
         functools.partial(skip_grads_kernel, count, width),
         out_shape=jax.ShapeDtypeStruct((D, columns), bf16),
@@ -810,17 +864,15 @@
     factor = factor_ref[0, 0]
     count, shard, _ = blocks_ref.shape
     width = skip_ref.shape[1] // count
-    padded = width + -width % 128
     blocks = [blocks_ref[k].astype(f32) * factor for k in range(count)]
     for part in range(2):
         skip_ref[part * shard : (part + 1) * shard, :] = jnp.concatenate(
-            [block[:, part * padded : part * padded + width] for block in blocks], axis=1
-        )
-    start = 2 * padded + 3 * width
-    gain_ref[...] = sum(block[:, start : start + 4] for block in blocks)
+            [block[:, (3 + part) * width : (4 + part) * width] for block in blocks], axis=1
+        )
+    gain_ref[...] = sum(block[:, 5 * width : 5 * width + 4] for block in blocks)
     input_ref[...] = jnp.concatenate(
         [
-            block[:, 2 * padded + part * width : 2 * padded + (part + 1) * width]
+            block[:, part * width : (part + 1) * width]
             for part in range(3)
             for block in blocks
         ],
@@ -869,7 +921,7 @@
     return copies
 
 
-def mix_kernel(count, padded, *refs):
+def mix_kernel(count, *refs):
     index_ref, bucket_ref = refs[:2]
     pieces = refs[2 : 2 + count]
     out_ref, weight = refs[-2:]
@@ -879,20 +931,19 @@
         for part in range(2):
             start = group * width + part * half
             weight[start : start + half, :] = bucket_ref[
-                group * half : (group + 1) * half, part * padded : part * padded + width
+                group * half : (group + 1) * half, (3 + part) * width : (4 + part) * width
             ]
     for piece in range(count):
         out_ref[piece ^ index_ref[0]] = kernel_dot(pieces[piece][...], weight[...]).astype(bf16)
 
 
 def mix(index, bucket, pieces, width, stamps):
-    count, padded = len(pieces), width + -width % 128
-    rows = pieces[0].shape[0]
+    count, rows = len(pieces), pieces[0].shape[0]
     return pl.pallas_call(
-        functools.partial(mix_kernel, count, padded),
+        functools.partial(mix_kernel, count),
         out_shape=jax.ShapeDtypeStruct((count, rows, width), bf16),
         grid=(1,),
-        in_specs=[SMEM_WHOLE, pl.BlockSpec((D, 2 * padded), lambda g: (0, 0))]
+        in_specs=[SMEM_WHOLE, pl.BlockSpec(bucket.shape, lambda g: (0, 0))]
         + [pl.BlockSpec(pieces[0].shape, lambda g: (0, 0))] * count
         + [ANY_WHOLE] * len(stamps),
         out_specs=pl.BlockSpec((count, rows, width), lambda g: (0, 0, 0)),
@@ -1066,19 +1117,17 @@
         out_ref,
         total_ref,
         raw_ref,
-    ) = refs[:12]
-    sources = refs[12 : 12 + 3 * count]
+        text_ref,
+    ) = refs[:13]
+    sources = refs[13 : 13 + 3 * count]
     (
-        late_grad_ref,
-        raw_grad_ref,
         mid_grad_ref,
-        mid_round_ref,
         attended_grad_ref,
-        key_grad_ref,
-        value_grad_ref,
+        rights_ref,
+        pairs_ref,
         gain_grad_ref,
-    ) = refs[12 + stamps + 3 * count : 20 + stamps + 3 * count]
-    weights, stage, sems = refs[20 + stamps + 3 * count :]
+    ) = refs[13 + stamps + 3 * count : 18 + stamps + 3 * count]
+    weights, stage, rounded, sems = refs[18 + stamps + 3 * count :]
     order = [2, 1, 0]
     copies = []
     for place in order:
@@ -1091,12 +1140,14 @@
     index = index_ref[0]
     width = D // count
 
-    def through(place, turn, source_ref):
+    def through(place, turn, part):
         total = 0.0
         for piece in range(count):
             copies[turn * count + piece].wait()
             rows = pl.ds(pl.multiple_of((piece ^ index) * width, 32), width)
-            total = total + kernel_dot(flip(source_ref[rows, :]), weights[place * count + piece])
+            value = rounded[rows, :]
+            rights_ref[piece, part] = value
+            total = total + kernel_dot(flip(value), weights[place * count + piece])
         return jnp.transpose(total)
 
     normed, scale = norm_rows(late_ref[...])
@@ -1106,8 +1157,9 @@
         normed, scale, grad * gain_ref[:, 3:4]
     )
     mid_grad_ref[...] = late_grad
-    late_grad_ref[...] = late_grad.astype(bf16)
-    stage[...] = through(2, 0, late_grad_ref).astype(bf16).astype(f32)
+    rounded[...] = late_grad.astype(bf16)
+    stage[...] = through(2, 0, 1).astype(bf16).astype(f32)
+    key_grads, value_grads = [], []
     for head in range(HEADS):
         rows = slice(head * HEAD, (head + 1) * HEAD)
         query, keys = query_ref[head], key_ref[head]
@@ -1119,44 +1171,48 @@
         weight_grad = kernel_dot(flip(value_ref[head]), scaled)
         score_grad = (attention * (weight_grad + total_grad)).astype(bf16)
         query_grad = (kernel_dot(keys, score_grad) * SCALING).astype(bf16).astype(f32)
-        key_grad_ref[head] = kernel_dot(query, score_grad, 1, 1) * SCALING
-        value_grad_ref[head] = kernel_dot(scaled, attention.astype(bf16), 1, 1)
+        key_grad = (kernel_dot(query, score_grad, 1, 1) * SCALING).astype(bf16).astype(f32)
+        key_grads.append(norm_rows_back(*norm_rows(text_ref[head]), key_grad))
+        value_grads.append(kernel_dot(scaled, attention.astype(bf16), 1, 1))
         normed, scale = norm_rows(raw_ref[head])
         stage[rows, :] = norm_rows_back(normed, scale, query_grad)
-    raw_grad_ref[...] = stage[...].astype(bf16)
-    grad = through(1, 1, raw_grad_ref)
+    per = 2 * HEADS // count
+    grads = key_grads + value_grads
+    for part in range(count):
+        block = jnp.concatenate(grads[part * per : (part + 1) * per], axis=0)
+        pairs_ref[part ^ index] = block.astype(bf16)
+    rounded[...] = stage[...].astype(bf16)
+    grad = through(1, 1, 0)
     normed, scale = norm_rows(mid_ref[...])
     gain_grad_ref[:, 0:1] = jnp.sum(grad * normed, axis=1, keepdims=True)
     mid_grad = mid_grad_ref[...] + norm_rows_back(normed, scale, grad * gain_ref[:, 2:3])
     mid_grad_ref[...] = mid_grad
-    mid_round_ref[...] = mid_grad.astype(bf16)
-    attended_grad_ref[...] = through(0, 2, mid_round_ref).astype(bf16)
+    rounded[...] = mid_grad.astype(bf16)
+    attended_grad_ref[...] = through(0, 2, 2).astype(bf16)
 
 
 def middle_backward(index, arrays, weights, stamps):
     count = len(weights) // 3
     tokens = arrays[0].shape[1]
     rounded = jax.ShapeDtypeStruct((D, tokens), bf16)
-    texts = jax.ShapeDtypeStruct((HEADS, HEAD, TEXT_PAD), f32)
+    width = D // count
     return pl.pallas_call(
         functools.partial(middle_backward_kernel, count, len(stamps)),
         out_shape=(
-            rounded,
-            rounded,
             jax.ShapeDtypeStruct((D, tokens), f32),
             rounded,
-            rounded,
-            texts,
-            texts,
+            jax.ShapeDtypeStruct((count, 3, width, tokens), bf16),
+            jax.ShapeDtypeStruct((count, 2 * width, TEXT_PAD), bf16),
             jax.ShapeDtypeStruct((D, 2), f32),
         ),
         in_specs=[SMEM_WHOLE]
-        + [VMEM_WHOLE] * 11
+        + [VMEM_WHOLE] * 12
         + [ANY_WHOLE] * (3 * count + len(stamps)),
-        out_specs=[VMEM_WHOLE] * 8,
+        out_specs=[VMEM_WHOLE] * 5,
         scratch_shapes=[
             pltpu.VMEM((3 * count, D // count, D), bf16),
             pltpu.VMEM((D, tokens), f32),
+            pltpu.VMEM((D, tokens), bf16),
             pltpu.SemaphoreType.DMA((3 * count,)),
         ],
         compiler_params=pltpu.CompilerParams(vmem_limit_bytes=VMEM_LIMIT),
@@ -1426,6 +1482,7 @@
         return lax.all_gather(bucket, GROUP, axis=0, tiled=True)
 
     skip_cols = split_columns(skip_weight)
+    plain = rows == CELL and packs == 1 and group_rows % 16 == 0
     gain_columns = norm_gains.shape[1]
     shard = self_output.shape[0]
     fill = -3 * width % 128
@@ -1433,37 +1490,55 @@
     input_blocks = jnp.swapaxes(jnp.pad(input_blocks, ((0, 0), (0, 0), (0, fill))), 0, 1)
     spare = jnp.pad(jnp.transpose(norm_gains), ((0, 0), (3 * width, fill - 4)))
     input_blocks = trade_cp(input_blocks + spare)
-    head_bucket = jnp.concatenate(
-        [
-            pack([skip_cols[:group_rows], skip_cols[group_rows:]]),
-            input_blocks.reshape(group_rows, -1),
-        ],
-        axis=1,
-    )
+    input_blocks = input_blocks.reshape(group_rows, -1)
+    if plain:
+        tail = 3 * width + -5 * width % 128
+        head_bucket = jnp.concatenate(
+            [
+                input_blocks[:, : 3 * width],
+                skip_cols[:group_rows],
+                skip_cols[group_rows:],
+                input_blocks[:, 3 * width : tail],
+            ],
+            axis=1,
+        )
+    else:
+        head_bucket = jnp.concatenate(
+            [pack([skip_cols[:group_rows], skip_cols[group_rows:]]), input_blocks], axis=1
+        )
     three = send_columns(
         tuple(after(member, head_bucket) for member in (self_output, cross_query, cross_output))
     )
-    expand_weight = after(expand_weight, head_bucket)
-    reduce_weight = after(reduce_weight, head_bucket)
-    pairs_cols = jnp.pad(
-        send_columns((after(cross_pairs, head_bucket),)), ((0, group_rows - group_text), (0, 0))
-    )
-    mid_bucket = pack(
-        [three[:, :width], three[:, width : 2 * width], three[:, 2 * width :], pairs_cols]
-    )
+    joined = jnp.concatenate([tokens.reshape(held, D), skip_in.reshape(held, D)], axis=1)
+    joined_all = pieces_cp(after(joined, head_bucket))
+    expand_weight = after(expand_weight, joined_all[-2])
+    reduce_weight = after(reduce_weight, joined_all[-2])
+    pairs_cols = send_columns((after(cross_pairs, head_bucket),))
+    if plain:
+        mid_bucket = lanes(jnp.concatenate([three, fold_rows(pairs_cols)], axis=1))
+    else:
+        pairs_cols = jnp.pad(pairs_cols, ((0, group_rows - group_text), (0, 0)))
+        mid_bucket = pack(
+            [three[:, :width], three[:, width : 2 * width], three[:, 2 * width :], pairs_cols]
+        )
     mid_gathered = gather_group(mid_bucket)
-    plain = rows == CELL and packs == 1 and group_rows % 16 == 0
     ff_bucket = send_columns((expand_weight, jnp.transpose(reduce_weight)))
     ff_gathered = gather_group(ff_bucket)
     expand_part, reduce_part = unpack(ff_gathered, (ff_width, ff_width))
 
     head_gathered = gather_group(head_bucket)
-    one, two, input_part = unpack(head_gathered, head_widths)
+    if plain:
+        input_part = head_gathered[:, : 3 * width]
+        one = head_gathered[:, 3 * width : 4 * width]
+        two = head_gathered[:, 4 * width : 5 * width]
+        gain_start = 5 * width
+    else:
+        one, two, input_part = unpack(head_gathered, head_widths)
+        gain_start = 2 * (width + -width % 128) + 3 * width
     skip_part = jnp.stack(
         [one.reshape(-1, group_rows, width), two.reshape(-1, group_rows, width)], axis=1
     ).reshape(2 * D, width)
     skip_part = after(skip_part, ff_bucket)
-    gain_start = 2 * (width + -width % 128) + 3 * width
     gain_columns_t = head_gathered[:, gain_start : gain_start + 4].astype(f32)
     gain_rows = jnp.transpose(gain_columns_t)
 
@@ -1545,11 +1620,9 @@
     )
     caption_rows = caption_shard.shape[0]
     caption_full = jnp.transpose(gather_every(caption_shard).reshape(DT, TEXT_PAD))
-    joined = jnp.concatenate([tokens.reshape(held, D), skip_in.reshape(held, D)], axis=1)
-    joined_all = pieces_cp(after(joined, head_bucket))
     piece_index = cp_index.reshape(1)
     if plain:
-        mixed_blocks = trade_cp(mix(piece_index, head_gathered, joined_all, width, (caption_full,)))
+        mixed_blocks = trade_cp(mix(piece_index, head_gathered, joined_all, width, ()))
         base_t, normed_self_t = start_forward(
             mixed_blocks, gain_columns_t, shifts.reshape(D, 1)
         )
@@ -1563,7 +1636,7 @@
         normed_all = pieces_cp(jnp.transpose(normed_self))
     cosine, sines = jax.vmap(rope_tables)(chunk_row, chunk_col)
     if plain:
-        offset = 2 * (width + -width % 128)
+        offset = 0
         qkv, raw = project(
             normed_all,
             head_gathered,
@@ -1571,7 +1644,7 @@
             group_heads,
             cosine[0],
             sines[0],
-            (),
+            (caption_full,),
         )
         qkv, raw = qkv[None], raw[None]
         query_raw, key_raw = raw[:, :, 0], raw[:, :, 1]
@@ -1588,8 +1661,17 @@
         value_rows = projected[:, :, 2].astype(bf16)
         qkv = jnp.stack([queries, key_rows, value_rows], axis=2)
 
+    cp_ids = jnp.arange(cp_count, dtype=jnp.int32)
+    turn_pick = (cp_ids[:, None] ^ cp_index) == cp_ids[None, :]
+    near_turned = jnp.sum(jnp.where(turn_pick, near[0][None, :], 0), axis=1)
+    near_null = jnp.sum(
+        jnp.where(near_turned[:, None] == slot_ids[None, :], null_mask[0][None, :], 0), axis=1
+    )
+    near_null = near_null.astype(f32)[None, :]
     if plain:
-        offered = offer(local[0, jnp.arange(cp_count) ^ cp_index], captions, (qkv,))
+        offered = offer(
+            jnp.sum(jnp.where(turn_pick, local[0][None, :], 0), axis=1), captions, (qkv,)
+        )
         arrived = jnp.stack(reorder_cp(exchange_cp(list(offered))))[:, None]
     else:
         offered = jnp.stack(
@@ -1721,6 +1803,8 @@
             text_values,
             mid_weights,
         )
+        attended_other = trade_bit(attended, "cp", 2)
+        (normed_ffn_t,) = gate((normed_ffn_t,), (attended_other,))
         ffn_pieces = pieces_cp(normed_ffn_t)
         (lefts,) = gate((lefts,), (ffn_pieces[2],))
         lefts_other = trade_bit(lefts, "cp", 2)
@@ -1754,10 +1838,11 @@
         ffn_part = dot(expand_in, expand_part, 1, 1).astype(bf16)
         ffn_part = by_piece(ffn_part)
         block_part = by_piece(dot(hidden, reduce_part, 1, 1))
+    if plain:
+        keep, send = reduce_grads(reduce_pieces, hidden, group_order, ())
+        first_half = trade_bit(send, *group_steps()[0][:2])
     ff_out = expand_grads(ffn_pieces, expand_in, (lefts_other,) if plain else ())
     if plain:
-        keep, send = reduce_grads(reduce_pieces, hidden, group_order)
-        first_half = trade_bit(send, *group_steps()[0][:2])
         ff_grads = sum_group(ff_out)
     else:
         reduce_out = dot(reduce_in, hidden, 1, 0).astype(bf16)
@@ -1766,21 +1851,17 @@
     ffn_grad = scatter_cp(ffn_part)
     texts = jnp.transpose(chosen.reshape(packs * TEXT_PAD, DT))
     if plain:
-        attended, texts = gate((attended, texts), (ff_out,))
-        attended_all = pieces_cp(attended)
+        (texts,) = gate((texts,), (ff_out,))
+        attended_all = [
+            attended,
+            trade_bit(attended, "cp", 1),
+            attended_other,
+            trade_bit(attended_other, "cp", 1),
+        ]
         lefts = [lefts, trade_bit(lefts, "cp", 1), lefts_other, trade_bit(lefts_other, "cp", 1)]
     texts = pieces_cp(texts)
     if plain:
-        (
-            late_round,
-            cross_raw_grad,
-            mid_grad,
-            mid_round,
-            attended_grad,
-            ck_grad,
-            cv_grad,
-            gain_pair,
-        ) = middle_backward(
+        mid_grad, attended_grad, rights, paired_rows, gain_pair = middle_backward(
             piece_index,
             (
                 ffn_grad,
@@ -1794,13 +1875,13 @@
                 out_cross,
                 totals_cross,
                 cross_raw,
+                text_raw,
             ),
             mid_weights,
-            (ff_out,),
-        )
-        cout_in, cross_raw_grad, self_in = (
-            reorder_cp(row_blocks(member)) for member in (late_round, cross_raw_grad, mid_round)
-        )
+            (ff_out, keep, send),
+        )
+        rights = exchange_cp([rights[k] for k in range(cp_count)])
+        pairs = exchange_cp([paired_rows[k] for k in range(cp_count)])
     else:
         ffn_back = jax.vjp(norm_gain, late_stream, gain_rows[3])[1]
         late_part, gain_ffn = ffn_back(ffn_grad)
@@ -1828,12 +1909,13 @@
     if not plain:
         lefts = pieces_cp(jnp.stack([normed_cross_t, crossed]))
         attended_all = pieces_cp(attended)
-    rights = exchange_cp(
-        [
-            jnp.stack([cross, late, mid])
-            for cross, late, mid in zip(cross_raw_grad, cout_in, self_in)
-        ]
-    )
+    if not plain:
+        rights = exchange_cp(
+            [
+                jnp.stack([cross, late, mid])
+                for cross, late, mid in zip(cross_raw_grad, cout_in, self_in)
+            ]
+        )
     if plain:
         attended_grad = lax.all_to_all(
             attended_grad.reshape(cp_count * sp_count, pairs_dev, HEAD, rows),
@@ -1853,28 +1935,26 @@
         last_cells,
         valid_cells,
         turned,
-        (first_half, *rights[1:]) if plain else (),
+        (*rights[1:], *pairs[1:], texts[2], first_half) if plain else (),
     )
     stamp = qkv_grad
     qkv_grad = from_heads(qkv_grad)
-    if plain:
-        block_part = reduce_parts(hidden, ff_gathered, stamp, cp_count)
-        block_out = jnp.transpose((late_t + scatter_cp(block_part)).astype(bf16))
-    else:
+    if not plain:
         block_out = (late_stream + scatter_cp(block_part)).astype(bf16)
 
-    ck_grad = ck_grad.astype(bf16).astype(f32)
-    text_raw_grad = jax.vjp(head_norm, text_raw)[1](ck_grad)[0].astype(bf16)
-    paired_grad = jnp.stack(
-        [
-            text_raw_grad.reshape(packs, D, TEXT_PAD),
-            cv_grad.reshape(packs, D, TEXT_PAD).astype(bf16),
-        ],
-        axis=1,
-    ).reshape(packs, 2 * D, TEXT_PAD)
-    paired_rows = jnp.swapaxes(paired_grad, 0, 1).reshape(2 * D, packs * TEXT_PAD)
-    paired_rows = reorder_cp(row_blocks(paired_rows))
-    pairs = exchange_cp(paired_rows)
+    if not plain:
+        ck_grad = ck_grad.astype(bf16).astype(f32)
+        text_raw_grad = jax.vjp(head_norm, text_raw)[1](ck_grad)[0].astype(bf16)
+        paired_grad = jnp.stack(
+            [
+                text_raw_grad.reshape(packs, D, TEXT_PAD),
+                cv_grad.reshape(packs, D, TEXT_PAD).astype(bf16),
+            ],
+            axis=1,
+        ).reshape(packs, 2 * D, TEXT_PAD)
+        paired_rows = jnp.swapaxes(paired_grad, 0, 1).reshape(2 * D, packs * TEXT_PAD)
+        paired_rows = reorder_cp(row_blocks(paired_rows))
+        pairs = exchange_cp(paired_rows)
     if plain:
         mid_out = mid_grads_bucket(
             lefts, attended_all, rights, texts, pairs, stamp, dp_count * sp_count
@@ -1895,10 +1975,7 @@
         )
     mid_grads = sum_group(mid_out)
     if plain:
-        near_null = jnp.take_along_axis(null_mask, near, axis=1)[0]
-        near_null = near_null[jnp.arange(cp_count) ^ cp_index].astype(bf16)
-        null_sum = sum(pairs[k].astype(f32) * near_null[k].astype(f32) for k in range(cp_count))
-        caption_grad = dot(pairs_part, null_sum.astype(bf16), 1, 0)
+        caption_grad = caption_product(near_null, pairs, pairs_part, mid_out)
     else:
         null_sum = jnp.einsum(
             "p,pnt->nt", own_null.astype(f32), paired_grad.astype(f32), precision=highest
@@ -1924,6 +2001,9 @@
     else:
         normed_part = dot(projected_grad, input_part, 0, 1).astype(bf16)
     self_input_grad = dot(normed_all, projected_grad, 1, 1).astype(bf16)
+    if plain:
+        block_part = reduce_parts(hidden, ff_gathered, normed_part[0], cp_count)
+        block_out = jnp.transpose((late_t + scatter_cp(block_part)).astype(bf16))
     if plain:
         mixed_grad, sums = start_backward(
             mixed_blocks,
@@ -1987,13 +2067,13 @@
 
     factor = all_packs * PACK / jnp.sum(lengths).astype(f32)
 
-    def join_columns(bucket, widths):
+    def join_columns(bucket, widths, tight=False):
         blocks = jnp.stack(send_cp(jnp.split(bucket, cp_count, axis=0)))
         start, parts = 0, []
         for size in widths:
             part = jnp.swapaxes(blocks[:, :, start : start + size], 0, 1)
             parts.append(part.astype(f32) * factor)
-            start += size + -size % 128
+            start += size if tight else size + -size % 128
         return parts
 
     def whole(part):
@@ -2002,12 +2082,21 @@
     mid_grads = after(mid_grads, head_out)
     (expand_out,) = join_columns(after(ff_grads, head_out), (ff_width,))
     (reduce_out,) = join_columns(reduce_sums, (ff_width,))
-    cross_query_out, cross_out_out, self_out_out = join_columns(
-        mid_grads[:, : 3 * (width + -width % 128)], (width, width, width)
-    )
-    (pairs_out,) = join_columns(
-        mid_grads[:group_text, 3 * (width + -width % 128) :], (2 * width,)
-    )
+    if plain:
+        cross_query_out, cross_out_out, self_out_out = join_columns(
+            mid_grads[:, : 3 * width], (width, width, width), True
+        )
+        folded = 2 * width * DT // D
+        (pairs_out,) = join_columns(
+            unfold_rows(mid_grads[:, 3 * width : 3 * width + folded]), (2 * width,)
+        )
+    else:
+        cross_query_out, cross_out_out, self_out_out = join_columns(
+            mid_grads[:, : 3 * (width + -width % 128)], (width, width, width)
+        )
+        (pairs_out,) = join_columns(
+            mid_grads[:group_text, 3 * (width + -width % 128) :], (2 * width,)
+        )
     if plain:
         skip_out, input_out, gains_grad = finish_head(
             trade_cp(head_grads.reshape(cp_count, shard, -1)), factor

time: 904 us -> 903 us (level)
    ppermute x30, waiting for transfers between devices: 77.3 us -> 116 us  [exchange_cp(): lax.ppermute(pieces[key], 'cp', [(k, k ^ key) for k in range(count)])]
    all_gather x3, waiting for transfers between devices: 22.3 us -> 0.04 us  [gather_group(): return lax.all_gather(bucket, GROUP, axis=0, tiled=True)]
    reduce_scatter x3, waiting for transfers between devices: 22.7 us -> 11.6 us  [sum_group(): return lax.psum_scatter(bucket, GROUP, scatter_dimension=0, tiled=True)]
    ppermute x64, starting transfers between devices: 50.6 us -> 41.4 us  [trade_bit(): return lax.ppermute(value, axis, [(k, k ^ bit) for k in range(count)])]
    unnamed x227 -> x189, local copies, waits for them, and re-layouts: 57.6 us -> 49.6 us
    dot_general x12 -> x11, matrix products: 40.2 us -> 35.4 us  [dot(): lax.dot_general(left, right, (((left_dim,), (right_dim,)), ((), ())), pre...]
    pallas_call x2 -> x3, Pallas kernels: 16.8 us -> 19.9 us  [the longest x1 11.3 us: reduce_grads(): pl.pallas_call(functools.partial(reduce_grads_kernel, len(pieces)), out_s...]
  transfers between devices with their start and end apart: 110 -> 110, of which waited for: 41 -> 44; matrix products, arithmetic and copies ran while one was open for 19% -> 19% of each run, Pallas kernels for 20% -> 20%
where the time goes in v4:
time: 903 us; the launch traced here: 890 us
  waiting for transfers between devices  340 us (38%)
  Pallas kernels  184 us (20%)
  starting transfers between devices  120 us (13%)
  local copies, waits for them, and re-layouts  106 us (12%)
  other arithmetic  73.4 us (8%)
  matrix products  37.4 us (4%)
  between operations  29.4 us (3%)
    ppermute x64, waiting for transfers between devices, trade_bit(): return lax.ppermute(value, axis, [(k, k ^ bit) for k in range(count)])  173 us
    ppermute x30, waiting for transfers between devices, exchange_cp(): lax.ppermute(pieces[key], 'cp', [(k, k ^ key) for k in range(count)])  116 us
    unnamed x189, local copies, waits for them, and re-layouts  49.6 us
    ppermute x64, starting transfers between devices, trade_bit(): return lax.ppermute(value, axis, [(k, k ^ bit) for k in range(count)])  41.4 us
    dot_general x11, matrix products, dot(): lax.dot_general(left, right, (((left_dim,), (right_dim,)), ((), ())), pre...  35.4 us
    all_to_all x5, waiting for transfers between devices, trade_cp(): return lax.all_to_all(blocks, 'cp', split_axis=0, concat_axis=0, tiled=True)  33 us
    pallas_call x1, Pallas kernels, feed_forward(): pl.pallas_call(functools.partial(ffn_kernel, count, len(stamps)), out_sha...  29.7 us
    pallas_call x1, Pallas kernels, middle_backward(): pl.pallas_call(functools.partial(middle_backward_kernel, count, len(stamp...  23.2 us
  transfers between devices with their start and end apart: 110, of which 44 were waited for; matrix products, arithmetic and copies ran while one was open for 19% of the time, Pallas kernels for 20%

profile of v4, /device:TPU:0, one launch (start us, length us, event | category | flops | bytes accessed | tf_op | source)
XLA Modules:
  0.0 890.1 jit_solution(4428034780899543459)
XLA Ops:
  23.1 7.8 all-to-all-done
  47.3 5.2 fusion.38
  60.1 31.1 %collective-permute-done.1.refs_4_.refs_2_ = bf16[256,2816]{1,0:T(8,128)(2,1)S(1)} collective-permute-done((bf16[256,2816]{1,0:T(8,128)(2,1)S(1)}, bf16[256,2816]{1,0:T(8,128)(2,1)S(1)}, u32[]{:S(2)}, u32[]{:S(2)}) %collective-permute-start.1) | collective-permute-done | bytes 1441824 | tf_op jit(solution)/shard_map/ppermute | solution.py:121
  96.2 7.3 collective-permute-done.45
  103.4 6.2 collective-permute-done.46
  128.2 6.2 mix.1
  137.6 4.4 all-to-all-start.2
  144.3 8.7 all-to-all-done.2
  164.1 13.2 %collective-permute-done.14 = bf16[2,2,32,384]{3,2,1,0:T(8,128)(2,1)S(1)} collective-permute-done((bf16[2,2,32,384]{3,2,1,0:T(8,128)(2,1)S(1)}, bf16[2,2,32,384]{3,2,1,0:T(8,128)(2,1)S(1)}, u32[]{:S(2)}, u32[]{:S(2)}) %collective-permute-start.14) | collective-permute-done | bytes 98336 | tf_op jit(solution)/shard_map/ppermute | solution.py:121
  194.4 10.2 %project.1 = (bf16[4,3,88,1024]{3,2,1,0:T(8,128)(2,1)}, f32[4,2,88,1024]{3,2,1,0:T(8,128)}) custom-call(bf16[1408,256]{1,0:T(8,128)(2,1)} %get-tuple-element.59.refs_0_, bf16[1408,256]{1,0:T(8,128)(2,1)} %collective-permute-done.9.refs_1_, bf16[1408,256]{1,0:T(8,128)(2,1)} %collective-permute-done.10.refs_2_, ...), custom_call_target="tpu_custom_call" | custom-call | flops 3045064704 | bytes 12582912 | tf_op jit(solution)/shard_map/project/pallas_call | solution.py:1382
  204.6 4.9 all-to-all-start.3
  224.7 7.1 collective-permute-done.18.refs_2_.stamp_ref.refs_6_
  231.8 4.7 unpack_mid.1
  248.7 16.1 %collective-permute-done.28 = bf16[384,1024]{1,0:T(8,128)(2,1)} collective-permute-done((bf16[384,1024]{1,0:T(8,128)(2,1)}, bf16[384,1024]{1,0:T(8,128)(2,1)}, u32[]{:S(2)}, u32[]{:S(2)}) %collective-permute-start.28) | collective-permute-done | bytes 786464 | tf_op jit(solution)/shard_map/ppermute | solution.py:177
  275.3 20.7 %collective-permute-done.26 = bf16[1024,704]{0,1:T(8,128)(2,1)} collective-permute-done((bf16[1024,704]{0,1:T(8,128)(2,1)}, bf16[1024,704]{0,1:T(8,128)(2,1)}, u32[]{:S(2)}, u32[]{:S(2)}) %collective-permute-start.26) | collective-permute-done | bytes 1441824 | tf_op jit(solution)/shard_map/ppermute | solution.py:121
  304.8 12.3 %self_forward.1 = (f32[4,1,88,1024]{3,2,1,0:T(8,128)S(1)}, f32[4,1,1,1024]{3,2,1,0:T(1,128)S(1)}, bf16[4,4,1,88,256]{4,3,2,1,0:T(8,128)(2,1)S(1)}) custom-call(s32[1,16]{1,0:T(1,128)S(1)} %get-tuple-element.386.first_ref, s32[1,16]{1,0:T(1,128)S(1)} %get-tuple-element.387.last_ref, s32[1]{0:T(128)} %bitcast.7.turned_ref, ...), custom_call_target="tpu_custom_call" | custom-call | flops 10000000000 | bytes 8388608 | tf_op jit(solution)/shard_map/self_forward/pallas_call | solution.py:420
  319.1 5.0 all-to-all-start.4
  332.5 18.4 %collective-permute-done.36.refs_12_.refs_19_ = bf16[352,1408]{1,0:T(8,128)(2,1)} collective-permute-done((bf16[352,1408]{1,0:T(8,128)(2,1)}, bf16[352,1408]{1,0:T(8,128)(2,1)}, u32[]{:S(2)}, u32[]{:S(2)}) %collective-permute-start.36) | collective-permute-done | bytes 991264 | tf_op jit(solution)/shard_map/ppermute | solution.py:121
  350.9 23.3 %collective-permute-done.39.refs_16_.refs_23_ = bf16[352,1408]{1,0:T(8,128)(2,1)} collective-permute-done((bf16[352,1408]{1,0:T(8,128)(2,1)}, bf16[352,1408]{1,0:T(8,128)(2,1)}, u32[]{:S(2)}, u32[]{:S(2)}) %collective-permute-start.39) | collective-permute-done | bytes 991264 | tf_op jit(solution)/shard_map/ppermute | solution.py:121
  379.1 19.7 %middle_forward.1 = (f32[1408,256]{1,0:T(8,128)}, f32[1408,256]{1,0:T(8,128)}, bf16[2,1408,256]{2,1,0:T(8,128)(2,1)}, f32[16,88,256]{2,1,0:T(8,128)}, bf16[16,88...) custom-call(s32[1]{0:T(128)} %bitcast.refs_0_, ...), custom_call_target="tpu_custom_call" | custom-call | flops 5075107840 | bytes 25165824 | tf_op jit(solution)/shard_map/middle_forward/pallas_call | solution.py:1080
  401.9 17.2 %collective-permute-done.43.refs_2_.refs_1_ = bf16[1408,256]{1,0:T(8,128)(2,1)} collective-permute-done((bf16[1408,256]{1,0:T(8,128)(2,1)}, bf16[1408,256]{1,0:T(8,128)(2,1)}, u32[]{:S(2)}, u32[]{:S(2)}) %collective-permute-start.43) | collective-permute-done | bytes 720928 | tf_op jit(solution)/shard_map/ppermute | solution.py:121
  422.7 29.7 %feed_forward.1 = (bf16[1024,1536]{1,0:T(8,128)(2,1)}, bf16[1024,1536]{1,0:T(8,128)(2,1)}, bf16[1408,256]{1,0:T(8,128)(2,1)S(1)}, bf16[1408,256]{1,0:T(8,128)(2,...) custom-call(bf16[1408,256]{1,0:T(8,128)(2,1)S(1)} %copy-done.32, ...), custom_call_target="tpu_custom_call" | custom-call | flops 13287555072 | bytes 25165824 | tf_op jit(solution)/shard_map/feed_forward/pallas_call | solution.py:1284
  454.7 8.6 expand_grads.1.refs_25_.refs_1_
  467.1 11.3 %reduce_grads.1 = (bf16[704,1536]{1,0:T(8,128)(2,1)S(1)}, bf16[704,1536]{1,0:T(8,128)(2,1)}) custom-call(s32[8]{0:T(128)S(1)} %broadcast_xor_fusion.group_ref, bf16[1408,256]{1,0:T(8,128)(2,1)} %turn_over.1.refs_0_.refs_4_.refs_2_, bf16[1408,256]{1,0:T(8,128)(2,1)} %collective-permute-done.17.refs_1_.refs_5_, ...), custom_call_target="tpu_custom_call" | custom-call | flops 4429185024 | bytes 12582912 | tf_op jit(solution)/shard_map/reduce_grads/pallas_call | solution.py:705
  487.9 23.2 %middle_backward.1 = (f32[1408,256]{1,0:T(8,128)}, bf16[1408,256]{1,0:T(8,128)(2,1)S(1)}, bf16[4,3,352,256]{3,2,1,0:T(8,128)(2,1)}, bf16[4,704,384]{2,1,0:T(8,128)(2,1)}, f32[1408,2]{1,0:T(8,128)S(1)}) custom-call(s32[1]{0:T(128)} %bitcast.refs_0_, f32[1408,256]{1,0:T(8,128)} %convert_add_fusion.2.refs_1_, ...), custom_call_target="tpu_custom_call" | custom-call | flops 7105150976 | bytes 31457280 | tf_op jit(solution)/shard_map/middle_backward/pallas_call | solution.py:1199
  512.9 5.8 all-to-all-start.5
  527.9 13.6 %collective-permute-done.53.refs_1_.refs_10_ = bf16[3,352,256]{2,1,0:T(8,128)(2,1)S(1)} collective-permute-done((bf16[3,352,256]{2,1,0:T(8,128)(2,1)S(1)}, bf16[3,352,256]{2,1,0:T(8,128)(2,1)S(1)}, u32[]{:S(2)}, u32[]{:S(2)}) %collective-permute-start.53) | collective-permute-done | bytes 540704 | tf_op jit(solution)/shard_map/ppermute | solution.py:177
  547.3 5.1 collective-permute-done.54.refs_2_.refs_11_
  552.4 12.4 %collective-permute-done.56.refs_4_.refs_18_.refs_2_ = bf16[704,384]{1,0:T(8,128)(2,1)} collective-permute-done((bf16[704,384]{1,0:T(8,128)(2,1)}, bf16[704,384]{1,0:T(8,128)(2,1)}, u32[]{:S(2)}, u32[]{:S(2)}) %collective-permute-start.56) | collective-permute-done | bytes 540704 | tf_op jit(solution)/shard_map/ppermute | solution.py:177
  564.8 10.8 %collective-permute-done.57.refs_5_.refs_19_.refs_3_ = bf16[704,384]{1,0:T(8,128)(2,1)} collective-permute-done((bf16[704,384]{1,0:T(8,128)(2,1)}, bf16[704,384]{1,0:T(8,128)(2,1)}, u32[]{:S(2)}, u32[]{:S(2)}) %collective-permute-start.57) | collective-permute-done | bytes 540704 | tf_op jit(solution)/shard_map/ppermute | solution.py:177
  579.0 14.2 %self_backward.1.refs_20_ = bf16[4,1,3,88,1024]{4,3,2,1,0:T(8,128)(2,1)} custom-call(s32[1,16]{1,0:T(1,128)S(1)} %get-tuple-element.386.first_ref, s32[1,16]{1,0:T(1,128)S(1)} %get-tuple-element.387.last_ref, s32[1]{0:T(128)S(6)} %select_n.1439.valid_ref, s32[1]{0:T(128)} %bitcast.7.turned_ref, bf16[4,1,3,88,1024]{4,3,2,1,0:T(8,128)(2,1)} %all-to-all-done.3.qkv_ref, ...), custom_call_target="tpu_custom_call" | custom-call | flops 17999998976 | bytes 16777216 | tf_op jit(solution)/shard_map/self_backward/pallas_call | solution.py:442
  593.2 4.6 all-to-all-start.6
  621.0 13.3 %mid_grads.1.refs_5_ = bf16[1408,1664]{1,0:T(8,128)(2,1)} custom-call(bf16[2,1408,256]{2,1,0:T(8,128)(2,1)} %gate.4.refs_0_, bf16[2,1408,256]{2,1,0:T(8,128)(2,1)} %copy-done.82, bf16[2,1408,256]{2,1,0:T(8,128)(2,1)} %collective-permute-done.51.refs_5_.refs_2_, bf16[2,1408,256]{2,1,0:T(8,128)(2,1)} %copy-done.83, bf16[1408,256]{1,0:T(8,128)(2,1)} %bitcast.58.refs_1_.refs_4_, ...), custom_call_target="tpu_custom_call" | custom-call | flops 6978273280 | bytes 25165824 | tf_op jit(solution)/shard_map/mid_grads/pallas_call | solution.py:798
  642.1 6.0 all-to-all-done.6
  656.5 4.6 convolution_convert_fusion.5
  662.3 7.9 reduce_parts.1
  671.2 7.0 convolution_convert_fusion
  686.2 5.4 copy.192.refs_8_
  693.6 6.3 collective-permute-done.65
  702.8 4.3 start_backward.1
  719.0 5.2 all-to-all-done.7
  731.9 7.4 skip_grads.1
  742.4 16.8 %all-to-all-start.9 = ((f32[32,1,1408]{2,1,0:T(1,128)}), f32[32,1,1408]{2,1,0:T(1,128)S(1)}, u32[]{:S(2)}, u32[]{:S(2)}) async-start(f32[32,1,1408]{2,1,0:T(1,128)} %broadcast_in_dim.207), calls=%async_computation.11 | async-start | bytes 360448 | tf_op jit(solution)/shard_map/all_to_all | solution.py:252
  776.9 4.4 collective-permute-done.90
  811.9 30.9 %collective-permute-done.75 = bf16[44,1056]{1,0:T(8,128)(2,1)S(1)} collective-permute-done((bf16[44,1056]{1,0:T(8,128)(2,1)S(1)}, bf16[44,1056]{1,0:T(8,128)(2,1)S(1)}, u32[]{:S(2)}, u32[]{:S(2)}) %collective-permute-start.75) | collective-permute-done | bytes 92960 | tf_op jit(solution)/shard_map/ppermute | solution.py:177
  848.8 4.7 convert_add_fusion
  853.5 11.6 %reduce-scatter.6.cloned.1.call-done = bf16[176,1792]{1,0:T(8,128)(2,1)} async-done(((bf16[1408,1792]{1,0:T(8,128)(2,1)}), bf16[176,1792]{1,0:T(8,128)(2,1)}) %reduce-scatter.6.cloned.1.call-update) | async-done | bytes 630800 | tf_op jit(solution)/shard_map/reduce_scatter | solution.py:1832
  873.7 7.5 all-to-all-done.8.blocks_ref
  (611 shorter events, 328.7 us)
Async XLA Ops:
  23.0 103.3 %all-gather.4.cloned.1.call-start = ((), (), s32[]{:S(2)}) async-start(), calls=%async_computation.13 | async-start | bytes 5677056 | tf_op jit(solution)/shard_map/all_gather | solution.py:1482
  32.2 192.5 %all-gather.6.cloned.1.call-start = ((), (), s32[]{:S(2)}) async-start(), calls=%async_computation.14 | async-start | bytes 5271552 | tf_op jit(solution)/shard_map/all_gather | solution.py:1482
  53.4 367.1 %all-gather.8.cloned.1.call-start = ((), (), s32[]{:S(2)}) async-start(), calls=%async_computation.15 | async-start | bytes 9732096 | tf_op jit(solution)/shard_map/all_gather | solution.py:1482
  57.0 69.2 %collective-permute-start = (bf16[256,2816]{1,0:T(8,128)(2,1)S(1)}, bf16[256,2816]{1,0:T(8,128)(2,1)S(1)}, u32[]{:S(2)}, u32[]{:S(2)}) collective-permute-start(bf16[256,2816]{1,0:T(8,128)(2,1)S(1)} %maximum_add_fusion.1.refs_2_.refs_0_), channel_id=1, source_target_pairs={{0,1},{1,0},{2,3},{3,2},{4,5},{5,4},{6,7},{7,6},{8,9},{9,8},{10,11... | collective-permute-start | bytes 4325384 | tf_op jit(solution)/shard_map/ppermute | solution.py:121
  57.1 34.0 %collective-permute-start.1 = (bf16[256,2816]{1,0:T(8,128)(2,1)S(1)}, bf16[256,2816]{1,0:T(8,128)(2,1)S(1)}, u32[]{:S(2)}, u32[]{:S(2)}) collective-permute-start(bf16[256,2816]{1,0:T(8,128)(2,1)S(1)} %maximum_add_fusion.1.refs_2_.refs_0_), channel_id=1, source_target_pairs={{0,2},{1,3},{2,0},{3,1},{4,6},{5,7},{6,4},{7,5},{8,10},{9,11},{10,... | collective-permute-start | bytes 4325384 | tf_op jit(solution)/shard_map/ppermute | solution.py:121
  60.0 36.0 %collective-permute-start.4 = (f32[2,8,1,1408]{3,2,1,0:T(1,128)S(1)}, f32[2,8,1,1408]{3,2,1,0:T(1,128)S(1)}, u32[]{:S(2)}, u32[]{:S(2)}) collective-permute-start(f32[2,8,1,1408]{3,2,1,0:T(1,128)S(1)} %fusion.56), channel_id=1, source_target_pairs={{0,1},{1,0},{2,3},{3,2},{4,5},{5,4},{6,7},{7,6},{8,9},{9,8},{10,11... | collective-permute-start | bytes 270344 | tf_op jit(solution)/shard_map/ppermute | solution.py:121
  204.6 100.2 %all-to-all-start.3 = ((bf16[4,1,3,88,1024]{4,3,2,1,0:T(8,128)(2,1)}), bf16[4,1,3,88,1024]{4,3,2,1,0:T(8,128)(2,1)}, u32[]{:S(2)}, u32[]{:S(2)}) async-start(bf16[4,1,3,88,1024]{4,3,2,1,0:T(8,128)(2,1)} %bitcast.52), calls=%async_computation.3 | async-start | bytes 4325376 | tf_op jit(solution)/shard_map/all_to_all | solution.py:1714
  222.3 26.3 %collective-permute-start.29 = (bf16[384,1024]{1,0:T(8,128)(2,1)}, bf16[384,1024]{1,0:T(8,128)(2,1)}, u32[]{:S(2)}, u32[]{:S(2)}) collective-permute-start(bf16[384,1024]{1,0:T(8,128)(2,1)} %get-tuple-element.65), channel_id=1, source_target_pairs={{0,2},{1,3},{2,0},{3,1},{4,6},{5,7},{6,4},{7,5},{8,10},{9,11},{10,... | collective-permute-start | bytes 2359304 | tf_op jit(solution)/shard_map/ppermute | solution.py:177
  223.8 40.9 %collective-permute-start.28 = (bf16[384,1024]{1,0:T(8,128)(2,1)}, bf16[384,1024]{1,0:T(8,128)(2,1)}, u32[]{:S(2)}, u32[]{:S(2)}) collective-permute-start(bf16[384,1024]{1,0:T(8,128)(2,1)} %get-tuple-element.64), channel_id=1, source_target_pairs={{0,3},{1,2},{2,1},{3,0},{4,7},{5,6},{6,5},{7,4},{8,11},{9,10},{10,... | collective-permute-start | bytes 2359304 | tf_op jit(solution)/shard_map/ppermute | solution.py:177
  224.1 41.6 %collective-permute-start.30 = (bf16[384,1024]{1,0:T(8,128)(2,1)}, bf16[384,1024]{1,0:T(8,128)(2,1)}, u32[]{:S(2)}, u32[]{:S(2)}) collective-permute-start(bf16[384,1024]{1,0:T(8,128)(2,1)} %get-tuple-element.66), channel_id=1, source_target_pairs={{0,1},{1,0},{2,3},{3,2},{4,5},{5,4},{6,7},{7,6},{8,9},{9,8},{10,11... | collective-permute-start | bytes 2359304 | tf_op jit(solution)/shard_map/ppermute | solution.py:177
  240.4 55.7 %collective-permute-start.26 = (bf16[1024,704]{0,1:T(8,128)(2,1)}, bf16[1024,704]{0,1:T(8,128)(2,1)}, u32[]{:S(2)}, u32[]{:S(2)}) collective-permute-start(bf16[1024,704]{0,1:T(8,128)(2,1)} %copy.181), channel_id=1, source_target_pairs={{0,2},{1,3},{2,0},{3,1},{4,6},{5,7},{6,4},{7,5},{8,10},{9,11},{10,... | collective-permute-start | bytes 4325384 | tf_op jit(solution)/shard_map/ppermute | solution.py:121
  241.3 58.0 %collective-permute-start.31 = (bf16[1024,704]{0,1:T(8,128)(2,1)}, bf16[1024,704]{0,1:T(8,128)(2,1)}, u32[]{:S(2)}, u32[]{:S(2)}) collective-permute-start(bf16[1024,704]{0,1:T(8,128)(2,1)} %copy.181), channel_id=1, source_target_pairs={{0,1},{1,0},{2,3},{3,2},{4,5},{5,4},{6,7},{7,6},{8,9},{9,8},{10,11... | collective-permute-start | bytes 4325384 | tf_op jit(solution)/shard_map/ppermute | solution.py:121
  248.7 54.6 %collective-permute-start.17 = (bf16[1408,256]{1,0:T(8,128)(2,1)}, bf16[1408,256]{1,0:T(8,128)(2,1)}, u32[]{:S(2)}, u32[]{:S(2)}) collective-permute-start(bf16[1408,256]{1,0:T(8,128)(2,1)} %turn_over.1.refs_0_.refs_4_.refs_2_), channel_id=1, source_target_pairs={{0,1},{1,0},{2,3},{3,2},{4,5},{5,4},{6,7},{7,6},{8,9},{9,8},{10,11... | collective-permute-start | bytes 2162696 | tf_op jit(solution)/shard_map/ppermute | solution.py:121
  264.8 67.2 %collective-permute-start.32 = (bf16[352,1408]{1,0:T(8,128)(2,1)}, bf16[352,1408]{1,0:T(8,128)(2,1)}, u32[]{:S(2)}, u32[]{:S(2)}) collective-permute-start(bf16[352,1408]{1,0:T(8,128)(2,1)} %get-tuple-element.68.refs_6_.refs_13_), channel_id=1, source_target_pairs={{0,1},{1,0},{2,3},{3,2},{4,5},{5,4},{6,7},{7,6},{8,9},{9,8},{10,11... | collective-permute-start | bytes 2973704 | tf_op jit(solution)/shard_map/ppermute | solution.py:121
  265.6 37.8 %collective-permute-start.19 = (bf16[1408,256]{1,0:T(8,128)(2,1)}, bf16[1408,256]{1,0:T(8,128)(2,1)}, u32[]{:S(2)}, u32[]{:S(2)}) collective-permute-start(bf16[1408,256]{1,0:T(8,128)(2,1)} %collective-permute-done.18.refs_2_.stamp_ref.refs_6_), channel_id=1, source_target_pairs={{0,1},{1,0},{2,3},{3,2},{4,5},{5,4},{6,7},{7,6},{8,9},{9,8},{10,11... | collective-permute-start | bytes 2162696 | tf_op jit(solution)/shard_map/ppermute | solution.py:121
  296.0 28.3 %collective-permute-start.27 = (bf16[1024,704]{0,1:T(8,128)(2,1)}, bf16[1024,704]{0,1:T(8,128)(2,1)}, u32[]{:S(2)}, u32[]{:S(2)}) collective-permute-start(bf16[1024,704]{0,1:T(8,128)(2,1)} %collective-permute-done.26), channel_id=1, source_target_pairs={{0,1},{1,0},{2,3},{3,2},{4,5},{5,4},{6,7},{7,6},{8,9},{9,8},{10,11... | collective-permute-start | bytes 4325384 | tf_op jit(solution)/shard_map/ppermute | solution.py:121
  299.3 32.7 %collective-permute-start.33 = (bf16[352,1408]{1,0:T(8,128)(2,1)}, bf16[352,1408]{1,0:T(8,128)(2,1)}, u32[]{:S(2)}, u32[]{:S(2)}) collective-permute-start(bf16[352,1408]{1,0:T(8,128)(2,1)} %get-tuple-element.68.refs_6_.refs_13_), channel_id=1, source_target_pairs={{0,2},{1,3},{2,0},{3,1},{4,6},{5,7},{6,4},{7,5},{8,10},{9,11},{10,... | collective-permute-start | bytes 2973704 | tf_op jit(solution)/shard_map/ppermute | solution.py:121
  303.2 72.5 %collective-permute-start.35 = (bf16[352,1408]{1,0:T(8,128)(2,1)}, bf16[352,1408]{1,0:T(8,128)(2,1)}, u32[]{:S(2)}, u32[]{:S(2)}) collective-permute-start(bf16[352,1408]{1,0:T(8,128)(2,1)} %get-tuple-element.69.refs_10_.refs_17_), channel_id=1, source_target_pairs={{0,1},{1,0},{2,3},{3,2},{4,5},{5,4},{6,7},{7,6},{8,9},{9,8},{10,11... | collective-permute-start | bytes 2973704 | tf_op jit(solution)/shard_map/ppermute | solution.py:121
  303.4 47.5 %collective-permute-start.36 = (bf16[352,1408]{1,0:T(8,128)(2,1)}, bf16[352,1408]{1,0:T(8,128)(2,1)}, u32[]{:S(2)}, u32[]{:S(2)}) collective-permute-start(bf16[352,1408]{1,0:T(8,128)(2,1)} %get-tuple-element.69.refs_10_.refs_17_), channel_id=1, source_target_pairs={{0,2},{1,3},{2,0},{3,1},{4,6},{5,7},{6,4},{7,5},{8,10},{9,11},{10,... | collective-permute-start | bytes 2973704 | tf_op jit(solution)/shard_map/ppermute | solution.py:121
  319.1 56.6 %all-to-all-start.4 = ((bf16[16,1,88,256]{3,2,1,0:T(8,128)(2,1)}), bf16[16,1,88,256]{3,2,1,0:T(8,128)(2,1)}, u32[]{:S(2)}, u32[]{:S(2)}) async-start(bf16[16,1,88,256]{3,2,1,0:T(8,128)(2,1)} %bitcast.361), calls=%async_computation.4 | async-start | bytes 1441792 | tf_op jit(solution)/shard_map/all_to_all | solution.py:1770
  324.1 316.1 %reduce-scatter.4.cloned.1.call-start = ((), (), s32[]{:S(2)}) async-start(), calls=%async_computation.16 | async-start | bytes 4866048 | tf_op jit(solution)/shard_map/reduce_scatter | solution.py:1832
  324.4 49.8 %collective-permute-start.39 = (bf16[352,1408]{1,0:T(8,128)(2,1)}, bf16[352,1408]{1,0:T(8,128)(2,1)}, u32[]{:S(2)}, u32[]{:S(2)}) collective-permute-start(bf16[352,1408]{1,0:T(8,128)(2,1)} %get-tuple-element.70.refs_14_.refs_21_), channel_id=1, source_target_pairs={{0,2},{1,3},{2,0},{3,1},{4,6},{5,7},{6,4},{7,5},{8,10},{9,11},{10,... | collective-permute-start | bytes 2973704 | tf_op jit(solution)/shard_map/ppermute | solution.py:121
  331.9 47.2 %collective-permute-start.38 = (bf16[352,1408]{1,0:T(8,128)(2,1)}, bf16[352,1408]{1,0:T(8,128)(2,1)}, u32[]{:S(2)}, u32[]{:S(2)}) collective-permute-start(bf16[352,1408]{1,0:T(8,128)(2,1)} %get-tuple-element.70.refs_14_.refs_21_), channel_id=1, source_target_pairs={{0,1},{1,0},{2,3},{3,2},{4,5},{5,4},{6,7},{7,6},{8,9},{9,8},{10,11... | collective-permute-start | bytes 2973704 | tf_op jit(solution)/shard_map/ppermute | solution.py:121
  332.0 47.1 %collective-permute-start.34 = (bf16[352,1408]{1,0:T(8,128)(2,1)}, bf16[352,1408]{1,0:T(8,128)(2,1)}, u32[]{:S(2)}, u32[]{:S(2)}) collective-permute-start(bf16[352,1408]{1,0:T(8,128)(2,1)} %collective-permute-done.33.refs_8_.refs_15_), channel_id=1, source_target_pairs={{0,1},{1,0},{2,3},{3,2},{4,5},{5,4},{6,7},{7,6},{8,9},{9,8},{10,11... | collective-permute-start | bytes 2973704 | tf_op jit(solution)/shard_map/ppermute | solution.py:121
  350.9 28.2 %collective-permute-start.37 = (bf16[352,1408]{1,0:T(8,128)(2,1)}, bf16[352,1408]{1,0:T(8,128)(2,1)}, u32[]{:S(2)}, u32[]{:S(2)}) collective-permute-start(bf16[352,1408]{1,0:T(8,128)(2,1)} %collective-permute-done.36.refs_12_.refs_19_), channel_id=1, source_target_pairs={{0,1},{1,0},{2,3},{3,2},{4,5},{5,4},{6,7},{7,6},{8,9},{9,8},{10,11... | collective-permute-start | bytes 2973704 | tf_op jit(solution)/shard_map/ppermute | solution.py:121
  419.1 35.6 %collective-permute-start.51 = (bf16[2,1408,256]{2,1,0:T(8,128)(2,1)}, bf16[2,1408,256]{2,1,0:T(8,128)(2,1)}, u32[]{:S(2)}, u32[]{:S(2)}) collective-permute-start(bf16[2,1408,256]{2,1,0:T(8,128)(2,1)} %gate.4.refs_0_), channel_id=1, source_target_pairs={{0,2},{1,3},{2,0},{3,1},{4,6},{5,7},{6,4},{7,5},{8,10},{9,11},{10,... | collective-permute-start | bytes 4325384 | tf_op jit(solution)/shard_map/ppermute | solution.py:121
  454.3 26.7 %collective-permute-start.48 = (bf16[1408,256]{1,0:T(8,128)(2,1)}, bf16[1408,256]{1,0:T(8,128)(2,1)}, u32[]{:S(2)}, u32[]{:S(2)}) collective-permute-start(bf16[1408,256]{1,0:T(8,128)(2,1)} %get-tuple-element.75), channel_id=1, source_target_pairs={{0,1},{1,0},{2,3},{3,2},{4,5},{5,4},{6,7},{7,6},{8,9},{9,8},{10,11... | collective-permute-start | bytes 2162696 | tf_op jit(solution)/shard_map/ppermute | solution.py:121
  479.7 95.9 %collective-permute-start.59 = (bf16[704,1536]{1,0:T(8,128)(2,1)}, bf16[704,1536]{1,0:T(8,128)(2,1)}, u32[]{:S(2)}, u32[]{:S(2)}) collective-permute-start(bf16[704,1536]{1,0:T(8,128)(2,1)} %get-tuple-element.86.refs_27_), channel_id=1, source_target_pairs={{0,16},{16,0},{1,17},{17,1},{2,18},{18,2},{3,19},{19,3},{4,20},{20... | collective-permute-start | bytes 6488072 | tf_op jit(solution)/shard_map/ppermute | solution.py:121
  480.4 44.6 %collective-permute-start.58 = (bf16[1024,384]{1,0:T(8,128)(2,1)}, bf16[1024,384]{1,0:T(8,128)(2,1)}, u32[]{:S(2)}, u32[]{:S(2)}) collective-permute-start(bf16[1024,384]{1,0:T(8,128)(2,1)} %gate.5.refs_12_), channel_id=1, source_target_pairs={{0,2},{1,3},{2,0},{3,1},{4,6},{5,7},{6,4},{7,5},{8,10},{9,11},{10,... | collective-permute-start | bytes 2359304 | tf_op jit(solution)/shard_map/ppermute | solution.py:121
  512.9 62.6 %all-to-all-start.5 = ((bf16[16,1,88,256]{3,2,1,0:T(8,128)(2,1)}), bf16[16,1,88,256]{3,2,1,0:T(8,128)(2,1)}, u32[]{:S(2)}, u32[]{:S(2)}) async-start(bf16[16,1,88,256]{3,2,1,0:T(8,128)(2,1)} %bitcast.360), calls=%async_computation.5 | async-start | bytes 1441792 | tf_op jit(solution)/shard_map/all_to_all | solution.py:1920
  523.5 28.8 %collective-permute-start.54 = (bf16[3,352,256]{2,1,0:T(8,128)(2,1)}, bf16[3,352,256]{2,1,0:T(8,128)(2,1)}, u32[]{:S(2)}, u32[]{:S(2)}) collective-permute-start(bf16[3,352,256]{2,1,0:T(8,128)(2,1)} %get-tuple-element.253), channel_id=1, source_target_pairs={{0,3},{1,2},{2,1},{3,0},{4,7},{5,6},{6,5},{7,4},{8,11},{9,10},{10,... | collective-permute-start | bytes 1622024 | tf_op jit(solution)/shard_map/ppermute | solution.py:177
  524.9 27.4 %collective-permute-start.55 = (bf16[704,384]{1,0:T(8,128)(2,1)}, bf16[704,384]{1,0:T(8,128)(2,1)}, u32[]{:S(2)}, u32[]{:S(2)}) collective-permute-start(bf16[704,384]{1,0:T(8,128)(2,1)} %get-tuple-element.251), channel_id=1, source_target_pairs={{0,1},{1,0},{2,3},{3,2},{4,5},{5,4},{6,7},{7,6},{8,9},{9,8},{10,11... | collective-permute-start | bytes 1622024 | tf_op jit(solution)/shard_map/ppermute | solution.py:177
  526.2 38.6 %collective-permute-start.56 = (bf16[704,384]{1,0:T(8,128)(2,1)}, bf16[704,384]{1,0:T(8,128)(2,1)}, u32[]{:S(2)}, u32[]{:S(2)}) collective-permute-start(bf16[704,384]{1,0:T(8,128)(2,1)} %get-tuple-element.250), channel_id=1, source_target_pairs={{0,2},{1,3},{2,0},{3,1},{4,6},{5,7},{6,4},{7,5},{8,10},{9,11},{10,... | collective-permute-start | bytes 1622024 | tf_op jit(solution)/shard_map/ppermute | solution.py:177
  542.3 33.2 %collective-permute-start.57 = (bf16[704,384]{1,0:T(8,128)(2,1)}, bf16[704,384]{1,0:T(8,128)(2,1)}, u32[]{:S(2)}, u32[]{:S(2)}) collective-permute-start(bf16[704,384]{1,0:T(8,128)(2,1)} %get-tuple-element.249), channel_id=1, source_target_pairs={{0,3},{1,2},{2,1},{3,0},{4,7},{5,6},{6,5},{7,4},{8,11},{9,10},{10,... | collective-permute-start | bytes 1622024 | tf_op jit(solution)/shard_map/ppermute | solution.py:177
  593.2 54.9 %all-to-all-start.6 = ((bf16[4,1,3,88,1024]{4,3,2,1,0:T(8,128)(2,1)}), bf16[4,1,3,88,1024]{4,3,2,1,0:T(8,128)(2,1)}, u32[]{:S(2)}, u32[]{:S(2)}) async-start(bf16[4,1,3,88,1024]{4,3,2,1,0:T(8,128)(2,1)} %self_backward.1.refs_20_), calls=%async_computation.6 | async-start | bytes 4325376 | tf_op jit(solution)/shard_map/all_to_all | solution.py:1717
  597.8 202.4 %reduce-scatter.8.cloned.1.call-start = ((), (), s32[]{:S(2)}) async-start(), calls=%async_computation.18 | async-start | bytes 5271552 | tf_op jit(solution)/shard_map/reduce_scatter | solution.py:1832
  615.8 67.9 %collective-permute-start.84 = (bf16[352,1536]{1,0:T(8,128)(2,1)}, bf16[352,1536]{1,0:T(8,128)(2,1)}, u32[]{:S(2)}, u32[]{:S(2)}) collective-permute-start(bf16[352,1536]{1,0:T(8,128)(2,1)} %slice.454), channel_id=1, source_target_pairs={{0,4},{4,0},{8,12},{12,8},{1,5},{5,1},{9,13},{13,9},{2,6},{6,2},{1... | collective-permute-start | bytes 3244040 | tf_op jit(solution)/shard_map/ppermute | solution.py:121
  670.7 42.5 %collective-permute-start.60 = (bf16[1408,256]{1,0:T(8,128)(2,1)}, bf16[1408,256]{1,0:T(8,128)(2,1)}, u32[]{:S(2)}, u32[]{:S(2)}) collective-permute-start(bf16[1408,256]{1,0:T(8,128)(2,1)} %get-tuple-element.94), channel_id=1, source_target_pairs={{0,1},{1,0},{2,3},{3,2},{4,5},{5,4},{6,7},{7,6},{8,9},{9,8},{10,11... | collective-permute-start | bytes 2162696 | tf_op jit(solution)/shard_map/ppermute | solution.py:121
  682.4 32.0 %collective-permute-start.62 = (bf16[1408,256]{1,0:T(8,128)(2,1)}, bf16[1408,256]{1,0:T(8,128)(2,1)}, u32[]{:S(2)}, u32[]{:S(2)}) collective-permute-start(bf16[1408,256]{1,0:T(8,128)(2,1)} %add_convert_fusion.7), channel_id=1, source_target_pairs={{0,2},{1,3},{2,0},{3,1},{4,6},{5,7},{6,4},{7,5},{8,10},{9,11},{10,... | collective-permute-start | bytes 2162696 | tf_op jit(solution)/shard_map/ppermute | solution.py:121
  693.6 71.8 %collective-permute-start.85 = (bf16[176,1536]{1,0:T(8,128)(2,1)}, bf16[176,1536]{1,0:T(8,128)(2,1)}, u32[]{:S(2)}, u32[]{:S(2)}) collective-permute-start(bf16[176,1536]{1,0:T(8,128)(2,1)} %slice.457), channel_id=1, source_target_pairs={{0,8},{4,12},{8,0},{12,4},{1,9},{5,13},{9,1},{13,5},{2,10},{6,14},... | collective-permute-start | bytes 1622024 | tf_op jit(solution)/shard_map/ppermute | solution.py:121
  713.2 151.8 %reduce-scatter.6.cloned.1.call-start = ((), (), s32[]{:S(2)}) async-start(), calls=%async_computation.17 | async-start | bytes 5677056 | tf_op jit(solution)/shard_map/reduce_scatter | solution.py:1832
  729.3 74.4 %collective-permute-start.67 = (bf16[256,2816]{1,0:T(8,128)(2,1)}, bf16[256,2816]{1,0:T(8,128)(2,1)}, u32[]{:S(2)}, u32[]{:S(2)}) collective-permute-start(bf16[256,2816]{1,0:T(8,128)(2,1)} %convolution_convert_fusion.1), channel_id=1, source_target_pairs={{0,1},{1,0},{2,3},{3,2},{4,5},{5,4},{6,7},{7,6},{8,9},{9,8},{10,11... | collective-permute-start | bytes 4325384 | tf_op jit(solution)/shard_map/ppermute | solution.py:121
  731.4 117.3 %collective-permute-start.66 = (bf16[256,2816]{1,0:T(8,128)(2,1)}, bf16[256,2816]{1,0:T(8,128)(2,1)}, u32[]{:S(2)}, u32[]{:S(2)}) collective-permute-start(bf16[256,2816]{1,0:T(8,128)(2,1)} %convolution_convert_fusion.3), channel_id=1, source_target_pairs={{0,1},{1,0},{2,3},{3,2},{4,5},{5,4},{6,7},{7,6},{8,9},{9,8},{10,11... | collective-permute-start | bytes 4325384 | tf_op jit(solution)/shard_map/ppermute | solution.py:121
  742.4 52.5 %all-to-all-start.9 = ((f32[32,1,1408]{2,1,0:T(1,128)}), f32[32,1,1408]{2,1,0:T(1,128)S(1)}, u32[]{:S(2)}, u32[]{:S(2)}) async-start(f32[32,1,1408]{2,1,0:T(1,128)} %broadcast_in_dim.207), calls=%async_computation.11 | async-start | bytes 360448 | tf_op jit(solution)/shard_map/all_to_all | solution.py:252
  806.8 42.0 %collective-permute-start.68 = (bf16[256,2816]{1,0:T(8,128)(2,1)S(1)}, bf16[256,2816]{1,0:T(8,128)(2,1)}, u32[]{:S(2)}, u32[]{:S(2)}) collective-permute-start(bf16[256,2816]{1,0:T(8,128)(2,1)S(1)} %add_convert_fusion.1), channel_id=1, source_target_pairs={{0,2},{1,3},{2,0},{3,1},{4,6},{5,7},{6,4},{7,5},{8,10},{9,11},{10,... | collective-permute-start | bytes 4325384 | tf_op jit(solution)/shard_map/ppermute | solution.py:121
  808.6 34.2 %collective-permute-start.75 = (bf16[44,1056]{1,0:T(8,128)(2,1)S(1)}, bf16[44,1056]{1,0:T(8,128)(2,1)S(1)}, u32[]{:S(2)}, u32[]{:S(2)}) collective-permute-start(bf16[44,1056]{1,0:T(8,128)(2,1)S(1)} %get-tuple-element.303), channel_id=1, source_target_pairs={{0,3},{1,2},{2,1},{3,0},{4,7},{5,6},{6,5},{7,4},{8,11},{9,10},{10,... | collective-permute-start | bytes 278792 | tf_op jit(solution)/shard_map/ppermute | solution.py:177
  808.7 36.7 %collective-permute-start.76 = (bf16[44,1056]{1,0:T(8,128)(2,1)S(1)}, bf16[44,1056]{1,0:T(8,128)(2,1)S(1)}, u32[]{:S(2)}, u32[]{:S(2)}) collective-permute-start(bf16[44,1056]{1,0:T(8,128)(2,1)S(1)} %get-tuple-element.304), channel_id=1, source_target_pairs={{0,2},{1,3},{2,0},{3,1},{4,6},{5,7},{6,4},{7,5},{8,10},{9,11},{10,... | collective-permute-start | bytes 278792 | tf_op jit(solution)/shard_map/ppermute | solution.py:177
  810.0 35.4 %collective-permute-start.77 = (bf16[44,1056]{1,0:T(8,128)(2,1)S(1)}, bf16[44,1056]{1,0:T(8,128)(2,1)S(1)}, u32[]{:S(2)}, u32[]{:S(2)}) collective-permute-start(bf16[44,1056]{1,0:T(8,128)(2,1)S(1)} %get-tuple-element.302), channel_id=1, source_target_pairs={{0,1},{1,0},{2,3},{3,2},{4,5},{5,4},{6,7},{7,6},{8,9},{9,8},{10,11... | collective-permute-start | bytes 278792 | tf_op jit(solution)/shard_map/ppermute | solution.py:177
  (152 other events, 1202.8 us)
Sparse Core Ops, SparseCore 0:
  32.4 84.8 all-gather.3
  120.0 77.2 all-gather.5
  199.4 181.5 all-gather.7
  463.4 104.2 reduce-scatter.3
  634.5 124.6 reduce-scatter.7
  763.2 101.7 reduce-scatter.5

commit v5 on v4

--- a/solution.py
+++ b/solution.py
@@ -1935,7 +1935,7 @@
         last_cells,
         valid_cells,
         turned,
-        (*rights[1:], *pairs[1:], texts[2], first_half) if plain else (),
+        (*pairs[1:], first_half) if plain else (),
     )
     stamp = qkv_grad
     qkv_grad = from_heads(qkv_grad)
@@ -2046,7 +2046,7 @@
     head_grads = sum_group(head_out)
     if plain:
         reduce_sums = scatter_group_halves(
-            keep, send, first_half, (stamp, normed_part[0], head_out)
+            keep, send, first_half, (mid_out, normed_part[0], head_out)
         )
     caption_grad = scatter_every(
         after(caption_sum, head_out).astype(bf16).reshape(-1, caption_rows, TEXT_PAD)

time: 903 us -> 897 us (level)
  Pallas kernels: 184 us -> 195 us
  waiting for transfers between devices: 340 us -> 351 us
  starting transfers between devices: 120 us -> 110 us
  local copies, waits for them, and re-layouts: 106 us -> 96.7 us
    all_to_all x1, starting transfers between devices: 16.8 us -> 3.03 us  [send_every(): return lax.all_to_all(value, EVERY, split_axis=0, concat_axis=0, tiled=True)]
    pallas_call x1, Pallas kernels: 14.2 us -> 23.7 us  [self_backward(): pl.pallas_call(self_backward_kernel, out_shape=jax.ShapeDtypeStruct(qkv.s...]
    unnamed x189 -> x173, local copies, waits for them, and re-layouts: 49.6 us -> 42.4 us
  transfers between devices with their start and end apart: 110 -> 110, of which waited for: 44 -> 42; matrix products, arithmetic and copies ran while one was open for 19% -> 19% of each run, Pallas kernels for 20% -> 22%
where the time goes in v5:
time: 897 us; the launch traced here: 891 us
  waiting for transfers between devices  351 us (39%)
  Pallas kernels  195 us (22%)
  starting transfers between devices  110 us (12%)
  local copies, waits for them, and re-layouts  96.7 us (11%)
  other arithmetic  70.8 us (8%)
  matrix products  37.6 us (4%)
  between operations  29.4 us (3%)
    ppermute x64, waiting for transfers between devices, trade_bit(): return lax.ppermute(value, axis, [(k, k ^ bit) for k in range(count)])  177 us
    ppermute x30, waiting for transfers between devices, exchange_cp(): lax.ppermute(pieces[key], 'cp', [(k, k ^ key) for k in range(count)])  122 us
    ppermute x64, starting transfers between devices, trade_bit(): return lax.ppermute(value, axis, [(k, k ^ bit) for k in range(count)])  44 us
    unnamed x173, local copies, waits for them, and re-layouts  42.4 us
    dot_general x11, matrix products, dot(): lax.dot_general(left, right, (((left_dim,), (right_dim,)), ((), ())), pre...  35.6 us
    all_to_all x5, waiting for transfers between devices, trade_cp(): return lax.all_to_all(blocks, 'cp', split_axis=0, concat_axis=0, tiled=True)  34.1 us
    pallas_call x1, Pallas kernels, feed_forward(): pl.pallas_call(functools.partial(ffn_kernel, count, len(stamps)), out_sha...  29.5 us
    pallas_call x1, Pallas kernels, self_backward(): pl.pallas_call(self_backward_kernel, out_shape=jax.ShapeDtypeStruct(qkv.s...  23.7 us
  transfers between devices with their start and end apart: 110, of which 42 were waited for; matrix products, arithmetic and copies ran while one was open for 19% of the time, Pallas kernels for 22%

profile of v5, /device:TPU:0, one launch (start us, length us, event | category | flops | bytes accessed | tf_op | source)
XLA Modules:
  0.0 890.7 jit_solution(3168240402400103004)
XLA Ops:
  23.1 7.8 all-to-all-done
  47.3 5.2 fusion.38
  60.0 31.1 %collective-permute-done.1.refs_4_.refs_2_ = bf16[256,2816]{1,0:T(8,128)(2,1)S(1)} collective-permute-done((bf16[256,2816]{1,0:T(8,128)(2,1)S(1)}, bf16[256,2816]{1,0:T(8,128)(2,1)S(1)}, u32[]{:S(2)}, u32[]{:S(2)}) %collective-permute-start.1) | collective-permute-done | bytes 1441824 | tf_op jit(solution)/shard_map/ppermute | solution.py:121
  96.2 7.3 collective-permute-done.45
  103.4 6.2 collective-permute-done.46
  128.2 6.2 mix.1
  137.6 4.4 all-to-all-start.2
  144.3 8.7 all-to-all-done.2
  164.1 13.2 %collective-permute-done.14 = bf16[2,2,32,384]{3,2,1,0:T(8,128)(2,1)S(1)} collective-permute-done((bf16[2,2,32,384]{3,2,1,0:T(8,128)(2,1)S(1)}, bf16[2,2,32,384]{3,2,1,0:T(8,128)(2,1)S(1)}, u32[]{:S(2)}, u32[]{:S(2)}) %collective-permute-start.14) | collective-permute-done | bytes 98336 | tf_op jit(solution)/shard_map/ppermute | solution.py:121
  194.4 10.2 %project.1 = (bf16[4,3,88,1024]{3,2,1,0:T(8,128)(2,1)}, f32[4,2,88,1024]{3,2,1,0:T(8,128)}) custom-call(bf16[1408,256]{1,0:T(8,128)(2,1)} %get-tuple-element.59.refs_0_, bf16[1408,256]{1,0:T(8,128)(2,1)} %collective-permute-done.9.refs_1_, bf16[1408,256]{1,0:T(8,128)(2,1)} %collective-permute-done.10.refs_2_, ...), custom_call_target="tpu_custom_call" | custom-call | flops 3045064704 | bytes 12582912 | tf_op jit(solution)/shard_map/project/pallas_call | solution.py:1382
  204.6 5.0 all-to-all-start.3
  225.1 6.7 collective-permute-done.18.refs_2_.stamp_ref.refs_6_
  231.8 4.8 unpack_mid.1
  248.7 16.1 %collective-permute-done.28 = bf16[384,1024]{1,0:T(8,128)(2,1)} collective-permute-done((bf16[384,1024]{1,0:T(8,128)(2,1)}, bf16[384,1024]{1,0:T(8,128)(2,1)}, u32[]{:S(2)}, u32[]{:S(2)}) %collective-permute-start.28) | collective-permute-done | bytes 786464 | tf_op jit(solution)/shard_map/ppermute | solution.py:177
  275.3 20.7 %collective-permute-done.26 = bf16[1024,704]{0,1:T(8,128)(2,1)} collective-permute-done((bf16[1024,704]{0,1:T(8,128)(2,1)}, bf16[1024,704]{0,1:T(8,128)(2,1)}, u32[]{:S(2)}, u32[]{:S(2)}) %collective-permute-start.26) | collective-permute-done | bytes 1441824 | tf_op jit(solution)/shard_map/ppermute | solution.py:121
  304.8 14.6 %self_forward.1 = (f32[4,1,88,1024]{3,2,1,0:T(8,128)S(1)}, f32[4,1,1,1024]{3,2,1,0:T(1,128)S(1)}, bf16[4,4,1,88,256]{4,3,2,1,0:T(8,128)(2,1)S(1)}) custom-call(s32[1,16]{1,0:T(1,128)S(1)} %get-tuple-element.386.first_ref, s32[1,16]{1,0:T(1,128)S(1)} %get-tuple-element.387.last_ref, s32[1]{0:T(128)} %bitcast.7.turned_ref, ...), custom_call_target="tpu_custom_call" | custom-call | flops 10000000000 | bytes 8388608 | tf_op jit(solution)/shard_map/self_forward/pallas_call | solution.py:420
  321.4 5.1 all-to-all-start.4
  334.9 16.1 %collective-permute-done.36.refs_12_.refs_19_ = bf16[352,1408]{1,0:T(8,128)(2,1)} collective-permute-done((bf16[352,1408]{1,0:T(8,128)(2,1)}, bf16[352,1408]{1,0:T(8,128)(2,1)}, u32[]{:S(2)}, u32[]{:S(2)}) %collective-permute-start.36) | collective-permute-done | bytes 991264 | tf_op jit(solution)/shard_map/ppermute | solution.py:121
  350.9 23.3 %collective-permute-done.39.refs_16_.refs_23_ = bf16[352,1408]{1,0:T(8,128)(2,1)} collective-permute-done((bf16[352,1408]{1,0:T(8,128)(2,1)}, bf16[352,1408]{1,0:T(8,128)(2,1)}, u32[]{:S(2)}, u32[]{:S(2)}) %collective-permute-start.39) | collective-permute-done | bytes 991264 | tf_op jit(solution)/shard_map/ppermute | solution.py:121
  379.1 19.7 %middle_forward.1 = (f32[1408,256]{1,0:T(8,128)}, f32[1408,256]{1,0:T(8,128)}, bf16[2,1408,256]{2,1,0:T(8,128)(2,1)}, f32[16,88,256]{2,1,0:T(8,128)}, bf16[16,88...) custom-call(s32[1]{0:T(128)} %bitcast.refs_0_, ...), custom_call_target="tpu_custom_call" | custom-call | flops 5075107840 | bytes 25165824 | tf_op jit(solution)/shard_map/middle_forward/pallas_call | solution.py:1080
  401.9 17.2 %collective-permute-done.43.refs_2_.refs_1_ = bf16[1408,256]{1,0:T(8,128)(2,1)} collective-permute-done((bf16[1408,256]{1,0:T(8,128)(2,1)}, bf16[1408,256]{1,0:T(8,128)(2,1)}, u32[]{:S(2)}, u32[]{:S(2)}) %collective-permute-start.43) | collective-permute-done | bytes 720928 | tf_op jit(solution)/shard_map/ppermute | solution.py:121
  422.8 29.5 %feed_forward.1 = (bf16[1024,1536]{1,0:T(8,128)(2,1)}, bf16[1024,1536]{1,0:T(8,128)(2,1)}, bf16[1408,256]{1,0:T(8,128)(2,1)S(1)}, bf16[1408,256]{1,0:T(8,128)(2,...) custom-call(bf16[1408,256]{1,0:T(8,128)(2,1)S(1)} %copy-done.33, ...), custom_call_target="tpu_custom_call" | custom-call | flops 13287555072 | bytes 25165824 | tf_op jit(solution)/shard_map/feed_forward/pallas_call | solution.py:1284
  455.0 8.6 expand_grads.1.refs_25_.refs_1_
  467.1 11.4 %reduce_grads.1 = (bf16[704,1536]{1,0:T(8,128)(2,1)S(1)}, bf16[704,1536]{1,0:T(8,128)(2,1)}) custom-call(s32[8]{0:T(128)S(1)} %broadcast_xor_fusion.group_ref, bf16[1408,256]{1,0:T(8,128)(2,1)} %turn_over.1.refs_0_.refs_4_.refs_2_, bf16[1408,256]{1,0:T(8,128)(2,1)} %collective-permute-done.17.refs_1_.refs_5_, ...), custom_call_target="tpu_custom_call" | custom-call | flops 4429185024 | bytes 12582912 | tf_op jit(solution)/shard_map/reduce_grads/pallas_call | solution.py:705
  479.2 4.7 collective-permute-done.50
  485.2 23.1 %middle_backward.1 = (f32[1408,256]{1,0:T(8,128)}, bf16[1408,256]{1,0:T(8,128)(2,1)S(1)}, bf16[4,3,352,256]{3,2,1,0:T(8,128)(2,1)}, bf16[4,704,384]{2,1,0:T(8,128)(2,1)}, f32[1408,2]{1,0:T(8,128)S(1)}) custom-call(s32[1]{0:T(128)} %bitcast.refs_0_, f32[1408,256]{1,0:T(8,128)} %convert_add_fusion.2.refs_1_, ...), custom_call_target="tpu_custom_call" | custom-call | flops 7105150976 | bytes 31457280 | tf_op jit(solution)/shard_map/middle_backward/pallas_call | solution.py:1199
  510.1 6.1 all-to-all-start.5
  525.5 15.0 %collective-permute-done.53.refs_1_.refs_18_.refs_2_ = bf16[704,384]{1,0:T(8,128)(2,1)} collective-permute-done((bf16[704,384]{1,0:T(8,128)(2,1)}, bf16[704,384]{1,0:T(8,128)(2,1)}, u32[]{:S(2)}, u32[]{:S(2)}) %collective-permute-start.53) | collective-permute-done | bytes 540704 | tf_op jit(solution)/shard_map/ppermute | solution.py:177
  541.4 10.1 %collective-permute-done.54.refs_2_.refs_19_.refs_3_ = bf16[704,384]{1,0:T(8,128)(2,1)} collective-permute-done((bf16[704,384]{1,0:T(8,128)(2,1)}, bf16[704,384]{1,0:T(8,128)(2,1)}, u32[]{:S(2)}, u32[]{:S(2)}) %collective-permute-start.54) | collective-permute-done | bytes 540704 | tf_op jit(solution)/shard_map/ppermute | solution.py:177
  552.9 23.7 %self_backward.1.refs_20_ = bf16[4,1,3,88,1024]{4,3,2,1,0:T(8,128)(2,1)S(1)} custom-call(s32[1,16]{1,0:T(1,128)S(1)} %get-tuple-element.386.first_ref, s32[1,16]{1,0:T(1,128)S(1)} %get-tuple-element.387.last_ref, s32[1]{0:T(128)S(6)} %select_n.1439.valid_ref, s32[1]{0:T(128)} %bitcast.7.turned_ref, bf16[4,1,3,88,1024]{4,3,2,1,0:T(8,128)(2,1)} %all-to-all-done.3.qkv_ref, ...), custom_call_target="tpu_custom_call" | custom-call | flops 17999998976 | bytes 16777216 | tf_op jit(solution)/shard_map/self_backward/pallas_call | solution.py:442
  578.0 4.8 all-to-all-start.6
  595.9 12.9 %collective-permute-done.70.refs_10_ = bf16[3,352,256]{2,1,0:T(8,128)(2,1)S(1)} collective-permute-done((bf16[3,352,256]{2,1,0:T(8,128)(2,1)S(1)}, bf16[3,352,256]{2,1,0:T(8,128)(2,1)S(1)}, u32[]{:S(2)}, u32[]{:S(2)}) %collective-permute-start.70) | collective-permute-done | bytes 540704 | tf_op jit(solution)/shard_map/ppermute | solution.py:177
  608.8 10.7 %collective-permute-done.71.refs_11_ = bf16[3,352,256]{2,1,0:T(8,128)(2,1)S(1)} collective-permute-done((bf16[3,352,256]{2,1,0:T(8,128)(2,1)S(1)}, bf16[3,352,256]{2,1,0:T(8,128)(2,1)S(1)}, u32[]{:S(2)}, u32[]{:S(2)}) %collective-permute-start.71) | collective-permute-done | bytes 540704 | tf_op jit(solution)/shard_map/ppermute | solution.py:177
  620.8 13.2 %mid_grads.1.refs_5_ = bf16[1408,1664]{1,0:T(8,128)(2,1)} custom-call(bf16[2,1408,256]{2,1,0:T(8,128)(2,1)} %gate.4.refs_0_, bf16[2,1408,256]{2,1,0:T(8,128)(2,1)} %collective-permute-done.65.refs_1_, bf16[2,1408,256]{2,1,0:T(8,128)(2,1)} %collective-permute-done.51.refs_5_.refs_2_, bf16[2,1408,256]{2,1,0:T(8,128)(2,1)} %copy-done.75, ...), custom_call_target="tpu_custom_call" | custom-call | flops 6978273280 | bytes 25165824 | tf_op jit(solution)/shard_map/mid_grads/pallas_call | solution.py:798
  656.9 4.6 convolution_convert_fusion.5
  663.1 7.9 reduce_parts.1
  671.7 7.1 convolution_convert_fusion
  684.2 12.1 %collective-permute-done.84 = bf16[352,1536]{1,0:T(8,128)(2,1)} collective-permute-done((bf16[352,1536]{1,0:T(8,128)(2,1)}, bf16[352,1536]{1,0:T(8,128)(2,1)}, u32[]{:S(2)}, u32[]{:S(2)}) %collective-permute-start.84) | collective-permute-done | bytes 1081376 | tf_op jit(solution)/shard_map/ppermute | solution.py:121
  698.9 5.4 copy.192.refs_8_
  710.4 4.3 start_backward.1
  716.6 4.3 all-to-all-start.7
  725.6 6.3 all-to-all-done.7
  739.6 7.3 skip_grads.1
  770.8 4.6 collective-permute-done.90
  807.2 30.9 %collective-permute-done.75 = bf16[44,1056]{1,0:T(8,128)(2,1)S(1)} collective-permute-done((bf16[44,1056]{1,0:T(8,128)(2,1)S(1)}, bf16[44,1056]{1,0:T(8,128)(2,1)S(1)}, u32[]{:S(2)}, u32[]{:S(2)}) %collective-permute-start.75) | collective-permute-done | bytes 92960 | tf_op jit(solution)/shard_map/ppermute | solution.py:177
  844.0 4.7 convert_add_fusion
  848.8 16.9 %reduce-scatter.6.cloned.1.call-done = bf16[176,1792]{1,0:T(8,128)(2,1)} async-done(((bf16[1408,1792]{1,0:T(8,128)(2,1)}), bf16[176,1792]{1,0:T(8,128)(2,1)}) %reduce-scatter.6.cloned.1.call-update) | async-done | bytes 630800 | tf_op jit(solution)/shard_map/reduce_scatter | solution.py:1832
  874.3 7.5 all-to-all-done.8.blocks_ref
  (595 shorter events, 314.5 us)
Async XLA Ops:
  23.0 103.2 %all-gather.4.cloned.1.call-start = ((), (), s32[]{:S(2)}) async-start(), calls=%async_computation.13 | async-start | bytes 5677056 | tf_op jit(solution)/shard_map/all_gather | solution.py:1482
  32.2 192.8 %all-gather.6.cloned.1.call-start = ((), (), s32[]{:S(2)}) async-start(), calls=%async_computation.14 | async-start | bytes 5271552 | tf_op jit(solution)/shard_map/all_gather | solution.py:1482
  53.4 367.1 %all-gather.8.cloned.1.call-start = ((), (), s32[]{:S(2)}) async-start(), calls=%async_computation.15 | async-start | bytes 9732096 | tf_op jit(solution)/shard_map/all_gather | solution.py:1482
  57.0 69.2 %collective-permute-start = (bf16[256,2816]{1,0:T(8,128)(2,1)S(1)}, bf16[256,2816]{1,0:T(8,128)(2,1)S(1)}, u32[]{:S(2)}, u32[]{:S(2)}) collective-permute-start(bf16[256,2816]{1,0:T(8,128)(2,1)S(1)} %maximum_add_fusion.1.refs_2_.refs_0_), channel_id=1, source_target_pairs={{0,1},{1,0},{2,3},{3,2},{4,5},{5,4},{6,7},{7,6},{8,9},{9,8},{10,11... | collective-permute-start | bytes 4325384 | tf_op jit(solution)/shard_map/ppermute | solution.py:121
  57.1 34.0 %collective-permute-start.1 = (bf16[256,2816]{1,0:T(8,128)(2,1)S(1)}, bf16[256,2816]{1,0:T(8,128)(2,1)S(1)}, u32[]{:S(2)}, u32[]{:S(2)}) collective-permute-start(bf16[256,2816]{1,0:T(8,128)(2,1)S(1)} %maximum_add_fusion.1.refs_2_.refs_0_), channel_id=1, source_target_pairs={{0,2},{1,3},{2,0},{3,1},{4,6},{5,7},{6,4},{7,5},{8,10},{9,11},{10,... | collective-permute-start | bytes 4325384 | tf_op jit(solution)/shard_map/ppermute | solution.py:121
  60.0 36.0 %collective-permute-start.4 = (f32[2,8,1,1408]{3,2,1,0:T(1,128)S(1)}, f32[2,8,1,1408]{3,2,1,0:T(1,128)S(1)}, u32[]{:S(2)}, u32[]{:S(2)}) collective-permute-start(f32[2,8,1,1408]{3,2,1,0:T(1,128)S(1)} %fusion.56), channel_id=1, source_target_pairs={{0,1},{1,0},{2,3},{3,2},{4,5},{5,4},{6,7},{7,6},{8,9},{9,8},{10,11... | collective-permute-start | bytes 270344 | tf_op jit(solution)/shard_map/ppermute | solution.py:121
  204.6 100.2 %all-to-all-start.3 = ((bf16[4,1,3,88,1024]{4,3,2,1,0:T(8,128)(2,1)}), bf16[4,1,3,88,1024]{4,3,2,1,0:T(8,128)(2,1)}, u32[]{:S(2)}, u32[]{:S(2)}) async-start(bf16[4,1,3,88,1024]{4,3,2,1,0:T(8,128)(2,1)} %bitcast.52), calls=%async_computation.3 | async-start | bytes 4325376 | tf_op jit(solution)/shard_map/all_to_all | solution.py:1714
  224.1 40.7 %collective-permute-start.28 = (bf16[384,1024]{1,0:T(8,128)(2,1)}, bf16[384,1024]{1,0:T(8,128)(2,1)}, u32[]{:S(2)}, u32[]{:S(2)}) collective-permute-start(bf16[384,1024]{1,0:T(8,128)(2,1)} %get-tuple-element.64), channel_id=1, source_target_pairs={{0,3},{1,2},{2,1},{3,0},{4,7},{5,6},{6,5},{7,4},{8,11},{9,10},{10,... | collective-permute-start | bytes 2359304 | tf_op jit(solution)/shard_map/ppermute | solution.py:177
  224.3 41.4 %collective-permute-start.30 = (bf16[384,1024]{1,0:T(8,128)(2,1)}, bf16[384,1024]{1,0:T(8,128)(2,1)}, u32[]{:S(2)}, u32[]{:S(2)}) collective-permute-start(bf16[384,1024]{1,0:T(8,128)(2,1)} %get-tuple-element.66), channel_id=1, source_target_pairs={{0,1},{1,0},{2,3},{3,2},{4,5},{5,4},{6,7},{7,6},{8,9},{9,8},{10,11... | collective-permute-start | bytes 2359304 | tf_op jit(solution)/shard_map/ppermute | solution.py:177
  240.4 55.6 %collective-permute-start.26 = (bf16[1024,704]{0,1:T(8,128)(2,1)}, bf16[1024,704]{0,1:T(8,128)(2,1)}, u32[]{:S(2)}, u32[]{:S(2)}) collective-permute-start(bf16[1024,704]{0,1:T(8,128)(2,1)} %copy.181), channel_id=1, source_target_pairs={{0,2},{1,3},{2,0},{3,1},{4,6},{5,7},{6,4},{7,5},{8,10},{9,11},{10,... | collective-permute-start | bytes 4325384 | tf_op jit(solution)/shard_map/ppermute | solution.py:121
  241.3 58.0 %collective-permute-start.31 = (bf16[1024,704]{0,1:T(8,128)(2,1)}, bf16[1024,704]{0,1:T(8,128)(2,1)}, u32[]{:S(2)}, u32[]{:S(2)}) collective-permute-start(bf16[1024,704]{0,1:T(8,128)(2,1)} %copy.181), channel_id=1, source_target_pairs={{0,1},{1,0},{2,3},{3,2},{4,5},{5,4},{6,7},{7,6},{8,9},{9,8},{10,11... | collective-permute-start | bytes 4325384 | tf_op jit(solution)/shard_map/ppermute | solution.py:121
  248.7 54.6 %collective-permute-start.17 = (bf16[1408,256]{1,0:T(8,128)(2,1)}, bf16[1408,256]{1,0:T(8,128)(2,1)}, u32[]{:S(2)}, u32[]{:S(2)}) collective-permute-start(bf16[1408,256]{1,0:T(8,128)(2,1)} %turn_over.1.refs_0_.refs_4_.refs_2_), channel_id=1, source_target_pairs={{0,1},{1,0},{2,3},{3,2},{4,5},{5,4},{6,7},{7,6},{8,9},{9,8},{10,11... | collective-permute-start | bytes 2162696 | tf_op jit(solution)/shard_map/ppermute | solution.py:121
  264.8 69.5 %collective-permute-start.32 = (bf16[352,1408]{1,0:T(8,128)(2,1)}, bf16[352,1408]{1,0:T(8,128)(2,1)}, u32[]{:S(2)}, u32[]{:S(2)}) collective-permute-start(bf16[352,1408]{1,0:T(8,128)(2,1)} %get-tuple-element.68.refs_6_.refs_13_), channel_id=1, source_target_pairs={{0,1},{1,0},{2,3},{3,2},{4,5},{5,4},{6,7},{7,6},{8,9},{9,8},{10,11... | collective-permute-start | bytes 2973704 | tf_op jit(solution)/shard_map/ppermute | solution.py:121
  265.6 37.8 %collective-permute-start.19 = (bf16[1408,256]{1,0:T(8,128)(2,1)}, bf16[1408,256]{1,0:T(8,128)(2,1)}, u32[]{:S(2)}, u32[]{:S(2)}) collective-permute-start(bf16[1408,256]{1,0:T(8,128)(2,1)} %collective-permute-done.18.refs_2_.stamp_ref.refs_6_), channel_id=1, source_target_pairs={{0,1},{1,0},{2,3},{3,2},{4,5},{5,4},{6,7},{7,6},{8,9},{9,8},{10,11... | collective-permute-start | bytes 2162696 | tf_op jit(solution)/shard_map/ppermute | solution.py:121
  296.0 30.7 %collective-permute-start.27 = (bf16[1024,704]{0,1:T(8,128)(2,1)}, bf16[1024,704]{0,1:T(8,128)(2,1)}, u32[]{:S(2)}, u32[]{:S(2)}) collective-permute-start(bf16[1024,704]{0,1:T(8,128)(2,1)} %collective-permute-done.26), channel_id=1, source_target_pairs={{0,1},{1,0},{2,3},{3,2},{4,5},{5,4},{6,7},{7,6},{8,9},{9,8},{10,11... | collective-permute-start | bytes 4325384 | tf_op jit(solution)/shard_map/ppermute | solution.py:121
  299.3 35.0 %collective-permute-start.33 = (bf16[352,1408]{1,0:T(8,128)(2,1)}, bf16[352,1408]{1,0:T(8,128)(2,1)}, u32[]{:S(2)}, u32[]{:S(2)}) collective-permute-start(bf16[352,1408]{1,0:T(8,128)(2,1)} %get-tuple-element.68.refs_6_.refs_13_), channel_id=1, source_target_pairs={{0,2},{1,3},{2,0},{3,1},{4,6},{5,7},{6,4},{7,5},{8,10},{9,11},{10,... | collective-permute-start | bytes 2973704 | tf_op jit(solution)/shard_map/ppermute | solution.py:121
  303.2 72.5 %collective-permute-start.35 = (bf16[352,1408]{1,0:T(8,128)(2,1)}, bf16[352,1408]{1,0:T(8,128)(2,1)}, u32[]{:S(2)}, u32[]{:S(2)}) collective-permute-start(bf16[352,1408]{1,0:T(8,128)(2,1)} %get-tuple-element.69.refs_10_.refs_17_), channel_id=1, source_target_pairs={{0,1},{1,0},{2,3},{3,2},{4,5},{5,4},{6,7},{7,6},{8,9},{9,8},{10,11... | collective-permute-start | bytes 2973704 | tf_op jit(solution)/shard_map/ppermute | solution.py:121
  303.5 47.5 %collective-permute-start.36 = (bf16[352,1408]{1,0:T(8,128)(2,1)}, bf16[352,1408]{1,0:T(8,128)(2,1)}, u32[]{:S(2)}, u32[]{:S(2)}) collective-permute-start(bf16[352,1408]{1,0:T(8,128)(2,1)} %get-tuple-element.69.refs_10_.refs_17_), channel_id=1, source_target_pairs={{0,2},{1,3},{2,0},{3,1},{4,6},{5,7},{6,4},{7,5},{8,10},{9,11},{10,... | collective-permute-start | bytes 2973704 | tf_op jit(solution)/shard_map/ppermute | solution.py:121
  321.4 54.3 %all-to-all-start.4 = ((bf16[16,1,88,256]{3,2,1,0:T(8,128)(2,1)}), bf16[16,1,88,256]{3,2,1,0:T(8,128)(2,1)}, u32[]{:S(2)}, u32[]{:S(2)}) async-start(bf16[16,1,88,256]{3,2,1,0:T(8,128)(2,1)} %bitcast.361), calls=%async_computation.4 | async-start | bytes 1441792 | tf_op jit(solution)/shard_map/all_to_all | solution.py:1770
  326.5 320.1 %reduce-scatter.4.cloned.1.call-start = ((), (), s32[]{:S(2)}) async-start(), calls=%async_computation.16 | async-start | bytes 4866048 | tf_op jit(solution)/shard_map/reduce_scatter | solution.py:1832
  326.7 47.5 %collective-permute-start.39 = (bf16[352,1408]{1,0:T(8,128)(2,1)}, bf16[352,1408]{1,0:T(8,128)(2,1)}, u32[]{:S(2)}, u32[]{:S(2)}) collective-permute-start(bf16[352,1408]{1,0:T(8,128)(2,1)} %get-tuple-element.70.refs_14_.refs_21_), channel_id=1, source_target_pairs={{0,2},{1,3},{2,0},{3,1},{4,6},{5,7},{6,4},{7,5},{8,10},{9,11},{10,... | collective-permute-start | bytes 2973704 | tf_op jit(solution)/shard_map/ppermute | solution.py:121
  334.3 44.8 %collective-permute-start.38 = (bf16[352,1408]{1,0:T(8,128)(2,1)}, bf16[352,1408]{1,0:T(8,128)(2,1)}, u32[]{:S(2)}, u32[]{:S(2)}) collective-permute-start(bf16[352,1408]{1,0:T(8,128)(2,1)} %get-tuple-element.70.refs_14_.refs_21_), channel_id=1, source_target_pairs={{0,1},{1,0},{2,3},{3,2},{4,5},{5,4},{6,7},{7,6},{8,9},{9,8},{10,11... | collective-permute-start | bytes 2973704 | tf_op jit(solution)/shard_map/ppermute | solution.py:121
  334.4 44.7 %collective-permute-start.34 = (bf16[352,1408]{1,0:T(8,128)(2,1)}, bf16[352,1408]{1,0:T(8,128)(2,1)}, u32[]{:S(2)}, u32[]{:S(2)}) collective-permute-start(bf16[352,1408]{1,0:T(8,128)(2,1)} %collective-permute-done.33.refs_8_.refs_15_), channel_id=1, source_target_pairs={{0,1},{1,0},{2,3},{3,2},{4,5},{5,4},{6,7},{7,6},{8,9},{9,8},{10,11... | collective-permute-start | bytes 2973704 | tf_op jit(solution)/shard_map/ppermute | solution.py:121
  350.9 28.2 %collective-permute-start.37 = (bf16[352,1408]{1,0:T(8,128)(2,1)}, bf16[352,1408]{1,0:T(8,128)(2,1)}, u32[]{:S(2)}, u32[]{:S(2)}) collective-permute-start(bf16[352,1408]{1,0:T(8,128)(2,1)} %collective-permute-done.36.refs_12_.refs_19_), channel_id=1, source_target_pairs={{0,1},{1,0},{2,3},{3,2},{4,5},{5,4},{6,7},{7,6},{8,9},{9,8},{10,11... | collective-permute-start | bytes 2973704 | tf_op jit(solution)/shard_map/ppermute | solution.py:121
  419.1 35.9 %collective-permute-start.51 = (bf16[2,1408,256]{2,1,0:T(8,128)(2,1)}, bf16[2,1408,256]{2,1,0:T(8,128)(2,1)}, u32[]{:S(2)}, u32[]{:S(2)}) collective-permute-start(bf16[2,1408,256]{2,1,0:T(8,128)(2,1)} %gate.4.refs_0_), channel_id=1, source_target_pairs={{0,2},{1,3},{2,0},{3,1},{4,6},{5,7},{6,4},{7,5},{8,10},{9,11},{10,... | collective-permute-start | bytes 4325384 | tf_op jit(solution)/shard_map/ppermute | solution.py:121
  478.4 73.1 %collective-permute-start.55 = (bf16[704,1536]{1,0:T(8,128)(2,1)}, bf16[704,1536]{1,0:T(8,128)(2,1)}, u32[]{:S(2)}, u32[]{:S(2)}) collective-permute-start(bf16[704,1536]{1,0:T(8,128)(2,1)} %get-tuple-element.86.refs_27_), channel_id=1, source_target_pairs={{0,16},{16,0},{1,17},{17,1},{2,18},{18,2},{3,19},{19,3},{4,20},{20... | collective-permute-start | bytes 6488072 | tf_op jit(solution)/shard_map/ppermute | solution.py:121
  510.1 41.5 %all-to-all-start.5 = ((bf16[16,1,88,256]{3,2,1,0:T(8,128)(2,1)}), bf16[16,1,88,256]{3,2,1,0:T(8,128)(2,1)}, u32[]{:S(2)}, u32[]{:S(2)}) async-start(bf16[16,1,88,256]{3,2,1,0:T(8,128)(2,1)} %bitcast.360), calls=%async_computation.5 | async-start | bytes 1441792 | tf_op jit(solution)/shard_map/all_to_all | solution.py:1920
  524.7 26.9 %collective-permute-start.54 = (bf16[704,384]{1,0:T(8,128)(2,1)}, bf16[704,384]{1,0:T(8,128)(2,1)}, u32[]{:S(2)}, u32[]{:S(2)}) collective-permute-start(bf16[704,384]{1,0:T(8,128)(2,1)} %get-tuple-element.249), channel_id=1, source_target_pairs={{0,3},{1,2},{2,1},{3,0},{4,7},{5,6},{6,5},{7,4},{8,11},{9,10},{10,... | collective-permute-start | bytes 1622024 | tf_op jit(solution)/shard_map/ppermute | solution.py:177
  524.9 61.0 %collective-permute-start.67 = (bf16[1408,256]{1,0:T(8,128)(2,1)}, bf16[1408,256]{1,0:T(8,128)(2,1)}, u32[]{:S(2)}, u32[]{:S(2)}) collective-permute-start(bf16[1408,256]{1,0:T(8,128)(2,1)} %bitcast.58.refs_1_.refs_4_), channel_id=1, source_target_pairs={{0,1},{1,0},{2,3},{3,2},{4,5},{5,4},{6,7},{7,6},{8,9},{9,8},{10,11... | collective-permute-start | bytes 2162696 | tf_op jit(solution)/shard_map/ppermute | solution.py:121
  525.4 68.3 %collective-permute-start.65 = (bf16[2,1408,256]{2,1,0:T(8,128)(2,1)}, bf16[2,1408,256]{2,1,0:T(8,128)(2,1)}, u32[]{:S(2)}, u32[]{:S(2)}) collective-permute-start(bf16[2,1408,256]{2,1,0:T(8,128)(2,1)} %gate.4.refs_0_), channel_id=1, source_target_pairs={{0,1},{1,0},{2,3},{3,2},{4,5},{5,4},{6,7},{7,6},{8,9},{9,8},{10,11... | collective-permute-start | bytes 4325384 | tf_op jit(solution)/shard_map/ppermute | solution.py:121
  540.6 50.9 %collective-permute-start.73 = (bf16[1024,384]{1,0:T(8,128)(2,1)}, bf16[1024,384]{1,0:T(8,128)(2,1)}, u32[]{:S(2)}, u32[]{:S(2)}) collective-permute-start(bf16[1024,384]{1,0:T(8,128)(2,1)} %gate.5.refs_12_), channel_id=1, source_target_pairs={{0,2},{1,3},{2,0},{3,1},{4,6},{5,7},{6,4},{7,5},{8,10},{9,11},{10,... | collective-permute-start | bytes 2359304 | tf_op jit(solution)/shard_map/ppermute | solution.py:121
  578.0 70.5 %all-to-all-start.6 = ((bf16[4,1,3,88,1024]{4,3,2,1,0:T(8,128)(2,1)}), bf16[4,1,3,88,1024]{4,3,2,1,0:T(8,128)(2,1)}, u32[]{:S(2)}, u32[]{:S(2)}) async-start(bf16[4,1,3,88,1024]{4,3,2,1,0:T(8,128)(2,1)} %copy-done.20), calls=%async_computation.6 | async-start | bytes 4325376 | tf_op jit(solution)/shard_map/all_to_all | solution.py:1717
  582.8 213.0 %reduce-scatter.8.cloned.1.call-start = ((), (), s32[]{:S(2)}) async-start(), calls=%async_computation.18 | async-start | bytes 5271552 | tf_op jit(solution)/shard_map/reduce_scatter | solution.py:1832
  585.9 33.6 %collective-permute-start.66 = (bf16[2,1408,256]{2,1,0:T(8,128)(2,1)}, bf16[2,1408,256]{2,1,0:T(8,128)(2,1)S(1)}, u32[]{:S(2)}, u32[]{:S(2)}) collective-permute-start(bf16[2,1408,256]{2,1,0:T(8,128)(2,1)} %collective-permute-done.51.refs_5_.refs_2_), channel_id=1, source_target_pairs={{0,1},{1,0},{2,3},{3,2},{4,5},{5,4},{6,7},{7,6},{8,9},{9,8},{10,11... | collective-permute-start | bytes 4325384 | tf_op jit(solution)/shard_map/ppermute | solution.py:121
  591.5 27.9 %collective-permute-start.74 = (bf16[1024,384]{1,0:T(8,128)(2,1)}, bf16[1024,384]{1,0:T(8,128)(2,1)S(1)}, u32[]{:S(2)}, u32[]{:S(2)}) collective-permute-start(bf16[1024,384]{1,0:T(8,128)(2,1)} %collective-permute-done.73.refs_14_), channel_id=1, source_target_pairs={{0,1},{1,0},{2,3},{3,2},{4,5},{5,4},{6,7},{7,6},{8,9},{9,8},{10,11... | collective-permute-start | bytes 2359304 | tf_op jit(solution)/shard_map/ppermute | solution.py:121
  640.6 55.8 %collective-permute-start.84 = (bf16[352,1536]{1,0:T(8,128)(2,1)}, bf16[352,1536]{1,0:T(8,128)(2,1)}, u32[]{:S(2)}, u32[]{:S(2)}) collective-permute-start(bf16[352,1536]{1,0:T(8,128)(2,1)} %slice.454), channel_id=1, source_target_pairs={{0,4},{4,0},{8,12},{12,8},{1,5},{5,1},{9,13},{13,9},{2,6},{6,2},{1... | collective-permute-start | bytes 3244040 | tf_op jit(solution)/shard_map/ppermute | solution.py:121
  671.1 49.8 %collective-permute-start.56 = (bf16[1408,256]{1,0:T(8,128)(2,1)}, bf16[1408,256]{1,0:T(8,128)(2,1)}, u32[]{:S(2)}, u32[]{:S(2)}) collective-permute-start(bf16[1408,256]{1,0:T(8,128)(2,1)} %get-tuple-element.93), channel_id=1, source_target_pairs={{0,1},{1,0},{2,3},{3,2},{4,5},{5,4},{6,7},{7,6},{8,9},{9,8},{10,11... | collective-permute-start | bytes 2162696 | tf_op jit(solution)/shard_map/ppermute | solution.py:121
  671.5 36.0 %collective-permute-start.59 = (bf16[1408,256]{1,0:T(8,128)(2,1)}, bf16[1408,256]{1,0:T(8,128)(2,1)}, u32[]{:S(2)}, u32[]{:S(2)}) collective-permute-start(bf16[1408,256]{1,0:T(8,128)(2,1)} %get-tuple-element.243), channel_id=1, source_target_pairs={{0,1},{1,0},{2,3},{3,2},{4,5},{5,4},{6,7},{7,6},{8,9},{9,8},{10,11... | collective-permute-start | bytes 2162696 | tf_op jit(solution)/shard_map/ppermute | solution.py:121
  683.1 37.9 %collective-permute-start.58 = (bf16[1408,256]{1,0:T(8,128)(2,1)}, bf16[1408,256]{1,0:T(8,128)(2,1)}, u32[]{:S(2)}, u32[]{:S(2)}) collective-permute-start(bf16[1408,256]{1,0:T(8,128)(2,1)} %add_convert_fusion.7), channel_id=1, source_target_pairs={{0,2},{1,3},{2,0},{3,1},{4,6},{5,7},{6,4},{7,5},{8,10},{9,11},{10,... | collective-permute-start | bytes 2162696 | tf_op jit(solution)/shard_map/ppermute | solution.py:121
  706.2 53.0 %collective-permute-start.85 = (bf16[176,1536]{1,0:T(8,128)(2,1)}, bf16[176,1536]{1,0:T(8,128)(2,1)}, u32[]{:S(2)}, u32[]{:S(2)}) collective-permute-start(bf16[176,1536]{1,0:T(8,128)(2,1)} %slice.457), channel_id=1, source_target_pairs={{0,8},{4,12},{8,0},{12,4},{1,9},{5,13},{9,1},{13,5},{2,10},{6,14},... | collective-permute-start | bytes 1622024 | tf_op jit(solution)/shard_map/ppermute | solution.py:121
  720.9 144.8 %reduce-scatter.6.cloned.1.call-start = ((), (), s32[]{:S(2)}) async-start(), calls=%async_computation.17 | async-start | bytes 5677056 | tf_op jit(solution)/shard_map/reduce_scatter | solution.py:1832
  737.0 62.2 %collective-permute-start.63 = (bf16[256,2816]{1,0:T(8,128)(2,1)}, bf16[256,2816]{1,0:T(8,128)(2,1)}, u32[]{:S(2)}, u32[]{:S(2)}) collective-permute-start(bf16[256,2816]{1,0:T(8,128)(2,1)} %convolution_convert_fusion.1), channel_id=1, source_target_pairs={{0,1},{1,0},{2,3},{3,2},{4,5},{5,4},{6,7},{7,6},{8,9},{9,8},{10,11... | collective-permute-start | bytes 4325384 | tf_op jit(solution)/shard_map/ppermute | solution.py:121
  739.1 104.9 %collective-permute-start.62 = (bf16[256,2816]{1,0:T(8,128)(2,1)}, bf16[256,2816]{1,0:T(8,128)(2,1)}, u32[]{:S(2)}, u32[]{:S(2)}) collective-permute-start(bf16[256,2816]{1,0:T(8,128)(2,1)} %convolution_convert_fusion.3), channel_id=1, source_target_pairs={{0,1},{1,0},{2,3},{3,2},{4,5},{5,4},{6,7},{7,6},{8,9},{9,8},{10,11... | collective-permute-start | bytes 4325384 | tf_op jit(solution)/shard_map/ppermute | solution.py:121
  750.1 41.0 %all-to-all-start.9 = ((f32[32,1,1408]{2,1,0:T(1,128)}), f32[32,1,1408]{2,1,0:T(1,128)S(1)}, u32[]{:S(2)}, u32[]{:S(2)}) async-start(f32[32,1,1408]{2,1,0:T(1,128)} %broadcast_in_dim.207), calls=%async_computation.11 | async-start | bytes 360448 | tf_op jit(solution)/shard_map/all_to_all | solution.py:252
  802.2 41.8 %collective-permute-start.64 = (bf16[256,2816]{1,0:T(8,128)(2,1)S(1)}, bf16[256,2816]{1,0:T(8,128)(2,1)}, u32[]{:S(2)}, u32[]{:S(2)}) collective-permute-start(bf16[256,2816]{1,0:T(8,128)(2,1)S(1)} %add_convert_fusion.1), channel_id=1, source_target_pairs={{0,2},{1,3},{2,0},{3,1},{4,6},{5,7},{6,4},{7,5},{8,10},{9,11},{10,... | collective-permute-start | bytes 4325384 | tf_op jit(solution)/shard_map/ppermute | solution.py:121
  803.9 34.2 %collective-permute-start.75 = (bf16[44,1056]{1,0:T(8,128)(2,1)S(1)}, bf16[44,1056]{1,0:T(8,128)(2,1)S(1)}, u32[]{:S(2)}, u32[]{:S(2)}) collective-permute-start(bf16[44,1056]{1,0:T(8,128)(2,1)S(1)} %get-tuple-element.303), channel_id=1, source_target_pairs={{0,3},{1,2},{2,1},{3,0},{4,7},{5,6},{6,5},{7,4},{8,11},{9,10},{10,... | collective-permute-start | bytes 278792 | tf_op jit(solution)/shard_map/ppermute | solution.py:177
  804.0 36.7 %collective-permute-start.76 = (bf16[44,1056]{1,0:T(8,128)(2,1)S(1)}, bf16[44,1056]{1,0:T(8,128)(2,1)S(1)}, u32[]{:S(2)}, u32[]{:S(2)}) collective-permute-start(bf16[44,1056]{1,0:T(8,128)(2,1)S(1)} %get-tuple-element.304), channel_id=1, source_target_pairs={{0,2},{1,3},{2,0},{3,1},{4,6},{5,7},{6,4},{7,5},{8,10},{9,11},{10,... | collective-permute-start | bytes 278792 | tf_op jit(solution)/shard_map/ppermute | solution.py:177
  805.3 35.4 %collective-permute-start.77 = (bf16[44,1056]{1,0:T(8,128)(2,1)S(1)}, bf16[44,1056]{1,0:T(8,128)(2,1)S(1)}, u32[]{:S(2)}, u32[]{:S(2)}) collective-permute-start(bf16[44,1056]{1,0:T(8,128)(2,1)S(1)} %get-tuple-element.302), channel_id=1, source_target_pairs={{0,1},{1,0},{2,3},{3,2},{4,5},{5,4},{6,7},{7,6},{8,9},{9,8},{10,11... | collective-permute-start | bytes 278792 | tf_op jit(solution)/shard_map/ppermute | solution.py:177
  (144 other events, 1177.2 us)
Sparse Core Ops, SparseCore 0:
  32.4 84.8 all-gather.3
  119.9 77.2 all-gather.5
  199.4 181.5 all-gather.7
  463.8 104.3 reduce-scatter.3
  635.4 124.0 reduce-scatter.7
  763.5 102.1 reduce-scatter.5
